TPU v7x, 32 devices: a whole 2x2x4 slice. The times are simulated.
32 devices in a mesh: member: 2 (over x), tile: 16 (over z, y, core).
Axes of the slice: x: 2, y: 2, z: 4, core: 2. Of those that a mesh axis runs over, the one named last changes fastest.
Arguments:
- state: float32 [32, 6, 6, 128, 128], P(('member', 'tile')), parts along dimension 0, may hold values from -6 to 6
- wave_coef: float32 [3], replicated, may hold values from 0.08 to 0.3
- visc_coef: float32 [3], replicated, may hold values from 0.03 to 0.2
- stencil_start: int32 [3, 128], replicated, may hold values from 0 to 124, as said below
- stencil_offset: float32 [3, 128], replicated, may hold values from 0.5 to 2.5
Outputs:
- new_state: float32 [32, 6, 6, 128, 128], P(('member', 'tile')), parts along dimension 0
There are 2 independent parts, one for each index of `member`. A program takes and returns all parts, laid end to end along the dimension named above; an argument that names none is the same for every part. Nothing has to cross between parts.
Inputs may be any that keep to these rules, and one draw needn't show every extreme that they name: stencil_start[h, k] lies within one cell of k - 1, kept inside the segment.
All inputs are finite; a program needn't handle non-finite values.
Results may differ from a plain program's by a relative error of at most 0.0001.
Values sent between devices are 32-bit elements; how exact they have to be, the bound alone decides.
No kernel may reach another device: no remote copies, remote signals or barrier semaphores. Data moves between devices by JAX's collectives and lax.ppermute only.
A program may use at most 128 MiB of HBM per device.

v0:
```python
import math

import jax
import jax.numpy as jnp
from jax import lax
from jax.sharding import PartitionSpec as P

SUBSTEPS = 4


HALO_WEIGHTS = (0.45, 0.35, 0.2)


def from_behind(x, axis, by):
    size = lax.axis_size(axis)
    pairs = [(i, i + by) for i in range(size) if 0 <= i + by < size]
    return lax.ppermute(x, axis, pairs)


def lagrange_weights(offset_value):
    return (
        -(offset_value - 1.0) * (offset_value - 2.0) * (offset_value - 3.0) / 6.0,
        offset_value * (offset_value - 2.0) * (offset_value - 3.0) / 2.0,
        -offset_value * (offset_value - 1.0) * (offset_value - 3.0) / 2.0,
        offset_value * (offset_value - 1.0) * (offset_value - 2.0) / 6.0,
    )


def interp_matrix(stencil_start, stencil_offset):
    halo_depth, seg_width = stencil_start.shape
    source_rows = jnp.arange(seg_width, dtype=jnp.int32)[None, :, None]
    matrix = jnp.zeros((halo_depth, seg_width, seg_width), jnp.float32)
    for shift_count, weight_row in enumerate(lagrange_weights(stencil_offset)):
        chosen = source_rows == stencil_start[:, None, :] + shift_count
        matrix = matrix + jnp.where(chosen, weight_row[:, None, :], 0.0)
    return matrix


def edge_strips(field_data, halo_depth):
    strip_east = jnp.swapaxes(jnp.flip(field_data[..., -halo_depth:], -1), -1, -2)
    strip_west = jnp.swapaxes(field_data[..., :halo_depth], -1, -2)
    strip_north = jnp.flip(field_data[..., -halo_depth:, :], -2)
    strip_south = field_data[..., :halo_depth, :]
    return (strip_east, strip_west, strip_north, strip_south)


def apply_operator(field_data, ghost_east, ghost_west, ghost_north, ghost_south):
    halo_depth = len(HALO_WEIGHTS)
    row_count = field_data.shape[-2]
    col_count = field_data.shape[-1]
    wide_grid = jnp.concatenate(
        [
            jnp.swapaxes(jnp.flip(ghost_west, -2), -1, -2),
            field_data,
            jnp.swapaxes(ghost_east, -1, -2),
        ],
        axis=-1,
    )
    tall_grid = jnp.concatenate([jnp.flip(ghost_south, -2), field_data, ghost_north], axis=-2)
    tendency = jnp.zeros_like(field_data)
    for reach, weight_value in enumerate(HALO_WEIGHTS, start=1):
        left_cells = wide_grid[..., halo_depth - reach : halo_depth - reach + col_count]
        right_cells = wide_grid[..., halo_depth + reach : halo_depth + reach + col_count]
        lower_cells = tall_grid[..., halo_depth - reach : halo_depth - reach + row_count, :]
        upper_cells = tall_grid[..., halo_depth + reach : halo_depth + reach + row_count, :]
        tendency = tendency + weight_value * (
            left_cells + right_cells + lower_cells + upper_cells - 4.0 * field_data
        )
    return tendency


def advance_fields(field_data, tendency, wave_coef, visc_coef):
    levels = wave_coef.shape[0]
    rate_new = (
        field_data[:, levels:]
        + wave_coef[:, None, None] * tendency[:, :levels]
        + visc_coef[:, None, None] * tendency[:, levels:]
    )
    pres_new = field_data[:, :levels] + rate_new
    return jnp.concatenate([pres_new, rate_new], axis=1)


def alternate_faces(even_faces, odd_faces):
    joined = jnp.stack([even_faces, odd_faces], axis=1)
    return joined.reshape((2 * even_faces.shape[0],) + even_faces.shape[1:])


def interp_block(raw_ghost, matrix):
    return jnp.einsum("fchj,hjk->fchk", raw_ghost, matrix, precision=lax.Precision.HIGHEST)


def turn_step(pair_data, move_first, move_second, step_by):
    sent = jnp.stack(
        [jnp.where(move_first, pair_data[0], 0.0), jnp.where(move_second, pair_data[1], 0.0)]
    )
    came = from_behind(sent, "tile", step_by)
    kept = jnp.stack(
        [jnp.where(move_first, 0.0, pair_data[0]), jnp.where(move_second, 0.0, pair_data[1])]
    )
    return kept + came


def on_device(state, wave_coef, visc_coef, stencil_start, stencil_offset):
    side = math.isqrt(lax.axis_size("tile"))
    bit_count = side.bit_length() - 1
    index_now = lax.axis_index("tile")
    col_pos = index_now % side
    row_pos = index_now // side
    matrix = interp_matrix(stencil_start, stencil_offset)
    dist_first = side - 1 - (row_pos - col_pos)
    dist_second = side - 1 - (col_pos - row_pos)
    current = state[0]
    for step_index in range(SUBSTEPS):
        strip_east, strip_west, strip_north, strip_south = edge_strips(current, len(HALO_WEIGHTS))
        inner = []
        for strip_data, step_by in (
            (strip_west, -1),
            (strip_east, 1),
            (strip_south, -side),
            (strip_north, side),
        ):
            inner.append(from_behind(strip_data, "tile", step_by))
        from_east, from_west, from_north, from_south = inner
        seams = []
        for strip_data, step_by in (
            (strip_west[1::2], side - 1),
            (strip_east[0::2], 1 - side),
            (jnp.roll(strip_south, -2, 0)[0::2], side * (side - 1)),
            (jnp.roll(strip_north, 1, 0)[0::2], -side * (side - 1)),
        ):
            seams.append(from_behind(strip_data, "tile", step_by))
        seam_east, seam_west, seam_north, seam_south = seams
        climb_first = jnp.roll(strip_west, -2, 0)[0::2]
        climb_second = jnp.roll(strip_south, -3, 0)[0::2]
        fall_first = jnp.roll(strip_north, 2, 0)[0::2]
        fall_second = jnp.roll(strip_east, 1, 0)[0::2]
        climb_pair = jnp.stack(
            [jnp.where(col_pos == 0, climb_first, 0.0), jnp.where(row_pos == 0, climb_second, 0.0)]
        )
        fall_pair = jnp.stack(
            [
                jnp.where(row_pos == side - 1, fall_first, 0.0),
                jnp.where(col_pos == side - 1, fall_second, 0.0),
            ]
        )
        for bit_index in range(bit_count):
            stride = (1 << bit_index) * (side + 1)
            move_first = dist_first >> bit_index & 1 == 1
            move_second = dist_second >> bit_index & 1 == 1
            climb_pair = turn_step(climb_pair, move_first, move_second, stride)
            fall_pair = turn_step(fall_pair, move_first, move_second, -stride)
        got_climb_first, got_climb_second = (climb_pair[0], climb_pair[1])
        got_fall_first, got_fall_second = (fall_pair[0], fall_pair[1])
        edge_east = interp_block(alternate_faces(seam_east, jnp.flip(got_climb_second, -1)), matrix)
        edge_west = interp_block(alternate_faces(jnp.flip(got_fall_first, -1), seam_west), matrix)
        edge_north = interp_block(
            alternate_faces(jnp.flip(got_climb_first, -1), seam_north), matrix
        )
        edge_south = interp_block(
            alternate_faces(seam_south, jnp.flip(got_fall_second, -1)), matrix
        )
        ghost_east = jnp.where(col_pos == side - 1, edge_east, from_east)
        ghost_west = jnp.where(col_pos == 0, edge_west, from_west)
        ghost_north = jnp.where(row_pos == side - 1, edge_north, from_north)
        ghost_south = jnp.where(row_pos == 0, edge_south, from_south)
        tendency = apply_operator(current, ghost_east, ghost_west, ghost_north, ghost_south)
        current = advance_fields(current, tendency, wave_coef, visc_coef)
    return current[None]


def solution(mesh):
    placed = (P(("member", "tile"), None, None, None, None), P(), P(), P(), P())
    return jax.shard_map(
        on_device,
        mesh=mesh,
        in_specs=placed,
        out_specs=P(("member", "tile"), None, None, None, None),
        check_vma=False,
    )
```

profile of v0, /device:TPU:0, one launch (start us, length us, event | category | flops | bytes accessed | tf_op | source)
XLA Modules:
  0.0 613.7 jit_solution(8511528254706143198)
XLA Ops:
  5.9 8.1 %collective-permute-start.10 = (f32[3,6,3,128]{3,1,2,0:T(8,128)}, f32[3,6,3,128]{3,1,2,0:T(8,128)}, u32[]{:S(2)}, u32[]{:S(2)}) collective-permute-start(f32[3,6,3,128]{3,1,2,0:T(8,128)} %copy.542), channel_id=1, source_target_pairs={{0,12},{1,13},{2,14},{3,15},{16,28},{17,29},{18,30},{19,31}} | collective-permute-start | bytes 82952 | tf_op jit(solution)/shard_map/ppermute | solution.py:17
  17.7 5.8 rev.99
  52.7 4.9 collective-permute-start.5
  59.9 4.2 collective-permute-start.6
  65.0 5.0 collective-permute-start.9
  81.6 5.0 fusion.64
  99.8 13.4 %fusion.5 = f32[6,6,128,128]{3,1,0,2:T(8,128)S(1)} fusion(f32[6,6,3,128]{3,1,0,2:T(8,128)S(1)} %fusion.79, f32[6,6,3,128]{3,1,0,2:T(8,128)S(1)} %rev.105, f32[6,6,128,128]{3,1,0,2:T(8,128)S(1)} %bitcast.316, f32[6,6,128,3]{3,1,0,2:T(8,128)} %fusion.64, f32[6,6,128,3]{3,1,0,2:T(8,128)} %copy.347), kind=kLoop, calls=%fused_computation.104 | loop fusion | flops 17694720 | bytes 4939776 | tf_op jit(solution)/shard_map/add | solution.py:66
  122.3 5.8 rev.107
  143.7 9.3 %collective-permute-start.22 = (f32[3,6,3,128]{3,1,2,0:T(8,128)}, f32[3,6,3,128]{3,1,2,0:T(8,128)}, u32[]{:S(2)}, u32[]{:S(2)}) collective-permute-start(f32[3,6,3,128]{3,1,2,0:T(8,128)} %copy.545), channel_id=1, source_target_pairs={{0,12},{1,13},{2,14},{3,15},{16,28},{17,29},{18,30},{19,31}} | collective-permute-start | bytes 82952 | tf_op jit(solution)/shard_map/ppermute | solution.py:17
  184.2 6.9 %collective-permute-start.17 = (f32[2,3,6,3,128]{4,0,3,2,1:T(2,128)S(1)}, f32[2,3,6,3,128]{4,0,3,2,1:T(2,128)S(1)}, u32[]{:S(2)}, u32[]{:S(2)}) collective-permute-start(f32[2,3,6,3,128]{4,0,3,2,1:T(2,128)S(1)} %pad_maximum_fusion.61), channel_id=1, source_target_pairs={{0,5},{1,6},{2,7},{3,8},{4,9},{5,10},{6,11},{7,12},{8,13},{9,14},{... | collective-permute-start | bytes 165896 | tf_op jit(solution)/shard_map/ppermute | solution.py:17
  206.5 8.2 %collective-permute-start.18 = (f32[2,3,6,3,128]{4,0,3,2,1:T(2,128)S(1)}, f32[2,3,6,3,128]{4,0,3,2,1:T(2,128)}, u32[]{:S(2)}, u32[]{:S(2)}) collective-permute-start(f32[2,3,6,3,128]{4,0,3,2,1:T(2,128)S(1)} %pad_maximum_fusion.63), channel_id=1, source_target_pairs={{0,10},{1,11},{2,12},{3,13},{4,14},{5,15},{16,26},{17,27},{18,28},... | collective-permute-start | bytes 165896 | tf_op jit(solution)/shard_map/ppermute | solution.py:17
  220.5 11.1 %copy.398 = f32[3,128,6,6]{0,3,2,1:T(8,128)} copy(f32[3,128,6,6]{1,3,2,0:T(8,128)} %fusion.96) | data formatting | bytes 110592 | tf_op jit(solution)/shard_map/fchj,hjk->fchk/dot_general | solution.py:89
  237.9 5.8 rev.109
  247.6 6.8 %maximum_maximum_fusion = (f32[6,6,128,131]{3,1,0,2:T(8,128)}, f32[6,6,128,131]{3,1,0,2:T(8,128)}) fusion(f32[6,3,128,128]{3,1,0,2:T(4,128)S(1)} %get-tuple-element.12, f32[6,3,128,128]{3,1,0,2:T(4,128)S(1)} %get-tuple-element.11, f32[6,6,128,3]{3,1,0,2:T(8,128)S(1)} %bitcast.331, f32[6,6,128,3]{3,1,0,2:T(8,128)S(1)} %fusion.63), kind=kLoop, calls=%fused_computation.83 | loop fusion | flops 2414592 | bytes 7299072 | tf_op jit(solution)/shard_map/concatenate | solution.py:51
  260.5 22.0 %fusion.50 = f32[6,6,128,128]{3,1,0,2:T(8,128)} fusion(f32[6,6,131,128]{3,1,0,2:T(8,128)} %get-tuple-element.44, f32[6,6,131,128]{3,1,0,2:T(8,128)} %get-tuple-element.43, f32[6,6,128,131]{3,1,0,2:T(8,128)} %get-tuple-element.42, f32[6,6,128,131]{3,1,0,2:T(8,128)} %get-tuple-element.41, f32[6,3,128,128]{3,1,0,2:T(4,128)S(1)} %get-tuple-element.12, ...), kind=kLoop, calls=%fused_computation.168 | loop fusion | flops 11206656 | bytes 33030144 | tf_op jit(solution)/shard_map/add | solution.py:66
  282.4 4.8 fusion.146
  292.2 5.8 rev.115
  313.6 7.7 %collective-permute-start.34 = (f32[3,6,3,128]{3,1,2,0:T(8,128)}, f32[3,6,3,128]{3,1,2,0:T(8,128)}, u32[]{:S(2)}, u32[]{:S(2)}) collective-permute-start(f32[3,6,3,128]{3,1,2,0:T(8,128)} %copy.548), channel_id=1, source_target_pairs={{0,12},{1,13},{2,14},{3,15},{16,28},{17,29},{18,30},{19,31}} | collective-permute-start | bytes 82952 | tf_op jit(solution)/shard_map/ppermute | solution.py:17
  352.9 8.1 %collective-permute-start.29 = (f32[2,3,6,3,128]{4,0,3,2,1:T(2,128)S(1)}, f32[2,3,6,3,128]{4,0,3,2,1:T(2,128)S(1)}, u32[]{:S(2)}, u32[]{:S(2)}) collective-permute-start(f32[2,3,6,3,128]{4,0,3,2,1:T(2,128)S(1)} %pad_maximum_fusion.66), channel_id=1, source_target_pairs={{0,5},{1,6},{2,7},{3,8},{4,9},{5,10},{6,11},{7,12},{8,13},{9,14},{... | collective-permute-start | bytes 165896 | tf_op jit(solution)/shard_map/ppermute | solution.py:17
  375.1 8.5 %collective-permute-start.30 = (f32[2,3,6,3,128]{4,0,3,2,1:T(2,128)S(1)}, f32[2,3,6,3,128]{4,0,3,2,1:T(2,128)}, u32[]{:S(2)}, u32[]{:S(2)}) collective-permute-start(f32[2,3,6,3,128]{4,0,3,2,1:T(2,128)S(1)} %pad_maximum_fusion.68), channel_id=1, source_target_pairs={{0,10},{1,11},{2,12},{3,13},{4,14},{5,15},{16,26},{17,27},{18,28},... | collective-permute-start | bytes 165896 | tf_op jit(solution)/shard_map/ppermute | solution.py:17
  399.2 5.8 rev.117
  408.9 6.8 %maximum_maximum_fusion.1 = (f32[6,6,128,131]{3,1,0,2:T(8,128)}, f32[6,6,128,131]{3,1,0,2:T(8,128)}) fusion(f32[6,3,128,128]{3,1,0,2:T(4,128)S(1)} %get-tuple-element.10, f32[6,3,128,128]{3,1,0,2:T(4,128)S(1)} %get-tuple-element.9, f32[6,6,128,3]{3,1,0,2:T(8,128)S(1)} %bitcast.332, f32[6,6,128,3]{3,1,0,2:T(8,128)S(1)} %fusion.62), kind=kLoop, calls=%fused_computation.85 | loop fusion | flops 2414592 | bytes 7299072 | tf_op jit(solution)/shard_map/concatenate | solution.py:51
  421.8 22.0 %fusion.42 = f32[6,6,128,128]{3,1,0,2:T(8,128)} fusion(f32[6,6,131,128]{3,1,0,2:T(8,128)} %get-tuple-element.30, f32[6,6,131,128]{3,1,0,2:T(8,128)} %get-tuple-element.29, f32[6,6,128,131]{3,1,0,2:T(8,128)} %get-tuple-element.28, f32[6,6,128,131]{3,1,0,2:T(8,128)} %get-tuple-element.27, f32[6,3,128,128]{3,1,0,2:T(4,128)S(1)} %get-tuple-element.10, ...), kind=kLoop, calls=%fused_computation.151 | loop fusion | flops 11206656 | bytes 33030144 | tf_op jit(solution)/shard_map/add | solution.py:66
  443.7 4.8 fusion.144
  453.2 5.8 rev.123
  482.0 7.6 %collective-permute-start.46 = (f32[3,6,3,128]{3,1,2,0:T(8,128)}, f32[3,6,3,128]{3,1,2,0:T(8,128)}, u32[]{:S(2)}, u32[]{:S(2)}) collective-permute-start(f32[3,6,3,128]{3,1,2,0:T(8,128)} %copy.551), channel_id=1, source_target_pairs={{0,12},{1,13},{2,14},{3,15},{16,28},{17,29},{18,30},{19,31}} | collective-permute-start | bytes 82952 | tf_op jit(solution)/shard_map/ppermute | solution.py:17
  511.5 4.2 collective-permute-start.39
  516.6 7.1 %collective-permute-start.41 = (f32[2,3,6,3,128]{4,0,3,2,1:T(2,128)}, f32[2,3,6,3,128]{4,0,3,2,1:T(2,128)S(1)}, u32[]{:S(2)}, u32[]{:S(2)}) collective-permute-start(f32[2,3,6,3,128]{4,0,3,2,1:T(2,128)} %pad_maximum_fusion.71), channel_id=1, source_target_pairs={{0,5},{1,6},{2,7},{3,8},{4,9},{5,10},{6,11},{7,12},{8,13},{9,14},{... | collective-permute-start | bytes 165896 | tf_op jit(solution)/shard_map/ppermute | solution.py:17
  538.5 8.7 %collective-permute-start.42 = (f32[2,3,6,3,128]{4,0,3,2,1:T(2,128)}, f32[2,3,6,3,128]{4,0,3,2,1:T(2,128)}, u32[]{:S(2)}, u32[]{:S(2)}) collective-permute-start(f32[2,3,6,3,128]{4,0,3,2,1:T(2,128)} %pad_maximum_fusion.73), channel_id=1, source_target_pairs={{0,10},{1,11},{2,12},{3,13},{4,14},{5,15},{16,26},{17,27},{18,28},... | collective-permute-start | bytes 165896 | tf_op jit(solution)/shard_map/ppermute | solution.py:17
  562.4 5.8 rev.125
  572.0 6.8 %maximum_maximum_fusion.2 = (f32[6,6,128,131]{3,1,0,2:T(8,128)}, f32[6,6,128,131]{3,1,0,2:T(8,128)}) fusion(f32[6,3,128,128]{3,1,0,2:T(4,128)S(1)} %get-tuple-element.8, f32[6,3,128,128]{3,1,0,2:T(4,128)S(1)} %get-tuple-element.7, f32[6,6,128,3]{3,1,0,2:T(8,128)S(1)} %bitcast.330, f32[6,6,128,3]{3,1,0,2:T(8,128)S(1)} %fusion.61), kind=kLoop, calls=%fused_computation.87 | loop fusion | flops 2414592 | bytes 7299072 | tf_op jit(solution)/shard_map/concatenate | solution.py:51
  584.9 21.9 %fusion.34 = f32[6,6,128,128]{3,1,0,2:T(8,128)} fusion(f32[6,6,131,128]{3,1,0,2:T(8,128)} %get-tuple-element.16, f32[6,6,131,128]{3,1,0,2:T(8,128)} %get-tuple-element.15, f32[6,6,128,131]{3,1,0,2:T(8,128)} %get-tuple-element.14, f32[6,6,128,131]{3,1,0,2:T(8,128)} %get-tuple-element.13, f32[6,3,128,128]{3,1,0,2:T(4,128)S(1)} %get-tuple-element.8, ...), kind=kLoop, calls=%fused_computation.134 | loop fusion | flops 11206656 | bytes 33030144 | tf_op jit(solution)/shard_map/add | solution.py:66
  (570 shorter events, 346.1 us)
Async XLA Ops:
  3.9 84.9 %collective-permute-start.8 = (f32[3,6,3,128]{3,1,0,2:T(8,128)}, f32[3,6,3,128]{3,1,0,2:T(8,128)}, u32[]{:S(2)}, u32[]{:S(2)}) collective-permute-start(f32[3,6,3,128]{3,1,0,2:T(8,128)} %slice.742), channel_id=1, source_target_pairs={{12,0},{13,1},{14,2},{15,3},{28,16},{29,17},{30,18},{31,19}} | collective-permute-start | bytes 82952 | tf_op jit(solution)/shard_map/ppermute | solution.py:17
  5.9 89.5 %collective-permute-start.10 = (f32[3,6,3,128]{3,1,2,0:T(8,128)}, f32[3,6,3,128]{3,1,2,0:T(8,128)}, u32[]{:S(2)}, u32[]{:S(2)}) collective-permute-start(f32[3,6,3,128]{3,1,2,0:T(8,128)} %copy.542), channel_id=1, source_target_pairs={{0,12},{1,13},{2,14},{3,15},{16,28},{17,29},{18,30},{19,31}} | collective-permute-start | bytes 82952 | tf_op jit(solution)/shard_map/ppermute | solution.py:17
  25.9 68.3 %collective-permute-start.3 = (f32[6,6,3,128]{3,1,0,2:T(8,128)S(1)}, f32[6,6,3,128]{3,1,0,2:T(8,128)}, u32[]{:S(2)}, u32[]{:S(2)}) collective-permute-start(f32[6,6,3,128]{3,1,0,2:T(8,128)S(1)} %bitcast.333), channel_id=1, source_target_pairs={{0,1},{1,2},{2,3},{3,4},{4,5},{5,6},{6,7},{7,8},{8,9},{9,10},{10,1... | collective-permute-start | bytes 165896 | tf_op jit(solution)/shard_map/ppermute | solution.py:17
  28.8 23.9 %collective-permute-start = (f32[2,3,6,3,128]{4,0,3,2,1:T(2,128)}, f32[2,3,6,3,128]{4,0,3,2,1:T(2,128)}, u32[]{:S(2)}, u32[]{:S(2)}) collective-permute-start(f32[2,3,6,3,128]{4,0,3,2,1:T(2,128)} %pad_maximum_fusion.53), channel_id=1, source_target_pairs={{5,0},{6,1},{7,2},{8,3},{9,4},{10,5},{11,6},{12,7},{13,8},{14,9},{... | collective-permute-start | bytes 165896 | tf_op jit(solution)/shard_map/ppermute | solution.py:17
  33.1 31.8 %collective-permute-start.7 = (f32[6,6,3,128]{3,1,2,0:T(8,128)}, f32[6,6,3,128]{3,1,2,0:T(8,128)}, u32[]{:S(2)}, u32[]{:S(2)}) collective-permute-start(f32[6,6,3,128]{3,1,2,0:T(8,128)} %copy.362), channel_id=1, source_target_pairs={{1,0},{2,1},{3,2},{4,3},{5,4},{6,5},{7,6},{8,7},{9,8},{10,9},{11,1... | collective-permute-start | bytes 165896 | tf_op jit(solution)/shard_map/ppermute | solution.py:17
  65.0 26.2 %collective-permute-start.9 = (f32[6,6,3,128]{3,1,0,2:T(8,128)S(1)}, f32[6,6,3,128]{3,1,0,2:T(8,128)}, u32[]{:S(2)}, u32[]{:S(2)}) collective-permute-start(f32[6,6,3,128]{3,1,0,2:T(8,128)S(1)} %rev.104), channel_id=1, source_target_pairs={{0,4},{1,5},{2,6},{3,7},{4,8},{5,9},{6,10},{7,11},{8,12},{9,13},{1... | collective-permute-start | bytes 165896 | tf_op jit(solution)/shard_map/ppermute | solution.py:17
  141.6 36.7 %collective-permute-start.20 = (f32[3,6,3,128]{3,1,2,0:T(8,128)}, f32[3,6,3,128]{3,1,2,0:T(8,128)}, u32[]{:S(2)}, u32[]{:S(2)}) collective-permute-start(f32[3,6,3,128]{3,1,2,0:T(8,128)} %slice.792), channel_id=1, source_target_pairs={{12,0},{13,1},{14,2},{15,3},{28,16},{29,17},{30,18},{31,19}} | collective-permute-start | bytes 82952 | tf_op jit(solution)/shard_map/ppermute | solution.py:17
  143.7 111.3 %collective-permute-start.22 = (f32[3,6,3,128]{3,1,2,0:T(8,128)}, f32[3,6,3,128]{3,1,2,0:T(8,128)}, u32[]{:S(2)}, u32[]{:S(2)}) collective-permute-start(f32[3,6,3,128]{3,1,2,0:T(8,128)} %copy.545), channel_id=1, source_target_pairs={{0,12},{1,13},{2,14},{3,15},{16,28},{17,29},{18,30},{19,31}} | collective-permute-start | bytes 82952 | tf_op jit(solution)/shard_map/ppermute | solution.py:17
  153.7 100.8 %collective-permute-start.21 = (f32[6,6,3,128]{3,1,0,2:T(8,128)}, f32[6,6,3,128]{3,1,0,2:T(8,128)}, u32[]{:S(2)}, u32[]{:S(2)}) collective-permute-start(f32[6,6,3,128]{3,1,0,2:T(8,128)} %rev.112), channel_id=1, source_target_pairs={{0,4},{1,5},{2,6},{3,7},{4,8},{5,9},{6,10},{7,11},{8,12},{9,13},{1... | collective-permute-start | bytes 165896 | tf_op jit(solution)/shard_map/ppermute | solution.py:17
  163.5 16.8 %collective-permute-start.14 = (f32[3,6,3,128]{3,1,2,0:T(8,128)}, f32[3,6,3,128]{3,1,2,0:T(8,128)}, u32[]{:S(2)}, u32[]{:S(2)}) collective-permute-start(f32[3,6,3,128]{3,1,2,0:T(8,128)} %copy.378), channel_id=1, source_target_pairs={{3,0},{4,1},{5,2},{6,3},{7,4},{8,5},{9,6},{10,7},{11,8},{12,9},{13... | collective-permute-start | bytes 82952 | tf_op jit(solution)/shard_map/ppermute | solution.py:17
  165.5 18.7 %collective-permute-start.12 = (f32[2,3,6,3,128]{4,0,3,2,1:T(2,128)}, f32[2,3,6,3,128]{4,0,3,2,1:T(2,128)}, u32[]{:S(2)}, u32[]{:S(2)}) collective-permute-start(f32[2,3,6,3,128]{4,0,3,2,1:T(2,128)} %pad_maximum_fusion.59), channel_id=1, source_target_pairs={{5,0},{6,1},{7,2},{8,3},{9,4},{10,5},{11,6},{12,7},{13,8},{14,9},{... | collective-permute-start | bytes 165896 | tf_op jit(solution)/shard_map/ppermute | solution.py:17
  178.3 21.3 %collective-permute-start.19 = (f32[6,6,3,128]{3,1,2,0:T(8,128)}, f32[6,6,3,128]{3,1,2,0:T(8,128)}, u32[]{:S(2)}, u32[]{:S(2)}) collective-permute-start(f32[6,6,3,128]{3,1,2,0:T(8,128)} %copy.399), channel_id=1, source_target_pairs={{1,0},{2,1},{3,2},{4,3},{5,4},{6,5},{7,6},{8,7},{9,8},{10,9},{11,1... | collective-permute-start | bytes 165896 | tf_op jit(solution)/shard_map/ppermute | solution.py:17
  180.4 14.1 %collective-permute-start.15 = (f32[6,6,3,128]{3,1,2,0:T(8,128)}, f32[6,6,3,128]{3,1,2,0:T(8,128)S(1)}, u32[]{:S(2)}, u32[]{:S(2)}) collective-permute-start(f32[6,6,3,128]{3,1,2,0:T(8,128)} %copy.383), channel_id=1, source_target_pairs={{0,1},{1,2},{2,3},{3,4},{4,5},{5,6},{6,7},{7,8},{8,9},{9,10},{10,1... | collective-permute-start | bytes 165896 | tf_op jit(solution)/shard_map/ppermute | solution.py:17
  195.2 60.6 %collective-permute-start.23 = (f32[6,6,3,128]{3,1,0,2:T(8,128)S(1)}, f32[6,6,3,128]{3,1,0,2:T(8,128)}, u32[]{:S(2)}, u32[]{:S(2)}) collective-permute-start(f32[6,6,3,128]{3,1,0,2:T(8,128)S(1)} %copy-done.15), channel_id=1, source_target_pairs={{4,0},{5,1},{6,2},{7,3},{8,4},{9,5},{10,6},{11,7},{12,8},{13,9},{1... | collective-permute-start | bytes 165896 | tf_op jit(solution)/shard_map/ppermute | solution.py:17
  199.6 18.4 %collective-permute-start.16 = (f32[3,6,3,128]{3,1,2,0:T(8,128)}, f32[3,6,3,128]{3,1,2,0:T(8,128)}, u32[]{:S(2)}, u32[]{:S(2)}) collective-permute-start(f32[3,6,3,128]{3,1,2,0:T(8,128)} %copy.385), channel_id=1, source_target_pairs={{0,3},{1,4},{2,5},{3,6},{4,7},{5,8},{6,9},{7,10},{8,11},{9,12},{10... | collective-permute-start | bytes 82952 | tf_op jit(solution)/shard_map/ppermute | solution.py:17
  311.5 35.2 %collective-permute-start.32 = (f32[3,6,3,128]{3,1,2,0:T(8,128)}, f32[3,6,3,128]{3,1,2,0:T(8,128)}, u32[]{:S(2)}, u32[]{:S(2)}) collective-permute-start(f32[3,6,3,128]{3,1,2,0:T(8,128)} %slice.842), channel_id=1, source_target_pairs={{12,0},{13,1},{14,2},{15,3},{28,16},{29,17},{30,18},{31,19}} | collective-permute-start | bytes 82952 | tf_op jit(solution)/shard_map/ppermute | solution.py:17
  313.6 102.7 %collective-permute-start.34 = (f32[3,6,3,128]{3,1,2,0:T(8,128)}, f32[3,6,3,128]{3,1,2,0:T(8,128)}, u32[]{:S(2)}, u32[]{:S(2)}) collective-permute-start(f32[3,6,3,128]{3,1,2,0:T(8,128)} %copy.548), channel_id=1, source_target_pairs={{0,12},{1,13},{2,14},{3,15},{16,28},{17,29},{18,30},{19,31}} | collective-permute-start | bytes 82952 | tf_op jit(solution)/shard_map/ppermute | solution.py:17
  321.9 93.8 %collective-permute-start.33 = (f32[6,6,3,128]{3,1,0,2:T(8,128)}, f32[6,6,3,128]{3,1,0,2:T(8,128)}, u32[]{:S(2)}, u32[]{:S(2)}) collective-permute-start(f32[6,6,3,128]{3,1,0,2:T(8,128)} %rev.120), channel_id=1, source_target_pairs={{0,4},{1,5},{2,6},{3,7},{4,8},{5,9},{6,10},{7,11},{8,12},{9,13},{1... | collective-permute-start | bytes 165896 | tf_op jit(solution)/shard_map/ppermute | solution.py:17
  332.0 16.8 %collective-permute-start.26 = (f32[3,6,3,128]{3,1,2,0:T(8,128)}, f32[3,6,3,128]{3,1,2,0:T(8,128)}, u32[]{:S(2)}, u32[]{:S(2)}) collective-permute-start(f32[3,6,3,128]{3,1,2,0:T(8,128)} %copy.418), channel_id=1, source_target_pairs={{3,0},{4,1},{5,2},{6,3},{7,4},{8,5},{9,6},{10,7},{11,8},{12,9},{13... | collective-permute-start | bytes 82952 | tf_op jit(solution)/shard_map/ppermute | solution.py:17
  333.9 19.0 %collective-permute-start.24 = (f32[2,3,6,3,128]{4,0,3,2,1:T(2,128)}, f32[2,3,6,3,128]{4,0,3,2,1:T(2,128)}, u32[]{:S(2)}, u32[]{:S(2)}) collective-permute-start(f32[2,3,6,3,128]{4,0,3,2,1:T(2,128)} %pad_maximum_fusion.64), channel_id=1, source_target_pairs={{5,0},{6,1},{7,2},{8,3},{9,4},{10,5},{11,6},{12,7},{13,8},{14,9},{... | collective-permute-start | bytes 165896 | tf_op jit(solution)/shard_map/ppermute | solution.py:17
  346.7 22.7 %collective-permute-start.31 = (f32[6,6,3,128]{3,1,2,0:T(8,128)}, f32[6,6,3,128]{3,1,2,0:T(8,128)}, u32[]{:S(2)}, u32[]{:S(2)}) collective-permute-start(f32[6,6,3,128]{3,1,2,0:T(8,128)} %copy.439), channel_id=1, source_target_pairs={{1,0},{2,1},{3,2},{4,3},{5,4},{6,5},{7,6},{8,7},{9,8},{10,9},{11,1... | collective-permute-start | bytes 165896 | tf_op jit(solution)/shard_map/ppermute | solution.py:17
  348.8 15.5 %collective-permute-start.27 = (f32[6,6,3,128]{3,1,2,0:T(8,128)}, f32[6,6,3,128]{3,1,2,0:T(8,128)S(1)}, u32[]{:S(2)}, u32[]{:S(2)}) collective-permute-start(f32[6,6,3,128]{3,1,2,0:T(8,128)} %copy.423), channel_id=1, source_target_pairs={{0,1},{1,2},{2,3},{3,4},{4,5},{5,6},{6,7},{7,8},{8,9},{9,10},{10,1... | collective-permute-start | bytes 165896 | tf_op jit(solution)/shard_map/ppermute | solution.py:17
  365.0 52.0 %collective-permute-start.35 = (f32[6,6,3,128]{3,1,0,2:T(8,128)S(1)}, f32[6,6,3,128]{3,1,0,2:T(8,128)}, u32[]{:S(2)}, u32[]{:S(2)}) collective-permute-start(f32[6,6,3,128]{3,1,0,2:T(8,128)S(1)} %copy-done.16), channel_id=1, source_target_pairs={{4,0},{5,1},{6,2},{7,3},{8,4},{9,5},{10,6},{11,7},{12,8},{13,9},{1... | collective-permute-start | bytes 165896 | tf_op jit(solution)/shard_map/ppermute | solution.py:17
  369.4 17.5 %collective-permute-start.28 = (f32[3,6,3,128]{3,1,2,0:T(8,128)}, f32[3,6,3,128]{3,1,2,0:T(8,128)}, u32[]{:S(2)}, u32[]{:S(2)}) collective-permute-start(f32[3,6,3,128]{3,1,2,0:T(8,128)} %copy.425), channel_id=1, source_target_pairs={{0,3},{1,4},{2,5},{3,6},{4,7},{5,8},{6,9},{7,10},{8,11},{9,12},{10... | collective-permute-start | bytes 82952 | tf_op jit(solution)/shard_map/ppermute | solution.py:17
  479.7 29.7 %collective-permute-start.44 = (f32[3,6,3,128]{3,1,2,0:T(8,128)}, f32[3,6,3,128]{3,1,2,0:T(8,128)}, u32[]{:S(2)}, u32[]{:S(2)}) collective-permute-start(f32[3,6,3,128]{3,1,2,0:T(8,128)} %slice.892), channel_id=1, source_target_pairs={{12,0},{13,1},{14,2},{15,3},{28,16},{29,17},{30,18},{31,19}} | collective-permute-start | bytes 82952 | tf_op jit(solution)/shard_map/ppermute | solution.py:17
  482.0 97.4 %collective-permute-start.46 = (f32[3,6,3,128]{3,1,2,0:T(8,128)}, f32[3,6,3,128]{3,1,2,0:T(8,128)}, u32[]{:S(2)}, u32[]{:S(2)}) collective-permute-start(f32[3,6,3,128]{3,1,2,0:T(8,128)} %copy.551), channel_id=1, source_target_pairs={{0,12},{1,13},{2,14},{3,15},{16,28},{17,29},{18,30},{19,31}} | collective-permute-start | bytes 82952 | tf_op jit(solution)/shard_map/ppermute | solution.py:17
  490.2 88.6 %collective-permute-start.45 = (f32[6,6,3,128]{3,1,0,2:T(8,128)}, f32[6,6,3,128]{3,1,0,2:T(8,128)}, u32[]{:S(2)}, u32[]{:S(2)}) collective-permute-start(f32[6,6,3,128]{3,1,0,2:T(8,128)} %rev.128), channel_id=1, source_target_pairs={{0,4},{1,5},{2,6},{3,7},{4,8},{5,9},{6,10},{7,11},{8,12},{9,13},{1... | collective-permute-start | bytes 165896 | tf_op jit(solution)/shard_map/ppermute | solution.py:17
  502.1 14.5 %collective-permute-start.36 = (f32[2,3,6,3,128]{4,0,3,2,1:T(2,128)}, f32[2,3,6,3,128]{4,0,3,2,1:T(2,128)}, u32[]{:S(2)}, u32[]{:S(2)}) collective-permute-start(f32[2,3,6,3,128]{4,0,3,2,1:T(2,128)} %pad_maximum_fusion.69), channel_id=1, source_target_pairs={{5,0},{6,1},{7,2},{8,3},{9,4},{10,5},{11,6},{12,7},{13,8},{14,9},{... | collective-permute-start | bytes 165896 | tf_op jit(solution)/shard_map/ppermute | solution.py:17
  509.5 24.4 %collective-permute-start.43 = (f32[6,6,3,128]{3,1,2,0:T(8,128)}, f32[6,6,3,128]{3,1,2,0:T(8,128)S(1)}, u32[]{:S(2)}, u32[]{:S(2)}) collective-permute-start(f32[6,6,3,128]{3,1,2,0:T(8,128)} %copy.479), channel_id=1, source_target_pairs={{1,0},{2,1},{3,2},{4,3},{5,4},{6,5},{7,6},{8,7},{9,8},{10,9},{11,1... | collective-permute-start | bytes 165896 | tf_op jit(solution)/shard_map/ppermute | solution.py:17
  511.5 17.2 %collective-permute-start.39 = (f32[6,6,3,128]{3,1,2,0:T(8,128)}, f32[6,6,3,128]{3,1,2,0:T(8,128)S(1)}, u32[]{:S(2)}, u32[]{:S(2)}) collective-permute-start(f32[6,6,3,128]{3,1,2,0:T(8,128)} %copy.463), channel_id=1, source_target_pairs={{0,1},{1,2},{2,3},{3,4},{4,5},{5,6},{6,7},{7,8},{8,9},{9,10},{10,1... | collective-permute-start | bytes 165896 | tf_op jit(solution)/shard_map/ppermute | solution.py:17
  529.4 50.8 %collective-permute-start.47 = (f32[6,6,3,128]{3,1,0,2:T(8,128)S(1)}, f32[6,6,3,128]{3,1,0,2:T(8,128)}, u32[]{:S(2)}, u32[]{:S(2)}) collective-permute-start(f32[6,6,3,128]{3,1,0,2:T(8,128)S(1)} %copy-done.14), channel_id=1, source_target_pairs={{4,0},{5,1},{6,2},{7,3},{8,4},{9,5},{10,6},{11,7},{12,8},{13,9},{1... | collective-permute-start | bytes 165896 | tf_op jit(solution)/shard_map/ppermute | solution.py:17
  533.8 16.6 %collective-permute-start.40 = (f32[3,6,3,128]{3,1,2,0:T(8,128)}, f32[3,6,3,128]{3,1,2,0:T(8,128)}, u32[]{:S(2)}, u32[]{:S(2)}) collective-permute-start(f32[3,6,3,128]{3,1,2,0:T(8,128)} %copy.465), channel_id=1, source_target_pairs={{0,3},{1,4},{2,5},{3,6},{4,7},{5,8},{6,9},{7,10},{8,11},{9,12},{10... | collective-permute-start | bytes 82952 | tf_op jit(solution)/shard_map/ppermute | solution.py:17
  (88 other events, 1588.6 us)
where the time goes:
time: 624 us; the launch traced here: 614 us
  local copies, waits for them, and re-layouts  234 us (38%)
  other arithmetic  198 us (32%)
  starting transfers between devices  155 us (25%)
  matrix products  17.8 us (3%)
  waiting for transfers between devices  6.33 us (1%)
    ppermute x48, starting transfers between devices, from_behind(): return lax.ppermute(x, axis, pairs)  155 us
    add x4, other arithmetic, apply_operator(): tendency + weight_value * (left_cells + right_cells + lower_cells + upper...  79.3 us
    slice x16, local copies, waits for them, and re-layouts, on_device(): climb_first = jnp.roll(strip_west, -2, 0)[0::2]  32.1 us
    dot_general x7, local copies, waits for them, and re-layouts, interp_block(): jnp.einsum('fchj,hjk->fchk', raw_ghost, matrix, precision=lax.Precision.H...  27 us
    rev x5, local copies, waits for them, and re-layouts, edge_strips(): jnp.flip(field_data[..., -halo_depth:], -1)  25.7 us
    ppermute x13, local copies, waits for them, and re-layouts, from_behind(): return lax.ppermute(x, axis, pairs)  25.2 us
    slice x13, local copies, waits for them, and re-layouts, on_device(): fall_second = jnp.roll(strip_east, 1, 0)[0::2]  22.1 us
    concatenate x3, other arithmetic, apply_operator(): jnp.concatenate([jnp.swapaxes(jnp.flip(ghost_west, -2), -1, -2), field_da...  20.5 us
  transfers between devices with their start and end apart: 48, of which 6 were waited for; matrix products, arithmetic and copies ran while one was open for 40% of the time, Pallas kernels for 0%

commit v1 on v0

v1 whole, which is shorter than its diff:
```python
import math

import jax
import jax.numpy as jnp
from jax import lax
from jax.experimental import pallas as pl
from jax.experimental.pallas import tpu as pltpu
from jax.sharding import PartitionSpec as P

SUBSTEPS = 4
FACES = 6
LEV = 3
DEPTH = 3
BLK = 128
PER_FACE = LEV * DEPTH
ROWS = 56
HALF = 64
WEST, EAST, SOUTH, NORTH = 0, 1, 2, 3
SCALE = 20.0
VMEM_LIMIT = 50 * 1024 * 1024


def whole_vmem():
    return pl.BlockSpec(memory_space=pltpu.VMEM)


def iota(shape, dim):
    return lax.broadcasted_iota(jnp.int32, shape, dim)


def weight_of(distance):
    return jnp.where(
        distance == 1, 9.0, jnp.where(distance == 2, 7.0, jnp.where(distance == 3, 4.0, 0.0))
    )


def split2(x):
    high = x.astype(jnp.bfloat16)
    low = (x - high.astype(jnp.float32)).astype(jnp.bfloat16)
    return high, low


def lagrange_weights(t):
    return (
        -(t - 1.0) * (t - 2.0) * (t - 3.0) / 6.0,
        t * (t - 2.0) * (t - 3.0) / 2.0,
        -t * (t - 1.0) * (t - 3.0) / 2.0,
        t * (t - 1.0) * (t - 2.0) / 6.0,
    )


def band_matrix():
    gap = jnp.abs(iota((BLK, BLK), 0) - iota((BLK, BLK), 1))
    return jnp.where(gap == 0, -40.0, weight_of(gap)).astype(jnp.bfloat16)


def edge_matrix():
    shape = (BLK, BLK)
    to, src = iota(shape, 0), iota(shape, 1)
    lower = to < HALF
    to_row = jnp.where(lower, to, to - HALF)
    src_row = jnp.where(src < HALF, src, src - HALF)
    to_plane = (to_row * 171) >> 9
    src_plane = (src_row * 171) >> 9
    to_j = to_row - 3 * to_plane
    src_j = src_row - 3 * src_plane
    same = ((to < HALF) == (src < HALF)) & (to_plane == src_plane)
    distance = jnp.where(lower, 3 + to_j - src_j, 3 + src_j - to_j)
    return jnp.where(same, weight_of(distance), 0.0).astype(jnp.bfloat16)


def seam_matrices(start_ref, offset_ref, out_ref):
    j = iota((BLK, BLK), 0)
    back = BLK - 1 - j
    for h in range(DEPTH):
        first = start_ref[h : h + 1, :]
        weights = lagrange_weights(offset_ref[h : h + 1, :])
        plain = jnp.zeros((BLK, BLK), jnp.float32)
        turned = jnp.zeros((BLK, BLK), jnp.float32)
        for m, weight in enumerate(weights):
            plain = plain + jnp.where(j == first + m, weight, 0.0)
            turned = turned + jnp.where(back == first + m, weight, 0.0)
        out_ref[:, h * BLK : (h + 1) * BLK] = plain
        out_ref[:, (DEPTH + h) * BLK : (DEPTH + h + 1) * BLK] = turned


def position(side):
    index = lax.axis_index("tile")
    return lax.rem(index, side), lax.div(index, side)


def row_codes(shape):
    row = iota(shape, 0)
    block = (row * 57) >> 9
    odd = (block & 1) == 1
    depth = row - 3 * ((row * 171) >> 9)
    return odd, depth


def take_edges(q, plane, columns, strips_ref):
    lane = iota((BLK, BLK), 1)
    low, high = 3 * plane, HALF + 3 * plane
    columns = jnp.where((lane >= low) & (lane < low + 3), pltpu.roll(q, low, 1), columns)
    turn = (high - (BLK - 3)) % BLK
    columns = jnp.where((lane >= high) & (lane < high + 3), pltpu.roll(q, turn, 1), columns)
    face, level = divmod(plane, LEV)
    strips_ref[SOUTH, face, 3 * level : 3 * level + 3, :] = q[:3, :]
    strips_ref[NORTH, face, 3 * level : 3 * level + 3, :] = q[BLK - 3 :, :]
    return columns


def pack(columns, strips_ref, side, outs):
    core_ref, mirror_ref, near_ref, far_ref, turn_ref, own_a_ref, own_b_ref = outs
    col, row = position(side)
    edges = columns.T
    for face in range(FACES):
        at = PER_FACE * face
        strips_ref[WEST, face, :PER_FACE, :] = edges[at : at + PER_FACE, :]
        strips_ref[EAST, face, :PER_FACE, :] = edges[HALF + at : HALF + at + PER_FACE, :]
    even_col, even_row = lax.rem(col, 2) == 0, lax.rem(row, 2) == 0

    def shift(place):
        return jnp.where(place == 0, 1, jnp.where(place == side - 1, FACES - 1, 0))

    plans = (
        (core_ref, jnp.where(even_col, EAST, WEST), 0),
        (mirror_ref, jnp.where(even_col, WEST, EAST), shift(col)),
        (near_ref, jnp.where(even_row, NORTH, SOUTH), 0),
        (far_ref, jnp.where(even_row, SOUTH, NORTH), shift(row)),
    )
    for out_ref, which, by in plans:
        for face in range(FACES):
            at = PER_FACE * face
            source = face + by
            source = jnp.where(source >= FACES, source - FACES, source)
            out_ref[at : at + PER_FACE, :] = strips_ref[which, source, :PER_FACE, :]
        out_ref[FACES * PER_FACE :, :] = jnp.zeros((ROWS - FACES * PER_FACE, BLK), jnp.float32)
    for face in range(FACES):
        at = PER_FACE * face
        if face % 2:
            a, b = (SOUTH, face + 2), (EAST, face - 2)
        else:
            a, b = (NORTH, face - 2), (WEST, face + 2)
        own_a_ref[at : at + PER_FACE, :] = strips_ref[a[0], a[1] % FACES, :PER_FACE, :]
        own_b_ref[at : at + PER_FACE, :] = strips_ref[b[0], b[1] % FACES, :PER_FACE, :]
    rest = jnp.zeros((ROWS - FACES * PER_FACE, BLK), jnp.float32)
    own_a_ref[FACES * PER_FACE :, :] = rest
    own_b_ref[FACES * PER_FACE :, :] = rest
    odd, _ = row_codes((ROWS, BLK))
    use_a = jnp.where(odd, (row == 0).astype(jnp.int32), (row == side - 1).astype(jnp.int32))
    turn_ref[...] = jnp.where(use_a == 1, own_a_ref[...], own_b_ref[...])


def first_kernel(side, wave_ref, visc_ref, state_ref, start_ref, offset_ref, *rest):
    matrix_ref, outs, strips_ref = rest[0], rest[1:-1], rest[-1]
    seam_matrices(start_ref, offset_ref, matrix_ref)
    columns = jnp.zeros((BLK, BLK), jnp.float32)
    for plane in range(FACES * LEV):
        face, level = divmod(plane, LEV)
        a, b = wave_ref[level] * (1.0 / SCALE), visc_ref[level] * (1.0 / SCALE)
        q = a * state_ref[face, level] + b * state_ref[face, LEV + level]
        columns = take_edges(q, plane, columns, strips_ref)
    pack(columns, strips_ref, side, outs)


def ghosts_of(side, received, own_a_ref, own_b_ref, matrix_ref):
    core, mirror, near, far, turned = [ref[...] for ref in received]
    col, row = position(side)
    even_col, even_row = lax.rem(col, 2) == 0, lax.rem(row, 2) == 0
    odd, depth = row_codes((ROWS, BLK))
    alone = ((row == 0) & (col == side - 1)) | ((col == 0) & (row == side - 1))
    turned_a = jnp.where(alone, own_a_ref[...], turned)
    turned_b = jnp.where(alone, own_b_ref[...], turned)
    sides = (
        (jnp.where(even_col, mirror, core), turned_a, col == 0, False, True),
        (jnp.where(even_col, core, mirror), turned_a, col == side - 1, True, False),
        (jnp.where(even_row, far, near), turned_b, row == 0, True, True),
        (jnp.where(even_row, near, far), turned_b, row == side - 1, False, False),
    )
    raws = []
    for straight, crossed, at_seam, turned_odd, _ in sides:
        is_turned = odd if turned_odd else ~odd
        raws.append(jnp.where(at_seam & is_turned, crossed, straight))
    mixed = jnp.dot(
        jnp.concatenate(raws, axis=0),
        matrix_ref[...],
        precision=lax.Precision.HIGHEST,
        preferred_element_type=jnp.float32,
    )
    ghosts = []
    for place, (_, _, at_seam, turned_odd, reverse) in enumerate(sides):
        part = mixed[place * ROWS : (place + 1) * ROWS, :]
        is_turned = odd if turned_odd else ~odd
        made = raws[place]
        for h in range(DEPTH):
            index = (DEPTH - 1 - h) if reverse else h
            plain = part[:, h * BLK : (h + 1) * BLK]
            turn = part[:, (DEPTH + h) * BLK : (DEPTH + h + 1) * BLK]
            made = jnp.where(at_seam & (depth == index), jnp.where(is_turned, turn, plain), made)
        ghosts.append(made)
    rest = jnp.zeros((HALF - ROWS, BLK), jnp.float32)
    west, east, south, north = ghosts
    return (
        jnp.concatenate([west, rest, east, rest], axis=0),
        jnp.concatenate([south, rest, north, rest], axis=0),
    )


def step_kernel(side, last, wave_ref, visc_ref, state_ref, matrix_ref, *rest):
    received, rest = rest[:5], rest[5:]
    own_a_ref, own_b_ref, new_ref = rest[:3]
    outs = rest[3:-1]
    strips_ref = rest[-1]
    across, along = ghosts_of(side, received, own_a_ref, own_b_ref, matrix_ref)
    edge = edge_matrix()
    both = jnp.concatenate([across, along], axis=1)
    high, low = split2(both)
    adds = jnp.dot(
        jnp.concatenate([edge, edge], axis=1),
        jnp.concatenate([high, low], axis=0),
        preferred_element_type=jnp.float32,
    )
    add_x = adds[:, :BLK].T
    add_y = adds[:, BLK:]
    band = band_matrix()
    band_x = jnp.concatenate([band, band], axis=0)
    band_y = jnp.concatenate([band, band], axis=1)
    lane = iota((BLK, BLK), 1)
    pad = jnp.zeros((5, BLK), jnp.float32)
    columns = jnp.zeros((BLK, BLK), jnp.float32)
    for plane in range(FACES * LEV):
        face, level = divmod(plane, LEV)
        a, b = wave_ref[level] * (1.0 / SCALE), visc_ref[level] * (1.0 / SCALE)
        pressure, rate = state_ref[face, level], state_ref[face, LEV + level]
        high, low = split2(a * pressure + b * rate)
        by_x = jnp.dot(
            jnp.concatenate([high, low], axis=1), band_x, preferred_element_type=jnp.float32
        )
        by_y = jnp.dot(
            band_y, jnp.concatenate([high, low], axis=0), preferred_element_type=jnp.float32
        )
        at_west = pltpu.roll(add_x, (-3 * plane) % BLK, 1)
        at_east = pltpu.roll(add_x, (BLK - 3 - HALF - 3 * plane) % BLK, 1)
        edge_x = jnp.where(lane < 3, at_west, jnp.where(lane >= BLK - 3, at_east, 0.0))
        rate = rate + by_x + by_y + edge_x
        at = 3 * plane
        bottom = rate[:8] + jnp.concatenate([add_y[at : at + 3], pad], axis=0)
        top = rate[BLK - 8 :] + jnp.concatenate([pad, add_y[HALF + at : HALF + at + 3]], axis=0)
        rate = jnp.concatenate([bottom, rate[8 : BLK - 8], top], axis=0)
        pressure = pressure + rate
        new_ref[face, level] = pressure
        new_ref[face, LEV + level] = rate
        if not last:
            columns = take_edges(a * pressure + b * rate, plane, columns, strips_ref)
    if not last:
        pack(columns, strips_ref, side, outs)


def exchange(payloads, side):
    def at(row, col):
        return row * side + col

    cells = [(row, col) for row in range(side) for col in range(side)]

    def swap(place, odd_first):
        return (place ^ 1) if not odd_first else (place + (1 if place % 2 else -1)) % side

    core = [(at(r, c), at(r, swap(c, False))) for r, c in cells]
    mirror = [(at(r, c), at(r, swap(c, True))) for r, c in cells]
    near = [(at(r, c), at(swap(r, False), c)) for r, c in cells]
    far = [(at(r, c), at(swap(r, True), c)) for r, c in cells]
    edge = side - 1
    turn = set()
    for x in range(edge):
        turn |= {(at(0, x), at(edge - x, edge)), (at(edge - x, edge), at(0, x))}
    for x in range(1, side):
        turn |= {(at(edge, x), at(edge - x, 0)), (at(edge - x, 0), at(edge, x))}
    core_out, mirror_out, near_out, far_out, turn_out = payloads
    core_in = lax.ppermute(core_out, "tile", core)
    mirror_in = lax.ppermute(mirror_out, "tile", mirror)
    near_in = lax.ppermute(near_out, "tile", near)
    far_in = lax.ppermute(far_out, "tile", far)
    turn_in = lax.ppermute(turn_out, "tile", sorted(turn))
    return core_in, mirror_in, near_in, far_in, turn_in


def on_device(state, wave_coef, visc_coef, stencil_start, stencil_offset):
    side = math.isqrt(lax.axis_size("tile"))
    current = state[0]
    scalars = pl.BlockSpec(memory_space=pltpu.SMEM)
    params = pltpu.CompilerParams(vmem_limit_bytes=VMEM_LIMIT)
    strip = jax.ShapeDtypeStruct((ROWS, BLK), jnp.float32)
    strips = pltpu.VMEM((4, FACES, 16, BLK), jnp.float32)
    matrix, *sent = pl.pallas_call(
        lambda *refs: first_kernel(side, *refs),
        out_shape=[jax.ShapeDtypeStruct((BLK, 2 * DEPTH * BLK), jnp.float32)] + [strip] * 7,
        in_specs=[scalars] * 2 + [whole_vmem()] * 3,
        out_specs=[whole_vmem()] * 8,
        scratch_shapes=[strips],
        compiler_params=params,
        name="first_edges",
    )(wave_coef, visc_coef, current, stencil_start, stencil_offset)
    for step in range(SUBSTEPS):
        last = step == SUBSTEPS - 1
        received = exchange(sent[:5], side)
        extra = 0 if last else 7
        current, *sent_next = pl.pallas_call(
            lambda *refs, last=last: step_kernel(side, last, *refs),
            out_shape=[jax.ShapeDtypeStruct(current.shape, jnp.float32)] + [strip] * extra,
            in_specs=[scalars] * 2 + [whole_vmem()] * 9,
            out_specs=[whole_vmem()] * (1 + extra),
            scratch_shapes=[strips],
            compiler_params=params,
            name="substep",
        )(wave_coef, visc_coef, current, matrix, *received, *sent[5:])
        sent = sent_next
    return current[None]


def solution(mesh):
    placed = (P(("member", "tile"), None, None, None, None), P(), P(), P(), P())
    return jax.shard_map(
        on_device,
        mesh=mesh,
        in_specs=placed,
        out_specs=P(("member", "tile"), None, None, None, None),
        check_vma=False,
    )
```

time: 624 us -> 73.2 us (0.12); the launches traced: 614 us -> 72.8 us
  local copies, waits for them, and re-layouts: 234 us -> 7.14 us
  other arithmetic: 198 us -> 0 us
  starting transfers between devices: 155 us -> 30.6 us
  Pallas kernels: 0 us -> 17.9 us
  matrix products: 17.8 us -> 0 us
  waiting for transfers between devices: 6.33 us -> 16.9 us
    ppermute x48 -> x20, starting transfers between devices: 155 us -> 30.6 us  [the longest x4 14.7 us: exchange(): turn_in = lax.ppermute(turn_out, 'tile', sorted(turn))]
    add x25 -> x0, other arithmetic: 107 us -> none  [the longest x4 79.3 us: apply_operator(): tendency + weight_value * (left_cells + right_cells + lower_cells + upper...]
    slice x75 -> x0, local copies, waits for them, and re-layouts: 95.8 us -> none  [the longest x16 32.1 us: on_device(): climb_first = jnp.roll(strip_west, -2, 0)[0::2]]
    concatenate x51 -> x0, other arithmetic: 47.4 us -> none  [the longest x3 20.5 us: apply_operator(): jnp.concatenate([jnp.swapaxes(jnp.flip(ghost_west, -2), -1, -2), field_da...]
    rev x32 -> x0, local copies, waits for them, and re-layouts: 46.6 us -> none  [the longest x5 25.7 us: edge_strips(): jnp.flip(field_data[..., -halo_depth:], -1)]
    dot_general x7 -> x0, local copies, waits for them, and re-layouts: 27 us -> none  [interp_block(): jnp.einsum('fchj,hjk->fchk', raw_ghost, matrix, precision=lax.Precision.H...]
    ppermute x13 -> x0, local copies, waits for them, and re-layouts: 25.2 us -> none  [from_behind(): return lax.ppermute(x, axis, pairs)]
    transpose x9 -> x0, local copies, waits for them, and re-layouts: 23.4 us -> none  [the longest x4 12.1 us: edge_strips(): strip_west = jnp.swapaxes(field_data[..., :halo_depth], -1, -2)]
  transfers between devices with their start and end apart: 48 -> 20, of which waited for: 6 -> 5; matrix products, arithmetic and copies ran while one was open for 40% -> 0% of each run, Pallas kernels for 0% -> 0%
where the time goes in v1:
time: 73.2 us; the launch traced here: 72.8 us
  starting transfers between devices  30.6 us (42%)
  Pallas kernels  17.9 us (24%)
  waiting for transfers between devices  16.9 us (23%)
  local copies, waits for them, and re-layouts  7.14 us (10%)
    pallas_call x4, Pallas kernels, on_device(): pl.pallas_call(lambda *refs, last=last: step_kernel(side, last, *refs), o...  16.5 us
    ppermute x4, waiting for transfers between devices, exchange(): turn_in = lax.ppermute(turn_out, 'tile', sorted(turn))  16 us
    ppermute x4, starting transfers between devices, exchange(): turn_in = lax.ppermute(turn_out, 'tile', sorted(turn))  14.7 us
    ppermute x4, starting transfers between devices, exchange(): far_in = lax.ppermute(far_out, 'tile', far)  8.98 us
    unnamed x14, local copies, waits for them, and re-layouts  7.14 us
    ppermute x4, starting transfers between devices, exchange(): near_in = lax.ppermute(near_out, 'tile', near)  3.57 us
    ppermute x4, starting transfers between devices, exchange(): mirror_in = lax.ppermute(mirror_out, 'tile', mirror)  2.72 us
  transfers between devices with their start and end apart: 20, of which 5 were waited for; matrix products, arithmetic and copies ran while one was open for 0% of the time, Pallas kernels for 0%

profile of v1, /device:TPU:0, one launch (start us, length us, event | category | flops | bytes accessed | tf_op | source)
XLA Modules:
  0.0 72.8 jit_solution(14483950961058782030)
XLA Ops:
  0.0 1.7 %copy-done = f32[1,6,6,128,128]{4,3,2,1,0:T(8,128)S(1)} copy-done((f32[1,6,6,128,128]{4,3,2,1,0:T(8,128)S(1)}, f32[1,6,6,128,128]{4,3,2,1,0:T(8,128)}, u32[]{:S(2)}) %copy-start) | copy-done | bytes 2359320
  1.7 0.7 copy-done.3
  2.3 0.7 copy-done.4
  3.0 0.7 copy-done.5
  3.7 0.7 copy-done.6
  4.3 1.4 %first_edges.1 = (f32[128,768]{1,0:T(8,128)S(1)}, f32[56,128]{1,0:T(8,128)S(1)}, f32[56,128]{1,0:T(8,128)S(1)}, f32[56,128]{1,0:T(8,128)S(1)}, f32[56,128]{1,0:T...) custom-call(f32[3]{0:T(128)S(1)} %copy-done.3, f32[3]{0:T(128)S(1)} %copy-done.4, ...), custom_call_target="tpu_custom_call" | custom-call | tf_op jit(solution)/shard_map/first_edges/pallas_call | solution.py:294
  5.8 0.5 collective-permute-start
  6.3 2.6 %collective-permute-start.1 = (f32[56,128]{1,0:T(8,128)S(1)}, f32[56,128]{1,0:T(8,128)S(1)}, u32[]{:S(2)}, u32[]{:S(2)}) collective-permute-start(f32[56,128]{1,0:T(8,128)S(1)} %get-tuple-element.39), channel_id=1, source_target_pairs={{0,3},{1,2},{2,1},{3,0},{4,7},{5,6},{6,5},{7,4},{8,11},{9,10},{10,... | collective-permute-start | bytes 86024 | tf_op jit(solution)/shard_map/ppermute | solution.py:280
  8.9 1.6 %collective-permute-start.2 = (f32[56,128]{1,0:T(8,128)S(1)}, f32[56,128]{1,0:T(8,128)S(1)}, u32[]{:S(2)}, u32[]{:S(2)}) collective-permute-start(f32[56,128]{1,0:T(8,128)S(1)} %get-tuple-element.40), channel_id=1, source_target_pairs={{0,4},{1,5},{2,6},{3,7},{4,0},{5,1},{6,2},{7,3},{8,12},{9,13},{10,... | collective-permute-start | bytes 86024 | tf_op jit(solution)/shard_map/ppermute | solution.py:281
  10.5 2.5 %collective-permute-start.3 = (f32[56,128]{1,0:T(8,128)S(1)}, f32[56,128]{1,0:T(8,128)S(1)}, u32[]{:S(2)}, u32[]{:S(2)}) collective-permute-start(f32[56,128]{1,0:T(8,128)S(1)} %get-tuple-element.41), channel_id=1, source_target_pairs={{0,12},{1,13},{2,14},{3,15},{4,8},{5,9},{6,10},{7,11},{8,4},{9,5},... | collective-permute-start | bytes 86024 | tf_op jit(solution)/shard_map/ppermute | solution.py:282
  13.0 2.3 %collective-permute-start.4 = (f32[56,128]{1,0:T(8,128)S(1)}, f32[56,128]{1,0:T(8,128)S(1)}, u32[]{:S(2)}, u32[]{:S(2)}) collective-permute-start(f32[56,128]{1,0:T(8,128)S(1)} %get-tuple-element.42), channel_id=1, source_target_pairs={{0,15},{1,11},{2,7},{4,14},{7,2},{8,13},{11,1},{13,8},{14,4},{15,0... | collective-permute-start | bytes 86024 | tf_op jit(solution)/shard_map/ppermute | solution.py:283
  15.3 0.9 %collective-permute-done.3.refs_7_ = f32[56,128]{1,0:T(8,128)S(1)} collective-permute-done((f32[56,128]{1,0:T(8,128)S(1)}, f32[56,128]{1,0:T(8,128)S(1)}, u32[]{:S(2)}, u32[]{:S(2)}) %collective-permute-start.3) | collective-permute-done | bytes 28704 | tf_op jit(solution)/shard_map/ppermute | solution.py:282
  16.2 4.8 %collective-permute-done.4.refs_8_ = f32[56,128]{1,0:T(8,128)S(1)} collective-permute-done((f32[56,128]{1,0:T(8,128)S(1)}, f32[56,128]{1,0:T(8,128)S(1)}, u32[]{:S(2)}, u32[]{:S(2)}) %collective-permute-start.4) | collective-permute-done | bytes 28704 | tf_op jit(solution)/shard_map/ppermute | solution.py:283
  21.0 4.2 %substep.4 = (f32[6,6,128,128]{3,2,1,0:T(8,128)S(1)}, f32[56,128]{1,0:T(8,128)S(1)}, f32[56,128]{1,0:T(8,128)S(1)}, f32[56,128]{1,0:T(8,128)S(1)}, f32[56,128]{1...) custom-call(f32[3]{0:T(128)S(1)} %copy-done.3, f32[3]{0:T(128)S(1)} %copy-done.4, ...), custom_call_target="tpu_custom_call" | custom-call | tf_op jit(solution)/shard_map/substep/pallas_call | solution.py:307
  25.2 1.4 %copy-done.2 = f32[6,6,128,128]{3,2,1,0:T(8,128)} copy-done((f32[6,6,128,128]{3,2,1,0:T(8,128)}, f32[6,6,128,128]{3,2,1,0:T(8,128)S(1)}, u32[]{:S(2)}) %copy-start.2) | copy-done | bytes 2359320
  26.6 0.3 collective-permute-start.7
  26.9 1.5 %collective-permute-start.8 = (f32[56,128]{1,0:T(8,128)S(1)}, f32[56,128]{1,0:T(8,128)S(1)}, u32[]{:S(2)}, u32[]{:S(2)}) collective-permute-start(f32[56,128]{1,0:T(8,128)S(1)} %get-tuple-element.49), channel_id=1, source_target_pairs={{0,12},{1,13},{2,14},{3,15},{4,8},{5,9},{6,10},{7,11},{8,4},{9,5},... | collective-permute-start | bytes 86024 | tf_op jit(solution)/shard_map/ppermute | solution.py:282
  28.4 4.8 %collective-permute-start.9 = (f32[56,128]{1,0:T(8,128)S(1)}, f32[56,128]{1,0:T(8,128)S(1)}, u32[]{:S(2)}, u32[]{:S(2)}) collective-permute-start(f32[56,128]{1,0:T(8,128)S(1)} %get-tuple-element.50), channel_id=1, source_target_pairs={{0,15},{1,11},{2,7},{4,14},{7,2},{8,13},{11,1},{13,8},{14,4},{15,0... | collective-permute-start | bytes 86024 | tf_op jit(solution)/shard_map/ppermute | solution.py:283
  33.3 3.1 %collective-permute-done.9.refs_8_ = f32[56,128]{1,0:T(8,128)S(1)} collective-permute-done((f32[56,128]{1,0:T(8,128)S(1)}, f32[56,128]{1,0:T(8,128)S(1)}, u32[]{:S(2)}, u32[]{:S(2)}) %collective-permute-start.9) | collective-permute-done | bytes 28704 | tf_op jit(solution)/shard_map/ppermute | solution.py:283
  36.4 4.2 %substep.5 = (f32[6,6,128,128]{3,2,1,0:T(8,128)S(1)}, f32[56,128]{1,0:T(8,128)S(1)}, f32[56,128]{1,0:T(8,128)S(1)}, f32[56,128]{1,0:T(8,128)S(1)}, f32[56,128]{1...) custom-call(f32[3]{0:T(128)S(1)} %copy-done.3, f32[3]{0:T(128)S(1)} %copy-done.4, ...), custom_call_target="tpu_custom_call" | custom-call | tf_op jit(solution)/shard_map/substep/pallas_call | solution.py:307
  40.6 1.4 %copy-done.1 = f32[6,6,128,128]{3,2,1,0:T(8,128)} copy-done((f32[6,6,128,128]{3,2,1,0:T(8,128)}, f32[6,6,128,128]{3,2,1,0:T(8,128)S(1)}, u32[]{:S(2)}) %copy-start.1) | copy-done | bytes 2359320
  42.0 0.8 %collective-permute-start.12 = (f32[56,128]{1,0:T(8,128)S(1)}, f32[56,128]{1,0:T(8,128)S(1)}, u32[]{:S(2)}, u32[]{:S(2)}) collective-permute-start(f32[56,128]{1,0:T(8,128)S(1)} %get-tuple-element.56), channel_id=1, source_target_pairs={{0,4},{1,5},{2,6},{3,7},{4,0},{5,1},{6,2},{7,3},{8,12},{9,13},{10,... | collective-permute-start | bytes 86024 | tf_op jit(solution)/shard_map/ppermute | solution.py:281
  42.8 3.6 %collective-permute-start.13 = (f32[56,128]{1,0:T(8,128)S(1)}, f32[56,128]{1,0:T(8,128)S(1)}, u32[]{:S(2)}, u32[]{:S(2)}) collective-permute-start(f32[56,128]{1,0:T(8,128)S(1)} %get-tuple-element.57), channel_id=1, source_target_pairs={{0,12},{1,13},{2,14},{3,15},{4,8},{5,9},{6,10},{7,11},{8,4},{9,5},... | collective-permute-start | bytes 86024 | tf_op jit(solution)/shard_map/ppermute | solution.py:282
  46.4 2.7 %collective-permute-start.14 = (f32[56,128]{1,0:T(8,128)S(1)}, f32[56,128]{1,0:T(8,128)S(1)}, u32[]{:S(2)}, u32[]{:S(2)}) collective-permute-start(f32[56,128]{1,0:T(8,128)S(1)} %get-tuple-element.58), channel_id=1, source_target_pairs={{0,15},{1,11},{2,7},{4,14},{7,2},{8,13},{11,1},{13,8},{14,4},{15,0... | collective-permute-start | bytes 86024 | tf_op jit(solution)/shard_map/ppermute | solution.py:283
  49.2 5.2 %collective-permute-done.14.refs_8_ = f32[56,128]{1,0:T(8,128)S(1)} collective-permute-done((f32[56,128]{1,0:T(8,128)S(1)}, f32[56,128]{1,0:T(8,128)S(1)}, u32[]{:S(2)}, u32[]{:S(2)}) %collective-permute-start.14) | collective-permute-done | bytes 28704 | tf_op jit(solution)/shard_map/ppermute | solution.py:283
  54.4 4.2 %substep.6 = (f32[6,6,128,128]{3,2,1,0:T(8,128)S(1)}, f32[56,128]{1,0:T(8,128)S(1)}, f32[56,128]{1,0:T(8,128)S(1)}, f32[56,128]{1,0:T(8,128)S(1)}, f32[56,128]{1...) custom-call(f32[3]{0:T(128)S(1)} %copy-done.3, f32[3]{0:T(128)S(1)} %copy-done.4, ...), custom_call_target="tpu_custom_call" | custom-call | tf_op jit(solution)/shard_map/substep/pallas_call | solution.py:307
  58.6 0.1 collective-permute-start.15
  58.8 0.9 %collective-permute-start.17 = (f32[56,128]{1,0:T(8,128)S(1)}, f32[56,128]{1,0:T(8,128)S(1)}, u32[]{:S(2)}, u32[]{:S(2)}) collective-permute-start(f32[56,128]{1,0:T(8,128)S(1)} %get-tuple-element.64), channel_id=1, source_target_pairs={{0,4},{1,5},{2,6},{3,7},{4,0},{5,1},{6,2},{7,3},{8,12},{9,13},{10,... | collective-permute-start | bytes 86024 | tf_op jit(solution)/shard_map/ppermute | solution.py:281
  59.6 1.4 %collective-permute-start.18 = (f32[56,128]{1,0:T(8,128)S(1)}, f32[56,128]{1,0:T(8,128)S(1)}, u32[]{:S(2)}, u32[]{:S(2)}) collective-permute-start(f32[56,128]{1,0:T(8,128)S(1)} %get-tuple-element.65), channel_id=1, source_target_pairs={{0,12},{1,13},{2,14},{3,15},{4,8},{5,9},{6,10},{7,11},{8,4},{9,5},... | collective-permute-start | bytes 86024 | tf_op jit(solution)/shard_map/ppermute | solution.py:282
  61.0 4.9 %collective-permute-start.19 = (f32[56,128]{1,0:T(8,128)S(1)}, f32[56,128]{1,0:T(8,128)S(1)}, u32[]{:S(2)}, u32[]{:S(2)}) collective-permute-start(f32[56,128]{1,0:T(8,128)S(1)} %get-tuple-element.66), channel_id=1, source_target_pairs={{0,15},{1,11},{2,7},{4,14},{7,2},{8,13},{11,1},{13,8},{14,4},{15,0... | collective-permute-start | bytes 86024 | tf_op jit(solution)/shard_map/ppermute | solution.py:283
  65.9 3.0 %collective-permute-done.19.refs_8_ = f32[56,128]{1,0:T(8,128)S(1)} collective-permute-done((f32[56,128]{1,0:T(8,128)S(1)}, f32[56,128]{1,0:T(8,128)S(1)}, u32[]{:S(2)}, u32[]{:S(2)}) %collective-permute-start.19) | collective-permute-done | bytes 28704 | tf_op jit(solution)/shard_map/ppermute | solution.py:283
  68.9 3.8 %substep.7 = f32[6,6,128,128]{3,2,1,0:T(8,128)} custom-call(f32[3]{0:T(128)S(1)} %copy-done.3, f32[3]{0:T(128)S(1)} %copy-done.4, f32[6,6,128,128]{3,2,1,0:T(8,128)S(1)} %get-tuple-element.61.refs_2_, f32[128,768]{1,0:T(8,128)S(1)} %get-tuple-element.37.refs_3_, f32[56,128]{1,0:T(8,128)S(1)} %collective-permute-done.15.refs_4_, ...), custom_call_target="tpu_custom_call" | custom-call | tf_op jit(solution)/shard_map/substep/pallas_call | solution.py:307
  (27 shorter events, 0.1 us)
Async XLA Ops:
  0.0 1.7 %copy-start = (f32[1,6,6,128,128]{4,3,2,1,0:T(8,128)S(1)}, f32[1,6,6,128,128]{4,3,2,1,0:T(8,128)}, u32[]{:S(2)}) copy-start(f32[1,6,6,128,128]{4,3,2,1,0:T(8,128)} %param.5) | copy-start | bytes 7077892
  1.7 0.7 copy-start.3
  2.3 0.7 copy-start.4
  3.0 0.7 copy-start.5
  3.7 0.7 copy-start.6
  5.8 9.5 %collective-permute-start = (f32[56,128]{1,0:T(8,128)S(1)}, f32[56,128]{1,0:T(8,128)S(1)}, u32[]{:S(2)}, u32[]{:S(2)}) collective-permute-start(f32[56,128]{1,0:T(8,128)S(1)} %get-tuple-element.38), channel_id=1, source_target_pairs={{0,1},{1,0},{2,3},{3,2},{4,5},{5,4},{6,7},{7,6},{8,9},{9,8},{10,11... | collective-permute-start | bytes 86024 | tf_op jit(solution)/shard_map/ppermute | solution.py:279
  6.3 9.0 %collective-permute-start.1 = (f32[56,128]{1,0:T(8,128)S(1)}, f32[56,128]{1,0:T(8,128)S(1)}, u32[]{:S(2)}, u32[]{:S(2)}) collective-permute-start(f32[56,128]{1,0:T(8,128)S(1)} %get-tuple-element.39), channel_id=1, source_target_pairs={{0,3},{1,2},{2,1},{3,0},{4,7},{5,6},{6,5},{7,4},{8,11},{9,10},{10,... | collective-permute-start | bytes 86024 | tf_op jit(solution)/shard_map/ppermute | solution.py:280
  8.9 6.4 %collective-permute-start.2 = (f32[56,128]{1,0:T(8,128)S(1)}, f32[56,128]{1,0:T(8,128)S(1)}, u32[]{:S(2)}, u32[]{:S(2)}) collective-permute-start(f32[56,128]{1,0:T(8,128)S(1)} %get-tuple-element.40), channel_id=1, source_target_pairs={{0,4},{1,5},{2,6},{3,7},{4,0},{5,1},{6,2},{7,3},{8,12},{9,13},{10,... | collective-permute-start | bytes 86024 | tf_op jit(solution)/shard_map/ppermute | solution.py:281
  10.5 5.7 %collective-permute-start.3 = (f32[56,128]{1,0:T(8,128)S(1)}, f32[56,128]{1,0:T(8,128)S(1)}, u32[]{:S(2)}, u32[]{:S(2)}) collective-permute-start(f32[56,128]{1,0:T(8,128)S(1)} %get-tuple-element.41), channel_id=1, source_target_pairs={{0,12},{1,13},{2,14},{3,15},{4,8},{5,9},{6,10},{7,11},{8,4},{9,5},... | collective-permute-start | bytes 86024 | tf_op jit(solution)/shard_map/ppermute | solution.py:282
  13.0 8.0 %collective-permute-start.4 = (f32[56,128]{1,0:T(8,128)S(1)}, f32[56,128]{1,0:T(8,128)S(1)}, u32[]{:S(2)}, u32[]{:S(2)}) collective-permute-start(f32[56,128]{1,0:T(8,128)S(1)} %get-tuple-element.42), channel_id=1, source_target_pairs={{0,15},{1,11},{2,7},{4,14},{7,2},{8,13},{11,1},{13,8},{14,4},{15,0... | collective-permute-start | bytes 86024 | tf_op jit(solution)/shard_map/ppermute | solution.py:283
  25.2 1.4 %copy-start.2 = (f32[6,6,128,128]{3,2,1,0:T(8,128)}, f32[6,6,128,128]{3,2,1,0:T(8,128)S(1)}, u32[]{:S(2)}) copy-start(f32[6,6,128,128]{3,2,1,0:T(8,128)S(1)} %get-tuple-element.45.refs_2_) | copy-start | bytes 7077892
  26.6 6.7 %collective-permute-start.5 = (f32[56,128]{1,0:T(8,128)S(1)}, f32[56,128]{1,0:T(8,128)S(1)}, u32[]{:S(2)}, u32[]{:S(2)}) collective-permute-start(f32[56,128]{1,0:T(8,128)S(1)} %get-tuple-element.46), channel_id=1, source_target_pairs={{0,1},{1,0},{2,3},{3,2},{4,5},{5,4},{6,7},{7,6},{8,9},{9,8},{10,11... | collective-permute-start | bytes 86024 | tf_op jit(solution)/shard_map/ppermute | solution.py:279
  26.6 6.7 %collective-permute-start.6 = (f32[56,128]{1,0:T(8,128)S(1)}, f32[56,128]{1,0:T(8,128)S(1)}, u32[]{:S(2)}, u32[]{:S(2)}) collective-permute-start(f32[56,128]{1,0:T(8,128)S(1)} %get-tuple-element.47), channel_id=1, source_target_pairs={{0,3},{1,2},{2,1},{3,0},{4,7},{5,6},{6,5},{7,4},{8,11},{9,10},{10,... | collective-permute-start | bytes 86024 | tf_op jit(solution)/shard_map/ppermute | solution.py:280
  26.6 6.7 %collective-permute-start.7 = (f32[56,128]{1,0:T(8,128)S(1)}, f32[56,128]{1,0:T(8,128)S(1)}, u32[]{:S(2)}, u32[]{:S(2)}) collective-permute-start(f32[56,128]{1,0:T(8,128)S(1)} %get-tuple-element.48), channel_id=1, source_target_pairs={{0,4},{1,5},{2,6},{3,7},{4,0},{5,1},{6,2},{7,3},{8,12},{9,13},{10,... | collective-permute-start | bytes 86024 | tf_op jit(solution)/shard_map/ppermute | solution.py:281
  26.9 6.4 %collective-permute-start.8 = (f32[56,128]{1,0:T(8,128)S(1)}, f32[56,128]{1,0:T(8,128)S(1)}, u32[]{:S(2)}, u32[]{:S(2)}) collective-permute-start(f32[56,128]{1,0:T(8,128)S(1)} %get-tuple-element.49), channel_id=1, source_target_pairs={{0,12},{1,13},{2,14},{3,15},{4,8},{5,9},{6,10},{7,11},{8,4},{9,5},... | collective-permute-start | bytes 86024 | tf_op jit(solution)/shard_map/ppermute | solution.py:282
  28.4 7.9 %collective-permute-start.9 = (f32[56,128]{1,0:T(8,128)S(1)}, f32[56,128]{1,0:T(8,128)S(1)}, u32[]{:S(2)}, u32[]{:S(2)}) collective-permute-start(f32[56,128]{1,0:T(8,128)S(1)} %get-tuple-element.50), channel_id=1, source_target_pairs={{0,15},{1,11},{2,7},{4,14},{7,2},{8,13},{11,1},{13,8},{14,4},{15,0... | collective-permute-start | bytes 86024 | tf_op jit(solution)/shard_map/ppermute | solution.py:283
  40.6 1.4 %copy-start.1 = (f32[6,6,128,128]{3,2,1,0:T(8,128)}, f32[6,6,128,128]{3,2,1,0:T(8,128)S(1)}, u32[]{:S(2)}) copy-start(f32[6,6,128,128]{3,2,1,0:T(8,128)S(1)} %get-tuple-element.53.refs_2_) | copy-start | bytes 7077892
  42.0 7.2 %collective-permute-start.10 = (f32[56,128]{1,0:T(8,128)S(1)}, f32[56,128]{1,0:T(8,128)S(1)}, u32[]{:S(2)}, u32[]{:S(2)}) collective-permute-start(f32[56,128]{1,0:T(8,128)S(1)} %get-tuple-element.54), channel_id=1, source_target_pairs={{0,1},{1,0},{2,3},{3,2},{4,5},{5,4},{6,7},{7,6},{8,9},{9,8},{10,11... | collective-permute-start | bytes 86024 | tf_op jit(solution)/shard_map/ppermute | solution.py:279
  42.0 7.2 %collective-permute-start.11 = (f32[56,128]{1,0:T(8,128)S(1)}, f32[56,128]{1,0:T(8,128)S(1)}, u32[]{:S(2)}, u32[]{:S(2)}) collective-permute-start(f32[56,128]{1,0:T(8,128)S(1)} %get-tuple-element.55), channel_id=1, source_target_pairs={{0,3},{1,2},{2,1},{3,0},{4,7},{5,6},{6,5},{7,4},{8,11},{9,10},{10,... | collective-permute-start | bytes 86024 | tf_op jit(solution)/shard_map/ppermute | solution.py:280
  42.0 7.2 %collective-permute-start.12 = (f32[56,128]{1,0:T(8,128)S(1)}, f32[56,128]{1,0:T(8,128)S(1)}, u32[]{:S(2)}, u32[]{:S(2)}) collective-permute-start(f32[56,128]{1,0:T(8,128)S(1)} %get-tuple-element.56), channel_id=1, source_target_pairs={{0,4},{1,5},{2,6},{3,7},{4,0},{5,1},{6,2},{7,3},{8,12},{9,13},{10,... | collective-permute-start | bytes 86024 | tf_op jit(solution)/shard_map/ppermute | solution.py:281
  42.8 6.4 %collective-permute-start.13 = (f32[56,128]{1,0:T(8,128)S(1)}, f32[56,128]{1,0:T(8,128)S(1)}, u32[]{:S(2)}, u32[]{:S(2)}) collective-permute-start(f32[56,128]{1,0:T(8,128)S(1)} %get-tuple-element.57), channel_id=1, source_target_pairs={{0,12},{1,13},{2,14},{3,15},{4,8},{5,9},{6,10},{7,11},{8,4},{9,5},... | collective-permute-start | bytes 86024 | tf_op jit(solution)/shard_map/ppermute | solution.py:282
  46.4 7.9 %collective-permute-start.14 = (f32[56,128]{1,0:T(8,128)S(1)}, f32[56,128]{1,0:T(8,128)S(1)}, u32[]{:S(2)}, u32[]{:S(2)}) collective-permute-start(f32[56,128]{1,0:T(8,128)S(1)} %get-tuple-element.58), channel_id=1, source_target_pairs={{0,15},{1,11},{2,7},{4,14},{7,2},{8,13},{11,1},{13,8},{14,4},{15,0... | collective-permute-start | bytes 86024 | tf_op jit(solution)/shard_map/ppermute | solution.py:283
  58.6 7.3 %collective-permute-start.15 = (f32[56,128]{1,0:T(8,128)S(1)}, f32[56,128]{1,0:T(8,128)S(1)}, u32[]{:S(2)}, u32[]{:S(2)}) collective-permute-start(f32[56,128]{1,0:T(8,128)S(1)} %get-tuple-element.62), channel_id=1, source_target_pairs={{0,1},{1,0},{2,3},{3,2},{4,5},{5,4},{6,7},{7,6},{8,9},{9,8},{10,11... | collective-permute-start | bytes 86024 | tf_op jit(solution)/shard_map/ppermute | solution.py:279
  58.7 7.2 %collective-permute-start.16 = (f32[56,128]{1,0:T(8,128)S(1)}, f32[56,128]{1,0:T(8,128)S(1)}, u32[]{:S(2)}, u32[]{:S(2)}) collective-permute-start(f32[56,128]{1,0:T(8,128)S(1)} %get-tuple-element.63), channel_id=1, source_target_pairs={{0,3},{1,2},{2,1},{3,0},{4,7},{5,6},{6,5},{7,4},{8,11},{9,10},{10,... | collective-permute-start | bytes 86024 | tf_op jit(solution)/shard_map/ppermute | solution.py:280
  58.8 7.2 %collective-permute-start.17 = (f32[56,128]{1,0:T(8,128)S(1)}, f32[56,128]{1,0:T(8,128)S(1)}, u32[]{:S(2)}, u32[]{:S(2)}) collective-permute-start(f32[56,128]{1,0:T(8,128)S(1)} %get-tuple-element.64), channel_id=1, source_target_pairs={{0,4},{1,5},{2,6},{3,7},{4,0},{5,1},{6,2},{7,3},{8,12},{9,13},{10,... | collective-permute-start | bytes 86024 | tf_op jit(solution)/shard_map/ppermute | solution.py:281
  59.6 6.3 %collective-permute-start.18 = (f32[56,128]{1,0:T(8,128)S(1)}, f32[56,128]{1,0:T(8,128)S(1)}, u32[]{:S(2)}, u32[]{:S(2)}) collective-permute-start(f32[56,128]{1,0:T(8,128)S(1)} %get-tuple-element.65), channel_id=1, source_target_pairs={{0,12},{1,13},{2,14},{3,15},{4,8},{5,9},{6,10},{7,11},{8,4},{9,5},... | collective-permute-start | bytes 86024 | tf_op jit(solution)/shard_map/ppermute | solution.py:282
  61.0 7.9 %collective-permute-start.19 = (f32[56,128]{1,0:T(8,128)S(1)}, f32[56,128]{1,0:T(8,128)S(1)}, u32[]{:S(2)}, u32[]{:S(2)}) collective-permute-start(f32[56,128]{1,0:T(8,128)S(1)} %get-tuple-element.66), channel_id=1, source_target_pairs={{0,15},{1,11},{2,7},{4,14},{7,2},{8,13},{11,1},{13,8},{14,4},{15,0... | collective-permute-start | bytes 86024 | tf_op jit(solution)/shard_map/ppermute | solution.py:283

commit v2 on v1

v2 whole, which is shorter than its diff:
```python
import math

import jax
import jax.numpy as jnp
from jax import lax
from jax.experimental import pallas as pl
from jax.experimental.pallas import tpu as pltpu
from jax.sharding import PartitionSpec as P

SUBSTEPS = 4
FACES = 6
LEV = 3
DEPTH = 3
BLK = 128
PER_FACE = LEV * DEPTH
ROWS = 56
HALF = 64
WEST, EAST, SOUTH, NORTH = 0, 1, 2, 3
SCALE = 20.0
VMEM_LIMIT = 16 * 1024 * 1024


def whole_vmem():
    return pl.BlockSpec(memory_space=pltpu.VMEM)


def iota(shape, dim):
    return lax.broadcasted_iota(jnp.int32, shape, dim)


def weight_of(distance):
    return jnp.where(
        distance == 1, 9.0, jnp.where(distance == 2, 7.0, jnp.where(distance == 3, 4.0, 0.0))
    )


def split2(x):
    high = x.astype(jnp.bfloat16)
    low = (x - high.astype(jnp.float32)).astype(jnp.bfloat16)
    return high, low


def lagrange_weights(t):
    return (
        -(t - 1.0) * (t - 2.0) * (t - 3.0) / 6.0,
        t * (t - 2.0) * (t - 3.0) / 2.0,
        -t * (t - 1.0) * (t - 3.0) / 2.0,
        t * (t - 1.0) * (t - 2.0) / 6.0,
    )


def band_matrix():
    gap = jnp.abs(iota((BLK, BLK), 0) - iota((BLK, BLK), 1))
    return jnp.where(gap == 0, -40.0, weight_of(gap)).astype(jnp.bfloat16)


def edge_matrix():
    shape = (BLK, BLK)
    to, src = iota(shape, 0), iota(shape, 1)
    lower = to < HALF
    to_row = jnp.where(lower, to, to - HALF)
    src_row = jnp.where(src < HALF, src, src - HALF)
    to_plane = (to_row * 171) >> 9
    src_plane = (src_row * 171) >> 9
    to_j = to_row - 3 * to_plane
    src_j = src_row - 3 * src_plane
    same = ((to < HALF) == (src < HALF)) & (to_plane == src_plane)
    distance = jnp.where(lower, 3 + to_j - src_j, 3 + src_j - to_j)
    return jnp.where(same, weight_of(distance), 0.0).astype(jnp.bfloat16)


def seam_matrices(starts, offsets, out_ref):
    j = iota((BLK, BLK), 0)
    back = BLK - 1 - j
    for h in range(DEPTH):
        first = starts[h : h + 1, :]
        weights = lagrange_weights(offsets[h : h + 1, :])
        for turned, place in ((0, j), (1, back)):
            matrix = jnp.zeros((BLK, BLK), jnp.float32)
            for m, weight in enumerate(weights):
                matrix = matrix + jnp.where(place == first + m, weight, 0.0)
            high, low = split2(matrix)
            at = (turned * DEPTH + h) * BLK
            out_ref[:BLK, at : at + BLK] = high
            out_ref[BLK : 2 * BLK, at : at + BLK] = high
            out_ref[2 * BLK :, at : at + BLK] = low


def position(side):
    index = lax.axis_index("tile")
    return lax.rem(index, side), lax.div(index, side)


def row_codes(shape):
    row = iota(shape, 0)
    block = (row * 57) >> 9
    odd = (block & 1) == 1
    depth = row - 3 * ((row * 171) >> 9)
    return odd, depth


def plane_row(shape, dim):
    row = iota(shape, dim)
    lower = row < HALF
    inside = jnp.where(lower, row, row - HALF)
    plane = (inside * 171) >> 9
    return lower, plane, inside - 3 * plane


def take_edges(q, plane, columns, rows_ref):
    lane = iota((BLK, BLK), 1)
    low, high = 3 * plane, HALF + 3 * plane
    columns = jnp.where((lane >= low) & (lane < low + 3), pltpu.roll(q, low, 1), columns)
    turn = (high - (BLK - 3)) % BLK
    columns = jnp.where((lane >= high) & (lane < high + 3), pltpu.roll(q, turn, 1), columns)
    rows_ref[low : low + 3, :] = q[:3, :]
    rows_ref[high : high + 3, :] = q[BLK - 3 :, :]
    return columns


def clear_rest(rows_ref):
    used = FACES * PER_FACE
    rest = jnp.zeros((HALF - used, BLK), jnp.float32)
    rows_ref[used:HALF, :] = rest
    rows_ref[HALF + used :, :] = rest


def pack(columns_ref, rows_ref, side, outs, strips_ref):
    core_ref, mirror_ref, near_ref, far_ref, turn_ref, own_a_ref, own_b_ref = outs
    col, row = position(side)
    for face in range(FACES):
        at = PER_FACE * face
        strips_ref[WEST, face, :PER_FACE, :] = columns_ref[at : at + PER_FACE, :]
        strips_ref[EAST, face, :PER_FACE, :] = columns_ref[HALF + at : HALF + at + PER_FACE, :]
        strips_ref[SOUTH, face, :PER_FACE, :] = rows_ref[at : at + PER_FACE, :]
        strips_ref[NORTH, face, :PER_FACE, :] = rows_ref[HALF + at : HALF + at + PER_FACE, :]
    even_col, even_row = lax.rem(col, 2) == 0, lax.rem(row, 2) == 0

    def shift(place):
        return jnp.where(place == 0, 1, jnp.where(place == side - 1, FACES - 1, 0))

    plans = (
        (core_ref, jnp.where(even_col, EAST, WEST), 0),
        (mirror_ref, jnp.where(even_col, WEST, EAST), shift(col)),
        (near_ref, jnp.where(even_row, NORTH, SOUTH), 0),
        (far_ref, jnp.where(even_row, SOUTH, NORTH), shift(row)),
    )
    rest = jnp.zeros((ROWS - FACES * PER_FACE, BLK), jnp.float32)
    for out_ref, which, by in plans:
        for face in range(FACES):
            at = PER_FACE * face
            source = face + by
            source = jnp.where(source >= FACES, source - FACES, source)
            out_ref[at : at + PER_FACE, :] = strips_ref[which, source, :PER_FACE, :]
        out_ref[FACES * PER_FACE :, :] = rest
    for face in range(FACES):
        at = PER_FACE * face
        if face % 2:
            a, b = (SOUTH, face + 2), (EAST, face - 2)
        else:
            a, b = (NORTH, face - 2), (WEST, face + 2)
        own_a_ref[at : at + PER_FACE, :] = strips_ref[a[0], a[1] % FACES, :PER_FACE, :]
        own_b_ref[at : at + PER_FACE, :] = strips_ref[b[0], b[1] % FACES, :PER_FACE, :]
    own_a_ref[FACES * PER_FACE :, :] = rest
    own_b_ref[FACES * PER_FACE :, :] = rest
    odd, _ = row_codes((ROWS, BLK))
    use_a = jnp.where(odd, (row == 0).astype(jnp.int32), (row == side - 1).astype(jnp.int32))
    turn_ref[...] = jnp.where(use_a == 1, own_a_ref[...], own_b_ref[...])


def first_kernel(side, state_hbm, wave_hbm, visc_hbm, start_hbm, offset_hbm, *rest):
    state_ref, coef_ref, gain_ref, matrix_ref = rest[:4]
    outs = rest[4:11]
    wave, visc, starts, offsets, columns_ref, rows_ref, strips_ref, sems = rest[11:]
    small = [
        pltpu.make_async_copy(src, dst, sems.at[FACES + place])
        for place, (src, dst) in enumerate(
            ((wave_hbm, wave), (visc_hbm, visc), (start_hbm, starts), (offset_hbm, offsets))
        )
    ]
    faces = [
        pltpu.make_async_copy(state_hbm.at[face], state_ref.at[face], sems.at[face])
        for face in range(FACES)
    ]
    for copy in small + faces:
        copy.start()
    clear_rest(rows_ref)
    for copy in small:
        copy.wait()
    seam_matrices(starts[...], offsets[...], matrix_ref)
    gain = jnp.zeros((BLK, BLK), jnp.float32)
    _, plane_of, _ = plane_row((BLK, BLK), 0)
    level_of = plane_of - 3 * ((plane_of * 171) >> 9)
    for level in range(LEV):
        a, b = wave[level] * (1.0 / SCALE), visc[level] * (1.0 / SCALE)
        coef_ref[level : level + 1, :] = jnp.full((1, BLK), a, jnp.float32)
        coef_ref[LEV + level : LEV + level + 1, :] = jnp.full((1, BLK), b, jnp.float32)
        gain = jnp.where(level_of == level, a + b, gain)
    coef_ref[2 * LEV :, :] = jnp.zeros((8 - 2 * LEV, BLK), jnp.float32)
    gain_ref[...] = gain
    columns = jnp.zeros((BLK, BLK), jnp.float32)
    for plane in range(FACES * LEV):
        face, level = divmod(plane, LEV)
        if level == 0:
            faces[face].wait()
        a, b = coef_ref[level : level + 1, :], coef_ref[LEV + level : LEV + level + 1, :]
        q = a * state_ref[face, level] + b * state_ref[face, LEV + level]
        columns = take_edges(q, plane, columns, rows_ref)
    columns_ref[...] = columns.T
    pack(columns_ref, rows_ref, side, outs, strips_ref)


def ghosts_of(side, received, own_a_ref, own_b_ref, matrix_ref):
    core, mirror, near, far, turned = [ref[...] for ref in received]
    col, row = position(side)
    even_col, even_row = lax.rem(col, 2) == 0, lax.rem(row, 2) == 0
    odd, depth = row_codes((ROWS, BLK))
    alone = ((row == 0) & (col == side - 1)) | ((col == 0) & (row == side - 1))
    turned_a = jnp.where(alone, own_a_ref[...], turned)
    turned_b = jnp.where(alone, own_b_ref[...], turned)
    sides = (
        (jnp.where(even_col, mirror, core), turned_a, col == 0, False, True),
        (jnp.where(even_col, core, mirror), turned_a, col == side - 1, True, False),
        (jnp.where(even_row, far, near), turned_b, row == 0, True, True),
        (jnp.where(even_row, near, far), turned_b, row == side - 1, False, False),
    )
    raws = []
    for straight, crossed, at_seam, turned_odd, _ in sides:
        is_turned = odd if turned_odd else ~odd
        raws.append(jnp.where(at_seam & is_turned, crossed, straight))
    high, low = split2(jnp.concatenate(raws, axis=0))
    mixed = jnp.dot(
        jnp.concatenate([high, low, high], axis=1),
        matrix_ref[...],
        preferred_element_type=jnp.float32,
    )
    ghosts = []
    for place, (_, _, at_seam, turned_odd, reverse) in enumerate(sides):
        part = mixed[place * ROWS : (place + 1) * ROWS, :]
        is_turned = odd if turned_odd else ~odd
        made = raws[place]
        for h in range(DEPTH):
            index = (DEPTH - 1 - h) if reverse else h
            plain = part[:, h * BLK : (h + 1) * BLK]
            turn = part[:, (DEPTH + h) * BLK : (DEPTH + h + 1) * BLK]
            made = jnp.where(at_seam & (depth == index), jnp.where(is_turned, turn, plain), made)
        ghosts.append(made)
    rest = jnp.zeros((HALF - ROWS, BLK), jnp.float32)
    west, east, south, north = ghosts
    return (
        jnp.concatenate([west, rest, east, rest], axis=0),
        jnp.concatenate([south, rest, north, rest], axis=0),
    )


def corner_part(adds_turned):
    shape = (BLK, BLK)
    lower, plane, cell = plane_row(shape, 0)
    lower_src, plane_src, cell_src = plane_row(shape, 1)
    low = jnp.where(
        cell == 0, adds_turned[0:1, :], jnp.where(cell == 1, adds_turned[1:2, :], adds_turned[2:3, :])
    )
    end = BLK - 3
    high = jnp.where(
        cell == 0,
        adds_turned[end : end + 1, :],
        jnp.where(cell == 1, adds_turned[end + 1 : end + 2, :], adds_turned[end + 2 : end + 3, :]),
    )
    kept = jnp.where(plane == plane_src, jnp.where(lower, low, high), 0.0)
    from_lower, from_plane, from_cell = plane_row(shape, 0)
    to = iota(shape, 1)
    fold = jnp.where(to == jnp.where(from_lower, from_cell, from_cell + end), 1.0, 0.0)
    fold = jnp.where(from_plane < FACES * LEV, fold, 0.0).astype(jnp.bfloat16)
    first, second = split2(kept)
    return jnp.dot(
        jnp.concatenate([first, second], axis=1),
        jnp.concatenate([fold, fold], axis=0),
        preferred_element_type=jnp.float32,
    )


def edge_kernel(side, last, *refs):
    received, refs = refs[:5], refs[5:]
    own_a_ref, own_b_ref, matrix_ref = refs[:3]
    refs = refs[3:]
    across, along = ghosts_of(side, received, own_a_ref, own_b_ref, matrix_ref)
    edge = edge_matrix()
    high, low = split2(jnp.concatenate([across, along], axis=1))
    adds = jnp.dot(
        jnp.concatenate([edge, edge], axis=1),
        jnp.concatenate([high, low], axis=0),
        preferred_element_type=jnp.float32,
    )
    add_x, add_y = adds[:, :BLK], adds[:, BLK:]
    turned_x = add_x.T
    if last:
        add_x_ref, add_y_ref = refs
        add_x_ref[...] = turned_x
        add_y_ref[...] = add_y
        return
    gain_ref, old_columns_ref, old_rows_ref, add_x_ref, add_y_ref = refs[:5]
    outs = refs[5:12]
    columns_ref, rows_ref, strips_ref = refs[12:]
    add_x_ref[...] = turned_x
    add_y_ref[...] = add_y
    gain = gain_ref[...]
    columns_ref[...] = old_columns_ref[...] + gain * (add_x + corner_part(add_y.T))
    rows_ref[...] = old_rows_ref[...] + gain * (add_y + corner_part(turned_x))
    pack(columns_ref, rows_ref, side, outs, strips_ref)


def edge_additions(plane, add_x, add_y, lane):
    at_west = pltpu.roll(add_x, (-3 * plane) % BLK, 1)
    at_east = pltpu.roll(add_x, (BLK - 3 - HALF - 3 * plane) % BLK, 1)
    add = jnp.where(lane < 3, at_west, jnp.where(lane >= BLK - 3, at_east, 0.0))
    at = 3 * plane
    pad = jnp.zeros((5, BLK), jnp.float32)
    bottom = add[:8] + jnp.concatenate([add_y[at : at + 3], pad], axis=0)
    top = add[BLK - 8 :] + jnp.concatenate([pad, add_y[HALF + at : HALF + at + 3]], axis=0)
    return jnp.concatenate([bottom, add[8 : BLK - 8], top], axis=0)


def inner_kernel(first, last, state_ref, coef_ref, *refs):
    if not first:
        add_x_ref, add_y_ref = refs[:2]
        refs = refs[2:]
        add_x, add_y = add_x_ref[...], add_y_ref[...]
    new_ref = refs[0]
    if not last:
        columns_ref, rows_ref = refs[1:]
        clear_rest(rows_ref)
    band = band_matrix()
    band_x = jnp.concatenate([band, band], axis=0)
    band_y = jnp.concatenate([band, band], axis=1)
    lane = iota((BLK, BLK), 1)
    columns = jnp.zeros((BLK, BLK), jnp.float32)
    for plane in range(FACES * LEV):
        face, level = divmod(plane, LEV)
        a, b = coef_ref[level : level + 1, :], coef_ref[LEV + level : LEV + level + 1, :]
        pressure, rate = state_ref[face, level], state_ref[face, LEV + level]
        if not first:
            add = edge_additions(plane, add_x, add_y, lane)
            pressure, rate = pressure + add, rate + add
        high, low = split2(a * pressure + b * rate)
        by_x = jnp.dot(
            jnp.concatenate([high, low], axis=1), band_x, preferred_element_type=jnp.float32
        )
        by_y = jnp.dot(
            band_y, jnp.concatenate([high, low], axis=0), preferred_element_type=jnp.float32
        )
        rate = rate + by_x + by_y
        pressure = pressure + rate
        new_ref[face, level] = pressure
        new_ref[face, LEV + level] = rate
        if not last:
            columns = take_edges(a * pressure + b * rate, plane, columns, rows_ref)
    if not last:
        columns_ref[...] = columns.T


def final_kernel(state_ref, add_x_ref, add_y_ref, out_hbm, buffer, sems):
    add_x, add_y = add_x_ref[...], add_y_ref[...]
    lane = iota((BLK, BLK), 1)
    copies = []
    for face in range(FACES):
        for level in range(LEV):
            add = edge_additions(face * LEV + level, add_x, add_y, lane)
            buffer[face, level] = state_ref[face, level] + add
            buffer[face, LEV + level] = state_ref[face, LEV + level] + add
        copy = pltpu.make_async_copy(buffer.at[face], out_hbm.at[face], sems.at[face])
        copy.start()
        copies.append(copy)
    for copy in copies:
        copy.wait()


def exchange(payloads, side):
    def at(row, col):
        return row * side + col

    cells = [(row, col) for row in range(side) for col in range(side)]

    def swap(place, odd_first):
        return (place ^ 1) if not odd_first else (place + (1 if place % 2 else -1)) % side

    core = [(at(r, c), at(r, swap(c, False))) for r, c in cells]
    mirror = [(at(r, c), at(r, swap(c, True))) for r, c in cells]
    near = [(at(r, c), at(swap(r, False), c)) for r, c in cells]
    far = [(at(r, c), at(swap(r, True), c)) for r, c in cells]
    edge = side - 1
    turn = set()
    for x in range(edge):
        turn |= {(at(0, x), at(edge - x, edge)), (at(edge - x, edge), at(0, x))}
    for x in range(1, side):
        turn |= {(at(edge, x), at(edge - x, 0)), (at(edge - x, 0), at(edge, x))}
    core_out, mirror_out, near_out, far_out, turn_out = payloads
    turn_in = lax.ppermute(turn_out, "tile", sorted(turn))
    far_in = lax.ppermute(far_out, "tile", far)
    near_in = lax.ppermute(near_out, "tile", near)
    mirror_in = lax.ppermute(mirror_out, "tile", mirror)
    core_in = lax.ppermute(core_out, "tile", core)
    return core_in, mirror_in, near_in, far_in, turn_in


def call(kernel, name, outs, ins, scratch=(), out_hbm=False, in_hbm=False, cost=0, aliases=None):
    hbm = pl.BlockSpec(memory_space=pltpu.HBM)
    vmem = pl.BlockSpec(memory_space=pltpu.VMEM)
    return pl.pallas_call(
        kernel,
        out_shape=outs,
        in_specs=[hbm if in_hbm else vmem] * len(ins),
        out_specs=[hbm if out_hbm else vmem] * len(outs),
        scratch_shapes=list(scratch),
        compiler_params=pltpu.CompilerParams(vmem_limit_bytes=VMEM_LIMIT),
        cost_estimate=pl.CostEstimate(flops=cost, bytes_accessed=cost // 500, transcendentals=0),
        input_output_aliases=aliases or {},
        name=name,
    )(*ins)


def on_device(state, wave_coef, visc_coef, stencil_start, stencil_offset):
    side = math.isqrt(lax.axis_size("tile"))
    field = state[0]

    def array(*shape, dtype=jnp.float32):
        return jax.ShapeDtypeStruct(shape, dtype)

    tile = array(BLK, BLK)
    strip = array(ROWS, BLK)
    whole = array(*field.shape)
    tile_scratch = pltpu.VMEM((BLK, BLK), jnp.float32)
    strips = pltpu.VMEM((4, FACES, 16, BLK), jnp.float32)
    field, coef, gain, matrix, *sent = call(
        lambda *refs: first_kernel(side, *refs),
        "first_edges",
        [whole, array(8, BLK), tile, array(3 * BLK, 2 * DEPTH * BLK, dtype=jnp.bfloat16)]
        + [strip] * 7,
        [field, wave_coef, visc_coef, stencil_start, stencil_offset],
        [
            pltpu.SMEM((LEV,), jnp.float32),
            pltpu.SMEM((LEV,), jnp.float32),
            pltpu.VMEM((DEPTH, BLK), jnp.int32),
            pltpu.VMEM((DEPTH, BLK), jnp.float32),
            tile_scratch,
            tile_scratch,
            strips,
            pltpu.SemaphoreType.DMA((FACES + 4,)),
        ],
        in_hbm=True,
    )
    adds = []
    for step in range(SUBSTEPS):
        last = step == SUBSTEPS - 1
        received = exchange(sent[:5], side)
        field, *edges = call(
            lambda *refs, first=step == 0, last=last: inner_kernel(first, last, *refs),
            "inner",
            [whole] + ([] if last else [tile] * 2),
            [field, coef, *adds],
            cost=2_000_000_000,
            aliases={0: 0},
        )
        adds_and_sent = call(
            lambda *refs, last=last: edge_kernel(side, last, *refs),
            "edges",
            [tile] * 2 + ([] if last else [strip] * 7),
            [*received, *sent[5:], matrix] + ([] if last else [gain, *edges]),
            [] if last else [tile_scratch, tile_scratch, strips],
        )
        adds, sent = adds_and_sent[:2], adds_and_sent[2:]
    (field,) = call(
        final_kernel,
        "final",
        [whole],
        [field, *adds],
        [pltpu.VMEM(field.shape, jnp.float32), pltpu.SemaphoreType.DMA((FACES,))],
        out_hbm=True,
    )
    return field[None]


def solution(mesh):
    placed = (P(("member", "tile"), None, None, None, None), P(), P(), P(), P())
    return jax.shard_map(
        on_device,
        mesh=mesh,
        in_specs=placed,
        out_specs=P(("member", "tile"), None, None, None, None),
        check_vma=False,
    )
```

time: 73.2 us -> 60.4 us (0.83)
  waiting for transfers between devices: 16.9 us -> 7.92 us
  local copies, waits for them, and re-layouts: 7.14 us -> 4.34 us
  Pallas kernels: 17.9 us -> 16.3 us
    ppermute x4, waiting for transfers between devices: 16 us -> 7.88 us  [exchange(): turn_in = lax.ppermute(turn_out, 'tile', sorted(turn))]
    unnamed x14 -> x10, local copies, waits for them, and re-layouts: 7.14 us -> 4.34 us
    pallas_call x5 -> x10, Pallas kernels: 17.9 us -> 16.3 us  [call(): pl.pallas_call(kernel, out_shape=outs, in_specs=[hbm if in_hbm else vmem]...]
    ppermute x4, waiting for transfers between devices: 0.86 us -> 0.01 us  [exchange(): far_in = lax.ppermute(far_out, 'tile', far)]
  transfers between devices with their start and end apart: 20 -> 20, of which waited for: 5 -> 4; matrix products, arithmetic and copies ran while one was open for 0% -> 0% of each run, Pallas kernels for 0% -> 15%
where the time goes in v2:
time: 60.4 us; the launch traced here: 60.1 us
  starting transfers between devices  31.3 us (52%)
  Pallas kernels  16.3 us (27%)
  waiting for transfers between devices  7.92 us (13%)
  local copies, waits for them, and re-layouts  4.34 us (7%)
    pallas_call x10, Pallas kernels, call(): pl.pallas_call(kernel, out_shape=outs, in_specs=[hbm if in_hbm else vmem]...  16.3 us
    ppermute x4, starting transfers between devices, exchange(): turn_in = lax.ppermute(turn_out, 'tile', sorted(turn))  14.8 us
    ppermute x4, starting transfers between devices, exchange(): far_in = lax.ppermute(far_out, 'tile', far)  8.75 us
    ppermute x4, waiting for transfers between devices, exchange(): turn_in = lax.ppermute(turn_out, 'tile', sorted(turn))  7.88 us
    unnamed x10, local copies, waits for them, and re-layouts  4.34 us
    ppermute x4, starting transfers between devices, exchange(): near_in = lax.ppermute(near_out, 'tile', near)  4.11 us
    ppermute x4, starting transfers between devices, exchange(): mirror_in = lax.ppermute(mirror_out, 'tile', mirror)  2.86 us
  transfers between devices with their start and end apart: 20, of which 4 were waited for; matrix products, arithmetic and copies ran while one was open for 0% of the time, Pallas kernels for 15%

profile of v2, /device:TPU:0, one launch (start us, length us, event | category | flops | bytes accessed | tf_op | source)
XLA Modules:
  0.0 60.1 jit_solution(5134473735381765602)
XLA Ops:
  0.0 1.7 %copy-done = f32[1,6,6,128,128]{4,3,2,1,0:T(8,128)S(1)} copy-done((f32[1,6,6,128,128]{4,3,2,1,0:T(8,128)S(1)}, f32[1,6,6,128,128]{4,3,2,1,0:T(8,128)}, u32[]{:S(2)}) %copy-start) | copy-done | bytes 2359320
  1.7 0.7 %copy-done.1 = s32[3,128]{1,0:T(4,128)S(1)} copy-done((s32[3,128]{1,0:T(4,128)S(1)}, s32[3,128]{1,0:T(4,128)}, u32[]{:S(2)}) %copy-start.1) | copy-done | bytes 1560
  2.4 0.7 %copy-done.2 = f32[3,128]{1,0:T(4,128)S(1)} copy-done((f32[3,128]{1,0:T(4,128)S(1)}, f32[3,128]{1,0:T(4,128)}, u32[]{:S(2)}) %copy-start.2) | copy-done | bytes 1560
  3.0 0.7 %copy-done.3 = f32[3]{0:T(128)S(1)} copy-done((f32[3]{0:T(128)S(1)}, f32[3]{0:T(128)}, u32[]{:S(2)}) %copy-start.3) | copy-done | bytes 36
  3.7 0.7 %copy-done.4 = f32[3]{0:T(128)S(1)} copy-done((f32[3]{0:T(128)S(1)}, f32[3]{0:T(128)}, u32[]{:S(2)}) %copy-start.4) | copy-done | bytes 36
  4.3 2.6 %first_edges.1 = (f32[6,6,128,128]{3,2,1,0:T(8,128)S(1)}, f32[8,128]{1,0:T(8,128)S(1)}, f32[128,128]{1,0:T(8,128)S(1)}, bf16[384,768]{1,0:T(8,128)(2,1)S(1)}, f3...) custom-call(f32[6,6,128,128]{3,2,1,0:T(8,128)S(1)} %bitcast.2, ...), custom_call_target="tpu_custom_call" | custom-call | tf_op jit(solution)/shard_map/first_edges/pallas_call | solution.py:408
  7.0 0.5 collective-permute-start
  7.5 2.6 %collective-permute-start.1 = (f32[56,128]{1,0:T(8,128)S(1)}, f32[56,128]{1,0:T(8,128)S(1)}, u32[]{:S(2)}, u32[]{:S(2)}) collective-permute-start(f32[56,128]{1,0:T(8,128)S(1)} %get-tuple-element.58), channel_id=1, source_target_pairs={{0,3},{1,2},{2,1},{3,0},{4,7},{5,6},{6,5},{7,4},{8,11},{9,10},{10,... | collective-permute-start | bytes 86024 | tf_op jit(solution)/shard_map/ppermute | solution.py:400
  10.1 1.6 %collective-permute-start.2 = (f32[56,128]{1,0:T(8,128)S(1)}, f32[56,128]{1,0:T(8,128)S(1)}, u32[]{:S(2)}, u32[]{:S(2)}) collective-permute-start(f32[56,128]{1,0:T(8,128)S(1)} %get-tuple-element.59), channel_id=1, source_target_pairs={{0,4},{1,5},{2,6},{3,7},{4,0},{5,1},{6,2},{7,3},{8,12},{9,13},{10,... | collective-permute-start | bytes 86024 | tf_op jit(solution)/shard_map/ppermute | solution.py:399
  11.7 2.5 %collective-permute-start.3 = (f32[56,128]{1,0:T(8,128)S(1)}, f32[56,128]{1,0:T(8,128)S(1)}, u32[]{:S(2)}, u32[]{:S(2)}) collective-permute-start(f32[56,128]{1,0:T(8,128)S(1)} %get-tuple-element.60), channel_id=1, source_target_pairs={{0,12},{1,13},{2,14},{3,15},{4,8},{5,9},{6,10},{7,11},{8,4},{9,5},... | collective-permute-start | bytes 86024 | tf_op jit(solution)/shard_map/ppermute | solution.py:398
  14.2 2.3 %collective-permute-start.4 = (f32[56,128]{1,0:T(8,128)S(1)}, f32[56,128]{1,0:T(8,128)S(1)}, u32[]{:S(2)}, u32[]{:S(2)}) collective-permute-start(f32[56,128]{1,0:T(8,128)S(1)} %get-tuple-element.61), channel_id=1, source_target_pairs={{0,15},{1,11},{2,7},{4,14},{7,2},{8,13},{11,1},{13,8},{14,4},{15,0... | collective-permute-start | bytes 86024 | tf_op jit(solution)/shard_map/ppermute | solution.py:397
  16.5 2.2 %inner.4 = (f32[6,6,128,128]{3,2,1,0:T(8,128)S(1)}, f32[128,128]{1,0:T(8,128)S(1)}, f32[128,128]{1,0:T(8,128)S(1)}) custom-call(f32[6,6,128,128]{3,2,1,0:T(8,128)S(1)} %get-tuple-element.54.refs_0_, f32[8,128]{1,0:T(8,128)S(1)} %get-tuple-element.55.refs_1_), custom_call_target="tpu_custom_call", output_to_operand_aliasing={{0}: (0, {})} | custom-call | flops 2000000000 | bytes 4000000 | tf_op jit(solution)/shard_map/inner/pallas_call | solution.py:408
  18.7 3.4 %collective-permute-done.4.refs_4_ = f32[56,128]{1,0:T(8,128)S(1)} collective-permute-done((f32[56,128]{1,0:T(8,128)S(1)}, f32[56,128]{1,0:T(8,128)S(1)}, u32[]{:S(2)}, u32[]{:S(2)}) %collective-permute-start.4) | collective-permute-done | bytes 28704 | tf_op jit(solution)/shard_map/ppermute | solution.py:397
  22.2 0.9 %edges.4 = (f32[128,128]{1,0:T(8,128)S(1)}, f32[128,128]{1,0:T(8,128)S(1)}, f32[56,128]{1,0:T(8,128)S(1)}, f32[56,128]{1,0:T(8,128)S(1)}, f32[56,128]{1,0:T(8,12...) custom-call(f32[56,128]{1,0:T(8,128)S(1)} %collective-permute-done.refs_0, ...), custom_call_target="tpu_custom_call" | custom-call | tf_op jit(solution)/shard_map/edges/pallas_call | solution.py:408
  23.2 0.4 collective-permute-start.7
  23.6 1.4 %collective-permute-start.8 = (f32[56,128]{1,0:T(8,128)S(1)}, f32[56,128]{1,0:T(8,128)S(1)}, u32[]{:S(2)}, u32[]{:S(2)}) collective-permute-start(f32[56,128]{1,0:T(8,128)S(1)} %get-tuple-element.74), channel_id=1, source_target_pairs={{0,12},{1,13},{2,14},{3,15},{4,8},{5,9},{6,10},{7,11},{8,4},{9,5},... | collective-permute-start | bytes 86024 | tf_op jit(solution)/shard_map/ppermute | solution.py:398
  25.0 4.9 %collective-permute-start.9 = (f32[56,128]{1,0:T(8,128)S(1)}, f32[56,128]{1,0:T(8,128)S(1)}, u32[]{:S(2)}, u32[]{:S(2)}) collective-permute-start(f32[56,128]{1,0:T(8,128)S(1)} %get-tuple-element.75), channel_id=1, source_target_pairs={{0,15},{1,11},{2,7},{4,14},{7,2},{8,13},{11,1},{13,8},{14,4},{15,0... | collective-permute-start | bytes 86024 | tf_op jit(solution)/shard_map/ppermute | solution.py:397
  29.9 2.7 %inner.5 = (f32[6,6,128,128]{3,2,1,0:T(8,128)S(1)}, f32[128,128]{1,0:T(8,128)S(1)}, f32[128,128]{1,0:T(8,128)S(1)}) custom-call(f32[6,6,128,128]{3,2,1,0:T(8,128)S(1)} %get-tuple-element.56.refs_0_, f32[8,128]{1,0:T(8,128)S(1)} %get-tuple-element.55.refs_1_, f32[128,128]{1,0:T(8,128)S(1)} %get-tuple-element.68.refs_2_, ...), custom_call_target="tpu_custom_call", output_to_operand_aliasing={{0}: (0, {})} | custom-call | flops 2000000000 | bytes 4000000 | tf_op jit(solution)/shard_map/inner/pallas_call | solution.py:408
  32.9 0.9 %edges.5 = (f32[128,128]{1,0:T(8,128)S(1)}, f32[128,128]{1,0:T(8,128)S(1)}, f32[56,128]{1,0:T(8,128)S(1)}, f32[56,128]{1,0:T(8,128)S(1)}, f32[56,128]{1,0:T(8,12...) custom-call(f32[56,128]{1,0:T(8,128)S(1)} %collective-permute-done.5.refs, ...), custom_call_target="tpu_custom_call" | custom-call | tf_op jit(solution)/shard_map/edges/pallas_call | solution.py:408
  34.0 1.3 %collective-permute-start.12 = (f32[56,128]{1,0:T(8,128)S(1)}, f32[56,128]{1,0:T(8,128)S(1)}, u32[]{:S(2)}, u32[]{:S(2)}) collective-permute-start(f32[56,128]{1,0:T(8,128)S(1)} %get-tuple-element.85), channel_id=1, source_target_pairs={{0,4},{1,5},{2,6},{3,7},{4,0},{5,1},{6,2},{7,3},{8,12},{9,13},{10,... | collective-permute-start | bytes 86024 | tf_op jit(solution)/shard_map/ppermute | solution.py:399
  35.2 3.2 %collective-permute-start.13 = (f32[56,128]{1,0:T(8,128)S(1)}, f32[56,128]{1,0:T(8,128)S(1)}, u32[]{:S(2)}, u32[]{:S(2)}) collective-permute-start(f32[56,128]{1,0:T(8,128)S(1)} %get-tuple-element.86), channel_id=1, source_target_pairs={{0,12},{1,13},{2,14},{3,15},{4,8},{5,9},{6,10},{7,11},{8,4},{9,5},... | collective-permute-start | bytes 86024 | tf_op jit(solution)/shard_map/ppermute | solution.py:398
  38.4 3.1 %collective-permute-start.14 = (f32[56,128]{1,0:T(8,128)S(1)}, f32[56,128]{1,0:T(8,128)S(1)}, u32[]{:S(2)}, u32[]{:S(2)}) collective-permute-start(f32[56,128]{1,0:T(8,128)S(1)} %get-tuple-element.87), channel_id=1, source_target_pairs={{0,15},{1,11},{2,7},{4,14},{7,2},{8,13},{11,1},{13,8},{14,4},{15,0... | collective-permute-start | bytes 86024 | tf_op jit(solution)/shard_map/ppermute | solution.py:397
  41.5 2.7 %inner.6 = (f32[6,6,128,128]{3,2,1,0:T(8,128)S(1)}, f32[128,128]{1,0:T(8,128)S(1)}, f32[128,128]{1,0:T(8,128)S(1)}) custom-call(f32[6,6,128,128]{3,2,1,0:T(8,128)S(1)} %get-tuple-element.70.refs_0_, f32[8,128]{1,0:T(8,128)S(1)} %get-tuple-element.55.refs_1_, f32[128,128]{1,0:T(8,128)S(1)} %get-tuple-element.80.refs_2_, ...), custom_call_target="tpu_custom_call", output_to_operand_aliasing={{0}: (0, {})} | custom-call | flops 2000000000 | bytes 4000000 | tf_op jit(solution)/shard_map/inner/pallas_call | solution.py:408
  44.2 2.1 %collective-permute-done.14.refs_4_ = f32[56,128]{1,0:T(8,128)S(1)} collective-permute-done((f32[56,128]{1,0:T(8,128)S(1)}, f32[56,128]{1,0:T(8,128)S(1)}, u32[]{:S(2)}, u32[]{:S(2)}) %collective-permute-start.14) | collective-permute-done | bytes 28704 | tf_op jit(solution)/shard_map/ppermute | solution.py:397
  46.3 0.9 %edges.6 = (f32[128,128]{1,0:T(8,128)S(1)}, f32[128,128]{1,0:T(8,128)S(1)}, f32[56,128]{1,0:T(8,128)S(1)}, f32[56,128]{1,0:T(8,128)S(1)}, f32[56,128]{1,0:T(8,12...) custom-call(f32[56,128]{1,0:T(8,128)S(1)} %collective-permute-done.10.ref, ...), custom_call_target="tpu_custom_call" | custom-call | tf_op jit(solution)/shard_map/edges/pallas_call | solution.py:408
  47.3 0.9 %collective-permute-start.17 = (f32[56,128]{1,0:T(8,128)S(1)}, f32[56,128]{1,0:T(8,128)S(1)}, u32[]{:S(2)}, u32[]{:S(2)}) collective-permute-start(f32[56,128]{1,0:T(8,128)S(1)} %get-tuple-element.96), channel_id=1, source_target_pairs={{0,4},{1,5},{2,6},{3,7},{4,0},{5,1},{6,2},{7,3},{8,12},{9,13},{10,... | collective-permute-start | bytes 86024 | tf_op jit(solution)/shard_map/ppermute | solution.py:399
  48.2 1.8 %collective-permute-start.18 = (f32[56,128]{1,0:T(8,128)S(1)}, f32[56,128]{1,0:T(8,128)S(1)}, u32[]{:S(2)}, u32[]{:S(2)}) collective-permute-start(f32[56,128]{1,0:T(8,128)S(1)} %get-tuple-element.97), channel_id=1, source_target_pairs={{0,12},{1,13},{2,14},{3,15},{4,8},{5,9},{6,10},{7,11},{8,4},{9,5},... | collective-permute-start | bytes 86024 | tf_op jit(solution)/shard_map/ppermute | solution.py:398
  50.0 4.5 %collective-permute-start.19 = (f32[56,128]{1,0:T(8,128)S(1)}, f32[56,128]{1,0:T(8,128)S(1)}, u32[]{:S(2)}, u32[]{:S(2)}) collective-permute-start(f32[56,128]{1,0:T(8,128)S(1)} %get-tuple-element.98), channel_id=1, source_target_pairs={{0,15},{1,11},{2,7},{4,14},{7,2},{8,13},{11,1},{13,8},{14,4},{15,0... | collective-permute-start | bytes 86024 | tf_op jit(solution)/shard_map/ppermute | solution.py:397
  54.5 1.3 %inner.7.state_ref = f32[6,6,128,128]{3,2,1,0:T(8,128)S(1)} custom-call(f32[6,6,128,128]{3,2,1,0:T(8,128)S(1)} %get-tuple-element.82.refs_0_, f32[8,128]{1,0:T(8,128)S(1)} %get-tuple-element.55.refs_1_, f32[128,128]{1,0:T(8,128)S(1)} %get-tuple-element.92.refs_2_, f32[128,128]{1,0:T(8,128)S(1)} %get-tuple-element.93.refs_3_), custom_call_target="tpu_custom_call", output_to_operand_aliasing={{}: (0, {})} | custom-call | flops 2000000000 | bytes 4000000 | tf_op jit(solution)/shard_map/inner/pallas_call | solution.py:408
  55.8 2.1 %collective-permute-done.19.refs_4_ = f32[56,128]{1,0:T(8,128)S(1)} collective-permute-done((f32[56,128]{1,0:T(8,128)S(1)}, f32[56,128]{1,0:T(8,128)S(1)}, u32[]{:S(2)}, u32[]{:S(2)}) %collective-permute-start.19) | collective-permute-done | bytes 28704 | tf_op jit(solution)/shard_map/ppermute | solution.py:397
  57.9 0.6 edges.7
  58.5 1.6 %final.1 = f32[6,6,128,128]{3,2,1,0:T(8,128)} custom-call(f32[6,6,128,128]{3,2,1,0:T(8,128)S(1)} %inner.7.state_ref, f32[128,128]{1,0:T(8,128)S(1)} %get-tuple-element.101.add_x_ref, f32[128,128]{1,0:T(8,128)S(1)} %get-tuple-element.102.add_y_ref), custom_call_target="tpu_custom_call" | custom-call | tf_op jit(solution)/shard_map/final/pallas_call | solution.py:408
  (28 shorter events, 0.7 us)
Async XLA Ops:
  0.0 1.7 %copy-start = (f32[1,6,6,128,128]{4,3,2,1,0:T(8,128)S(1)}, f32[1,6,6,128,128]{4,3,2,1,0:T(8,128)}, u32[]{:S(2)}) copy-start(f32[1,6,6,128,128]{4,3,2,1,0:T(8,128)} %param.5) | copy-start | bytes 7077892
  1.7 0.7 %copy-start.1 = (s32[3,128]{1,0:T(4,128)S(1)}, s32[3,128]{1,0:T(4,128)}, u32[]{:S(2)}) copy-start(s32[3,128]{1,0:T(4,128)} %refs_3_.1) | copy-start | bytes 4612
  2.3 0.7 %copy-start.2 = (f32[3,128]{1,0:T(4,128)S(1)}, f32[3,128]{1,0:T(4,128)}, u32[]{:S(2)}) copy-start(f32[3,128]{1,0:T(4,128)} %refs_4_.1) | copy-start | bytes 4612
  3.0 0.7 %copy-start.3 = (f32[3]{0:T(128)S(1)}, f32[3]{0:T(128)}, u32[]{:S(2)}) copy-start(f32[3]{0:T(128)} %refs_1_.1) | copy-start | bytes 40
  3.7 0.7 %copy-start.4 = (f32[3]{0:T(128)S(1)}, f32[3]{0:T(128)}, u32[]{:S(2)}) copy-start(f32[3]{0:T(128)} %refs_2_.1) | copy-start | bytes 40
  7.0 11.7 %collective-permute-start = (f32[56,128]{1,0:T(8,128)S(1)}, f32[56,128]{1,0:T(8,128)S(1)}, u32[]{:S(2)}, u32[]{:S(2)}) collective-permute-start(f32[56,128]{1,0:T(8,128)S(1)} %get-tuple-element.57), channel_id=1, source_target_pairs={{0,1},{1,0},{2,3},{3,2},{4,5},{5,4},{6,7},{7,6},{8,9},{9,8},{10,11... | collective-permute-start | bytes 86024 | tf_op jit(solution)/shard_map/ppermute | solution.py:401
  7.5 11.2 %collective-permute-start.1 = (f32[56,128]{1,0:T(8,128)S(1)}, f32[56,128]{1,0:T(8,128)S(1)}, u32[]{:S(2)}, u32[]{:S(2)}) collective-permute-start(f32[56,128]{1,0:T(8,128)S(1)} %get-tuple-element.58), channel_id=1, source_target_pairs={{0,3},{1,2},{2,1},{3,0},{4,7},{5,6},{6,5},{7,4},{8,11},{9,10},{10,... | collective-permute-start | bytes 86024 | tf_op jit(solution)/shard_map/ppermute | solution.py:400
  10.1 8.6 %collective-permute-start.2 = (f32[56,128]{1,0:T(8,128)S(1)}, f32[56,128]{1,0:T(8,128)S(1)}, u32[]{:S(2)}, u32[]{:S(2)}) collective-permute-start(f32[56,128]{1,0:T(8,128)S(1)} %get-tuple-element.59), channel_id=1, source_target_pairs={{0,4},{1,5},{2,6},{3,7},{4,0},{5,1},{6,2},{7,3},{8,12},{9,13},{10,... | collective-permute-start | bytes 86024 | tf_op jit(solution)/shard_map/ppermute | solution.py:399
  11.7 7.0 %collective-permute-start.3 = (f32[56,128]{1,0:T(8,128)S(1)}, f32[56,128]{1,0:T(8,128)S(1)}, u32[]{:S(2)}, u32[]{:S(2)}) collective-permute-start(f32[56,128]{1,0:T(8,128)S(1)} %get-tuple-element.60), channel_id=1, source_target_pairs={{0,12},{1,13},{2,14},{3,15},{4,8},{5,9},{6,10},{7,11},{8,4},{9,5},... | collective-permute-start | bytes 86024 | tf_op jit(solution)/shard_map/ppermute | solution.py:398
  14.2 8.0 %collective-permute-start.4 = (f32[56,128]{1,0:T(8,128)S(1)}, f32[56,128]{1,0:T(8,128)S(1)}, u32[]{:S(2)}, u32[]{:S(2)}) collective-permute-start(f32[56,128]{1,0:T(8,128)S(1)} %get-tuple-element.61), channel_id=1, source_target_pairs={{0,15},{1,11},{2,7},{4,14},{7,2},{8,13},{11,1},{13,8},{14,4},{15,0... | collective-permute-start | bytes 86024 | tf_op jit(solution)/shard_map/ppermute | solution.py:397
  23.0 9.6 %collective-permute-start.5 = (f32[56,128]{1,0:T(8,128)S(1)}, f32[56,128]{1,0:T(8,128)S(1)}, u32[]{:S(2)}, u32[]{:S(2)}) collective-permute-start(f32[56,128]{1,0:T(8,128)S(1)} %get-tuple-element.71), channel_id=1, source_target_pairs={{0,1},{1,0},{2,3},{3,2},{4,5},{5,4},{6,7},{7,6},{8,9},{9,8},{10,11... | collective-permute-start | bytes 86024 | tf_op jit(solution)/shard_map/ppermute | solution.py:401
  23.1 9.5 %collective-permute-start.6 = (f32[56,128]{1,0:T(8,128)S(1)}, f32[56,128]{1,0:T(8,128)S(1)}, u32[]{:S(2)}, u32[]{:S(2)}) collective-permute-start(f32[56,128]{1,0:T(8,128)S(1)} %get-tuple-element.72), channel_id=1, source_target_pairs={{0,3},{1,2},{2,1},{3,0},{4,7},{5,6},{6,5},{7,4},{8,11},{9,10},{10,... | collective-permute-start | bytes 86024 | tf_op jit(solution)/shard_map/ppermute | solution.py:400
  23.2 9.4 %collective-permute-start.7 = (f32[56,128]{1,0:T(8,128)S(1)}, f32[56,128]{1,0:T(8,128)S(1)}, u32[]{:S(2)}, u32[]{:S(2)}) collective-permute-start(f32[56,128]{1,0:T(8,128)S(1)} %get-tuple-element.73), channel_id=1, source_target_pairs={{0,4},{1,5},{2,6},{3,7},{4,0},{5,1},{6,2},{7,3},{8,12},{9,13},{10,... | collective-permute-start | bytes 86024 | tf_op jit(solution)/shard_map/ppermute | solution.py:399
  23.6 9.0 %collective-permute-start.8 = (f32[56,128]{1,0:T(8,128)S(1)}, f32[56,128]{1,0:T(8,128)S(1)}, u32[]{:S(2)}, u32[]{:S(2)}) collective-permute-start(f32[56,128]{1,0:T(8,128)S(1)} %get-tuple-element.74), channel_id=1, source_target_pairs={{0,12},{1,13},{2,14},{3,15},{4,8},{5,9},{6,10},{7,11},{8,4},{9,5},... | collective-permute-start | bytes 86024 | tf_op jit(solution)/shard_map/ppermute | solution.py:398
  25.0 7.9 %collective-permute-start.9 = (f32[56,128]{1,0:T(8,128)S(1)}, f32[56,128]{1,0:T(8,128)S(1)}, u32[]{:S(2)}, u32[]{:S(2)}) collective-permute-start(f32[56,128]{1,0:T(8,128)S(1)} %get-tuple-element.75), channel_id=1, source_target_pairs={{0,15},{1,11},{2,7},{4,14},{7,2},{8,13},{11,1},{13,8},{14,4},{15,0... | collective-permute-start | bytes 86024 | tf_op jit(solution)/shard_map/ppermute | solution.py:397
  33.8 10.4 %collective-permute-start.10 = (f32[56,128]{1,0:T(8,128)S(1)}, f32[56,128]{1,0:T(8,128)S(1)}, u32[]{:S(2)}, u32[]{:S(2)}) collective-permute-start(f32[56,128]{1,0:T(8,128)S(1)} %get-tuple-element.83), channel_id=1, source_target_pairs={{0,1},{1,0},{2,3},{3,2},{4,5},{5,4},{6,7},{7,6},{8,9},{9,8},{10,11... | collective-permute-start | bytes 86024 | tf_op jit(solution)/shard_map/ppermute | solution.py:401
  33.9 10.3 %collective-permute-start.11 = (f32[56,128]{1,0:T(8,128)S(1)}, f32[56,128]{1,0:T(8,128)S(1)}, u32[]{:S(2)}, u32[]{:S(2)}) collective-permute-start(f32[56,128]{1,0:T(8,128)S(1)} %get-tuple-element.84), channel_id=1, source_target_pairs={{0,3},{1,2},{2,1},{3,0},{4,7},{5,6},{6,5},{7,4},{8,11},{9,10},{10,... | collective-permute-start | bytes 86024 | tf_op jit(solution)/shard_map/ppermute | solution.py:400
  34.0 10.3 %collective-permute-start.12 = (f32[56,128]{1,0:T(8,128)S(1)}, f32[56,128]{1,0:T(8,128)S(1)}, u32[]{:S(2)}, u32[]{:S(2)}) collective-permute-start(f32[56,128]{1,0:T(8,128)S(1)} %get-tuple-element.85), channel_id=1, source_target_pairs={{0,4},{1,5},{2,6},{3,7},{4,0},{5,1},{6,2},{7,3},{8,12},{9,13},{10,... | collective-permute-start | bytes 86024 | tf_op jit(solution)/shard_map/ppermute | solution.py:399
  35.2 9.0 %collective-permute-start.13 = (f32[56,128]{1,0:T(8,128)S(1)}, f32[56,128]{1,0:T(8,128)S(1)}, u32[]{:S(2)}, u32[]{:S(2)}) collective-permute-start(f32[56,128]{1,0:T(8,128)S(1)} %get-tuple-element.86), channel_id=1, source_target_pairs={{0,12},{1,13},{2,14},{3,15},{4,8},{5,9},{6,10},{7,11},{8,4},{9,5},... | collective-permute-start | bytes 86024 | tf_op jit(solution)/shard_map/ppermute | solution.py:398
  38.4 7.9 %collective-permute-start.14 = (f32[56,128]{1,0:T(8,128)S(1)}, f32[56,128]{1,0:T(8,128)S(1)}, u32[]{:S(2)}, u32[]{:S(2)}) collective-permute-start(f32[56,128]{1,0:T(8,128)S(1)} %get-tuple-element.87), channel_id=1, source_target_pairs={{0,15},{1,11},{2,7},{4,14},{7,2},{8,13},{11,1},{13,8},{14,4},{15,0... | collective-permute-start | bytes 86024 | tf_op jit(solution)/shard_map/ppermute | solution.py:397
  47.2 8.6 %collective-permute-start.15 = (f32[56,128]{1,0:T(8,128)S(1)}, f32[56,128]{1,0:T(8,128)S(1)}, u32[]{:S(2)}, u32[]{:S(2)}) collective-permute-start(f32[56,128]{1,0:T(8,128)S(1)} %get-tuple-element.94), channel_id=1, source_target_pairs={{0,1},{1,0},{2,3},{3,2},{4,5},{5,4},{6,7},{7,6},{8,9},{9,8},{10,11... | collective-permute-start | bytes 86024 | tf_op jit(solution)/shard_map/ppermute | solution.py:401
  47.3 8.5 %collective-permute-start.16 = (f32[56,128]{1,0:T(8,128)S(1)}, f32[56,128]{1,0:T(8,128)S(1)}, u32[]{:S(2)}, u32[]{:S(2)}) collective-permute-start(f32[56,128]{1,0:T(8,128)S(1)} %get-tuple-element.95), channel_id=1, source_target_pairs={{0,3},{1,2},{2,1},{3,0},{4,7},{5,6},{6,5},{7,4},{8,11},{9,10},{10,... | collective-permute-start | bytes 86024 | tf_op jit(solution)/shard_map/ppermute | solution.py:400
  47.3 8.4 %collective-permute-start.17 = (f32[56,128]{1,0:T(8,128)S(1)}, f32[56,128]{1,0:T(8,128)S(1)}, u32[]{:S(2)}, u32[]{:S(2)}) collective-permute-start(f32[56,128]{1,0:T(8,128)S(1)} %get-tuple-element.96), channel_id=1, source_target_pairs={{0,4},{1,5},{2,6},{3,7},{4,0},{5,1},{6,2},{7,3},{8,12},{9,13},{10,... | collective-permute-start | bytes 86024 | tf_op jit(solution)/shard_map/ppermute | solution.py:399
  48.2 7.6 %collective-permute-start.18 = (f32[56,128]{1,0:T(8,128)S(1)}, f32[56,128]{1,0:T(8,128)S(1)}, u32[]{:S(2)}, u32[]{:S(2)}) collective-permute-start(f32[56,128]{1,0:T(8,128)S(1)} %get-tuple-element.97), channel_id=1, source_target_pairs={{0,12},{1,13},{2,14},{3,15},{4,8},{5,9},{6,10},{7,11},{8,4},{9,5},... | collective-permute-start | bytes 86024 | tf_op jit(solution)/shard_map/ppermute | solution.py:398
  50.0 7.9 %collective-permute-start.19 = (f32[56,128]{1,0:T(8,128)S(1)}, f32[56,128]{1,0:T(8,128)S(1)}, u32[]{:S(2)}, u32[]{:S(2)}) collective-permute-start(f32[56,128]{1,0:T(8,128)S(1)} %get-tuple-element.98), channel_id=1, source_target_pairs={{0,15},{1,11},{2,7},{4,14},{7,2},{8,13},{11,1},{13,8},{14,4},{15,0... | collective-permute-start | bytes 86024 | tf_op jit(solution)/shard_map/ppermute | solution.py:397

commit v3 on v2

v3 whole, which is shorter than its diff:
```python
import math

import jax
import jax.numpy as jnp
from jax import lax
from jax.experimental import pallas as pl
from jax.experimental.pallas import tpu as pltpu
from jax.sharding import PartitionSpec as P

SUBSTEPS = 4
FACES = 6
LEV = 3
DEPTH = 3
BLK = 128
PER_FACE = LEV * DEPTH
ROWS = 56
HALF = 64
WEST, EAST, SOUTH, NORTH = 0, 1, 2, 3
SCALE = 20.0
VMEM_LIMIT = 16 * 1024 * 1024
FIRST_LIMIT = 60 * 1024 * 1024


def whole_vmem():
    return pl.BlockSpec(memory_space=pltpu.VMEM)


def iota(shape, dim):
    return lax.broadcasted_iota(jnp.int32, shape, dim)


def weight_of(distance):
    return jnp.where(
        distance == 1, 9.0, jnp.where(distance == 2, 7.0, jnp.where(distance == 3, 4.0, 0.0))
    )


def split2(x):
    high = x.astype(jnp.bfloat16)
    low = (x - high.astype(jnp.float32)).astype(jnp.bfloat16)
    return high, low


def lagrange_weights(t):
    return (
        -(t - 1.0) * (t - 2.0) * (t - 3.0) / 6.0,
        t * (t - 2.0) * (t - 3.0) / 2.0,
        -t * (t - 1.0) * (t - 3.0) / 2.0,
        t * (t - 1.0) * (t - 2.0) / 6.0,
    )


def band_matrix():
    gap = jnp.abs(iota((BLK, BLK), 0) - iota((BLK, BLK), 1))
    return jnp.where(gap == 0, -40.0, weight_of(gap)).astype(jnp.bfloat16)


def edge_matrix():
    shape = (BLK, BLK)
    to, src = iota(shape, 0), iota(shape, 1)
    lower = to < HALF
    to_row = jnp.where(lower, to, to - HALF)
    src_row = jnp.where(src < HALF, src, src - HALF)
    to_plane = (to_row * 171) >> 9
    src_plane = (src_row * 171) >> 9
    to_j = to_row - 3 * to_plane
    src_j = src_row - 3 * src_plane
    same = ((to < HALF) == (src < HALF)) & (to_plane == src_plane)
    distance = jnp.where(lower, 3 + to_j - src_j, 3 + src_j - to_j)
    return jnp.where(same, weight_of(distance), 0.0).astype(jnp.bfloat16)


def seam_matrices(starts, offsets, out_ref):
    j = iota((BLK, BLK), 0)
    back = BLK - 1 - j
    for h in range(DEPTH):
        first = starts[h : h + 1, :]
        weights = lagrange_weights(offsets[h : h + 1, :])
        for turned, place in ((0, j), (1, back)):
            matrix = jnp.zeros((BLK, BLK), jnp.float32)
            for m, weight in enumerate(weights):
                matrix = matrix + jnp.where(place == first + m, weight, 0.0)
            high, low = split2(matrix)
            at = (turned * DEPTH + h) * BLK
            out_ref[:BLK, at : at + BLK] = high
            out_ref[BLK : 2 * BLK, at : at + BLK] = high
            out_ref[2 * BLK :, at : at + BLK] = low


def position(side):
    index = lax.axis_index("tile")
    return lax.rem(index, side), lax.div(index, side)


def row_codes(shape):
    row = iota(shape, 0)
    block = (row * 57) >> 9
    odd = (block & 1) == 1
    depth = row - 3 * ((row * 171) >> 9)
    return odd, depth


def plane_row(shape, dim):
    row = iota(shape, dim)
    lower = row < HALF
    inside = jnp.where(lower, row, row - HALF)
    plane = (inside * 171) >> 9
    return lower, plane, inside - 3 * plane


def tiles_of(plane_value):
    return plane_value.reshape(BLK // 8, 8, BLK)


def lane_of_tile():
    return iota((1, 8, BLK), 2)


def take_edges(q, plane, columns, rows_ref):
    lane, at = lane_of_tile(), 6 * plane
    turned = pltpu.roll(q, (at + 3) % BLK, 2)
    columns = jnp.where((lane >= at) & (lane < at + 6), turned, columns)
    low, high = 3 * plane, HALF + 3 * plane
    rows_ref[low : low + 3, :] = q[0, :3, :]
    rows_ref[high : high + 3, :] = q[BLK // 8 - 1, 5:, :]
    return columns


def lane_order():
    lower, plane, cell = plane_row((BLK, BLK), 0)
    lane = 6 * plane + cell + jnp.where(lower, 3, 0)
    right = (lane == iota((BLK, BLK), 1)) & (plane < FACES * LEV)
    return jnp.where(right, 1.0, 0.0).astype(jnp.bfloat16)


def rows_from_columns(columns, order):
    high, low = split2(columns.reshape(BLK, BLK))
    return lax.dot_general(
        order,
        jnp.concatenate([high, low], axis=1),
        (((1,), (1,)), ((), ())),
        preferred_element_type=jnp.float32,
    )


def clear_rest(rows_ref):
    used = FACES * PER_FACE
    rest = jnp.zeros((HALF - used, BLK), jnp.float32)
    rows_ref[used:HALF, :] = rest
    rows_ref[HALF + used :, :] = rest


def pack(columns_ref, rows_ref, side, outs, strips_ref):
    turn_ref, far_ref, near_ref, mirror_ref, core_ref, own_a_ref, own_b_ref = outs
    col, row = position(side)
    for face in range(FACES):
        at = PER_FACE * face
        strips_ref[WEST, face, :PER_FACE, :] = columns_ref[at : at + PER_FACE, :]
        strips_ref[EAST, face, :PER_FACE, :] = columns_ref[HALF + at : HALF + at + PER_FACE, :]
        strips_ref[SOUTH, face, :PER_FACE, :] = rows_ref[at : at + PER_FACE, :]
        strips_ref[NORTH, face, :PER_FACE, :] = rows_ref[HALF + at : HALF + at + PER_FACE, :]
    even_col, even_row = lax.rem(col, 2) == 0, lax.rem(row, 2) == 0

    def shift(place):
        return jnp.where(place == 0, 1, jnp.where(place == side - 1, FACES - 1, 0))

    plans = (
        (core_ref, jnp.where(even_col, EAST, WEST), 0),
        (mirror_ref, jnp.where(even_col, WEST, EAST), shift(col)),
        (near_ref, jnp.where(even_row, NORTH, SOUTH), 0),
        (far_ref, jnp.where(even_row, SOUTH, NORTH), shift(row)),
    )
    rest = jnp.zeros((ROWS - FACES * PER_FACE, BLK), jnp.float32)
    for out_ref, which, by in plans:
        for face in range(FACES):
            at = PER_FACE * face
            source = face + by
            source = jnp.where(source >= FACES, source - FACES, source)
            out_ref[at : at + PER_FACE, :] = strips_ref[which, source, :PER_FACE, :]
        out_ref[FACES * PER_FACE :, :] = rest
    for face in range(FACES):
        at = PER_FACE * face
        if face % 2:
            a, b = (SOUTH, face + 2), (EAST, face - 2)
        else:
            a, b = (NORTH, face - 2), (WEST, face + 2)
        own_a_ref[at : at + PER_FACE, :] = strips_ref[a[0], a[1] % FACES, :PER_FACE, :]
        own_b_ref[at : at + PER_FACE, :] = strips_ref[b[0], b[1] % FACES, :PER_FACE, :]
    own_a_ref[FACES * PER_FACE :, :] = rest
    own_b_ref[FACES * PER_FACE :, :] = rest
    odd, _ = row_codes((ROWS, BLK))
    use_a = jnp.where(odd, (row == 0).astype(jnp.int32), (row == side - 1).astype(jnp.int32))
    turn_ref[...] = jnp.where(use_a == 1, own_a_ref[...], own_b_ref[...])


CONSTANTS = (
    ("coef", (8, BLK), jnp.float32),
    ("gain", (BLK, BLK), jnp.float32),
    ("matrix", (3 * BLK, 2 * DEPTH * BLK), jnp.bfloat16),
    ("edge", (BLK, 2 * BLK), jnp.bfloat16),
    ("fold", (2 * BLK, BLK), jnp.bfloat16),
    ("same", (BLK, BLK), jnp.float32),
    ("order", (BLK, 2 * BLK), jnp.bfloat16),
    ("spread", (2 * BLK, BLK), jnp.bfloat16),
    ("band_x", (2 * BLK, BLK), jnp.bfloat16),
    ("band_y", (BLK, 2 * BLK), jnp.bfloat16),
)


def make_constants(wave, visc, starts, offsets, refs):
    coef, gain, matrix, edge, fold, same, order, spread, band_x, band_y = refs
    seam_matrices(starts, offsets, matrix)
    _, plane, cell = plane_row((BLK, BLK), 0)
    lower, _, _ = plane_row((BLK, BLK), 0)
    _, plane_src, _ = plane_row((BLK, BLK), 1)
    level_of = plane - 3 * ((plane * 171) >> 9)
    total = jnp.zeros((BLK, BLK), jnp.float32)
    for level in range(LEV):
        a, b = wave[level] * (1.0 / SCALE), visc[level] * (1.0 / SCALE)
        coef[level : level + 1, :] = jnp.full((1, BLK), a, jnp.float32)
        coef[LEV + level : LEV + level + 1, :] = jnp.full((1, BLK), b, jnp.float32)
        total = jnp.where(level_of == level, a + b, total)
    coef[2 * LEV :, :] = jnp.zeros((8 - 2 * LEV, BLK), jnp.float32)
    gain[...] = total
    for ref, value, axis in (
        (edge, edge_matrix(), 1),
        (order, lane_order(), 1),
        (band_x, band_matrix(), 0),
        (band_y, band_matrix(), 1),
    ):
        ref[...] = jnp.concatenate([value, value], axis=axis)
    used = plane < FACES * LEV
    to = iota((BLK, BLK), 1)
    back = jnp.where(lower, cell, cell + BLK - 3)
    value = jnp.where((to == back) & used, 1.0, 0.0).astype(jnp.bfloat16)
    fold[...] = jnp.concatenate([value, value], axis=0)
    spread[...] = jnp.concatenate([lane_order()] * 2, axis=0)
    same[...] = jnp.where(plane == plane_src, 1.0, 0.0)


def first_kernel(side, state_hbm, wave_hbm, visc_hbm, *rest):
    outs = rest[:7]
    state_ref, wave, visc, columns_ref, rows_ref, strips_ref, sems = rest[7:]
    small = [
        pltpu.make_async_copy(wave_hbm, wave, sems.at[FACES]),
        pltpu.make_async_copy(visc_hbm, visc, sems.at[FACES + 1]),
    ]
    faces = [
        pltpu.make_async_copy(state_hbm.at[face], state_ref.at[face], sems.at[face])
        for face in range(FACES)
    ]
    for copy in small + faces:
        copy.start()
    clear_rest(rows_ref)
    for copy in small:
        copy.wait()
    columns = jnp.zeros((BLK // 8, 8, BLK), jnp.float32)
    for plane in range(FACES * LEV):
        face, level = divmod(plane, LEV)
        if level == 0:
            faces[face].wait()
        a, b = wave[level] * (1.0 / SCALE), visc[level] * (1.0 / SCALE)
        q = a * state_ref[face, level] + b * state_ref[face, LEV + level]
        columns = take_edges(tiles_of(q), plane, columns, rows_ref)
    order = lane_order()
    columns_ref[...] = rows_from_columns(columns, jnp.concatenate([order, order], axis=1))
    pack(columns_ref, rows_ref, side, outs, strips_ref)


def ghosts_of(side, received, own_a_ref, own_b_ref, matrix_ref):
    turned, far, near, mirror, core = [ref[...] for ref in received]
    col, row = position(side)
    even_col, even_row = lax.rem(col, 2) == 0, lax.rem(row, 2) == 0
    odd, depth = row_codes((ROWS, BLK))
    alone = ((row == 0) & (col == side - 1)) | ((col == 0) & (row == side - 1))
    pairs = (
        (
            jnp.where(even_col, mirror, core),
            jnp.where(even_col, core, mirror),
            jnp.where(alone, own_a_ref[...], turned),
            col,
            0,
        ),
        (
            jnp.where(even_row, far, near),
            jnp.where(even_row, near, far),
            jnp.where(alone, own_b_ref[...], turned),
            row,
            1,
        ),
    )
    seams, marks = [], []
    for low, high, crossed, place, low_turned in pairs:
        at_low = (place == 0).astype(jnp.int32)
        parity = at_low ^ (1 - low_turned)
        is_turned = odd.astype(jnp.int32) == parity
        seams.append(jnp.where(is_turned, crossed, jnp.where(place == 0, low, high)))
        marks.append((is_turned, jnp.where(place == 0, DEPTH - 1 - depth, depth)))
    first, second = split2(jnp.concatenate(seams, axis=0))
    mixed = jnp.dot(
        jnp.concatenate([first, second, first], axis=1),
        matrix_ref[...],
        preferred_element_type=jnp.float32,
    )
    rest = jnp.zeros((HALF - ROWS, BLK), jnp.float32)
    ghosts = []
    for index, (low, high, _, place, _) in enumerate(pairs):
        part = mixed[index * ROWS : (index + 1) * ROWS, :]
        is_turned, h_of = marks[index]
        made = jnp.zeros((ROWS, BLK), jnp.float32)
        for h in range(DEPTH):
            plain = part[:, h * BLK : (h + 1) * BLK]
            turn = part[:, (DEPTH + h) * BLK : (DEPTH + h + 1) * BLK]
            made = jnp.where(h_of == h, jnp.where(is_turned, turn, plain), made)
        ghosts.append(
            jnp.concatenate(
                [
                    jnp.where(place == 0, made, low),
                    rest,
                    jnp.where(place == side - 1, made, high),
                    rest,
                ],
                axis=0,
            )
        )
    return ghosts


def ghost_additions(side, received, own_a_ref, own_b_ref, matrix_ref, edge_ref):
    ghosts = ghosts_of(side, received, own_a_ref, own_b_ref, matrix_ref)
    high, low = split2(jnp.concatenate(ghosts, axis=1))
    adds = jnp.dot(
        edge_ref[...],
        jnp.concatenate([high, low], axis=0),
        preferred_element_type=jnp.float32,
    )
    return adds[:, :BLK], adds[:, BLK:]


def corner_part(adds_turned, same):
    cell = plane_row((HALF, BLK), 0)[2]
    halves = []
    for first in (0, BLK - 3):
        lines = [adds_turned[first + at : first + at + 1, :] for at in range(3)]
        halves.append(jnp.where(cell == 0, lines[0], jnp.where(cell == 1, lines[1], lines[2])))
    return split2(jnp.concatenate(halves, axis=0) * same)


def edge_kernel(side, *refs):
    add_x, add_y = ghost_additions(side, refs[:5], *refs[5:9])
    fold_ref, same_ref, gain_ref, old_columns_ref, old_rows_ref = refs[9:14]
    add_x_ref, add_y_ref = refs[14:16]
    outs = refs[16:23]
    columns_ref, rows_ref, strips_ref = refs[23:]
    turned_x, turned_y = add_x.T, add_y.T
    add_x_ref[...] = turned_x
    add_y_ref[...] = add_y
    same = same_ref[...]
    corners = jnp.dot(
        jnp.concatenate(
            [
                jnp.concatenate(corner_part(turned_y, same), axis=1),
                jnp.concatenate(corner_part(turned_x, same), axis=1),
            ],
            axis=0,
        ),
        fold_ref[...],
        preferred_element_type=jnp.float32,
    )
    gain = gain_ref[...]
    columns_ref[...] = old_columns_ref[...] + gain * (add_x + corners[:BLK])
    rows_ref[...] = old_rows_ref[...] + gain * (add_y + corners[BLK:])
    pack(columns_ref, rows_ref, side, outs, strips_ref)


def spread_lanes(turned_x, spread_ref):
    high, low = split2(turned_x)
    return tiles_of(
        jnp.dot(
            jnp.concatenate([high, low], axis=1),
            spread_ref[...],
            preferred_element_type=jnp.float32,
        )
    )


def edge_additions(plane, add_x, add_y):
    lane = lane_of_tile()
    turned = pltpu.roll(add_x, (BLK - 3 - 6 * plane) % BLK, 2)
    add = jnp.where((lane < 3) | (lane >= BLK - 3), turned, 0.0)
    at = 3 * plane
    pad = jnp.zeros((5, BLK), jnp.float32)
    bottom = add[:1] + jnp.concatenate([add_y[at : at + 3], pad], axis=0)[None]
    top = add[-1:] + jnp.concatenate([pad, add_y[HALF + at : HALF + at + 3]], axis=0)[None]
    return jnp.concatenate([bottom, add[1:-1], top], axis=0)


def inner_kernel(first, last, state_ref, *refs):
    if first:
        wave, visc, starts, offsets = refs[:4]
        new_ref, columns_ref, rows_ref = refs[4:7]
        made = refs[7:]
        make_constants(wave, visc, starts[...], offsets[...], made)
        coef_ref, band_x_ref, band_y_ref, order_ref = made[0], made[8], made[9], made[6]
    else:
        coef_ref, band_x_ref, band_y_ref, order_ref, spread_ref = refs[:5]
        add_x_ref, add_y_ref = refs[5:7]
        new_ref = refs[7]
        add_x, add_y = spread_lanes(add_x_ref[...], spread_ref), add_y_ref[...]
        if not last:
            columns_ref, rows_ref = refs[8:]
    if not last:
        clear_rest(rows_ref)
    columns = jnp.zeros((BLK // 8, 8, BLK), jnp.float32)
    group = 2
    for begin in range(0, FACES * LEV, group):
        fields, highs, lows = [], [], []
        for plane in range(begin, begin + group):
            face, level = divmod(plane, LEV)
            a, b = coef_ref[level : level + 1, :], coef_ref[LEV + level : LEV + level + 1, :]
            pressure = tiles_of(state_ref[face, level])
            rate = tiles_of(state_ref[face, LEV + level])
            if not first:
                add = edge_additions(plane, add_x, add_y)
                pressure, rate = pressure + add, rate + add
            high, low = split2((a * pressure + b * rate).reshape(BLK, BLK))
            fields.append((pressure, rate))
            highs.append(high)
            lows.append(low)
        by_x = jnp.dot(
            jnp.concatenate(
                [jnp.concatenate(pair, axis=1) for pair in zip(highs, lows)], axis=0
            ),
            band_x_ref[...],
            preferred_element_type=jnp.float32,
        )
        by_y = jnp.dot(
            band_y_ref[...],
            jnp.concatenate(
                [jnp.concatenate(highs, axis=1), jnp.concatenate(lows, axis=1)], axis=0
            ),
            preferred_element_type=jnp.float32,
        )
        for place, (pressure, rate) in enumerate(fields):
            plane = begin + place
            face, level = divmod(plane, LEV)
            a, b = coef_ref[level : level + 1, :], coef_ref[LEV + level : LEV + level + 1, :]
            at = place * BLK
            rate = rate + tiles_of(by_x[at : at + BLK, :] + by_y[:, at : at + BLK])
            pressure = pressure + rate
            new_ref[face, level] = pressure.reshape(BLK, BLK)
            new_ref[face, LEV + level] = rate.reshape(BLK, BLK)
            if not last:
                columns = take_edges(a * pressure + b * rate, plane, columns, rows_ref)
    if not last:
        columns_ref[...] = rows_from_columns(columns, order_ref[...])


def final_kernel(side, *refs):
    add_x, add_y = ghost_additions(side, refs[:5], *refs[5:9])
    spread_ref, state_ref, out_hbm, buffer, sems = refs[9:]
    add_x = spread_lanes(add_x.T, spread_ref)
    copies = []
    for face in range(FACES):
        for level in range(LEV):
            add = edge_additions(face * LEV + level, add_x, add_y)
            for channel in (level, LEV + level):
                value = tiles_of(state_ref[face, channel]) + add
                buffer[face, channel] = value.reshape(BLK, BLK)
        copy = pltpu.make_async_copy(buffer.at[face], out_hbm.at[face], sems.at[face])
        copy.start()
        copies.append(copy)
    for copy in copies:
        copy.wait()


def exchange(payloads, side):
    def at(row, col):
        return row * side + col

    cells = [(row, col) for row in range(side) for col in range(side)]

    def swap(place, odd_first):
        return (place ^ 1) if not odd_first else (place + (1 if place % 2 else -1)) % side

    core = [(at(r, c), at(r, swap(c, False))) for r, c in cells]
    mirror = [(at(r, c), at(r, swap(c, True))) for r, c in cells]
    near = [(at(r, c), at(swap(r, False), c)) for r, c in cells]
    far = [(at(r, c), at(swap(r, True), c)) for r, c in cells]
    edge = side - 1
    turn = set()
    for x in range(edge):
        turn |= {(at(0, x), at(edge - x, edge)), (at(edge - x, edge), at(0, x))}
    for x in range(1, side):
        turn |= {(at(edge, x), at(edge - x, 0)), (at(edge - x, 0), at(edge, x))}
    turn_out, far_out, near_out, mirror_out, core_out = payloads
    turn_in = lax.ppermute(turn_out, "tile", sorted(turn))
    far_in = lax.ppermute(far_out, "tile", far)
    near_in = lax.ppermute(near_out, "tile", near)
    mirror_in = lax.ppermute(mirror_out, "tile", mirror)
    core_in = lax.ppermute(core_out, "tile", core)
    return turn_in, far_in, near_in, mirror_in, core_in


def call(
    kernel,
    name,
    outs,
    ins,
    scratch=(),
    scalars=(),
    out_hbm=False,
    in_hbm=False,
    limit=VMEM_LIMIT,
    cost=0,
    aliases=None,
):
    hbm = pl.BlockSpec(memory_space=pltpu.HBM)
    vmem = pl.BlockSpec(memory_space=pltpu.VMEM)
    smem = pl.BlockSpec(memory_space=pltpu.SMEM)
    in_specs = [hbm if in_hbm else smem if at in scalars else vmem for at in range(len(ins))]
    return pl.pallas_call(
        kernel,
        out_shape=outs,
        in_specs=in_specs,
        out_specs=[hbm if out_hbm else vmem] * len(outs),
        scratch_shapes=list(scratch),
        compiler_params=pltpu.CompilerParams(vmem_limit_bytes=limit),
        cost_estimate=pl.CostEstimate(flops=cost, bytes_accessed=cost // 500, transcendentals=0),
        input_output_aliases=aliases or {},
        name=name,
    )(*ins)


def on_device(state, wave_coef, visc_coef, stencil_start, stencil_offset):
    side = math.isqrt(lax.axis_size("tile"))
    field = state[0]

    def array(*shape, dtype=jnp.float32):
        return jax.ShapeDtypeStruct(shape, dtype)

    tile = array(BLK, BLK)
    strip = array(ROWS, BLK)
    whole = array(*field.shape)
    work = [
        pltpu.VMEM((BLK, BLK), jnp.float32),
        pltpu.VMEM((BLK, BLK), jnp.float32),
        pltpu.VMEM((4, FACES, 16, BLK), jnp.float32),
    ]
    scalars = pltpu.SMEM((LEV,), jnp.float32)
    sent = call(
        lambda *refs: first_kernel(side, *refs),
        "first_edges",
        [strip] * 7,
        [field, wave_coef, visc_coef],
        [
            pltpu.VMEM(field.shape, jnp.float32),
            scalars,
            scalars,
            *work,
            pltpu.SemaphoreType.DMA((FACES + 2,)),
        ],
        in_hbm=True,
        limit=FIRST_LIMIT,
        cost=1_000_000_000,
    )
    made = {}
    adds = []
    for step in range(SUBSTEPS):
        first, last = step == 0, step == SUBSTEPS - 1
        received = exchange(sent[:5], side)

        def inner(*refs, first=first, last=last):
            inner_kernel(first, last, *refs)

        if first:
            field, *rest = call(
                inner,
                "inner",
                [whole] + [tile] * 2 + [array(*shape, dtype=kind) for _, shape, kind in CONSTANTS],
                [field, wave_coef, visc_coef, stencil_start, stencil_offset],
                scalars=(1, 2),
                cost=2_000_000_000,
            )
            edges = rest[:2]
            made = dict(zip((name for name, _, _ in CONSTANTS), rest[2:]))
        else:
            names = ("coef", "band_x", "band_y", "order", "spread")
            field, *edges = call(
                inner,
                "inner",
                [whole] + ([] if last else [tile] * 2),
                [field, *(made[name] for name in names), *adds],
                cost=2_000_000_000,
                aliases={0: 0},
            )
        ghosts = [*received, *sent[5:], made["matrix"], made["edge"]]
        if last:
            break
        updates = call(
            lambda *refs: edge_kernel(side, *refs),
            "edges",
            [tile] * 2 + [strip] * 7,
            [*ghosts, made["fold"], made["same"], made["gain"], *edges],
            work,
        )
        adds, sent = updates[:2], updates[2:]
    (field,) = call(
        lambda *refs: final_kernel(side, *refs),
        "final",
        [whole],
        [*ghosts, made["spread"], field],
        [pltpu.VMEM(field.shape, jnp.float32), pltpu.SemaphoreType.DMA((FACES,))],
        out_hbm=True,
    )
    return field[None]


def solution(mesh):
    placed = (P(("member", "tile"), None, None, None, None), P(), P(), P(), P())
    return jax.shard_map(
        on_device,
        mesh=mesh,
        in_specs=placed,
        out_specs=P(("member", "tile"), None, None, None, None),
        check_vma=False,
    )
```

time: 60.4 us -> 49.2 us (0.81)
  local copies, waits for them, and re-layouts: 4.34 us -> 0.03 us
  waiting for transfers between devices: 7.92 us -> 5.08 us
  Pallas kernels: 16.3 us -> 13.9 us
  starting transfers between devices: 31.3 us -> 29.7 us
    ppermute x4, starting transfers between devices: 8.75 us -> 0.28 us  [exchange(): far_in = lax.ppermute(far_out, 'tile', far)]
    ppermute x4, waiting for transfers between devices: 7.88 us -> 0.05 us  [exchange(): turn_in = lax.ppermute(turn_out, 'tile', sorted(turn))]
    ppermute x4, waiting for transfers between devices: 0.01 us -> 5 us  [exchange(): far_in = lax.ppermute(far_out, 'tile', far)]
    unnamed x10 -> x14, local copies, waits for them, and re-layouts: 4.34 us -> 0.03 us
    ppermute x4, starting transfers between devices: 2.86 us -> 5.71 us  [exchange(): mirror_in = lax.ppermute(mirror_out, 'tile', mirror)]
    ppermute x4, starting transfers between devices: 14.8 us -> 17.6 us  [exchange(): turn_in = lax.ppermute(turn_out, 'tile', sorted(turn))]
    pallas_call x10 -> x9, Pallas kernels: 16.3 us -> 13.9 us  [call(): pl.pallas_call(kernel, out_shape=outs, in_specs=in_specs, out_specs=[hbm...]
    ppermute x4, starting transfers between devices: 4.11 us -> 5.11 us  [exchange(): near_in = lax.ppermute(near_out, 'tile', near)]
  transfers between devices with their start and end apart: 20 -> 20, of which waited for: 4 -> 4; matrix products, arithmetic and copies ran while one was open for 0% -> 0% of each run, Pallas kernels for 15% -> 13%
where the time goes in v3:
time: 49.2 us; the launch traced here: 48.9 us
  starting transfers between devices  29.7 us (60%)
  Pallas kernels  13.9 us (28%)
  waiting for transfers between devices  5.08 us (10%)
    ppermute x4, starting transfers between devices, exchange(): turn_in = lax.ppermute(turn_out, 'tile', sorted(turn))  17.6 us
    pallas_call x9, Pallas kernels, call(): pl.pallas_call(kernel, out_shape=outs, in_specs=in_specs, out_specs=[hbm...  13.9 us
    ppermute x4, starting transfers between devices, exchange(): mirror_in = lax.ppermute(mirror_out, 'tile', mirror)  5.71 us
    ppermute x4, starting transfers between devices, exchange(): near_in = lax.ppermute(near_out, 'tile', near)  5.11 us
    ppermute x4, waiting for transfers between devices, exchange(): far_in = lax.ppermute(far_out, 'tile', far)  5 us
  transfers between devices with their start and end apart: 20, of which 4 were waited for; matrix products, arithmetic and copies ran while one was open for 0% of the time, Pallas kernels for 13%

profile of v3, /device:TPU:0, one launch (start us, length us, event | category | flops | bytes accessed | tf_op | source)
XLA Modules:
  0.0 48.9 jit_solution(6928564134339609688)
XLA Ops:
  0.0 2.8 %first_edges.1 = (f32[56,128]{1,0:T(8,128)}, f32[56,128]{1,0:T(8,128)}, f32[56,128]{1,0:T(8,128)}, f32[56,128]{1,0:T(8,128)}, f32[56,128]{1,0:T(8,128)}, /*index=5*/f32[56,128]{1,0:T(8,128)}, f32[56,128]{1,0:T(8,128)}) custom-call(f32[6,6,128,128]{3,2,1,0:T(8,128)} %bitcast.2, f32[3]{0:T(128)} %refs_1_.3, f32[3]{0:T(128)} %refs_2_.3), custom_call_target="tpu_custom_call" | custom-call | flops 1000000000 | bytes 2000000 | tf_op jit(solution)/shard_map/first_edges/pallas_call | solution.py:522
  2.9 7.4 %collective-permute-start = (f32[56,128]{1,0:T(8,128)}, f32[56,128]{1,0:T(8,128)S(1)}, u32[]{:S(2)}, u32[]{:S(2)}) collective-permute-start(f32[56,128]{1,0:T(8,128)} %get-tuple-element.58), channel_id=1, source_target_pairs={{0,15},{1,11},{2,7},{4,14},{7,2},{8,13},{11,1},{13,8},{14,4},{15,0... | collective-permute-start | bytes 86024 | tf_op jit(solution)/shard_map/ppermute | solution.py:497
  10.2 0.1 collective-permute-start.1
  10.3 1.2 %collective-permute-start.2 = (f32[56,128]{1,0:T(8,128)}, f32[56,128]{1,0:T(8,128)S(1)}, u32[]{:S(2)}, u32[]{:S(2)}) collective-permute-start(f32[56,128]{1,0:T(8,128)} %get-tuple-element.60), channel_id=1, source_target_pairs={{0,4},{1,5},{2,6},{3,7},{4,0},{5,1},{6,2},{7,3},{8,12},{9,13},{10,... | collective-permute-start | bytes 86024 | tf_op jit(solution)/shard_map/ppermute | solution.py:499
  11.5 0.3 collective-permute-start.4
  11.8 1.8 %inner.4 = (f32[6,6,128,128]{3,2,1,0:T(8,128)S(1)}, f32[128,128]{1,0:T(8,128)S(1)}, f32[128,128]{1,0:T(8,128)S(1)}, f32[8,128]{1,0:T(8,128)S(1)}, f32[128,128]{1...) custom-call(f32[6,6,128,128]{3,2,1,0:T(8,128)S(1)} %bitcast.3, ...), custom_call_target="tpu_custom_call" | custom-call | flops 2000000000 | bytes 4000000 | tf_op jit(solution)/shard_map/inner/pallas_call | solution.py:522
  13.6 2.5 %collective-permute-done.1.refs_1_ = f32[56,128]{1,0:T(8,128)S(1)} collective-permute-done((f32[56,128]{1,0:T(8,128)}, f32[56,128]{1,0:T(8,128)S(1)}, u32[]{:S(2)}, u32[]{:S(2)}) %collective-permute-start.1) | collective-permute-done | bytes 28704 | tf_op jit(solution)/shard_map/ppermute | solution.py:498
  16.2 0.8 %edges.3 = (f32[128,128]{1,0:T(8,128)S(1)}, f32[128,128]{1,0:T(8,128)S(1)}, f32[56,128]{1,0:T(8,128)S(1)}, f32[56,128]{1,0:T(8,128)S(1)}, f32[56,128]{1,0:T(8,12...) custom-call(f32[56,128]{1,0:T(8,128)S(1)} %collective-permute-done.refs_0, ...), custom_call_target="tpu_custom_call" | custom-call | tf_op jit(solution)/shard_map/edges/pallas_call | solution.py:522
  17.0 3.1 %collective-permute-start.5 = (f32[56,128]{1,0:T(8,128)S(1)}, f32[56,128]{1,0:T(8,128)S(1)}, u32[]{:S(2)}, u32[]{:S(2)}) collective-permute-start(f32[56,128]{1,0:T(8,128)S(1)} %get-tuple-element.72), channel_id=1, source_target_pairs={{0,15},{1,11},{2,7},{4,14},{7,2},{8,13},{11,1},{13,8},{14,4},{15,0... | collective-permute-start | bytes 86024 | tf_op jit(solution)/shard_map/ppermute | solution.py:497
  20.1 0.1 collective-permute-start.6
  20.2 1.3 %collective-permute-start.7 = (f32[56,128]{1,0:T(8,128)S(1)}, f32[56,128]{1,0:T(8,128)S(1)}, u32[]{:S(2)}, u32[]{:S(2)}) collective-permute-start(f32[56,128]{1,0:T(8,128)S(1)} %get-tuple-element.74), channel_id=1, source_target_pairs={{0,4},{1,5},{2,6},{3,7},{4,0},{5,1},{6,2},{7,3},{8,12},{9,13},{10,... | collective-permute-start | bytes 86024 | tf_op jit(solution)/shard_map/ppermute | solution.py:499
  21.6 2.2 %collective-permute-start.8 = (f32[56,128]{1,0:T(8,128)S(1)}, f32[56,128]{1,0:T(8,128)S(1)}, u32[]{:S(2)}, u32[]{:S(2)}) collective-permute-start(f32[56,128]{1,0:T(8,128)S(1)} %get-tuple-element.75), channel_id=1, source_target_pairs={{0,3},{1,2},{2,1},{3,0},{4,7},{5,6},{6,5},{7,4},{8,11},{9,10},{10,... | collective-permute-start | bytes 86024 | tf_op jit(solution)/shard_map/ppermute | solution.py:500
  23.7 1.6 %inner.5 = (f32[6,6,128,128]{3,2,1,0:T(8,128)S(1)}, f32[128,128]{1,0:T(8,128)S(1)}, f32[128,128]{1,0:T(8,128)S(1)}) custom-call(f32[6,6,128,128]{3,2,1,0:T(8,128)S(1)} %get-tuple-element.79.refs_0_, f32[8,128]{1,0:T(8,128)S(1)} %get-tuple-element.80.refs_1_, bf16[256,128]{1,0:T(8,128)(2,1)S(1)} %get-tuple-element.81.refs_2_, ...), custom_call_target="tpu_custom_call", output_to_operand_aliasing={{0}: (0, {})} | custom-call | flops 2000000000 | bytes 4000000 | tf_op jit(solution)/shard_map/inner/pallas_call | solution.py:522
  25.3 0.6 %collective-permute-done.6.refs_1_ = f32[56,128]{1,0:T(8,128)S(1)} collective-permute-done((f32[56,128]{1,0:T(8,128)S(1)}, f32[56,128]{1,0:T(8,128)S(1)}, u32[]{:S(2)}, u32[]{:S(2)}) %collective-permute-start.6) | collective-permute-done | bytes 28704 | tf_op jit(solution)/shard_map/ppermute | solution.py:498
  26.0 0.8 %edges.4 = (f32[128,128]{1,0:T(8,128)S(1)}, f32[128,128]{1,0:T(8,128)S(1)}, f32[56,128]{1,0:T(8,128)S(1)}, f32[56,128]{1,0:T(8,128)S(1)}, f32[56,128]{1,0:T(8,12...) custom-call(f32[56,128]{1,0:T(8,128)S(1)} %collective-permute-done.5.refs, ...), custom_call_target="tpu_custom_call" | custom-call | tf_op jit(solution)/shard_map/edges/pallas_call | solution.py:522
  26.8 3.9 %collective-permute-start.10 = (f32[56,128]{1,0:T(8,128)S(1)}, f32[56,128]{1,0:T(8,128)S(1)}, u32[]{:S(2)}, u32[]{:S(2)}) collective-permute-start(f32[56,128]{1,0:T(8,128)S(1)} %get-tuple-element.89), channel_id=1, source_target_pairs={{0,15},{1,11},{2,7},{4,14},{7,2},{8,13},{11,1},{13,8},{14,4},{15,0... | collective-permute-start | bytes 86024 | tf_op jit(solution)/shard_map/ppermute | solution.py:497
  30.7 0.1 collective-permute-start.11
  30.7 0.7 %collective-permute-start.12 = (f32[56,128]{1,0:T(8,128)S(1)}, f32[56,128]{1,0:T(8,128)S(1)}, u32[]{:S(2)}, u32[]{:S(2)}) collective-permute-start(f32[56,128]{1,0:T(8,128)S(1)} %get-tuple-element.91), channel_id=1, source_target_pairs={{0,4},{1,5},{2,6},{3,7},{4,0},{5,1},{6,2},{7,3},{8,12},{9,13},{10,... | collective-permute-start | bytes 86024 | tf_op jit(solution)/shard_map/ppermute | solution.py:499
  31.5 2.0 %collective-permute-start.13 = (f32[56,128]{1,0:T(8,128)S(1)}, f32[56,128]{1,0:T(8,128)S(1)}, u32[]{:S(2)}, u32[]{:S(2)}) collective-permute-start(f32[56,128]{1,0:T(8,128)S(1)} %get-tuple-element.92), channel_id=1, source_target_pairs={{0,3},{1,2},{2,1},{3,0},{4,7},{5,6},{6,5},{7,4},{8,11},{9,10},{10,... | collective-permute-start | bytes 86024 | tf_op jit(solution)/shard_map/ppermute | solution.py:500
  33.5 0.3 collective-permute-start.14
  33.8 1.6 %inner.6 = (f32[6,6,128,128]{3,2,1,0:T(8,128)S(1)}, f32[128,128]{1,0:T(8,128)S(1)}, f32[128,128]{1,0:T(8,128)S(1)}) custom-call(f32[6,6,128,128]{3,2,1,0:T(8,128)S(1)} %get-tuple-element.96.refs_0_, f32[8,128]{1,0:T(8,128)S(1)} %get-tuple-element.80.refs_1_, bf16[256,128]{1,0:T(8,128)(2,1)S(1)} %get-tuple-element.81.refs_2_, ...), custom_call_target="tpu_custom_call", output_to_operand_aliasing={{0}: (0, {})} | custom-call | flops 2000000000 | bytes 4000000 | tf_op jit(solution)/shard_map/inner/pallas_call | solution.py:522
  35.4 0.0 collective-permute-done.10.refs_0_
  35.4 1.0 %collective-permute-done.11.refs_1_ = f32[56,128]{1,0:T(8,128)S(1)} collective-permute-done((f32[56,128]{1,0:T(8,128)S(1)}, f32[56,128]{1,0:T(8,128)S(1)}, u32[]{:S(2)}, u32[]{:S(2)}) %collective-permute-start.11) | collective-permute-done | bytes 28704 | tf_op jit(solution)/shard_map/ppermute | solution.py:498
  36.4 0.8 %edges.5 = (f32[128,128]{1,0:T(8,128)S(1)}, f32[128,128]{1,0:T(8,128)S(1)}, f32[56,128]{1,0:T(8,128)S(1)}, f32[56,128]{1,0:T(8,128)S(1)}, f32[56,128]{1,0:T(8,12...) custom-call(f32[56,128]{1,0:T(8,128)S(1)} %collective-permute-done.10.ref, ...), custom_call_target="tpu_custom_call" | custom-call | tf_op jit(solution)/shard_map/edges/pallas_call | solution.py:522
  37.2 3.2 %collective-permute-start.15 = (f32[56,128]{1,0:T(8,128)S(1)}, f32[56,128]{1,0:T(8,128)S(1)}, u32[]{:S(2)}, u32[]{:S(2)}) collective-permute-start(f32[56,128]{1,0:T(8,128)S(1)} %get-tuple-element.101), channel_id=1, source_target_pairs={{0,15},{1,11},{2,7},{4,14},{7,2},{8,13},{11,1},{13,8},{14,4},{15,0... | collective-permute-start | bytes 86024 | tf_op jit(solution)/shard_map/ppermute | solution.py:497
  40.4 0.1 collective-permute-start.16
  40.5 1.9 %collective-permute-start.17 = (f32[56,128]{1,0:T(8,128)S(1)}, f32[56,128]{1,0:T(8,128)S(1)}, u32[]{:S(2)}, u32[]{:S(2)}) collective-permute-start(f32[56,128]{1,0:T(8,128)S(1)} %get-tuple-element.103), channel_id=1, source_target_pairs={{0,4},{1,5},{2,6},{3,7},{4,0},{5,1},{6,2},{7,3},{8,12},{9,13},{10,... | collective-permute-start | bytes 86024 | tf_op jit(solution)/shard_map/ppermute | solution.py:499
  42.4 1.5 %collective-permute-start.18 = (f32[56,128]{1,0:T(8,128)S(1)}, f32[56,128]{1,0:T(8,128)S(1)}, u32[]{:S(2)}, u32[]{:S(2)}) collective-permute-start(f32[56,128]{1,0:T(8,128)S(1)} %get-tuple-element.104), channel_id=1, source_target_pairs={{0,3},{1,2},{2,1},{3,0},{4,7},{5,6},{6,5},{7,4},{8,11},{9,10},{10,... | collective-permute-start | bytes 86024 | tf_op jit(solution)/shard_map/ppermute | solution.py:500
  43.9 0.3 collective-permute-start.19
  44.2 1.3 %inner.7.refs_10_ = f32[6,6,128,128]{3,2,1,0:T(8,128)S(1)} custom-call(f32[6,6,128,128]{3,2,1,0:T(8,128)S(1)} %get-tuple-element.108.refs_0_, f32[8,128]{1,0:T(8,128)S(1)} %get-tuple-element.80.refs_1_, bf16[256,128]{1,0:T(8,128)(2,1)S(1)} %get-tuple-element.81.refs_2_, ...), custom_call_target="tpu_custom_call", output_to_operand_aliasing={{}: (0, {})} | custom-call | flops 2000000000 | bytes 4000000 | tf_op jit(solution)/shard_map/inner/pallas_call | solution.py:522
  45.5 0.9 %collective-permute-done.16.refs_1_ = f32[56,128]{1,0:T(8,128)S(1)} collective-permute-done((f32[56,128]{1,0:T(8,128)S(1)}, f32[56,128]{1,0:T(8,128)S(1)}, u32[]{:S(2)}, u32[]{:S(2)}) %collective-permute-start.16) | collective-permute-done | bytes 28704 | tf_op jit(solution)/shard_map/ppermute | solution.py:498
  46.4 2.5 %final.1 = f32[6,6,128,128]{3,2,1,0:T(8,128)} custom-call(f32[56,128]{1,0:T(8,128)S(1)} %collective-permute-done.15.refs_0_, f32[56,128]{1,0:T(8,128)S(1)} %collective-permute-done.16.refs_1_, f32[56,128]{1,0:T(8,128)S(1)} %collective-permute-done.17.refs_2_, f32[56,128]{1,0:T(8,128)S(1)} %collective-permute-done.18.refs_3_, ...), custom_call_target="tpu_custom_call" | custom-call | tf_op jit(solution)/shard_map/final/pallas_call | solution.py:522
  (31 shorter events, 0.1 us)
Async XLA Ops:
  0.0 11.8 %copy-start.6 = (f32[3]{0:T(128)S(1)}, f32[3]{0:T(128)}, u32[]{:S(2)}) copy-start(f32[3]{0:T(128)} %refs_2_.3) | copy-start | bytes 40
  0.0 11.8 %copy-start.5 = (f32[3]{0:T(128)S(1)}, f32[3]{0:T(128)}, u32[]{:S(2)}) copy-start(f32[3]{0:T(128)} %refs_1_.3) | copy-start | bytes 40
  0.0 11.8 %copy-start.2 = (f32[1,6,6,128,128]{4,3,2,1,0:T(8,128)S(1)}, f32[1,6,6,128,128]{4,3,2,1,0:T(8,128)}, u32[]{:S(2)}) copy-start(f32[1,6,6,128,128]{4,3,2,1,0:T(8,128)} %param.5) | copy-start | bytes 7077892
  0.0 11.8 %copy-start.4 = (f32[3,128]{1,0:T(4,128)S(1)}, f32[3,128]{1,0:T(4,128)}, u32[]{:S(2)}) copy-start(f32[3,128]{1,0:T(4,128)} %refs_4_.1) | copy-start | bytes 4612
  0.0 11.8 %copy-start.3 = (s32[3,128]{1,0:T(4,128)S(1)}, s32[3,128]{1,0:T(4,128)}, u32[]{:S(2)}) copy-start(s32[3,128]{1,0:T(4,128)} %refs_3_.1) | copy-start | bytes 4612
  2.9 10.8 %collective-permute-start = (f32[56,128]{1,0:T(8,128)}, f32[56,128]{1,0:T(8,128)S(1)}, u32[]{:S(2)}, u32[]{:S(2)}) collective-permute-start(f32[56,128]{1,0:T(8,128)} %get-tuple-element.58), channel_id=1, source_target_pairs={{0,15},{1,11},{2,7},{4,14},{7,2},{8,13},{11,1},{13,8},{14,4},{15,0... | collective-permute-start | bytes 86024 | tf_op jit(solution)/shard_map/ppermute | solution.py:497
  10.2 5.9 %collective-permute-start.1 = (f32[56,128]{1,0:T(8,128)}, f32[56,128]{1,0:T(8,128)S(1)}, u32[]{:S(2)}, u32[]{:S(2)}) collective-permute-start(f32[56,128]{1,0:T(8,128)} %get-tuple-element.59), channel_id=1, source_target_pairs={{0,12},{1,13},{2,14},{3,15},{4,8},{5,9},{6,10},{7,11},{8,4},{9,5},... | collective-permute-start | bytes 86024 | tf_op jit(solution)/shard_map/ppermute | solution.py:498
  10.3 5.9 %collective-permute-start.2 = (f32[56,128]{1,0:T(8,128)}, f32[56,128]{1,0:T(8,128)S(1)}, u32[]{:S(2)}, u32[]{:S(2)}) collective-permute-start(f32[56,128]{1,0:T(8,128)} %get-tuple-element.60), channel_id=1, source_target_pairs={{0,4},{1,5},{2,6},{3,7},{4,0},{5,1},{6,2},{7,3},{8,12},{9,13},{10,... | collective-permute-start | bytes 86024 | tf_op jit(solution)/shard_map/ppermute | solution.py:499
  11.5 4.7 %collective-permute-start.3 = (f32[56,128]{1,0:T(8,128)}, f32[56,128]{1,0:T(8,128)S(1)}, u32[]{:S(2)}, u32[]{:S(2)}) collective-permute-start(f32[56,128]{1,0:T(8,128)} %get-tuple-element.61), channel_id=1, source_target_pairs={{0,3},{1,2},{2,1},{3,0},{4,7},{5,6},{6,5},{7,4},{8,11},{9,10},{10,... | collective-permute-start | bytes 86024 | tf_op jit(solution)/shard_map/ppermute | solution.py:500
  11.5 4.7 %copy-start = (f32[56,128]{1,0:T(8,128)S(1)}, f32[56,128]{1,0:T(8,128)}, u32[]{:S(2)}) copy-start(f32[56,128]{1,0:T(8,128)} %get-tuple-element.63.refs_5_) | copy-start | bytes 86020
  11.5 4.7 %copy-start.1 = (f32[56,128]{1,0:T(8,128)S(1)}, f32[56,128]{1,0:T(8,128)}, u32[]{:S(2)}) copy-start(f32[56,128]{1,0:T(8,128)} %get-tuple-element.64.refs_6_) | copy-start | bytes 86020
  11.5 4.7 %collective-permute-start.4 = (f32[56,128]{1,0:T(8,128)}, f32[56,128]{1,0:T(8,128)S(1)}, u32[]{:S(2)}, u32[]{:S(2)}) collective-permute-start(f32[56,128]{1,0:T(8,128)} %get-tuple-element.62), channel_id=1, source_target_pairs={{0,1},{1,0},{2,3},{3,2},{4,5},{5,4},{6,7},{7,6},{8,9},{9,8},{10,11... | collective-permute-start | bytes 86024 | tf_op jit(solution)/shard_map/ppermute | solution.py:501
  17.0 8.3 %collective-permute-start.5 = (f32[56,128]{1,0:T(8,128)S(1)}, f32[56,128]{1,0:T(8,128)S(1)}, u32[]{:S(2)}, u32[]{:S(2)}) collective-permute-start(f32[56,128]{1,0:T(8,128)S(1)} %get-tuple-element.72), channel_id=1, source_target_pairs={{0,15},{1,11},{2,7},{4,14},{7,2},{8,13},{11,1},{13,8},{14,4},{15,0... | collective-permute-start | bytes 86024 | tf_op jit(solution)/shard_map/ppermute | solution.py:497
  20.1 5.8 %collective-permute-start.6 = (f32[56,128]{1,0:T(8,128)S(1)}, f32[56,128]{1,0:T(8,128)S(1)}, u32[]{:S(2)}, u32[]{:S(2)}) collective-permute-start(f32[56,128]{1,0:T(8,128)S(1)} %get-tuple-element.73), channel_id=1, source_target_pairs={{0,12},{1,13},{2,14},{3,15},{4,8},{5,9},{6,10},{7,11},{8,4},{9,5},... | collective-permute-start | bytes 86024 | tf_op jit(solution)/shard_map/ppermute | solution.py:498
  20.2 5.8 %collective-permute-start.7 = (f32[56,128]{1,0:T(8,128)S(1)}, f32[56,128]{1,0:T(8,128)S(1)}, u32[]{:S(2)}, u32[]{:S(2)}) collective-permute-start(f32[56,128]{1,0:T(8,128)S(1)} %get-tuple-element.74), channel_id=1, source_target_pairs={{0,4},{1,5},{2,6},{3,7},{4,0},{5,1},{6,2},{7,3},{8,12},{9,13},{10,... | collective-permute-start | bytes 86024 | tf_op jit(solution)/shard_map/ppermute | solution.py:499
  21.6 4.4 %collective-permute-start.8 = (f32[56,128]{1,0:T(8,128)S(1)}, f32[56,128]{1,0:T(8,128)S(1)}, u32[]{:S(2)}, u32[]{:S(2)}) collective-permute-start(f32[56,128]{1,0:T(8,128)S(1)} %get-tuple-element.75), channel_id=1, source_target_pairs={{0,3},{1,2},{2,1},{3,0},{4,7},{5,6},{6,5},{7,4},{8,11},{9,10},{10,... | collective-permute-start | bytes 86024 | tf_op jit(solution)/shard_map/ppermute | solution.py:500
  23.7 2.3 %collective-permute-start.9 = (f32[56,128]{1,0:T(8,128)S(1)}, f32[56,128]{1,0:T(8,128)S(1)}, u32[]{:S(2)}, u32[]{:S(2)}) collective-permute-start(f32[56,128]{1,0:T(8,128)S(1)} %get-tuple-element.76), channel_id=1, source_target_pairs={{0,1},{1,0},{2,3},{3,2},{4,5},{5,4},{6,7},{7,6},{8,9},{9,8},{10,11... | collective-permute-start | bytes 86024 | tf_op jit(solution)/shard_map/ppermute | solution.py:501
  26.8 8.7 %collective-permute-start.10 = (f32[56,128]{1,0:T(8,128)S(1)}, f32[56,128]{1,0:T(8,128)S(1)}, u32[]{:S(2)}, u32[]{:S(2)}) collective-permute-start(f32[56,128]{1,0:T(8,128)S(1)} %get-tuple-element.89), channel_id=1, source_target_pairs={{0,15},{1,11},{2,7},{4,14},{7,2},{8,13},{11,1},{13,8},{14,4},{15,0... | collective-permute-start | bytes 86024 | tf_op jit(solution)/shard_map/ppermute | solution.py:497
  30.7 5.7 %collective-permute-start.11 = (f32[56,128]{1,0:T(8,128)S(1)}, f32[56,128]{1,0:T(8,128)S(1)}, u32[]{:S(2)}, u32[]{:S(2)}) collective-permute-start(f32[56,128]{1,0:T(8,128)S(1)} %get-tuple-element.90), channel_id=1, source_target_pairs={{0,12},{1,13},{2,14},{3,15},{4,8},{5,9},{6,10},{7,11},{8,4},{9,5},... | collective-permute-start | bytes 86024 | tf_op jit(solution)/shard_map/ppermute | solution.py:498
  30.7 5.7 %collective-permute-start.12 = (f32[56,128]{1,0:T(8,128)S(1)}, f32[56,128]{1,0:T(8,128)S(1)}, u32[]{:S(2)}, u32[]{:S(2)}) collective-permute-start(f32[56,128]{1,0:T(8,128)S(1)} %get-tuple-element.91), channel_id=1, source_target_pairs={{0,4},{1,5},{2,6},{3,7},{4,0},{5,1},{6,2},{7,3},{8,12},{9,13},{10,... | collective-permute-start | bytes 86024 | tf_op jit(solution)/shard_map/ppermute | solution.py:499
  31.5 4.9 %collective-permute-start.13 = (f32[56,128]{1,0:T(8,128)S(1)}, f32[56,128]{1,0:T(8,128)S(1)}, u32[]{:S(2)}, u32[]{:S(2)}) collective-permute-start(f32[56,128]{1,0:T(8,128)S(1)} %get-tuple-element.92), channel_id=1, source_target_pairs={{0,3},{1,2},{2,1},{3,0},{4,7},{5,6},{6,5},{7,4},{8,11},{9,10},{10,... | collective-permute-start | bytes 86024 | tf_op jit(solution)/shard_map/ppermute | solution.py:500
  33.5 2.9 %collective-permute-start.14 = (f32[56,128]{1,0:T(8,128)S(1)}, f32[56,128]{1,0:T(8,128)S(1)}, u32[]{:S(2)}, u32[]{:S(2)}) collective-permute-start(f32[56,128]{1,0:T(8,128)S(1)} %get-tuple-element.93), channel_id=1, source_target_pairs={{0,1},{1,0},{2,3},{3,2},{4,5},{5,4},{6,7},{7,6},{8,9},{9,8},{10,11... | collective-permute-start | bytes 86024 | tf_op jit(solution)/shard_map/ppermute | solution.py:501
  37.2 8.3 %collective-permute-start.15 = (f32[56,128]{1,0:T(8,128)S(1)}, f32[56,128]{1,0:T(8,128)S(1)}, u32[]{:S(2)}, u32[]{:S(2)}) collective-permute-start(f32[56,128]{1,0:T(8,128)S(1)} %get-tuple-element.101), channel_id=1, source_target_pairs={{0,15},{1,11},{2,7},{4,14},{7,2},{8,13},{11,1},{13,8},{14,4},{15,0... | collective-permute-start | bytes 86024 | tf_op jit(solution)/shard_map/ppermute | solution.py:497
  40.4 5.9 %collective-permute-start.16 = (f32[56,128]{1,0:T(8,128)S(1)}, f32[56,128]{1,0:T(8,128)S(1)}, u32[]{:S(2)}, u32[]{:S(2)}) collective-permute-start(f32[56,128]{1,0:T(8,128)S(1)} %get-tuple-element.102), channel_id=1, source_target_pairs={{0,12},{1,13},{2,14},{3,15},{4,8},{5,9},{6,10},{7,11},{8,4},{9,5},... | collective-permute-start | bytes 86024 | tf_op jit(solution)/shard_map/ppermute | solution.py:498
  40.5 5.9 %collective-permute-start.17 = (f32[56,128]{1,0:T(8,128)S(1)}, f32[56,128]{1,0:T(8,128)S(1)}, u32[]{:S(2)}, u32[]{:S(2)}) collective-permute-start(f32[56,128]{1,0:T(8,128)S(1)} %get-tuple-element.103), channel_id=1, source_target_pairs={{0,4},{1,5},{2,6},{3,7},{4,0},{5,1},{6,2},{7,3},{8,12},{9,13},{10,... | collective-permute-start | bytes 86024 | tf_op jit(solution)/shard_map/ppermute | solution.py:499
  42.4 4.0 %collective-permute-start.18 = (f32[56,128]{1,0:T(8,128)S(1)}, f32[56,128]{1,0:T(8,128)S(1)}, u32[]{:S(2)}, u32[]{:S(2)}) collective-permute-start(f32[56,128]{1,0:T(8,128)S(1)} %get-tuple-element.104), channel_id=1, source_target_pairs={{0,3},{1,2},{2,1},{3,0},{4,7},{5,6},{6,5},{7,4},{8,11},{9,10},{10,... | collective-permute-start | bytes 86024 | tf_op jit(solution)/shard_map/ppermute | solution.py:500
  43.9 2.5 %collective-permute-start.19 = (f32[56,128]{1,0:T(8,128)S(1)}, f32[56,128]{1,0:T(8,128)S(1)}, u32[]{:S(2)}, u32[]{:S(2)}) collective-permute-start(f32[56,128]{1,0:T(8,128)S(1)} %get-tuple-element.105), channel_id=1, source_target_pairs={{0,1},{1,0},{2,3},{3,2},{4,5},{5,4},{6,7},{7,6},{8,9},{9,8},{10,11... | collective-permute-start | bytes 86024 | tf_op jit(solution)/shard_map/ppermute | solution.py:501

commit v4 on v3

--- a/solution.py
+++ b/solution.py
@@ -90,6 +90,10 @@
 def position(side):
     index = lax.axis_index("tile")
     return lax.rem(index, side), lax.div(index, side)
+
+
+def is_inner(row, col, side):
+    return 0 < row < side - 1 and 0 < col < side - 1
 
 
 def row_codes(shape):
@@ -493,6 +497,12 @@
         turn |= {(at(0, x), at(edge - x, edge)), (at(edge - x, edge), at(0, x))}
     for x in range(1, side):
         turn |= {(at(edge, x), at(edge - x, 0)), (at(edge - x, 0), at(edge, x))}
+    spare = [pair for pair in mirror if is_inner(pair[0] // side, pair[0] % side, side)]
+    first_end, last_end = at(1, edge - 1), at(edge - 1, 1)
+    left = [b for a, b in spare if a in (first_end, last_end)]
+    spare = [pair for pair in spare if not {*pair} & {first_end, last_end}]
+    spare += [(at(0, edge), first_end), (at(edge, 0), last_end), (left[0], left[1])]
+    turn |= {(a, b) for a, b in spare} | {(b, a) for a, b in spare}
     turn_out, far_out, near_out, mirror_out, core_out = payloads
     turn_in = lax.ppermute(turn_out, "tile", sorted(turn))
     far_in = lax.ppermute(far_out, "tile", far)

time: 49.2 us -> 41.4 us (0.84)
  starting transfers between devices: 29.7 us -> 22.1 us
    ppermute x4, starting transfers between devices: 17.6 us -> 10.2 us  [exchange(): turn_in = lax.ppermute(turn_out, 'tile', sorted(turn))]
    ppermute x4, starting transfers between devices: 0.28 us -> 3.23 us  [exchange(): far_in = lax.ppermute(far_out, 'tile', far)]
    ppermute x4, starting transfers between devices: 5.11 us -> 2.45 us  [exchange(): near_in = lax.ppermute(near_out, 'tile', near)]
    ppermute x4, starting transfers between devices: 5.71 us -> 5.12 us  [exchange(): mirror_in = lax.ppermute(mirror_out, 'tile', mirror)]
  transfers between devices with their start and end apart: 20 -> 20, of which waited for: 4 -> 4; matrix products, arithmetic and copies ran while one was open for 0% -> 0% of each run, Pallas kernels for 13% -> 15%
where the time goes in v4:
time: 41.4 us; the launch traced here: 41.3 us
  starting transfers between devices  22.1 us (53%)
  Pallas kernels  13.9 us (34%)
  waiting for transfers between devices  5.07 us (12%)
    pallas_call x9, Pallas kernels, call(): pl.pallas_call(kernel, out_shape=outs, in_specs=in_specs, out_specs=[hbm...  13.9 us
    ppermute x4, starting transfers between devices, exchange(): turn_in = lax.ppermute(turn_out, 'tile', sorted(turn))  10.2 us
    ppermute x4, starting transfers between devices, exchange(): mirror_in = lax.ppermute(mirror_out, 'tile', mirror)  5.12 us
    ppermute x4, waiting for transfers between devices, exchange(): far_in = lax.ppermute(far_out, 'tile', far)  5 us
    ppermute x4, starting transfers between devices, exchange(): far_in = lax.ppermute(far_out, 'tile', far)  3.23 us
    ppermute x4, starting transfers between devices, exchange(): near_in = lax.ppermute(near_out, 'tile', near)  2.45 us
    ppermute x4, starting transfers between devices, exchange(): core_in = lax.ppermute(core_out, 'tile', core)  1.04 us
  transfers between devices with their start and end apart: 20, of which 4 were waited for; matrix products, arithmetic and copies ran while one was open for 0% of the time, Pallas kernels for 15%

profile of v4, /device:TPU:0, one launch (start us, length us, event | category | flops | bytes accessed | tf_op | source)
XLA Modules:
  0.0 41.3 jit_solution(1859844976278461346)
XLA Ops:
  0.0 2.8 %first_edges.1 = (f32[56,128]{1,0:T(8,128)}, f32[56,128]{1,0:T(8,128)}, f32[56,128]{1,0:T(8,128)}, f32[56,128]{1,0:T(8,128)}, f32[56,128]{1,0:T(8,128)}, /*index=5*/f32[56,128]{1,0:T(8,128)}, f32[56,128]{1,0:T(8,128)}) custom-call(f32[6,6,128,128]{3,2,1,0:T(8,128)} %bitcast.2, f32[3]{0:T(128)} %refs_1_.3, f32[3]{0:T(128)} %refs_2_.3), custom_call_target="tpu_custom_call" | custom-call | flops 1000000000 | bytes 2000000 | tf_op jit(solution)/shard_map/first_edges/pallas_call | solution.py:532
  2.9 5.5 %collective-permute-start = (f32[56,128]{1,0:T(8,128)}, f32[56,128]{1,0:T(8,128)S(1)}, u32[]{:S(2)}, u32[]{:S(2)}) collective-permute-start(f32[56,128]{1,0:T(8,128)} %get-tuple-element.58), channel_id=1, source_target_pairs={{0,15},{1,11},{2,7},{3,6},{4,14},{5,10},{6,3},{7,2},{8,13},{9,12},... | collective-permute-start | bytes 86024 | tf_op jit(solution)/shard_map/ppermute | solution.py:507
  8.4 1.1 %collective-permute-start.2 = (f32[56,128]{1,0:T(8,128)}, f32[56,128]{1,0:T(8,128)S(1)}, u32[]{:S(2)}, u32[]{:S(2)}) collective-permute-start(f32[56,128]{1,0:T(8,128)} %get-tuple-element.60), channel_id=1, source_target_pairs={{0,4},{1,5},{2,6},{3,7},{4,0},{5,1},{6,2},{7,3},{8,12},{9,13},{10,... | collective-permute-start | bytes 86024 | tf_op jit(solution)/shard_map/ppermute | solution.py:509
  9.5 0.4 collective-permute-start.4
  9.9 1.8 %inner.4 = (f32[6,6,128,128]{3,2,1,0:T(8,128)S(1)}, f32[128,128]{1,0:T(8,128)S(1)}, f32[128,128]{1,0:T(8,128)S(1)}, f32[8,128]{1,0:T(8,128)S(1)}, f32[128,128]{1...) custom-call(f32[6,6,128,128]{3,2,1,0:T(8,128)S(1)} %bitcast.3, ...), custom_call_target="tpu_custom_call" | custom-call | flops 2000000000 | bytes 4000000 | tf_op jit(solution)/shard_map/inner/pallas_call | solution.py:532
  11.7 2.5 %collective-permute-done.1.refs_1_ = f32[56,128]{1,0:T(8,128)S(1)} collective-permute-done((f32[56,128]{1,0:T(8,128)}, f32[56,128]{1,0:T(8,128)S(1)}, u32[]{:S(2)}, u32[]{:S(2)}) %collective-permute-start.1) | collective-permute-done | bytes 28704 | tf_op jit(solution)/shard_map/ppermute | solution.py:508
  14.3 0.0 collective-permute-done.2.refs_2_
  14.3 0.8 %edges.3 = (f32[128,128]{1,0:T(8,128)S(1)}, f32[128,128]{1,0:T(8,128)S(1)}, f32[56,128]{1,0:T(8,128)S(1)}, f32[56,128]{1,0:T(8,128)S(1)}, f32[56,128]{1,0:T(8,12...) custom-call(f32[56,128]{1,0:T(8,128)S(1)} %collective-permute-done.refs_0, ...), custom_call_target="tpu_custom_call" | custom-call | tf_op jit(solution)/shard_map/edges/pallas_call | solution.py:532
  15.1 1.3 %collective-permute-start.5 = (f32[56,128]{1,0:T(8,128)S(1)}, f32[56,128]{1,0:T(8,128)S(1)}, u32[]{:S(2)}, u32[]{:S(2)}) collective-permute-start(f32[56,128]{1,0:T(8,128)S(1)} %get-tuple-element.72), channel_id=1, source_target_pairs={{0,15},{1,11},{2,7},{3,6},{4,14},{5,10},{6,3},{7,2},{8,13},{9,12},... | collective-permute-start | bytes 86024 | tf_op jit(solution)/shard_map/ppermute | solution.py:507
  16.4 0.9 %collective-permute-start.6 = (f32[56,128]{1,0:T(8,128)S(1)}, f32[56,128]{1,0:T(8,128)S(1)}, u32[]{:S(2)}, u32[]{:S(2)}) collective-permute-start(f32[56,128]{1,0:T(8,128)S(1)} %get-tuple-element.73), channel_id=1, source_target_pairs={{0,12},{1,13},{2,14},{3,15},{4,8},{5,9},{6,10},{7,11},{8,4},{9,5},... | collective-permute-start | bytes 86024 | tf_op jit(solution)/shard_map/ppermute | solution.py:508
  17.2 0.5 %collective-permute-start.7 = (f32[56,128]{1,0:T(8,128)S(1)}, f32[56,128]{1,0:T(8,128)S(1)}, u32[]{:S(2)}, u32[]{:S(2)}) collective-permute-start(f32[56,128]{1,0:T(8,128)S(1)} %get-tuple-element.74), channel_id=1, source_target_pairs={{0,4},{1,5},{2,6},{3,7},{4,0},{5,1},{6,2},{7,3},{8,12},{9,13},{10,... | collective-permute-start | bytes 86024 | tf_op jit(solution)/shard_map/ppermute | solution.py:509
  17.8 2.1 %collective-permute-start.8 = (f32[56,128]{1,0:T(8,128)S(1)}, f32[56,128]{1,0:T(8,128)S(1)}, u32[]{:S(2)}, u32[]{:S(2)}) collective-permute-start(f32[56,128]{1,0:T(8,128)S(1)} %get-tuple-element.75), channel_id=1, source_target_pairs={{0,3},{1,2},{2,1},{3,0},{4,7},{5,6},{6,5},{7,4},{8,11},{9,10},{10,... | collective-permute-start | bytes 86024 | tf_op jit(solution)/shard_map/ppermute | solution.py:510
  19.9 1.6 %inner.5 = (f32[6,6,128,128]{3,2,1,0:T(8,128)S(1)}, f32[128,128]{1,0:T(8,128)S(1)}, f32[128,128]{1,0:T(8,128)S(1)}) custom-call(f32[6,6,128,128]{3,2,1,0:T(8,128)S(1)} %get-tuple-element.79.refs_0_, f32[8,128]{1,0:T(8,128)S(1)} %get-tuple-element.80.refs_1_, bf16[256,128]{1,0:T(8,128)(2,1)S(1)} %get-tuple-element.81.refs_2_, ...), custom_call_target="tpu_custom_call", output_to_operand_aliasing={{0}: (0, {})} | custom-call | flops 2000000000 | bytes 4000000 | tf_op jit(solution)/shard_map/inner/pallas_call | solution.py:532
  21.5 0.0 collective-permute-done.5.refs_0_
  21.5 0.6 %collective-permute-done.6.refs_1_ = f32[56,128]{1,0:T(8,128)S(1)} collective-permute-done((f32[56,128]{1,0:T(8,128)S(1)}, f32[56,128]{1,0:T(8,128)S(1)}, u32[]{:S(2)}, u32[]{:S(2)}) %collective-permute-start.6) | collective-permute-done | bytes 28704 | tf_op jit(solution)/shard_map/ppermute | solution.py:508
  22.2 0.8 %edges.4 = (f32[128,128]{1,0:T(8,128)S(1)}, f32[128,128]{1,0:T(8,128)S(1)}, f32[56,128]{1,0:T(8,128)S(1)}, f32[56,128]{1,0:T(8,128)S(1)}, f32[56,128]{1,0:T(8,12...) custom-call(f32[56,128]{1,0:T(8,128)S(1)} %collective-permute-done.5.refs, ...), custom_call_target="tpu_custom_call" | custom-call | tf_op jit(solution)/shard_map/edges/pallas_call | solution.py:532
  22.9 2.0 %collective-permute-start.10 = (f32[56,128]{1,0:T(8,128)S(1)}, f32[56,128]{1,0:T(8,128)S(1)}, u32[]{:S(2)}, u32[]{:S(2)}) collective-permute-start(f32[56,128]{1,0:T(8,128)S(1)} %get-tuple-element.89), channel_id=1, source_target_pairs={{0,15},{1,11},{2,7},{3,6},{4,14},{5,10},{6,3},{7,2},{8,13},{9,12},... | collective-permute-start | bytes 86024 | tf_op jit(solution)/shard_map/ppermute | solution.py:507
  25.0 1.3 %collective-permute-start.11 = (f32[56,128]{1,0:T(8,128)S(1)}, f32[56,128]{1,0:T(8,128)S(1)}, u32[]{:S(2)}, u32[]{:S(2)}) collective-permute-start(f32[56,128]{1,0:T(8,128)S(1)} %get-tuple-element.90), channel_id=1, source_target_pairs={{0,12},{1,13},{2,14},{3,15},{4,8},{5,9},{6,10},{7,11},{8,4},{9,5},... | collective-permute-start | bytes 86024 | tf_op jit(solution)/shard_map/ppermute | solution.py:508
  26.3 1.4 %collective-permute-start.13 = (f32[56,128]{1,0:T(8,128)S(1)}, f32[56,128]{1,0:T(8,128)S(1)}, u32[]{:S(2)}, u32[]{:S(2)}) collective-permute-start(f32[56,128]{1,0:T(8,128)S(1)} %get-tuple-element.92), channel_id=1, source_target_pairs={{0,3},{1,2},{2,1},{3,0},{4,7},{5,6},{6,5},{7,4},{8,11},{9,10},{10,... | collective-permute-start | bytes 86024 | tf_op jit(solution)/shard_map/ppermute | solution.py:510
  27.7 0.3 collective-permute-start.14
  28.1 1.6 %inner.6 = (f32[6,6,128,128]{3,2,1,0:T(8,128)S(1)}, f32[128,128]{1,0:T(8,128)S(1)}, f32[128,128]{1,0:T(8,128)S(1)}) custom-call(f32[6,6,128,128]{3,2,1,0:T(8,128)S(1)} %get-tuple-element.96.refs_0_, f32[8,128]{1,0:T(8,128)S(1)} %get-tuple-element.80.refs_1_, bf16[256,128]{1,0:T(8,128)(2,1)S(1)} %get-tuple-element.81.refs_2_, ...), custom_call_target="tpu_custom_call", output_to_operand_aliasing={{0}: (0, {})} | custom-call | flops 2000000000 | bytes 4000000 | tf_op jit(solution)/shard_map/inner/pallas_call | solution.py:532
  29.7 0.0 collective-permute-done.10.refs_0_
  29.7 1.0 %collective-permute-done.11.refs_1_ = f32[56,128]{1,0:T(8,128)S(1)} collective-permute-done((f32[56,128]{1,0:T(8,128)S(1)}, f32[56,128]{1,0:T(8,128)S(1)}, u32[]{:S(2)}, u32[]{:S(2)}) %collective-permute-start.11) | collective-permute-done | bytes 28704 | tf_op jit(solution)/shard_map/ppermute | solution.py:508
  30.7 0.8 %edges.5 = (f32[128,128]{1,0:T(8,128)S(1)}, f32[128,128]{1,0:T(8,128)S(1)}, f32[56,128]{1,0:T(8,128)S(1)}, f32[56,128]{1,0:T(8,128)S(1)}, f32[56,128]{1,0:T(8,12...) custom-call(f32[56,128]{1,0:T(8,128)S(1)} %collective-permute-done.10.ref, ...), custom_call_target="tpu_custom_call" | custom-call | tf_op jit(solution)/shard_map/edges/pallas_call | solution.py:532
  31.5 1.4 %collective-permute-start.15 = (f32[56,128]{1,0:T(8,128)S(1)}, f32[56,128]{1,0:T(8,128)S(1)}, u32[]{:S(2)}, u32[]{:S(2)}) collective-permute-start(f32[56,128]{1,0:T(8,128)S(1)} %get-tuple-element.101), channel_id=1, source_target_pairs={{0,15},{1,11},{2,7},{3,6},{4,14},{5,10},{6,3},{7,2},{8,13},{9,12},... | collective-permute-start | bytes 86024 | tf_op jit(solution)/shard_map/ppermute | solution.py:507
  32.8 1.0 %collective-permute-start.16 = (f32[56,128]{1,0:T(8,128)S(1)}, f32[56,128]{1,0:T(8,128)S(1)}, u32[]{:S(2)}, u32[]{:S(2)}) collective-permute-start(f32[56,128]{1,0:T(8,128)S(1)} %get-tuple-element.102), channel_id=1, source_target_pairs={{0,12},{1,13},{2,14},{3,15},{4,8},{5,9},{6,10},{7,11},{8,4},{9,5},... | collective-permute-start | bytes 86024 | tf_op jit(solution)/shard_map/ppermute | solution.py:508
  33.9 0.8 %collective-permute-start.17 = (f32[56,128]{1,0:T(8,128)S(1)}, f32[56,128]{1,0:T(8,128)S(1)}, u32[]{:S(2)}, u32[]{:S(2)}) collective-permute-start(f32[56,128]{1,0:T(8,128)S(1)} %get-tuple-element.103), channel_id=1, source_target_pairs={{0,4},{1,5},{2,6},{3,7},{4,0},{5,1},{6,2},{7,3},{8,12},{9,13},{10,... | collective-permute-start | bytes 86024 | tf_op jit(solution)/shard_map/ppermute | solution.py:509
  34.6 1.6 %collective-permute-start.18 = (f32[56,128]{1,0:T(8,128)S(1)}, f32[56,128]{1,0:T(8,128)S(1)}, u32[]{:S(2)}, u32[]{:S(2)}) collective-permute-start(f32[56,128]{1,0:T(8,128)S(1)} %get-tuple-element.104), channel_id=1, source_target_pairs={{0,3},{1,2},{2,1},{3,0},{4,7},{5,6},{6,5},{7,4},{8,11},{9,10},{10,... | collective-permute-start | bytes 86024 | tf_op jit(solution)/shard_map/ppermute | solution.py:510
  36.3 0.3 collective-permute-start.19
  36.6 1.3 %inner.7.refs_10_ = f32[6,6,128,128]{3,2,1,0:T(8,128)S(1)} custom-call(f32[6,6,128,128]{3,2,1,0:T(8,128)S(1)} %get-tuple-element.108.refs_0_, f32[8,128]{1,0:T(8,128)S(1)} %get-tuple-element.80.refs_1_, bf16[256,128]{1,0:T(8,128)(2,1)S(1)} %get-tuple-element.81.refs_2_, ...), custom_call_target="tpu_custom_call", output_to_operand_aliasing={{}: (0, {})} | custom-call | flops 2000000000 | bytes 4000000 | tf_op jit(solution)/shard_map/inner/pallas_call | solution.py:532
  37.9 0.9 %collective-permute-done.16.refs_1_ = f32[56,128]{1,0:T(8,128)S(1)} collective-permute-done((f32[56,128]{1,0:T(8,128)S(1)}, f32[56,128]{1,0:T(8,128)S(1)}, u32[]{:S(2)}, u32[]{:S(2)}) %collective-permute-start.16) | collective-permute-done | bytes 28704 | tf_op jit(solution)/shard_map/ppermute | solution.py:508
  38.7 2.5 %final.1 = f32[6,6,128,128]{3,2,1,0:T(8,128)} custom-call(f32[56,128]{1,0:T(8,128)S(1)} %collective-permute-done.15.refs_0_, f32[56,128]{1,0:T(8,128)S(1)} %collective-permute-done.16.refs_1_, f32[56,128]{1,0:T(8,128)S(1)} %collective-permute-done.17.refs_2_, f32[56,128]{1,0:T(8,128)S(1)} %collective-permute-done.18.refs_3_, ...), custom_call_target="tpu_custom_call" | custom-call | tf_op jit(solution)/shard_map/final/pallas_call | solution.py:532
  (31 shorter events, 0.1 us)
Async XLA Ops:
  0.0 9.9 %copy-start.6 = (f32[3]{0:T(128)S(1)}, f32[3]{0:T(128)}, u32[]{:S(2)}) copy-start(f32[3]{0:T(128)} %refs_2_.3) | copy-start | bytes 40
  0.0 9.9 %copy-start.5 = (f32[3]{0:T(128)S(1)}, f32[3]{0:T(128)}, u32[]{:S(2)}) copy-start(f32[3]{0:T(128)} %refs_1_.3) | copy-start | bytes 40
  0.0 9.9 %copy-start.2 = (f32[1,6,6,128,128]{4,3,2,1,0:T(8,128)S(1)}, f32[1,6,6,128,128]{4,3,2,1,0:T(8,128)}, u32[]{:S(2)}) copy-start(f32[1,6,6,128,128]{4,3,2,1,0:T(8,128)} %param.5) | copy-start | bytes 7077892
  0.0 9.9 %copy-start.4 = (f32[3,128]{1,0:T(4,128)S(1)}, f32[3,128]{1,0:T(4,128)}, u32[]{:S(2)}) copy-start(f32[3,128]{1,0:T(4,128)} %refs_4_.1) | copy-start | bytes 4612
  0.0 9.9 %copy-start.3 = (s32[3,128]{1,0:T(4,128)S(1)}, s32[3,128]{1,0:T(4,128)}, u32[]{:S(2)}) copy-start(s32[3,128]{1,0:T(4,128)} %refs_3_.1) | copy-start | bytes 4612
  2.9 8.9 %collective-permute-start = (f32[56,128]{1,0:T(8,128)}, f32[56,128]{1,0:T(8,128)S(1)}, u32[]{:S(2)}, u32[]{:S(2)}) collective-permute-start(f32[56,128]{1,0:T(8,128)} %get-tuple-element.58), channel_id=1, source_target_pairs={{0,15},{1,11},{2,7},{3,6},{4,14},{5,10},{6,3},{7,2},{8,13},{9,12},... | collective-permute-start | bytes 86024 | tf_op jit(solution)/shard_map/ppermute | solution.py:507
  8.4 5.9 %collective-permute-start.1 = (f32[56,128]{1,0:T(8,128)}, f32[56,128]{1,0:T(8,128)S(1)}, u32[]{:S(2)}, u32[]{:S(2)}) collective-permute-start(f32[56,128]{1,0:T(8,128)} %get-tuple-element.59), channel_id=1, source_target_pairs={{0,12},{1,13},{2,14},{3,15},{4,8},{5,9},{6,10},{7,11},{8,4},{9,5},... | collective-permute-start | bytes 86024 | tf_op jit(solution)/shard_map/ppermute | solution.py:508
  8.4 5.9 %collective-permute-start.2 = (f32[56,128]{1,0:T(8,128)}, f32[56,128]{1,0:T(8,128)S(1)}, u32[]{:S(2)}, u32[]{:S(2)}) collective-permute-start(f32[56,128]{1,0:T(8,128)} %get-tuple-element.60), channel_id=1, source_target_pairs={{0,4},{1,5},{2,6},{3,7},{4,0},{5,1},{6,2},{7,3},{8,12},{9,13},{10,... | collective-permute-start | bytes 86024 | tf_op jit(solution)/shard_map/ppermute | solution.py:509
  9.5 4.8 %collective-permute-start.3 = (f32[56,128]{1,0:T(8,128)}, f32[56,128]{1,0:T(8,128)S(1)}, u32[]{:S(2)}, u32[]{:S(2)}) collective-permute-start(f32[56,128]{1,0:T(8,128)} %get-tuple-element.61), channel_id=1, source_target_pairs={{0,3},{1,2},{2,1},{3,0},{4,7},{5,6},{6,5},{7,4},{8,11},{9,10},{10,... | collective-permute-start | bytes 86024 | tf_op jit(solution)/shard_map/ppermute | solution.py:510
  9.5 4.8 %copy-start = (f32[56,128]{1,0:T(8,128)S(1)}, f32[56,128]{1,0:T(8,128)}, u32[]{:S(2)}) copy-start(f32[56,128]{1,0:T(8,128)} %get-tuple-element.63.refs_5_) | copy-start | bytes 86020
  9.5 4.8 %copy-start.1 = (f32[56,128]{1,0:T(8,128)S(1)}, f32[56,128]{1,0:T(8,128)}, u32[]{:S(2)}) copy-start(f32[56,128]{1,0:T(8,128)} %get-tuple-element.64.refs_6_) | copy-start | bytes 86020
  9.5 4.8 %collective-permute-start.4 = (f32[56,128]{1,0:T(8,128)}, f32[56,128]{1,0:T(8,128)S(1)}, u32[]{:S(2)}, u32[]{:S(2)}) collective-permute-start(f32[56,128]{1,0:T(8,128)} %get-tuple-element.62), channel_id=1, source_target_pairs={{0,1},{1,0},{2,3},{3,2},{4,5},{5,4},{6,7},{7,6},{8,9},{9,8},{10,11... | collective-permute-start | bytes 86024 | tf_op jit(solution)/shard_map/ppermute | solution.py:511
  15.1 6.4 %collective-permute-start.5 = (f32[56,128]{1,0:T(8,128)S(1)}, f32[56,128]{1,0:T(8,128)S(1)}, u32[]{:S(2)}, u32[]{:S(2)}) collective-permute-start(f32[56,128]{1,0:T(8,128)S(1)} %get-tuple-element.72), channel_id=1, source_target_pairs={{0,15},{1,11},{2,7},{3,6},{4,14},{5,10},{6,3},{7,2},{8,13},{9,12},... | collective-permute-start | bytes 86024 | tf_op jit(solution)/shard_map/ppermute | solution.py:507
  16.4 5.8 %collective-permute-start.6 = (f32[56,128]{1,0:T(8,128)S(1)}, f32[56,128]{1,0:T(8,128)S(1)}, u32[]{:S(2)}, u32[]{:S(2)}) collective-permute-start(f32[56,128]{1,0:T(8,128)S(1)} %get-tuple-element.73), channel_id=1, source_target_pairs={{0,12},{1,13},{2,14},{3,15},{4,8},{5,9},{6,10},{7,11},{8,4},{9,5},... | collective-permute-start | bytes 86024 | tf_op jit(solution)/shard_map/ppermute | solution.py:508
  17.2 4.9 %collective-permute-start.7 = (f32[56,128]{1,0:T(8,128)S(1)}, f32[56,128]{1,0:T(8,128)S(1)}, u32[]{:S(2)}, u32[]{:S(2)}) collective-permute-start(f32[56,128]{1,0:T(8,128)S(1)} %get-tuple-element.74), channel_id=1, source_target_pairs={{0,4},{1,5},{2,6},{3,7},{4,0},{5,1},{6,2},{7,3},{8,12},{9,13},{10,... | collective-permute-start | bytes 86024 | tf_op jit(solution)/shard_map/ppermute | solution.py:509
  17.8 4.4 %collective-permute-start.8 = (f32[56,128]{1,0:T(8,128)S(1)}, f32[56,128]{1,0:T(8,128)S(1)}, u32[]{:S(2)}, u32[]{:S(2)}) collective-permute-start(f32[56,128]{1,0:T(8,128)S(1)} %get-tuple-element.75), channel_id=1, source_target_pairs={{0,3},{1,2},{2,1},{3,0},{4,7},{5,6},{6,5},{7,4},{8,11},{9,10},{10,... | collective-permute-start | bytes 86024 | tf_op jit(solution)/shard_map/ppermute | solution.py:510
  19.9 2.3 %collective-permute-start.9 = (f32[56,128]{1,0:T(8,128)S(1)}, f32[56,128]{1,0:T(8,128)S(1)}, u32[]{:S(2)}, u32[]{:S(2)}) collective-permute-start(f32[56,128]{1,0:T(8,128)S(1)} %get-tuple-element.76), channel_id=1, source_target_pairs={{0,1},{1,0},{2,3},{3,2},{4,5},{5,4},{6,7},{7,6},{8,9},{9,8},{10,11... | collective-permute-start | bytes 86024 | tf_op jit(solution)/shard_map/ppermute | solution.py:511
  22.9 6.7 %collective-permute-start.10 = (f32[56,128]{1,0:T(8,128)S(1)}, f32[56,128]{1,0:T(8,128)S(1)}, u32[]{:S(2)}, u32[]{:S(2)}) collective-permute-start(f32[56,128]{1,0:T(8,128)S(1)} %get-tuple-element.89), channel_id=1, source_target_pairs={{0,15},{1,11},{2,7},{3,6},{4,14},{5,10},{6,3},{7,2},{8,13},{9,12},... | collective-permute-start | bytes 86024 | tf_op jit(solution)/shard_map/ppermute | solution.py:507
  25.0 5.7 %collective-permute-start.11 = (f32[56,128]{1,0:T(8,128)S(1)}, f32[56,128]{1,0:T(8,128)S(1)}, u32[]{:S(2)}, u32[]{:S(2)}) collective-permute-start(f32[56,128]{1,0:T(8,128)S(1)} %get-tuple-element.90), channel_id=1, source_target_pairs={{0,12},{1,13},{2,14},{3,15},{4,8},{5,9},{6,10},{7,11},{8,4},{9,5},... | collective-permute-start | bytes 86024 | tf_op jit(solution)/shard_map/ppermute | solution.py:508
  26.3 4.3 %collective-permute-start.12 = (f32[56,128]{1,0:T(8,128)S(1)}, f32[56,128]{1,0:T(8,128)S(1)}, u32[]{:S(2)}, u32[]{:S(2)}) collective-permute-start(f32[56,128]{1,0:T(8,128)S(1)} %get-tuple-element.91), channel_id=1, source_target_pairs={{0,4},{1,5},{2,6},{3,7},{4,0},{5,1},{6,2},{7,3},{8,12},{9,13},{10,... | collective-permute-start | bytes 86024 | tf_op jit(solution)/shard_map/ppermute | solution.py:509
  26.3 4.3 %collective-permute-start.13 = (f32[56,128]{1,0:T(8,128)S(1)}, f32[56,128]{1,0:T(8,128)S(1)}, u32[]{:S(2)}, u32[]{:S(2)}) collective-permute-start(f32[56,128]{1,0:T(8,128)S(1)} %get-tuple-element.92), channel_id=1, source_target_pairs={{0,3},{1,2},{2,1},{3,0},{4,7},{5,6},{6,5},{7,4},{8,11},{9,10},{10,... | collective-permute-start | bytes 86024 | tf_op jit(solution)/shard_map/ppermute | solution.py:510
  27.7 2.9 %collective-permute-start.14 = (f32[56,128]{1,0:T(8,128)S(1)}, f32[56,128]{1,0:T(8,128)S(1)}, u32[]{:S(2)}, u32[]{:S(2)}) collective-permute-start(f32[56,128]{1,0:T(8,128)S(1)} %get-tuple-element.93), channel_id=1, source_target_pairs={{0,1},{1,0},{2,3},{3,2},{4,5},{5,4},{6,7},{7,6},{8,9},{9,8},{10,11... | collective-permute-start | bytes 86024 | tf_op jit(solution)/shard_map/ppermute | solution.py:511
  31.5 6.4 %collective-permute-start.15 = (f32[56,128]{1,0:T(8,128)S(1)}, f32[56,128]{1,0:T(8,128)S(1)}, u32[]{:S(2)}, u32[]{:S(2)}) collective-permute-start(f32[56,128]{1,0:T(8,128)S(1)} %get-tuple-element.101), channel_id=1, source_target_pairs={{0,15},{1,11},{2,7},{3,6},{4,14},{5,10},{6,3},{7,2},{8,13},{9,12},... | collective-permute-start | bytes 86024 | tf_op jit(solution)/shard_map/ppermute | solution.py:507
  32.8 5.9 %collective-permute-start.16 = (f32[56,128]{1,0:T(8,128)S(1)}, f32[56,128]{1,0:T(8,128)S(1)}, u32[]{:S(2)}, u32[]{:S(2)}) collective-permute-start(f32[56,128]{1,0:T(8,128)S(1)} %get-tuple-element.102), channel_id=1, source_target_pairs={{0,12},{1,13},{2,14},{3,15},{4,8},{5,9},{6,10},{7,11},{8,4},{9,5},... | collective-permute-start | bytes 86024 | tf_op jit(solution)/shard_map/ppermute | solution.py:508
  33.9 4.9 %collective-permute-start.17 = (f32[56,128]{1,0:T(8,128)S(1)}, f32[56,128]{1,0:T(8,128)S(1)}, u32[]{:S(2)}, u32[]{:S(2)}) collective-permute-start(f32[56,128]{1,0:T(8,128)S(1)} %get-tuple-element.103), channel_id=1, source_target_pairs={{0,4},{1,5},{2,6},{3,7},{4,0},{5,1},{6,2},{7,3},{8,12},{9,13},{10,... | collective-permute-start | bytes 86024 | tf_op jit(solution)/shard_map/ppermute | solution.py:509
  34.6 4.1 %collective-permute-start.18 = (f32[56,128]{1,0:T(8,128)S(1)}, f32[56,128]{1,0:T(8,128)S(1)}, u32[]{:S(2)}, u32[]{:S(2)}) collective-permute-start(f32[56,128]{1,0:T(8,128)S(1)} %get-tuple-element.104), channel_id=1, source_target_pairs={{0,3},{1,2},{2,1},{3,0},{4,7},{5,6},{6,5},{7,4},{8,11},{9,10},{10,... | collective-permute-start | bytes 86024 | tf_op jit(solution)/shard_map/ppermute | solution.py:510
  36.3 2.5 %collective-permute-start.19 = (f32[56,128]{1,0:T(8,128)S(1)}, f32[56,128]{1,0:T(8,128)S(1)}, u32[]{:S(2)}, u32[]{:S(2)}) collective-permute-start(f32[56,128]{1,0:T(8,128)S(1)} %get-tuple-element.105), channel_id=1, source_target_pairs={{0,1},{1,0},{2,3},{3,2},{4,5},{5,4},{6,7},{7,6},{8,9},{9,8},{10,11... | collective-permute-start | bytes 86024 | tf_op jit(solution)/shard_map/ppermute | solution.py:511

commit v5 on v4

--- a/solution.py
+++ b/solution.py
@@ -18,7 +18,6 @@
 WEST, EAST, SOUTH, NORTH = 0, 1, 2, 3
 SCALE = 20.0
 VMEM_LIMIT = 16 * 1024 * 1024
-FIRST_LIMIT = 60 * 1024 * 1024
 
 
 def whole_vmem():
@@ -197,35 +196,25 @@
     turn_ref[...] = jnp.where(use_a == 1, own_a_ref[...], own_b_ref[...])
 
 
-CONSTANTS = (
-    ("coef", (8, BLK), jnp.float32),
-    ("gain", (BLK, BLK), jnp.float32),
-    ("matrix", (3 * BLK, 2 * DEPTH * BLK), jnp.bfloat16),
+TABLES = (
     ("edge", (BLK, 2 * BLK), jnp.bfloat16),
-    ("fold", (2 * BLK, BLK), jnp.bfloat16),
+    ("reach", (2 * BLK, BLK), jnp.bfloat16),
     ("same", (BLK, BLK), jnp.float32),
     ("order", (BLK, 2 * BLK), jnp.bfloat16),
     ("spread", (2 * BLK, BLK), jnp.bfloat16),
     ("band_x", (2 * BLK, BLK), jnp.bfloat16),
     ("band_y", (BLK, 2 * BLK), jnp.bfloat16),
 )
-
-
-def make_constants(wave, visc, starts, offsets, refs):
-    coef, gain, matrix, edge, fold, same, order, spread, band_x, band_y = refs
-    seam_matrices(starts, offsets, matrix)
-    _, plane, cell = plane_row((BLK, BLK), 0)
-    lower, _, _ = plane_row((BLK, BLK), 0)
+CONSTANTS = (
+    ("coef", (8, BLK), jnp.float32),
+    ("gain", (BLK, BLK), jnp.float32),
+    ("matrix", (3 * BLK, 2 * DEPTH * BLK), jnp.bfloat16),
+)
+
+
+def tables_kernel(edge, reach, same, order, spread, band_x, band_y):
+    lower, plane, cell = plane_row((BLK, BLK), 0)
     _, plane_src, _ = plane_row((BLK, BLK), 1)
-    level_of = plane - 3 * ((plane * 171) >> 9)
-    total = jnp.zeros((BLK, BLK), jnp.float32)
-    for level in range(LEV):
-        a, b = wave[level] * (1.0 / SCALE), visc[level] * (1.0 / SCALE)
-        coef[level : level + 1, :] = jnp.full((1, BLK), a, jnp.float32)
-        coef[LEV + level : LEV + level + 1, :] = jnp.full((1, BLK), b, jnp.float32)
-        total = jnp.where(level_of == level, a + b, total)
-    coef[2 * LEV :, :] = jnp.zeros((8 - 2 * LEV, BLK), jnp.float32)
-    gain[...] = total
     for ref, value, axis in (
         (edge, edge_matrix(), 1),
         (order, lane_order(), 1),
@@ -233,41 +222,43 @@
         (band_y, band_matrix(), 1),
     ):
         ref[...] = jnp.concatenate([value, value], axis=axis)
-    used = plane < FACES * LEV
     to = iota((BLK, BLK), 1)
-    back = jnp.where(lower, cell, cell + BLK - 3)
-    value = jnp.where((to == back) & used, 1.0, 0.0).astype(jnp.bfloat16)
-    fold[...] = jnp.concatenate([value, value], axis=0)
+    low = weight_of(jnp.where(to < 3, 3 + to - cell, 0))
+    high = weight_of(jnp.where(to >= BLK - 3, 3 + cell - (to - (BLK - 3)), 0))
+    value = jnp.where(plane < FACES * LEV, jnp.where(lower, low, high), 0.0).astype(jnp.bfloat16)
+    reach[...] = jnp.concatenate([value, value], axis=0)
     spread[...] = jnp.concatenate([lane_order()] * 2, axis=0)
     same[...] = jnp.where(plane == plane_src, 1.0, 0.0)
 
 
-def first_kernel(side, state_hbm, wave_hbm, visc_hbm, *rest):
+def constants_kernel(wave_ref, visc_ref, start_ref, offset_ref, coef_ref, gain_ref, matrix_ref):
+    seam_matrices(start_ref[...], offset_ref[...], matrix_ref)
+    _, plane, _ = plane_row((BLK, BLK), 0)
+    level_of = plane - 3 * ((plane * 171) >> 9)
+    gain = jnp.zeros((BLK, BLK), jnp.float32)
+    for level in range(LEV):
+        a, b = [
+            jnp.broadcast_to(ref[:, level : level + 1] * (1.0 / SCALE), (1, BLK))
+            for ref in (wave_ref, visc_ref)
+        ]
+        coef_ref[level : level + 1, :] = a
+        coef_ref[LEV + level : LEV + level + 1, :] = b
+        gain = jnp.where(level_of == level, a + b, gain)
+    coef_ref[2 * LEV :, :] = jnp.zeros((8 - 2 * LEV, BLK), jnp.float32)
+    gain_ref[...] = gain
+
+
+def first_kernel(side, state_ref, coef_ref, order_ref, *rest):
     outs = rest[:7]
-    state_ref, wave, visc, columns_ref, rows_ref, strips_ref, sems = rest[7:]
-    small = [
-        pltpu.make_async_copy(wave_hbm, wave, sems.at[FACES]),
-        pltpu.make_async_copy(visc_hbm, visc, sems.at[FACES + 1]),
-    ]
-    faces = [
-        pltpu.make_async_copy(state_hbm.at[face], state_ref.at[face], sems.at[face])
-        for face in range(FACES)
-    ]
-    for copy in small + faces:
-        copy.start()
+    columns_ref, rows_ref, strips_ref = rest[7:]
     clear_rest(rows_ref)
-    for copy in small:
-        copy.wait()
     columns = jnp.zeros((BLK // 8, 8, BLK), jnp.float32)
     for plane in range(FACES * LEV):
         face, level = divmod(plane, LEV)
-        if level == 0:
-            faces[face].wait()
-        a, b = wave[level] * (1.0 / SCALE), visc[level] * (1.0 / SCALE)
+        a, b = coef_ref[level : level + 1, :], coef_ref[LEV + level : LEV + level + 1, :]
         q = a * state_ref[face, level] + b * state_ref[face, LEV + level]
         columns = take_edges(tiles_of(q), plane, columns, rows_ref)
-    order = lane_order()
-    columns_ref[...] = rows_from_columns(columns, jnp.concatenate([order, order], axis=1))
+    columns_ref[...] = rows_from_columns(columns, order_ref[...])
     pack(columns_ref, rows_ref, side, outs, strips_ref)
 
 
@@ -330,8 +321,7 @@
     return ghosts
 
 
-def ghost_additions(side, received, own_a_ref, own_b_ref, matrix_ref, edge_ref):
-    ghosts = ghosts_of(side, received, own_a_ref, own_b_ref, matrix_ref)
+def ghost_additions(ghosts, edge_ref):
     high, low = split2(jnp.concatenate(ghosts, axis=1))
     adds = jnp.dot(
         edge_ref[...],
@@ -341,44 +331,39 @@
     return adds[:, :BLK], adds[:, BLK:]
 
 
-def corner_part(adds_turned, same):
+def corner_part(ghosts, same):
+    turned = ghosts.T
     cell = plane_row((HALF, BLK), 0)[2]
     halves = []
     for first in (0, BLK - 3):
-        lines = [adds_turned[first + at : first + at + 1, :] for at in range(3)]
+        lines = [turned[first + at : first + at + 1, :] for at in range(3)]
         halves.append(jnp.where(cell == 0, lines[0], jnp.where(cell == 1, lines[1], lines[2])))
-    return split2(jnp.concatenate(halves, axis=0) * same)
+    return jnp.concatenate(split2(jnp.concatenate(halves, axis=0) * same), axis=1)
 
 
 def edge_kernel(side, *refs):
-    add_x, add_y = ghost_additions(side, refs[:5], *refs[5:9])
-    fold_ref, same_ref, gain_ref, old_columns_ref, old_rows_ref = refs[9:14]
+    across, along = ghosts_of(side, refs[:5], *refs[5:8])
+    edge_ref, reach_ref, same_ref, gain_ref, old_columns_ref, old_rows_ref = refs[8:14]
     add_x_ref, add_y_ref = refs[14:16]
     outs = refs[16:23]
     columns_ref, rows_ref, strips_ref = refs[23:]
-    turned_x, turned_y = add_x.T, add_y.T
-    add_x_ref[...] = turned_x
-    add_y_ref[...] = add_y
+    add_x, add_y = ghost_additions((across, along), edge_ref)
     same = same_ref[...]
     corners = jnp.dot(
-        jnp.concatenate(
-            [
-                jnp.concatenate(corner_part(turned_y, same), axis=1),
-                jnp.concatenate(corner_part(turned_x, same), axis=1),
-            ],
-            axis=0,
-        ),
-        fold_ref[...],
+        jnp.concatenate([corner_part(along, same), corner_part(across, same)], axis=0),
+        reach_ref[...],
         preferred_element_type=jnp.float32,
     )
     gain = gain_ref[...]
     columns_ref[...] = old_columns_ref[...] + gain * (add_x + corners[:BLK])
     rows_ref[...] = old_rows_ref[...] + gain * (add_y + corners[BLK:])
+    add_x_ref[...] = add_x
+    add_y_ref[...] = add_y
     pack(columns_ref, rows_ref, side, outs, strips_ref)
 
 
-def spread_lanes(turned_x, spread_ref):
-    high, low = split2(turned_x)
+def spread_lanes(add_x, spread_ref):
+    high, low = split2(add_x.T)
     return tiles_of(
         jnp.dot(
             jnp.concatenate([high, low], axis=1),
@@ -400,19 +385,14 @@
 
 
 def inner_kernel(first, last, state_ref, *refs):
-    if first:
-        wave, visc, starts, offsets = refs[:4]
-        new_ref, columns_ref, rows_ref = refs[4:7]
-        made = refs[7:]
-        make_constants(wave, visc, starts[...], offsets[...], made)
-        coef_ref, band_x_ref, band_y_ref, order_ref = made[0], made[8], made[9], made[6]
-    else:
-        coef_ref, band_x_ref, band_y_ref, order_ref, spread_ref = refs[:5]
-        add_x_ref, add_y_ref = refs[5:7]
-        new_ref = refs[7]
-        add_x, add_y = spread_lanes(add_x_ref[...], spread_ref), add_y_ref[...]
-        if not last:
-            columns_ref, rows_ref = refs[8:]
+    coef_ref, band_x_ref, band_y_ref, order_ref, spread_ref = refs[:5]
+    refs = refs[5:]
+    if not first:
+        add_x, add_y = spread_lanes(refs[0][...], spread_ref), refs[1][...]
+        refs = refs[2:]
+    new_ref = refs[0]
+    if not last:
+        columns_ref, rows_ref = refs[1:]
     if not last:
         clear_rest(rows_ref)
     columns = jnp.zeros((BLK // 8, 8, BLK), jnp.float32)
@@ -461,9 +441,9 @@
 
 
 def final_kernel(side, *refs):
-    add_x, add_y = ghost_additions(side, refs[:5], *refs[5:9])
-    spread_ref, state_ref, out_hbm, buffer, sems = refs[9:]
-    add_x = spread_lanes(add_x.T, spread_ref)
+    edge_ref, spread_ref, state_ref, out_hbm, buffer, sems = refs[8:]
+    add_x, add_y = ghost_additions(ghosts_of(side, refs[:5], *refs[5:8]), edge_ref)
+    add_x = spread_lanes(add_x, spread_ref)
     copies = []
     for face in range(FACES):
         for level in range(LEV):
@@ -512,30 +492,16 @@
     return turn_in, far_in, near_in, mirror_in, core_in
 
 
-def call(
-    kernel,
-    name,
-    outs,
-    ins,
-    scratch=(),
-    scalars=(),
-    out_hbm=False,
-    in_hbm=False,
-    limit=VMEM_LIMIT,
-    cost=0,
-    aliases=None,
-):
+def call(kernel, name, outs, ins, scratch=(), out_hbm=False, cost=0, aliases=None):
     hbm = pl.BlockSpec(memory_space=pltpu.HBM)
     vmem = pl.BlockSpec(memory_space=pltpu.VMEM)
-    smem = pl.BlockSpec(memory_space=pltpu.SMEM)
-    in_specs = [hbm if in_hbm else smem if at in scalars else vmem for at in range(len(ins))]
     return pl.pallas_call(
         kernel,
         out_shape=outs,
-        in_specs=in_specs,
+        in_specs=[vmem] * len(ins),
         out_specs=[hbm if out_hbm else vmem] * len(outs),
         scratch_shapes=list(scratch),
-        compiler_params=pltpu.CompilerParams(vmem_limit_bytes=limit),
+        compiler_params=pltpu.CompilerParams(vmem_limit_bytes=VMEM_LIMIT),
         cost_estimate=pl.CostEstimate(flops=cost, bytes_accessed=cost // 500, transcendentals=0),
         input_output_aliases=aliases or {},
         name=name,
@@ -557,53 +523,43 @@
         pltpu.VMEM((BLK, BLK), jnp.float32),
         pltpu.VMEM((4, FACES, 16, BLK), jnp.float32),
     ]
-    scalars = pltpu.SMEM((LEV,), jnp.float32)
+    values = call(
+        tables_kernel,
+        "tables",
+        [array(*shape, dtype=kind) for _, shape, kind in TABLES],
+        [],
+        cost=4_000_000_000,
+    )
+    made = dict(zip((name for name, _, _ in TABLES), values))
+    values = call(
+        constants_kernel,
+        "constants",
+        [array(*shape, dtype=kind) for _, shape, kind in CONSTANTS],
+        [wave_coef[None], visc_coef[None], stencil_start, stencil_offset],
+        cost=1_000_000_000,
+    )
+    made.update(zip((name for name, _, _ in CONSTANTS), values))
     sent = call(
         lambda *refs: first_kernel(side, *refs),
         "first_edges",
         [strip] * 7,
-        [field, wave_coef, visc_coef],
-        [
-            pltpu.VMEM(field.shape, jnp.float32),
-            scalars,
-            scalars,
-            *work,
-            pltpu.SemaphoreType.DMA((FACES + 2,)),
-        ],
-        in_hbm=True,
-        limit=FIRST_LIMIT,
+        [field, made["coef"], made["order"]],
+        work,
         cost=1_000_000_000,
     )
-    made = {}
     adds = []
+    names = ("coef", "band_x", "band_y", "order", "spread")
     for step in range(SUBSTEPS):
         first, last = step == 0, step == SUBSTEPS - 1
         received = exchange(sent[:5], side)
-
-        def inner(*refs, first=first, last=last):
-            inner_kernel(first, last, *refs)
-
-        if first:
-            field, *rest = call(
-                inner,
-                "inner",
-                [whole] + [tile] * 2 + [array(*shape, dtype=kind) for _, shape, kind in CONSTANTS],
-                [field, wave_coef, visc_coef, stencil_start, stencil_offset],
-                scalars=(1, 2),
-                cost=2_000_000_000,
-            )
-            edges = rest[:2]
-            made = dict(zip((name for name, _, _ in CONSTANTS), rest[2:]))
-        else:
-            names = ("coef", "band_x", "band_y", "order", "spread")
-            field, *edges = call(
-                inner,
-                "inner",
-                [whole] + ([] if last else [tile] * 2),
-                [field, *(made[name] for name in names), *adds],
-                cost=2_000_000_000,
-                aliases={0: 0},
-            )
+        field, *edges = call(
+            lambda *refs, first=first, last=last: inner_kernel(first, last, *refs),
+            "inner",
+            [whole] + ([] if last else [tile] * 2),
+            [field, *(made[name] for name in names), *adds],
+            cost=2_000_000_000,
+            aliases=None if first else {0: 0},
+        )
         ghosts = [*received, *sent[5:], made["matrix"], made["edge"]]
         if last:
             break
@@ -611,7 +567,7 @@
             lambda *refs: edge_kernel(side, *refs),
             "edges",
             [tile] * 2 + [strip] * 7,
-            [*ghosts, made["fold"], made["same"], made["gain"], *edges],
+            [*ghosts, made["reach"], made["same"], made["gain"], *edges],
             work,
         )
         adds, sent = updates[:2], updates[2:]

time: 41.4 us -> 40.3 us (0.973)
  Pallas kernels: 13.9 us -> 10.9 us
  local copies, waits for them, and re-layouts: 0.03 us -> 1.38 us
  waiting for transfers between devices: 5.07 us -> 5.52 us
    pallas_call x9 -> x11, Pallas kernels: 13.9 us -> 10.9 us  [call(): pl.pallas_call(kernel, out_shape=outs, in_specs=[vmem] * len(ins), out_sp...]
    unnamed x14 -> x10, local copies, waits for them, and re-layouts: 0.03 us -> 1.38 us
    ppermute x4, waiting for transfers between devices: 5 us -> 5.45 us  [exchange(): far_in = lax.ppermute(far_out, 'tile', far)]
  transfers between devices with their start and end apart: 20 -> 20, of which waited for: 4 -> 4; matrix products, arithmetic and copies ran while one was open for 0% -> 0% of each run, Pallas kernels for 15% -> 14%
where the time goes in v5:
time: 40.3 us; the launch traced here: 40.1 us
  starting transfers between devices  22.2 us (55%)
  Pallas kernels  10.9 us (27%)
  waiting for transfers between devices  5.52 us (14%)
  local copies, waits for them, and re-layouts  1.38 us (3%)
    pallas_call x11, Pallas kernels, call(): pl.pallas_call(kernel, out_shape=outs, in_specs=[vmem] * len(ins), out_sp...  10.9 us
    ppermute x4, starting transfers between devices, exchange(): turn_in = lax.ppermute(turn_out, 'tile', sorted(turn))  10.2 us
    ppermute x4, waiting for transfers between devices, exchange(): far_in = lax.ppermute(far_out, 'tile', far)  5.45 us
    ppermute x4, starting transfers between devices, exchange(): mirror_in = lax.ppermute(mirror_out, 'tile', mirror)  5.11 us
    ppermute x4, starting transfers between devices, exchange(): far_in = lax.ppermute(far_out, 'tile', far)  3.32 us
    ppermute x4, starting transfers between devices, exchange(): near_in = lax.ppermute(near_out, 'tile', near)  2.44 us
    unnamed x10, local copies, waits for them, and re-layouts  1.38 us
    ppermute x4, starting transfers between devices, exchange(): core_in = lax.ppermute(core_out, 'tile', core)  1.19 us
  transfers between devices with their start and end apart: 20, of which 4 were waited for; matrix products, arithmetic and copies ran while one was open for 0% of the time, Pallas kernels for 14%

profile of v5, /device:TPU:0, one launch (start us, length us, event | category | flops | bytes accessed | tf_op | source)
XLA Modules:
  0.0 40.1 jit_solution(3236150516841502778)
XLA Ops:
  0.1 0.5 %copy-done.2 = f32[3,128]{1,0:T(4,128)S(1)} copy-done((f32[3,128]{1,0:T(4,128)S(1)}, f32[3,128]{1,0:T(4,128)}, u32[]{:S(2)}) %copy-start.2) | copy-done | bytes 1560
  0.7 0.3 constants.1
  1.0 0.8 %copy-done = f32[1,6,6,128,128]{4,3,2,1,0:T(8,128)S(1)} copy-done((f32[1,6,6,128,128]{4,3,2,1,0:T(8,128)S(1)}, f32[1,6,6,128,128]{4,3,2,1,0:T(8,128)}, u32[]{:S(2)}) %copy-start) | copy-done | bytes 2359320
  1.8 0.6 %first_edges.1 = (f32[56,128]{1,0:T(8,128)S(1)}, f32[56,128]{1,0:T(8,128)S(1)}, f32[56,128]{1,0:T(8,128)S(1)}, f32[56,128]{1,0:T(8,128)S(1)}, f32[56,128]{1,0:T(...) custom-call(f32[6,6,128,128]{3,2,1,0:T(8,128)S(1)} %bitcast.4, f32[8,128]{1,0:T(8,128)S(1)} %get-tuple-element.58.refs_1_, ...), custom_call_target="tpu_custom_call" | custom-call | flops 1000000000 | bytes 2000000 | tf_op jit(solution)/shard_map/first_edges/pallas_call | solution.py:498
  2.4 5.5 %collective-permute-start = (f32[56,128]{1,0:T(8,128)S(1)}, f32[56,128]{1,0:T(8,128)S(1)}, u32[]{:S(2)}, u32[]{:S(2)}) collective-permute-start(f32[56,128]{1,0:T(8,128)S(1)} %get-tuple-element.60), channel_id=1, source_target_pairs={{0,15},{1,11},{2,7},{3,6},{4,14},{5,10},{6,3},{7,2},{8,13},{9,12},... | collective-permute-start | bytes 86024 | tf_op jit(solution)/shard_map/ppermute | solution.py:487
  7.9 1.1 %collective-permute-start.2 = (f32[56,128]{1,0:T(8,128)S(1)}, f32[56,128]{1,0:T(8,128)S(1)}, u32[]{:S(2)}, u32[]{:S(2)}) collective-permute-start(f32[56,128]{1,0:T(8,128)S(1)} %get-tuple-element.62), channel_id=1, source_target_pairs={{0,4},{1,5},{2,6},{3,7},{4,0},{5,1},{6,2},{7,3},{8,12},{9,13},{10,... | collective-permute-start | bytes 86024 | tf_op jit(solution)/shard_map/ppermute | solution.py:489
  9.0 0.4 collective-permute-start.4
  9.4 1.0 %inner.4 = (f32[6,6,128,128]{3,2,1,0:T(8,128)S(1)}, f32[128,128]{1,0:T(8,128)S(1)}, f32[128,128]{1,0:T(8,128)S(1)}) custom-call(f32[6,6,128,128]{3,2,1,0:T(8,128)S(1)} %bitcast.5, f32[8,128]{1,0:T(8,128)S(1)} %get-tuple-element.58.refs_1_, bf16[256,128]{1,0:T(8,128)(2,1)S(1)} %get-tuple-element.72.refs_2_, bf16[128,256]{1,0:T(8,128)(2,1)S(1)} %get-tuple-element.73.refs_3_, ...), custom_call_target="tpu_custom_call" | custom-call | flops 2000000000 | bytes 4000000 | tf_op jit(solution)/shard_map/inner/pallas_call | solution.py:498
  10.4 3.2 %collective-permute-done.1.refs_1_ = f32[56,128]{1,0:T(8,128)S(1)} collective-permute-done((f32[56,128]{1,0:T(8,128)S(1)}, f32[56,128]{1,0:T(8,128)S(1)}, u32[]{:S(2)}, u32[]{:S(2)}) %collective-permute-start.1) | collective-permute-done | bytes 28704 | tf_op jit(solution)/shard_map/ppermute | solution.py:488
  13.6 0.6 %edges.3 = (f32[128,128]{1,0:T(8,128)S(1)}, f32[128,128]{1,0:T(8,128)S(1)}, f32[56,128]{1,0:T(8,128)S(1)}, f32[56,128]{1,0:T(8,128)S(1)}, f32[56,128]{1,0:T(8,12...) custom-call(f32[56,128]{1,0:T(8,128)S(1)} %collective-permute-done.refs_0, ...), custom_call_target="tpu_custom_call" | custom-call | tf_op jit(solution)/shard_map/edges/pallas_call | solution.py:498
  14.2 1.2 %collective-permute-start.5 = (f32[56,128]{1,0:T(8,128)S(1)}, f32[56,128]{1,0:T(8,128)S(1)}, u32[]{:S(2)}, u32[]{:S(2)}) collective-permute-start(f32[56,128]{1,0:T(8,128)S(1)} %get-tuple-element.77), channel_id=1, source_target_pairs={{0,15},{1,11},{2,7},{3,6},{4,14},{5,10},{6,3},{7,2},{8,13},{9,12},... | collective-permute-start | bytes 86024 | tf_op jit(solution)/shard_map/ppermute | solution.py:487
  15.4 1.0 %collective-permute-start.6 = (f32[56,128]{1,0:T(8,128)S(1)}, f32[56,128]{1,0:T(8,128)S(1)}, u32[]{:S(2)}, u32[]{:S(2)}) collective-permute-start(f32[56,128]{1,0:T(8,128)S(1)} %get-tuple-element.78), channel_id=1, source_target_pairs={{0,12},{1,13},{2,14},{3,15},{4,8},{5,9},{6,10},{7,11},{8,4},{9,5},... | collective-permute-start | bytes 86024 | tf_op jit(solution)/shard_map/ppermute | solution.py:488
  16.4 0.6 %collective-permute-start.7 = (f32[56,128]{1,0:T(8,128)S(1)}, f32[56,128]{1,0:T(8,128)S(1)}, u32[]{:S(2)}, u32[]{:S(2)}) collective-permute-start(f32[56,128]{1,0:T(8,128)S(1)} %get-tuple-element.79), channel_id=1, source_target_pairs={{0,4},{1,5},{2,6},{3,7},{4,0},{5,1},{6,2},{7,3},{8,12},{9,13},{10,... | collective-permute-start | bytes 86024 | tf_op jit(solution)/shard_map/ppermute | solution.py:489
  16.9 2.1 %collective-permute-start.8 = (f32[56,128]{1,0:T(8,128)S(1)}, f32[56,128]{1,0:T(8,128)S(1)}, u32[]{:S(2)}, u32[]{:S(2)}) collective-permute-start(f32[56,128]{1,0:T(8,128)S(1)} %get-tuple-element.80), channel_id=1, source_target_pairs={{0,3},{1,2},{2,1},{3,0},{4,7},{5,6},{6,5},{7,4},{8,11},{9,10},{10,... | collective-permute-start | bytes 86024 | tf_op jit(solution)/shard_map/ppermute | solution.py:490
  19.0 1.6 %inner.5 = (f32[6,6,128,128]{3,2,1,0:T(8,128)S(1)}, f32[128,128]{1,0:T(8,128)S(1)}, f32[128,128]{1,0:T(8,128)S(1)}) custom-call(f32[6,6,128,128]{3,2,1,0:T(8,128)S(1)} %get-tuple-element.84.refs_0_, f32[8,128]{1,0:T(8,128)S(1)} %get-tuple-element.58.refs_1_, bf16[256,128]{1,0:T(8,128)(2,1)S(1)} %get-tuple-element.72.refs_2_, ...), custom_call_target="tpu_custom_call", output_to_operand_aliasing={{0}: (0, {})} | custom-call | flops 2000000000 | bytes 4000000 | tf_op jit(solution)/shard_map/inner/pallas_call | solution.py:498
  20.7 0.5 %collective-permute-done.6.refs_1_ = f32[56,128]{1,0:T(8,128)S(1)} collective-permute-done((f32[56,128]{1,0:T(8,128)S(1)}, f32[56,128]{1,0:T(8,128)S(1)}, u32[]{:S(2)}, u32[]{:S(2)}) %collective-permute-start.6) | collective-permute-done | bytes 28704 | tf_op jit(solution)/shard_map/ppermute | solution.py:488
  21.2 0.6 %edges.4 = (f32[128,128]{1,0:T(8,128)S(1)}, f32[128,128]{1,0:T(8,128)S(1)}, f32[56,128]{1,0:T(8,128)S(1)}, f32[56,128]{1,0:T(8,128)S(1)}, f32[56,128]{1,0:T(8,12...) custom-call(f32[56,128]{1,0:T(8,128)S(1)} %collective-permute-done.5.refs, ...), custom_call_target="tpu_custom_call" | custom-call | tf_op jit(solution)/shard_map/edges/pallas_call | solution.py:498
  21.8 2.1 %collective-permute-start.10 = (f32[56,128]{1,0:T(8,128)S(1)}, f32[56,128]{1,0:T(8,128)S(1)}, u32[]{:S(2)}, u32[]{:S(2)}) collective-permute-start(f32[56,128]{1,0:T(8,128)S(1)} %get-tuple-element.89), channel_id=1, source_target_pairs={{0,15},{1,11},{2,7},{3,6},{4,14},{5,10},{6,3},{7,2},{8,13},{9,12},... | collective-permute-start | bytes 86024 | tf_op jit(solution)/shard_map/ppermute | solution.py:487
  24.0 1.2 %collective-permute-start.11 = (f32[56,128]{1,0:T(8,128)S(1)}, f32[56,128]{1,0:T(8,128)S(1)}, u32[]{:S(2)}, u32[]{:S(2)}) collective-permute-start(f32[56,128]{1,0:T(8,128)S(1)} %get-tuple-element.90), channel_id=1, source_target_pairs={{0,12},{1,13},{2,14},{3,15},{4,8},{5,9},{6,10},{7,11},{8,4},{9,5},... | collective-permute-start | bytes 86024 | tf_op jit(solution)/shard_map/ppermute | solution.py:488
  25.2 1.4 %collective-permute-start.13 = (f32[56,128]{1,0:T(8,128)S(1)}, f32[56,128]{1,0:T(8,128)S(1)}, u32[]{:S(2)}, u32[]{:S(2)}) collective-permute-start(f32[56,128]{1,0:T(8,128)S(1)} %get-tuple-element.92), channel_id=1, source_target_pairs={{0,3},{1,2},{2,1},{3,0},{4,7},{5,6},{6,5},{7,4},{8,11},{9,10},{10,... | collective-permute-start | bytes 86024 | tf_op jit(solution)/shard_map/ppermute | solution.py:490
  26.6 0.5 %collective-permute-start.14 = (f32[56,128]{1,0:T(8,128)S(1)}, f32[56,128]{1,0:T(8,128)S(1)}, u32[]{:S(2)}, u32[]{:S(2)}) collective-permute-start(f32[56,128]{1,0:T(8,128)S(1)} %get-tuple-element.93), channel_id=1, source_target_pairs={{0,1},{1,0},{2,3},{3,2},{4,5},{5,4},{6,7},{7,6},{8,9},{9,8},{10,11... | collective-permute-start | bytes 86024 | tf_op jit(solution)/shard_map/ppermute | solution.py:491
  27.1 1.6 %inner.6 = (f32[6,6,128,128]{3,2,1,0:T(8,128)S(1)}, f32[128,128]{1,0:T(8,128)S(1)}, f32[128,128]{1,0:T(8,128)S(1)}) custom-call(f32[6,6,128,128]{3,2,1,0:T(8,128)S(1)} %get-tuple-element.96.refs_0_, f32[8,128]{1,0:T(8,128)S(1)} %get-tuple-element.58.refs_1_, bf16[256,128]{1,0:T(8,128)(2,1)S(1)} %get-tuple-element.72.refs_2_, ...), custom_call_target="tpu_custom_call", output_to_operand_aliasing={{0}: (0, {})} | custom-call | flops 2000000000 | bytes 4000000 | tf_op jit(solution)/shard_map/inner/pallas_call | solution.py:498
  28.7 0.9 %collective-permute-done.11.refs_1_ = f32[56,128]{1,0:T(8,128)S(1)} collective-permute-done((f32[56,128]{1,0:T(8,128)S(1)}, f32[56,128]{1,0:T(8,128)S(1)}, u32[]{:S(2)}, u32[]{:S(2)}) %collective-permute-start.11) | collective-permute-done | bytes 28704 | tf_op jit(solution)/shard_map/ppermute | solution.py:488
  29.7 0.6 %edges.5 = (f32[128,128]{1,0:T(8,128)S(1)}, f32[128,128]{1,0:T(8,128)S(1)}, f32[56,128]{1,0:T(8,128)S(1)}, f32[56,128]{1,0:T(8,128)S(1)}, f32[56,128]{1,0:T(8,12...) custom-call(f32[56,128]{1,0:T(8,128)S(1)} %collective-permute-done.10.ref, ...), custom_call_target="tpu_custom_call" | custom-call | tf_op jit(solution)/shard_map/edges/pallas_call | solution.py:498
  30.3 1.3 %collective-permute-start.15 = (f32[56,128]{1,0:T(8,128)S(1)}, f32[56,128]{1,0:T(8,128)S(1)}, u32[]{:S(2)}, u32[]{:S(2)}) collective-permute-start(f32[56,128]{1,0:T(8,128)S(1)} %get-tuple-element.101), channel_id=1, source_target_pairs={{0,15},{1,11},{2,7},{3,6},{4,14},{5,10},{6,3},{7,2},{8,13},{9,12},... | collective-permute-start | bytes 86024 | tf_op jit(solution)/shard_map/ppermute | solution.py:487
  31.6 1.1 %collective-permute-start.16 = (f32[56,128]{1,0:T(8,128)S(1)}, f32[56,128]{1,0:T(8,128)S(1)}, u32[]{:S(2)}, u32[]{:S(2)}) collective-permute-start(f32[56,128]{1,0:T(8,128)S(1)} %get-tuple-element.102), channel_id=1, source_target_pairs={{0,12},{1,13},{2,14},{3,15},{4,8},{5,9},{6,10},{7,11},{8,4},{9,5},... | collective-permute-start | bytes 86024 | tf_op jit(solution)/shard_map/ppermute | solution.py:488
  32.7 0.8 %collective-permute-start.17 = (f32[56,128]{1,0:T(8,128)S(1)}, f32[56,128]{1,0:T(8,128)S(1)}, u32[]{:S(2)}, u32[]{:S(2)}) collective-permute-start(f32[56,128]{1,0:T(8,128)S(1)} %get-tuple-element.103), channel_id=1, source_target_pairs={{0,4},{1,5},{2,6},{3,7},{4,0},{5,1},{6,2},{7,3},{8,12},{9,13},{10,... | collective-permute-start | bytes 86024 | tf_op jit(solution)/shard_map/ppermute | solution.py:489
  33.5 1.6 %collective-permute-start.18 = (f32[56,128]{1,0:T(8,128)S(1)}, f32[56,128]{1,0:T(8,128)S(1)}, u32[]{:S(2)}, u32[]{:S(2)}) collective-permute-start(f32[56,128]{1,0:T(8,128)S(1)} %get-tuple-element.104), channel_id=1, source_target_pairs={{0,3},{1,2},{2,1},{3,0},{4,7},{5,6},{6,5},{7,4},{8,11},{9,10},{10,... | collective-permute-start | bytes 86024 | tf_op jit(solution)/shard_map/ppermute | solution.py:490
  35.1 0.3 collective-permute-start.19
  35.4 1.3 %inner.7.refs_10_ = f32[6,6,128,128]{3,2,1,0:T(8,128)S(1)} custom-call(f32[6,6,128,128]{3,2,1,0:T(8,128)S(1)} %get-tuple-element.108.refs_0_, f32[8,128]{1,0:T(8,128)S(1)} %get-tuple-element.58.refs_1_, bf16[256,128]{1,0:T(8,128)(2,1)S(1)} %get-tuple-element.72.refs_2_, ...), custom_call_target="tpu_custom_call", output_to_operand_aliasing={{}: (0, {})} | custom-call | flops 2000000000 | bytes 4000000 | tf_op jit(solution)/shard_map/inner/pallas_call | solution.py:498
  36.8 0.8 %collective-permute-done.16.refs_1_ = f32[56,128]{1,0:T(8,128)S(1)} collective-permute-done((f32[56,128]{1,0:T(8,128)S(1)}, f32[56,128]{1,0:T(8,128)S(1)}, u32[]{:S(2)}, u32[]{:S(2)}) %collective-permute-start.16) | collective-permute-done | bytes 28704 | tf_op jit(solution)/shard_map/ppermute | solution.py:488
  37.6 2.5 %final.1 = f32[6,6,128,128]{3,2,1,0:T(8,128)} custom-call(f32[56,128]{1,0:T(8,128)S(1)} %collective-permute-done.15.refs_0_, f32[56,128]{1,0:T(8,128)S(1)} %collective-permute-done.16.refs_1_, f32[56,128]{1,0:T(8,128)S(1)} %collective-permute-done.17.refs_2_, f32[56,128]{1,0:T(8,128)S(1)} %collective-permute-done.18.refs_3_, ...), custom_call_target="tpu_custom_call" | custom-call | tf_op jit(solution)/shard_map/final/pallas_call | solution.py:498
  (29 shorter events, 0.2 us)
Async XLA Ops:
  0.0 0.7 %copy-start.2 = (f32[3,128]{1,0:T(4,128)S(1)}, f32[3,128]{1,0:T(4,128)}, u32[]{:S(2)}) copy-start(f32[3,128]{1,0:T(4,128)} %offset_ref.1) | copy-start | bytes 4612
  0.0 0.7 %copy-start.1 = (s32[3,128]{1,0:T(4,128)S(1)}, s32[3,128]{1,0:T(4,128)}, u32[]{:S(2)}) copy-start(s32[3,128]{1,0:T(4,128)} %start_ref.1) | copy-start | bytes 4612
  0.0 0.7 %copy-start.4 = (f32[3]{0:T(128)S(1)}, f32[3]{0:T(128)}, u32[]{:S(2)}) copy-start(f32[3]{0:T(128)} %param.7) | copy-start | bytes 40
  0.0 0.7 %copy-start.3 = (f32[3]{0:T(128)S(1)}, f32[3]{0:T(128)}, u32[]{:S(2)}) copy-start(f32[3]{0:T(128)} %param.6) | copy-start | bytes 40
  0.1 1.7 %copy-start = (f32[1,6,6,128,128]{4,3,2,1,0:T(8,128)S(1)}, f32[1,6,6,128,128]{4,3,2,1,0:T(8,128)}, u32[]{:S(2)}) copy-start(f32[1,6,6,128,128]{4,3,2,1,0:T(8,128)} %param.5) | copy-start | bytes 7077892
  2.4 8.0 %collective-permute-start = (f32[56,128]{1,0:T(8,128)S(1)}, f32[56,128]{1,0:T(8,128)S(1)}, u32[]{:S(2)}, u32[]{:S(2)}) collective-permute-start(f32[56,128]{1,0:T(8,128)S(1)} %get-tuple-element.60), channel_id=1, source_target_pairs={{0,15},{1,11},{2,7},{3,6},{4,14},{5,10},{6,3},{7,2},{8,13},{9,12},... | collective-permute-start | bytes 86024 | tf_op jit(solution)/shard_map/ppermute | solution.py:487
  7.9 5.7 %collective-permute-start.1 = (f32[56,128]{1,0:T(8,128)S(1)}, f32[56,128]{1,0:T(8,128)S(1)}, u32[]{:S(2)}, u32[]{:S(2)}) collective-permute-start(f32[56,128]{1,0:T(8,128)S(1)} %get-tuple-element.61), channel_id=1, source_target_pairs={{0,12},{1,13},{2,14},{3,15},{4,8},{5,9},{6,10},{7,11},{8,4},{9,5},... | collective-permute-start | bytes 86024 | tf_op jit(solution)/shard_map/ppermute | solution.py:488
  7.9 5.7 %collective-permute-start.2 = (f32[56,128]{1,0:T(8,128)S(1)}, f32[56,128]{1,0:T(8,128)S(1)}, u32[]{:S(2)}, u32[]{:S(2)}) collective-permute-start(f32[56,128]{1,0:T(8,128)S(1)} %get-tuple-element.62), channel_id=1, source_target_pairs={{0,4},{1,5},{2,6},{3,7},{4,0},{5,1},{6,2},{7,3},{8,12},{9,13},{10,... | collective-permute-start | bytes 86024 | tf_op jit(solution)/shard_map/ppermute | solution.py:489
  9.0 4.5 %collective-permute-start.3 = (f32[56,128]{1,0:T(8,128)S(1)}, f32[56,128]{1,0:T(8,128)S(1)}, u32[]{:S(2)}, u32[]{:S(2)}) collective-permute-start(f32[56,128]{1,0:T(8,128)S(1)} %get-tuple-element.63), channel_id=1, source_target_pairs={{0,3},{1,2},{2,1},{3,0},{4,7},{5,6},{6,5},{7,4},{8,11},{9,10},{10,... | collective-permute-start | bytes 86024 | tf_op jit(solution)/shard_map/ppermute | solution.py:490
  9.0 4.5 %collective-permute-start.4 = (f32[56,128]{1,0:T(8,128)S(1)}, f32[56,128]{1,0:T(8,128)S(1)}, u32[]{:S(2)}, u32[]{:S(2)}) collective-permute-start(f32[56,128]{1,0:T(8,128)S(1)} %get-tuple-element.64), channel_id=1, source_target_pairs={{0,1},{1,0},{2,3},{3,2},{4,5},{5,4},{6,7},{7,6},{8,9},{9,8},{10,11... | collective-permute-start | bytes 86024 | tf_op jit(solution)/shard_map/ppermute | solution.py:491
  14.2 6.4 %collective-permute-start.5 = (f32[56,128]{1,0:T(8,128)S(1)}, f32[56,128]{1,0:T(8,128)S(1)}, u32[]{:S(2)}, u32[]{:S(2)}) collective-permute-start(f32[56,128]{1,0:T(8,128)S(1)} %get-tuple-element.77), channel_id=1, source_target_pairs={{0,15},{1,11},{2,7},{3,6},{4,14},{5,10},{6,3},{7,2},{8,13},{9,12},... | collective-permute-start | bytes 86024 | tf_op jit(solution)/shard_map/ppermute | solution.py:487
  15.4 5.8 %collective-permute-start.6 = (f32[56,128]{1,0:T(8,128)S(1)}, f32[56,128]{1,0:T(8,128)S(1)}, u32[]{:S(2)}, u32[]{:S(2)}) collective-permute-start(f32[56,128]{1,0:T(8,128)S(1)} %get-tuple-element.78), channel_id=1, source_target_pairs={{0,12},{1,13},{2,14},{3,15},{4,8},{5,9},{6,10},{7,11},{8,4},{9,5},... | collective-permute-start | bytes 86024 | tf_op jit(solution)/shard_map/ppermute | solution.py:488
  16.4 4.8 %collective-permute-start.7 = (f32[56,128]{1,0:T(8,128)S(1)}, f32[56,128]{1,0:T(8,128)S(1)}, u32[]{:S(2)}, u32[]{:S(2)}) collective-permute-start(f32[56,128]{1,0:T(8,128)S(1)} %get-tuple-element.79), channel_id=1, source_target_pairs={{0,4},{1,5},{2,6},{3,7},{4,0},{5,1},{6,2},{7,3},{8,12},{9,13},{10,... | collective-permute-start | bytes 86024 | tf_op jit(solution)/shard_map/ppermute | solution.py:489
  16.9 4.2 %collective-permute-start.8 = (f32[56,128]{1,0:T(8,128)S(1)}, f32[56,128]{1,0:T(8,128)S(1)}, u32[]{:S(2)}, u32[]{:S(2)}) collective-permute-start(f32[56,128]{1,0:T(8,128)S(1)} %get-tuple-element.80), channel_id=1, source_target_pairs={{0,3},{1,2},{2,1},{3,0},{4,7},{5,6},{6,5},{7,4},{8,11},{9,10},{10,... | collective-permute-start | bytes 86024 | tf_op jit(solution)/shard_map/ppermute | solution.py:490
  19.0 2.2 %collective-permute-start.9 = (f32[56,128]{1,0:T(8,128)S(1)}, f32[56,128]{1,0:T(8,128)S(1)}, u32[]{:S(2)}, u32[]{:S(2)}) collective-permute-start(f32[56,128]{1,0:T(8,128)S(1)} %get-tuple-element.81), channel_id=1, source_target_pairs={{0,1},{1,0},{2,3},{3,2},{4,5},{5,4},{6,7},{7,6},{8,9},{9,8},{10,11... | collective-permute-start | bytes 86024 | tf_op jit(solution)/shard_map/ppermute | solution.py:491
  21.8 6.9 %collective-permute-start.10 = (f32[56,128]{1,0:T(8,128)S(1)}, f32[56,128]{1,0:T(8,128)S(1)}, u32[]{:S(2)}, u32[]{:S(2)}) collective-permute-start(f32[56,128]{1,0:T(8,128)S(1)} %get-tuple-element.89), channel_id=1, source_target_pairs={{0,15},{1,11},{2,7},{3,6},{4,14},{5,10},{6,3},{7,2},{8,13},{9,12},... | collective-permute-start | bytes 86024 | tf_op jit(solution)/shard_map/ppermute | solution.py:487
  24.0 5.7 %collective-permute-start.11 = (f32[56,128]{1,0:T(8,128)S(1)}, f32[56,128]{1,0:T(8,128)S(1)}, u32[]{:S(2)}, u32[]{:S(2)}) collective-permute-start(f32[56,128]{1,0:T(8,128)S(1)} %get-tuple-element.90), channel_id=1, source_target_pairs={{0,12},{1,13},{2,14},{3,15},{4,8},{5,9},{6,10},{7,11},{8,4},{9,5},... | collective-permute-start | bytes 86024 | tf_op jit(solution)/shard_map/ppermute | solution.py:488
  25.2 4.4 %collective-permute-start.12 = (f32[56,128]{1,0:T(8,128)S(1)}, f32[56,128]{1,0:T(8,128)S(1)}, u32[]{:S(2)}, u32[]{:S(2)}) collective-permute-start(f32[56,128]{1,0:T(8,128)S(1)} %get-tuple-element.91), channel_id=1, source_target_pairs={{0,4},{1,5},{2,6},{3,7},{4,0},{5,1},{6,2},{7,3},{8,12},{9,13},{10,... | collective-permute-start | bytes 86024 | tf_op jit(solution)/shard_map/ppermute | solution.py:489
  25.2 4.4 %collective-permute-start.13 = (f32[56,128]{1,0:T(8,128)S(1)}, f32[56,128]{1,0:T(8,128)S(1)}, u32[]{:S(2)}, u32[]{:S(2)}) collective-permute-start(f32[56,128]{1,0:T(8,128)S(1)} %get-tuple-element.92), channel_id=1, source_target_pairs={{0,3},{1,2},{2,1},{3,0},{4,7},{5,6},{6,5},{7,4},{8,11},{9,10},{10,... | collective-permute-start | bytes 86024 | tf_op jit(solution)/shard_map/ppermute | solution.py:490
  26.6 3.0 %collective-permute-start.14 = (f32[56,128]{1,0:T(8,128)S(1)}, f32[56,128]{1,0:T(8,128)S(1)}, u32[]{:S(2)}, u32[]{:S(2)}) collective-permute-start(f32[56,128]{1,0:T(8,128)S(1)} %get-tuple-element.93), channel_id=1, source_target_pairs={{0,1},{1,0},{2,3},{3,2},{4,5},{5,4},{6,7},{7,6},{8,9},{9,8},{10,11... | collective-permute-start | bytes 86024 | tf_op jit(solution)/shard_map/ppermute | solution.py:491
  30.3 6.5 %collective-permute-start.15 = (f32[56,128]{1,0:T(8,128)S(1)}, f32[56,128]{1,0:T(8,128)S(1)}, u32[]{:S(2)}, u32[]{:S(2)}) collective-permute-start(f32[56,128]{1,0:T(8,128)S(1)} %get-tuple-element.101), channel_id=1, source_target_pairs={{0,15},{1,11},{2,7},{3,6},{4,14},{5,10},{6,3},{7,2},{8,13},{9,12},... | collective-permute-start | bytes 86024 | tf_op jit(solution)/shard_map/ppermute | solution.py:487
  31.6 6.0 %collective-permute-start.16 = (f32[56,128]{1,0:T(8,128)S(1)}, f32[56,128]{1,0:T(8,128)S(1)}, u32[]{:S(2)}, u32[]{:S(2)}) collective-permute-start(f32[56,128]{1,0:T(8,128)S(1)} %get-tuple-element.102), channel_id=1, source_target_pairs={{0,12},{1,13},{2,14},{3,15},{4,8},{5,9},{6,10},{7,11},{8,4},{9,5},... | collective-permute-start | bytes 86024 | tf_op jit(solution)/shard_map/ppermute | solution.py:488
  32.7 4.9 %collective-permute-start.17 = (f32[56,128]{1,0:T(8,128)S(1)}, f32[56,128]{1,0:T(8,128)S(1)}, u32[]{:S(2)}, u32[]{:S(2)}) collective-permute-start(f32[56,128]{1,0:T(8,128)S(1)} %get-tuple-element.103), channel_id=1, source_target_pairs={{0,4},{1,5},{2,6},{3,7},{4,0},{5,1},{6,2},{7,3},{8,12},{9,13},{10,... | collective-permute-start | bytes 86024 | tf_op jit(solution)/shard_map/ppermute | solution.py:489
  33.5 4.1 %collective-permute-start.18 = (f32[56,128]{1,0:T(8,128)S(1)}, f32[56,128]{1,0:T(8,128)S(1)}, u32[]{:S(2)}, u32[]{:S(2)}) collective-permute-start(f32[56,128]{1,0:T(8,128)S(1)} %get-tuple-element.104), channel_id=1, source_target_pairs={{0,3},{1,2},{2,1},{3,0},{4,7},{5,6},{6,5},{7,4},{8,11},{9,10},{10,... | collective-permute-start | bytes 86024 | tf_op jit(solution)/shard_map/ppermute | solution.py:490
  35.1 2.5 %collective-permute-start.19 = (f32[56,128]{1,0:T(8,128)S(1)}, f32[56,128]{1,0:T(8,128)S(1)}, u32[]{:S(2)}, u32[]{:S(2)}) collective-permute-start(f32[56,128]{1,0:T(8,128)S(1)} %get-tuple-element.105), channel_id=1, source_target_pairs={{0,1},{1,0},{2,3},{3,2},{4,5},{5,4},{6,7},{7,6},{8,9},{9,8},{10,11... | collective-permute-start | bytes 86024 | tf_op jit(solution)/shard_map/ppermute | solution.py:491

commit v6 on v5

--- a/solution.py
+++ b/solution.py
@@ -14,6 +14,7 @@
 BLK = 128
 PER_FACE = LEV * DEPTH
 ROWS = 56
+TAPS = 4
 HALF = 64
 WEST, EAST, SOUTH, NORTH = 0, 1, 2, 3
 SCALE = 20.0
@@ -52,38 +53,6 @@
 def band_matrix():
     gap = jnp.abs(iota((BLK, BLK), 0) - iota((BLK, BLK), 1))
     return jnp.where(gap == 0, -40.0, weight_of(gap)).astype(jnp.bfloat16)
-
-
-def edge_matrix():
-    shape = (BLK, BLK)
-    to, src = iota(shape, 0), iota(shape, 1)
-    lower = to < HALF
-    to_row = jnp.where(lower, to, to - HALF)
-    src_row = jnp.where(src < HALF, src, src - HALF)
-    to_plane = (to_row * 171) >> 9
-    src_plane = (src_row * 171) >> 9
-    to_j = to_row - 3 * to_plane
-    src_j = src_row - 3 * src_plane
-    same = ((to < HALF) == (src < HALF)) & (to_plane == src_plane)
-    distance = jnp.where(lower, 3 + to_j - src_j, 3 + src_j - to_j)
-    return jnp.where(same, weight_of(distance), 0.0).astype(jnp.bfloat16)
-
-
-def seam_matrices(starts, offsets, out_ref):
-    j = iota((BLK, BLK), 0)
-    back = BLK - 1 - j
-    for h in range(DEPTH):
-        first = starts[h : h + 1, :]
-        weights = lagrange_weights(offsets[h : h + 1, :])
-        for turned, place in ((0, j), (1, back)):
-            matrix = jnp.zeros((BLK, BLK), jnp.float32)
-            for m, weight in enumerate(weights):
-                matrix = matrix + jnp.where(place == first + m, weight, 0.0)
-            high, low = split2(matrix)
-            at = (turned * DEPTH + h) * BLK
-            out_ref[:BLK, at : at + BLK] = high
-            out_ref[BLK : 2 * BLK, at : at + BLK] = high
-            out_ref[2 * BLK :, at : at + BLK] = low
 
 
 def position(side):
@@ -197,7 +166,6 @@
 
 
 TABLES = (
-    ("edge", (BLK, 2 * BLK), jnp.bfloat16),
     ("reach", (2 * BLK, BLK), jnp.bfloat16),
     ("same", (BLK, BLK), jnp.float32),
     ("order", (BLK, 2 * BLK), jnp.bfloat16),
@@ -208,15 +176,15 @@
 CONSTANTS = (
     ("coef", (8, BLK), jnp.float32),
     ("gain", (BLK, BLK), jnp.float32),
-    ("matrix", (3 * BLK, 2 * DEPTH * BLK), jnp.bfloat16),
+    ("taps", (TAPS, 2 * ROWS, BLK), jnp.int32),
+    ("weights", (TAPS, 2 * ROWS, BLK), jnp.float32),
 )
 
 
-def tables_kernel(edge, reach, same, order, spread, band_x, band_y):
+def tables_kernel(reach, same, order, spread, band_x, band_y):
     lower, plane, cell = plane_row((BLK, BLK), 0)
     _, plane_src, _ = plane_row((BLK, BLK), 1)
     for ref, value, axis in (
-        (edge, edge_matrix(), 1),
         (order, lane_order(), 1),
         (band_x, band_matrix(), 0),
         (band_y, band_matrix(), 1),
@@ -231,8 +199,28 @@
     same[...] = jnp.where(plane == plane_src, 1.0, 0.0)
 
 
-def constants_kernel(wave_ref, visc_ref, start_ref, offset_ref, coef_ref, gain_ref, matrix_ref):
-    seam_matrices(start_ref[...], offset_ref[...], matrix_ref)
+def seam_rows(place, low_turned):
+    odd, depth = row_codes((ROWS, BLK))
+    at_low = (place == 0).astype(jnp.int32)
+    is_turned = odd.astype(jnp.int32) == at_low ^ (1 - low_turned)
+    return is_turned, jnp.where(place == 0, DEPTH - 1 - depth, depth)
+
+
+def constants_kernel(
+    side, wave_ref, visc_ref, start_ref, offset_ref, coef_ref, gain_ref, taps_ref, weights_ref
+):
+    col, row = position(side)
+    for axis, place in enumerate((col, row)):
+        is_turned, h_of = seam_rows(place, axis)
+        first, offset = [
+            jnp.where(h_of == 0, ref[0:1, :], jnp.where(h_of == 1, ref[1:2, :], ref[2:3, :]))
+            for ref in (start_ref, offset_ref)
+        ]
+        at = axis * ROWS
+        for m, weight in enumerate(lagrange_weights(offset)):
+            tap = jnp.where(is_turned, BLK - 1 - first - m, first + m)
+            taps_ref[m, at : at + ROWS, :] = tap
+            weights_ref[m, at : at + ROWS, :] = weight
     _, plane, _ = plane_row((BLK, BLK), 0)
     level_of = plane - 3 * ((plane * 171) >> 9)
     gain = jnp.zeros((BLK, BLK), jnp.float32)
@@ -262,11 +250,10 @@
     pack(columns_ref, rows_ref, side, outs, strips_ref)
 
 
-def ghosts_of(side, received, own_a_ref, own_b_ref, matrix_ref):
+def ghosts_of(side, received, own_a_ref, own_b_ref, taps_ref, weights_ref):
     turned, far, near, mirror, core = [ref[...] for ref in received]
     col, row = position(side)
     even_col, even_row = lax.rem(col, 2) == 0, lax.rem(row, 2) == 0
-    odd, depth = row_codes((ROWS, BLK))
     alone = ((row == 0) & (col == side - 1)) | ((col == 0) & (row == side - 1))
     pairs = (
         (
@@ -284,29 +271,19 @@
             1,
         ),
     )
-    seams, marks = [], []
+    seams = []
     for low, high, crossed, place, low_turned in pairs:
-        at_low = (place == 0).astype(jnp.int32)
-        parity = at_low ^ (1 - low_turned)
-        is_turned = odd.astype(jnp.int32) == parity
+        is_turned, _ = seam_rows(place, low_turned)
         seams.append(jnp.where(is_turned, crossed, jnp.where(place == 0, low, high)))
-        marks.append((is_turned, jnp.where(place == 0, DEPTH - 1 - depth, depth)))
-    first, second = split2(jnp.concatenate(seams, axis=0))
-    mixed = jnp.dot(
-        jnp.concatenate([first, second, first], axis=1),
-        matrix_ref[...],
-        preferred_element_type=jnp.float32,
-    )
+    raw = jnp.concatenate(seams, axis=0)
+    mixed = jnp.zeros((2 * ROWS, BLK), jnp.float32)
+    for m in range(TAPS):
+        source = jnp.take_along_axis(raw, taps_ref[m], axis=1, mode="promise_in_bounds")
+        mixed = mixed + weights_ref[m] * source
     rest = jnp.zeros((HALF - ROWS, BLK), jnp.float32)
     ghosts = []
     for index, (low, high, _, place, _) in enumerate(pairs):
-        part = mixed[index * ROWS : (index + 1) * ROWS, :]
-        is_turned, h_of = marks[index]
-        made = jnp.zeros((ROWS, BLK), jnp.float32)
-        for h in range(DEPTH):
-            plain = part[:, h * BLK : (h + 1) * BLK]
-            turn = part[:, (DEPTH + h) * BLK : (DEPTH + h + 1) * BLK]
-            made = jnp.where(h_of == h, jnp.where(is_turned, turn, plain), made)
+        made = mixed[index * ROWS : (index + 1) * ROWS, :]
         ghosts.append(
             jnp.concatenate(
                 [
@@ -321,13 +298,17 @@
     return ghosts
 
 
-def ghost_additions(ghosts, edge_ref):
-    high, low = split2(jnp.concatenate(ghosts, axis=1))
-    adds = jnp.dot(
-        edge_ref[...],
-        jnp.concatenate([high, low], axis=0),
-        preferred_element_type=jnp.float32,
-    )
+def ghost_additions(ghosts):
+    row = iota((HALF, 1), 0)
+    cell = row - 3 * ((row * 171) >> 9)
+    halves = []
+    both = jnp.concatenate(ghosts, axis=1)
+    for half, step, index in ((both[:HALF], -1, cell), (both[HALF:], 1, 2 - cell)):
+        one = pltpu.roll(half, step % HALF, 0)
+        two = pltpu.roll(half, (2 * step) % HALF, 0)
+        near, next_ = jnp.where(index <= 1, 7.0, 0.0), jnp.where(index == 0, 9.0, 0.0)
+        halves.append(4.0 * half + near * one + next_ * two)
+    adds = jnp.concatenate(halves, axis=0)
     return adds[:, :BLK], adds[:, BLK:]
 
 
@@ -342,12 +323,12 @@
 
 
 def edge_kernel(side, *refs):
-    across, along = ghosts_of(side, refs[:5], *refs[5:8])
-    edge_ref, reach_ref, same_ref, gain_ref, old_columns_ref, old_rows_ref = refs[8:14]
+    across, along = ghosts_of(side, refs[:5], *refs[5:9])
+    reach_ref, same_ref, gain_ref, old_columns_ref, old_rows_ref = refs[9:14]
     add_x_ref, add_y_ref = refs[14:16]
     outs = refs[16:23]
     columns_ref, rows_ref, strips_ref = refs[23:]
-    add_x, add_y = ghost_additions((across, along), edge_ref)
+    add_x, add_y = ghost_additions((across, along))
     same = same_ref[...]
     corners = jnp.dot(
         jnp.concatenate([corner_part(along, same), corner_part(across, same)], axis=0),
@@ -441,8 +422,8 @@
 
 
 def final_kernel(side, *refs):
-    edge_ref, spread_ref, state_ref, out_hbm, buffer, sems = refs[8:]
-    add_x, add_y = ghost_additions(ghosts_of(side, refs[:5], *refs[5:8]), edge_ref)
+    spread_ref, state_ref, out_hbm, buffer, sems = refs[9:]
+    add_x, add_y = ghost_additions(ghosts_of(side, refs[:5], *refs[5:9]))
     add_x = spread_lanes(add_x, spread_ref)
     copies = []
     for face in range(FACES):
@@ -532,7 +513,7 @@
     )
     made = dict(zip((name for name, _, _ in TABLES), values))
     values = call(
-        constants_kernel,
+        lambda *refs: constants_kernel(side, *refs),
         "constants",
         [array(*shape, dtype=kind) for _, shape, kind in CONSTANTS],
         [wave_coef[None], visc_coef[None], stencil_start, stencil_offset],
@@ -560,7 +541,7 @@
             cost=2_000_000_000,
             aliases=None if first else {0: 0},
         )
-        ghosts = [*received, *sent[5:], made["matrix"], made["edge"]]
+        ghosts = [*received, *sent[5:], made["taps"], made["weights"]]
         if last:
             break
         updates = call(

time: 40.3 us -> 39.6 us (0.983)
  Pallas kernels: 10.9 us -> 10.1 us
    pallas_call x11, Pallas kernels: 10.9 us -> 10.1 us  [call(): pl.pallas_call(kernel, out_shape=outs, in_specs=[vmem] * len(ins), out_sp...]
where the time goes in v6:
time: 39.6 us; the launch traced here: 39.5 us
  starting transfers between devices  22.3 us (56%)
  Pallas kernels  10.1 us (26%)
  waiting for transfers between devices  5.47 us (14%)
  local copies, waits for them, and re-layouts  1.49 us (4%)
    ppermute x4, starting transfers between devices, exchange(): turn_in = lax.ppermute(turn_out, 'tile', sorted(turn))  10.2 us
    pallas_call x11, Pallas kernels, call(): pl.pallas_call(kernel, out_shape=outs, in_specs=[vmem] * len(ins), out_sp...  10.1 us
    ppermute x4, waiting for transfers between devices, exchange(): far_in = lax.ppermute(far_out, 'tile', far)  5.4 us
    ppermute x4, starting transfers between devices, exchange(): mirror_in = lax.ppermute(mirror_out, 'tile', mirror)  5.14 us
    ppermute x4, starting transfers between devices, exchange(): far_in = lax.ppermute(far_out, 'tile', far)  3.31 us
    ppermute x4, starting transfers between devices, exchange(): near_in = lax.ppermute(near_out, 'tile', near)  2.44 us
    unnamed x10, local copies, waits for them, and re-layouts  1.49 us
    ppermute x4, starting transfers between devices, exchange(): core_in = lax.ppermute(core_out, 'tile', core)  1.22 us
  transfers between devices with their start and end apart: 20, of which 4 were waited for; matrix products, arithmetic and copies ran while one was open for 0% of the time, Pallas kernels for 14%

profile of v6, /device:TPU:0, one launch (start us, length us, event | category | flops | bytes accessed | tf_op | source)
XLA Modules:
  0.0 39.5 jit_solution(11334795101864554332)
XLA Ops:
  0.1 0.6 %copy-done.2 = f32[3,128]{1,0:T(4,128)S(1)} copy-done((f32[3,128]{1,0:T(4,128)S(1)}, f32[3,128]{1,0:T(4,128)}, u32[]{:S(2)}) %copy-start.2) | copy-done | bytes 1560
  0.7 0.2 constants.1
  0.9 0.9 %copy-done = f32[1,6,6,128,128]{4,3,2,1,0:T(8,128)S(1)} copy-done((f32[1,6,6,128,128]{4,3,2,1,0:T(8,128)S(1)}, f32[1,6,6,128,128]{4,3,2,1,0:T(8,128)}, u32[]{:S(2)}) %copy-start) | copy-done | bytes 2359320
  1.8 0.6 %first_edges.1 = (f32[56,128]{1,0:T(8,128)S(1)}, f32[56,128]{1,0:T(8,128)S(1)}, f32[56,128]{1,0:T(8,128)S(1)}, f32[56,128]{1,0:T(8,128)S(1)}, f32[56,128]{1,0:T(...) custom-call(f32[6,6,128,128]{3,2,1,0:T(8,128)S(1)} %bitcast.4, f32[8,128]{1,0:T(8,128)S(1)} %get-tuple-element.58.refs_1_, ...), custom_call_target="tpu_custom_call" | custom-call | flops 1000000000 | bytes 2000000 | tf_op jit(solution)/shard_map/first_edges/pallas_call | solution.py:479
  2.4 5.5 %collective-permute-start = (f32[56,128]{1,0:T(8,128)S(1)}, f32[56,128]{1,0:T(8,128)S(1)}, u32[]{:S(2)}, u32[]{:S(2)}) collective-permute-start(f32[56,128]{1,0:T(8,128)S(1)} %get-tuple-element.60), channel_id=1, source_target_pairs={{0,15},{1,11},{2,7},{3,6},{4,14},{5,10},{6,3},{7,2},{8,13},{9,12},... | collective-permute-start | bytes 86024 | tf_op jit(solution)/shard_map/ppermute | solution.py:468
  7.9 1.1 %collective-permute-start.2 = (f32[56,128]{1,0:T(8,128)S(1)}, f32[56,128]{1,0:T(8,128)S(1)}, u32[]{:S(2)}, u32[]{:S(2)}) collective-permute-start(f32[56,128]{1,0:T(8,128)S(1)} %get-tuple-element.62), channel_id=1, source_target_pairs={{0,4},{1,5},{2,6},{3,7},{4,0},{5,1},{6,2},{7,3},{8,12},{9,13},{10,... | collective-permute-start | bytes 86024 | tf_op jit(solution)/shard_map/ppermute | solution.py:470
  9.0 0.4 collective-permute-start.4
  9.4 1.0 %inner.4 = (f32[6,6,128,128]{3,2,1,0:T(8,128)S(1)}, f32[128,128]{1,0:T(8,128)S(1)}, f32[128,128]{1,0:T(8,128)S(1)}) custom-call(f32[6,6,128,128]{3,2,1,0:T(8,128)S(1)} %bitcast.5, f32[8,128]{1,0:T(8,128)S(1)} %get-tuple-element.58.refs_1_, bf16[256,128]{1,0:T(8,128)(2,1)S(1)} %get-tuple-element.72.refs_2_, bf16[128,256]{1,0:T(8,128)(2,1)S(1)} %get-tuple-element.73.refs_3_, ...), custom_call_target="tpu_custom_call" | custom-call | flops 2000000000 | bytes 4000000 | tf_op jit(solution)/shard_map/inner/pallas_call | solution.py:479
  10.4 3.2 %collective-permute-done.1.refs_1_ = f32[56,128]{1,0:T(8,128)S(1)} collective-permute-done((f32[56,128]{1,0:T(8,128)S(1)}, f32[56,128]{1,0:T(8,128)S(1)}, u32[]{:S(2)}, u32[]{:S(2)}) %collective-permute-start.1) | collective-permute-done | bytes 28704 | tf_op jit(solution)/shard_map/ppermute | solution.py:469
  13.6 0.5 %edges.3 = (f32[128,128]{1,0:T(8,128)S(1)}, f32[128,128]{1,0:T(8,128)S(1)}, f32[56,128]{1,0:T(8,128)S(1)}, f32[56,128]{1,0:T(8,128)S(1)}, f32[56,128]{1,0:T(8,12...) custom-call(f32[56,128]{1,0:T(8,128)S(1)} %collective-permute-done.refs_0, ...), custom_call_target="tpu_custom_call" | custom-call | tf_op jit(solution)/shard_map/edges/pallas_call | solution.py:479
  14.1 1.2 %collective-permute-start.5 = (f32[56,128]{1,0:T(8,128)S(1)}, f32[56,128]{1,0:T(8,128)S(1)}, u32[]{:S(2)}, u32[]{:S(2)}) collective-permute-start(f32[56,128]{1,0:T(8,128)S(1)} %get-tuple-element.77), channel_id=1, source_target_pairs={{0,15},{1,11},{2,7},{3,6},{4,14},{5,10},{6,3},{7,2},{8,13},{9,12},... | collective-permute-start | bytes 86024 | tf_op jit(solution)/shard_map/ppermute | solution.py:468
  15.3 1.0 %collective-permute-start.6 = (f32[56,128]{1,0:T(8,128)S(1)}, f32[56,128]{1,0:T(8,128)S(1)}, u32[]{:S(2)}, u32[]{:S(2)}) collective-permute-start(f32[56,128]{1,0:T(8,128)S(1)} %get-tuple-element.78), channel_id=1, source_target_pairs={{0,12},{1,13},{2,14},{3,15},{4,8},{5,9},{6,10},{7,11},{8,4},{9,5},... | collective-permute-start | bytes 86024 | tf_op jit(solution)/shard_map/ppermute | solution.py:469
  16.3 0.5 %collective-permute-start.7 = (f32[56,128]{1,0:T(8,128)S(1)}, f32[56,128]{1,0:T(8,128)S(1)}, u32[]{:S(2)}, u32[]{:S(2)}) collective-permute-start(f32[56,128]{1,0:T(8,128)S(1)} %get-tuple-element.79), channel_id=1, source_target_pairs={{0,4},{1,5},{2,6},{3,7},{4,0},{5,1},{6,2},{7,3},{8,12},{9,13},{10,... | collective-permute-start | bytes 86024 | tf_op jit(solution)/shard_map/ppermute | solution.py:470
  16.8 2.1 %collective-permute-start.8 = (f32[56,128]{1,0:T(8,128)S(1)}, f32[56,128]{1,0:T(8,128)S(1)}, u32[]{:S(2)}, u32[]{:S(2)}) collective-permute-start(f32[56,128]{1,0:T(8,128)S(1)} %get-tuple-element.80), channel_id=1, source_target_pairs={{0,3},{1,2},{2,1},{3,0},{4,7},{5,6},{6,5},{7,4},{8,11},{9,10},{10,... | collective-permute-start | bytes 86024 | tf_op jit(solution)/shard_map/ppermute | solution.py:471
  18.9 1.6 %inner.5 = (f32[6,6,128,128]{3,2,1,0:T(8,128)S(1)}, f32[128,128]{1,0:T(8,128)S(1)}, f32[128,128]{1,0:T(8,128)S(1)}) custom-call(f32[6,6,128,128]{3,2,1,0:T(8,128)S(1)} %get-tuple-element.84.refs_0_, f32[8,128]{1,0:T(8,128)S(1)} %get-tuple-element.58.refs_1_, bf16[256,128]{1,0:T(8,128)(2,1)S(1)} %get-tuple-element.72.refs_2_, ...), custom_call_target="tpu_custom_call", output_to_operand_aliasing={{0}: (0, {})} | custom-call | flops 2000000000 | bytes 4000000 | tf_op jit(solution)/shard_map/inner/pallas_call | solution.py:479
  20.5 0.5 %collective-permute-done.6.refs_1_ = f32[56,128]{1,0:T(8,128)S(1)} collective-permute-done((f32[56,128]{1,0:T(8,128)S(1)}, f32[56,128]{1,0:T(8,128)S(1)}, u32[]{:S(2)}, u32[]{:S(2)}) %collective-permute-start.6) | collective-permute-done | bytes 28704 | tf_op jit(solution)/shard_map/ppermute | solution.py:469
  21.1 0.5 %edges.4 = (f32[128,128]{1,0:T(8,128)S(1)}, f32[128,128]{1,0:T(8,128)S(1)}, f32[56,128]{1,0:T(8,128)S(1)}, f32[56,128]{1,0:T(8,128)S(1)}, f32[56,128]{1,0:T(8,12...) custom-call(f32[56,128]{1,0:T(8,128)S(1)} %collective-permute-done.5.refs, ...), custom_call_target="tpu_custom_call" | custom-call | tf_op jit(solution)/shard_map/edges/pallas_call | solution.py:479
  21.6 2.1 %collective-permute-start.10 = (f32[56,128]{1,0:T(8,128)S(1)}, f32[56,128]{1,0:T(8,128)S(1)}, u32[]{:S(2)}, u32[]{:S(2)}) collective-permute-start(f32[56,128]{1,0:T(8,128)S(1)} %get-tuple-element.89), channel_id=1, source_target_pairs={{0,15},{1,11},{2,7},{3,6},{4,14},{5,10},{6,3},{7,2},{8,13},{9,12},... | collective-permute-start | bytes 86024 | tf_op jit(solution)/shard_map/ppermute | solution.py:468
  23.8 1.2 %collective-permute-start.11 = (f32[56,128]{1,0:T(8,128)S(1)}, f32[56,128]{1,0:T(8,128)S(1)}, u32[]{:S(2)}, u32[]{:S(2)}) collective-permute-start(f32[56,128]{1,0:T(8,128)S(1)} %get-tuple-element.90), channel_id=1, source_target_pairs={{0,12},{1,13},{2,14},{3,15},{4,8},{5,9},{6,10},{7,11},{8,4},{9,5},... | collective-permute-start | bytes 86024 | tf_op jit(solution)/shard_map/ppermute | solution.py:469
  25.0 1.4 %collective-permute-start.13 = (f32[56,128]{1,0:T(8,128)S(1)}, f32[56,128]{1,0:T(8,128)S(1)}, u32[]{:S(2)}, u32[]{:S(2)}) collective-permute-start(f32[56,128]{1,0:T(8,128)S(1)} %get-tuple-element.92), channel_id=1, source_target_pairs={{0,3},{1,2},{2,1},{3,0},{4,7},{5,6},{6,5},{7,4},{8,11},{9,10},{10,... | collective-permute-start | bytes 86024 | tf_op jit(solution)/shard_map/ppermute | solution.py:471
  26.4 0.5 %collective-permute-start.14 = (f32[56,128]{1,0:T(8,128)S(1)}, f32[56,128]{1,0:T(8,128)S(1)}, u32[]{:S(2)}, u32[]{:S(2)}) collective-permute-start(f32[56,128]{1,0:T(8,128)S(1)} %get-tuple-element.93), channel_id=1, source_target_pairs={{0,1},{1,0},{2,3},{3,2},{4,5},{5,4},{6,7},{7,6},{8,9},{9,8},{10,11... | collective-permute-start | bytes 86024 | tf_op jit(solution)/shard_map/ppermute | solution.py:472
  26.9 1.6 %inner.6 = (f32[6,6,128,128]{3,2,1,0:T(8,128)S(1)}, f32[128,128]{1,0:T(8,128)S(1)}, f32[128,128]{1,0:T(8,128)S(1)}) custom-call(f32[6,6,128,128]{3,2,1,0:T(8,128)S(1)} %get-tuple-element.96.refs_0_, f32[8,128]{1,0:T(8,128)S(1)} %get-tuple-element.58.refs_1_, bf16[256,128]{1,0:T(8,128)(2,1)S(1)} %get-tuple-element.72.refs_2_, ...), custom_call_target="tpu_custom_call", output_to_operand_aliasing={{0}: (0, {})} | custom-call | flops 2000000000 | bytes 4000000 | tf_op jit(solution)/shard_map/inner/pallas_call | solution.py:479
  28.5 0.9 %collective-permute-done.11.refs_1_ = f32[56,128]{1,0:T(8,128)S(1)} collective-permute-done((f32[56,128]{1,0:T(8,128)S(1)}, f32[56,128]{1,0:T(8,128)S(1)}, u32[]{:S(2)}, u32[]{:S(2)}) %collective-permute-start.11) | collective-permute-done | bytes 28704 | tf_op jit(solution)/shard_map/ppermute | solution.py:469
  29.4 0.5 %edges.5 = (f32[128,128]{1,0:T(8,128)S(1)}, f32[128,128]{1,0:T(8,128)S(1)}, f32[56,128]{1,0:T(8,128)S(1)}, f32[56,128]{1,0:T(8,128)S(1)}, f32[56,128]{1,0:T(8,12...) custom-call(f32[56,128]{1,0:T(8,128)S(1)} %collective-permute-done.10.ref, ...), custom_call_target="tpu_custom_call" | custom-call | tf_op jit(solution)/shard_map/edges/pallas_call | solution.py:479
  30.0 1.3 %collective-permute-start.15 = (f32[56,128]{1,0:T(8,128)S(1)}, f32[56,128]{1,0:T(8,128)S(1)}, u32[]{:S(2)}, u32[]{:S(2)}) collective-permute-start(f32[56,128]{1,0:T(8,128)S(1)} %get-tuple-element.101), channel_id=1, source_target_pairs={{0,15},{1,11},{2,7},{3,6},{4,14},{5,10},{6,3},{7,2},{8,13},{9,12},... | collective-permute-start | bytes 86024 | tf_op jit(solution)/shard_map/ppermute | solution.py:468
  31.3 1.1 %collective-permute-start.16 = (f32[56,128]{1,0:T(8,128)S(1)}, f32[56,128]{1,0:T(8,128)S(1)}, u32[]{:S(2)}, u32[]{:S(2)}) collective-permute-start(f32[56,128]{1,0:T(8,128)S(1)} %get-tuple-element.102), channel_id=1, source_target_pairs={{0,12},{1,13},{2,14},{3,15},{4,8},{5,9},{6,10},{7,11},{8,4},{9,5},... | collective-permute-start | bytes 86024 | tf_op jit(solution)/shard_map/ppermute | solution.py:469
  32.4 0.8 %collective-permute-start.17 = (f32[56,128]{1,0:T(8,128)S(1)}, f32[56,128]{1,0:T(8,128)S(1)}, u32[]{:S(2)}, u32[]{:S(2)}) collective-permute-start(f32[56,128]{1,0:T(8,128)S(1)} %get-tuple-element.103), channel_id=1, source_target_pairs={{0,4},{1,5},{2,6},{3,7},{4,0},{5,1},{6,2},{7,3},{8,12},{9,13},{10,... | collective-permute-start | bytes 86024 | tf_op jit(solution)/shard_map/ppermute | solution.py:470
  33.2 1.6 %collective-permute-start.18 = (f32[56,128]{1,0:T(8,128)S(1)}, f32[56,128]{1,0:T(8,128)S(1)}, u32[]{:S(2)}, u32[]{:S(2)}) collective-permute-start(f32[56,128]{1,0:T(8,128)S(1)} %get-tuple-element.104), channel_id=1, source_target_pairs={{0,3},{1,2},{2,1},{3,0},{4,7},{5,6},{6,5},{7,4},{8,11},{9,10},{10,... | collective-permute-start | bytes 86024 | tf_op jit(solution)/shard_map/ppermute | solution.py:471
  34.8 0.3 collective-permute-start.19
  35.1 1.3 %inner.7.refs_10_ = f32[6,6,128,128]{3,2,1,0:T(8,128)S(1)} custom-call(f32[6,6,128,128]{3,2,1,0:T(8,128)S(1)} %get-tuple-element.108.refs_0_, f32[8,128]{1,0:T(8,128)S(1)} %get-tuple-element.58.refs_1_, bf16[256,128]{1,0:T(8,128)(2,1)S(1)} %get-tuple-element.72.refs_2_, ...), custom_call_target="tpu_custom_call", output_to_operand_aliasing={{}: (0, {})} | custom-call | flops 2000000000 | bytes 4000000 | tf_op jit(solution)/shard_map/inner/pallas_call | solution.py:479
  36.5 0.8 %collective-permute-done.16.refs_1_ = f32[56,128]{1,0:T(8,128)S(1)} collective-permute-done((f32[56,128]{1,0:T(8,128)S(1)}, f32[56,128]{1,0:T(8,128)S(1)}, u32[]{:S(2)}, u32[]{:S(2)}) %collective-permute-start.16) | collective-permute-done | bytes 28704 | tf_op jit(solution)/shard_map/ppermute | solution.py:469
  37.3 2.2 %final.1 = f32[6,6,128,128]{3,2,1,0:T(8,128)} custom-call(f32[56,128]{1,0:T(8,128)S(1)} %collective-permute-done.15.refs_0_, f32[56,128]{1,0:T(8,128)S(1)} %collective-permute-done.16.refs_1_, f32[56,128]{1,0:T(8,128)S(1)} %collective-permute-done.17.refs_2_, f32[56,128]{1,0:T(8,128)S(1)} %collective-permute-done.18.refs_3_, ...), custom_call_target="tpu_custom_call" | custom-call | tf_op jit(solution)/shard_map/final/pallas_call | solution.py:479
  (29 shorter events, 0.2 us)
Async XLA Ops:
  0.0 0.7 %copy-start.2 = (f32[3,128]{1,0:T(4,128)S(1)}, f32[3,128]{1,0:T(4,128)}, u32[]{:S(2)}) copy-start(f32[3,128]{1,0:T(4,128)} %refs_3_.1) | copy-start | bytes 4612
  0.0 0.7 %copy-start.1 = (s32[3,128]{1,0:T(4,128)S(1)}, s32[3,128]{1,0:T(4,128)}, u32[]{:S(2)}) copy-start(s32[3,128]{1,0:T(4,128)} %refs_2_.1) | copy-start | bytes 4612
  0.0 0.7 %copy-start.4 = (f32[3]{0:T(128)S(1)}, f32[3]{0:T(128)}, u32[]{:S(2)}) copy-start(f32[3]{0:T(128)} %param.7) | copy-start | bytes 40
  0.0 0.7 %copy-start.3 = (f32[3]{0:T(128)S(1)}, f32[3]{0:T(128)}, u32[]{:S(2)}) copy-start(f32[3]{0:T(128)} %param.6) | copy-start | bytes 40
  0.1 1.7 %copy-start = (f32[1,6,6,128,128]{4,3,2,1,0:T(8,128)S(1)}, f32[1,6,6,128,128]{4,3,2,1,0:T(8,128)}, u32[]{:S(2)}) copy-start(f32[1,6,6,128,128]{4,3,2,1,0:T(8,128)} %param.5) | copy-start | bytes 7077892
  2.4 8.0 %collective-permute-start = (f32[56,128]{1,0:T(8,128)S(1)}, f32[56,128]{1,0:T(8,128)S(1)}, u32[]{:S(2)}, u32[]{:S(2)}) collective-permute-start(f32[56,128]{1,0:T(8,128)S(1)} %get-tuple-element.60), channel_id=1, source_target_pairs={{0,15},{1,11},{2,7},{3,6},{4,14},{5,10},{6,3},{7,2},{8,13},{9,12},... | collective-permute-start | bytes 86024 | tf_op jit(solution)/shard_map/ppermute | solution.py:468
  7.9 5.7 %collective-permute-start.1 = (f32[56,128]{1,0:T(8,128)S(1)}, f32[56,128]{1,0:T(8,128)S(1)}, u32[]{:S(2)}, u32[]{:S(2)}) collective-permute-start(f32[56,128]{1,0:T(8,128)S(1)} %get-tuple-element.61), channel_id=1, source_target_pairs={{0,12},{1,13},{2,14},{3,15},{4,8},{5,9},{6,10},{7,11},{8,4},{9,5},... | collective-permute-start | bytes 86024 | tf_op jit(solution)/shard_map/ppermute | solution.py:469
  7.9 5.7 %collective-permute-start.2 = (f32[56,128]{1,0:T(8,128)S(1)}, f32[56,128]{1,0:T(8,128)S(1)}, u32[]{:S(2)}, u32[]{:S(2)}) collective-permute-start(f32[56,128]{1,0:T(8,128)S(1)} %get-tuple-element.62), channel_id=1, source_target_pairs={{0,4},{1,5},{2,6},{3,7},{4,0},{5,1},{6,2},{7,3},{8,12},{9,13},{10,... | collective-permute-start | bytes 86024 | tf_op jit(solution)/shard_map/ppermute | solution.py:470
  9.0 4.5 %collective-permute-start.3 = (f32[56,128]{1,0:T(8,128)S(1)}, f32[56,128]{1,0:T(8,128)S(1)}, u32[]{:S(2)}, u32[]{:S(2)}) collective-permute-start(f32[56,128]{1,0:T(8,128)S(1)} %get-tuple-element.63), channel_id=1, source_target_pairs={{0,3},{1,2},{2,1},{3,0},{4,7},{5,6},{6,5},{7,4},{8,11},{9,10},{10,... | collective-permute-start | bytes 86024 | tf_op jit(solution)/shard_map/ppermute | solution.py:471
  9.0 4.5 %collective-permute-start.4 = (f32[56,128]{1,0:T(8,128)S(1)}, f32[56,128]{1,0:T(8,128)S(1)}, u32[]{:S(2)}, u32[]{:S(2)}) collective-permute-start(f32[56,128]{1,0:T(8,128)S(1)} %get-tuple-element.64), channel_id=1, source_target_pairs={{0,1},{1,0},{2,3},{3,2},{4,5},{5,4},{6,7},{7,6},{8,9},{9,8},{10,11... | collective-permute-start | bytes 86024 | tf_op jit(solution)/shard_map/ppermute | solution.py:472
  14.1 6.4 %collective-permute-start.5 = (f32[56,128]{1,0:T(8,128)S(1)}, f32[56,128]{1,0:T(8,128)S(1)}, u32[]{:S(2)}, u32[]{:S(2)}) collective-permute-start(f32[56,128]{1,0:T(8,128)S(1)} %get-tuple-element.77), channel_id=1, source_target_pairs={{0,15},{1,11},{2,7},{3,6},{4,14},{5,10},{6,3},{7,2},{8,13},{9,12},... | collective-permute-start | bytes 86024 | tf_op jit(solution)/shard_map/ppermute | solution.py:468
  15.3 5.8 %collective-permute-start.6 = (f32[56,128]{1,0:T(8,128)S(1)}, f32[56,128]{1,0:T(8,128)S(1)}, u32[]{:S(2)}, u32[]{:S(2)}) collective-permute-start(f32[56,128]{1,0:T(8,128)S(1)} %get-tuple-element.78), channel_id=1, source_target_pairs={{0,12},{1,13},{2,14},{3,15},{4,8},{5,9},{6,10},{7,11},{8,4},{9,5},... | collective-permute-start | bytes 86024 | tf_op jit(solution)/shard_map/ppermute | solution.py:469
  16.3 4.8 %collective-permute-start.7 = (f32[56,128]{1,0:T(8,128)S(1)}, f32[56,128]{1,0:T(8,128)S(1)}, u32[]{:S(2)}, u32[]{:S(2)}) collective-permute-start(f32[56,128]{1,0:T(8,128)S(1)} %get-tuple-element.79), channel_id=1, source_target_pairs={{0,4},{1,5},{2,6},{3,7},{4,0},{5,1},{6,2},{7,3},{8,12},{9,13},{10,... | collective-permute-start | bytes 86024 | tf_op jit(solution)/shard_map/ppermute | solution.py:470
  16.8 4.2 %collective-permute-start.8 = (f32[56,128]{1,0:T(8,128)S(1)}, f32[56,128]{1,0:T(8,128)S(1)}, u32[]{:S(2)}, u32[]{:S(2)}) collective-permute-start(f32[56,128]{1,0:T(8,128)S(1)} %get-tuple-element.80), channel_id=1, source_target_pairs={{0,3},{1,2},{2,1},{3,0},{4,7},{5,6},{6,5},{7,4},{8,11},{9,10},{10,... | collective-permute-start | bytes 86024 | tf_op jit(solution)/shard_map/ppermute | solution.py:471
  18.9 2.2 %collective-permute-start.9 = (f32[56,128]{1,0:T(8,128)S(1)}, f32[56,128]{1,0:T(8,128)S(1)}, u32[]{:S(2)}, u32[]{:S(2)}) collective-permute-start(f32[56,128]{1,0:T(8,128)S(1)} %get-tuple-element.81), channel_id=1, source_target_pairs={{0,1},{1,0},{2,3},{3,2},{4,5},{5,4},{6,7},{7,6},{8,9},{9,8},{10,11... | collective-permute-start | bytes 86024 | tf_op jit(solution)/shard_map/ppermute | solution.py:472
  21.6 6.9 %collective-permute-start.10 = (f32[56,128]{1,0:T(8,128)S(1)}, f32[56,128]{1,0:T(8,128)S(1)}, u32[]{:S(2)}, u32[]{:S(2)}) collective-permute-start(f32[56,128]{1,0:T(8,128)S(1)} %get-tuple-element.89), channel_id=1, source_target_pairs={{0,15},{1,11},{2,7},{3,6},{4,14},{5,10},{6,3},{7,2},{8,13},{9,12},... | collective-permute-start | bytes 86024 | tf_op jit(solution)/shard_map/ppermute | solution.py:468
  23.8 5.7 %collective-permute-start.11 = (f32[56,128]{1,0:T(8,128)S(1)}, f32[56,128]{1,0:T(8,128)S(1)}, u32[]{:S(2)}, u32[]{:S(2)}) collective-permute-start(f32[56,128]{1,0:T(8,128)S(1)} %get-tuple-element.90), channel_id=1, source_target_pairs={{0,12},{1,13},{2,14},{3,15},{4,8},{5,9},{6,10},{7,11},{8,4},{9,5},... | collective-permute-start | bytes 86024 | tf_op jit(solution)/shard_map/ppermute | solution.py:469
  25.0 4.4 %collective-permute-start.12 = (f32[56,128]{1,0:T(8,128)S(1)}, f32[56,128]{1,0:T(8,128)S(1)}, u32[]{:S(2)}, u32[]{:S(2)}) collective-permute-start(f32[56,128]{1,0:T(8,128)S(1)} %get-tuple-element.91), channel_id=1, source_target_pairs={{0,4},{1,5},{2,6},{3,7},{4,0},{5,1},{6,2},{7,3},{8,12},{9,13},{10,... | collective-permute-start | bytes 86024 | tf_op jit(solution)/shard_map/ppermute | solution.py:470
  25.0 4.4 %collective-permute-start.13 = (f32[56,128]{1,0:T(8,128)S(1)}, f32[56,128]{1,0:T(8,128)S(1)}, u32[]{:S(2)}, u32[]{:S(2)}) collective-permute-start(f32[56,128]{1,0:T(8,128)S(1)} %get-tuple-element.92), channel_id=1, source_target_pairs={{0,3},{1,2},{2,1},{3,0},{4,7},{5,6},{6,5},{7,4},{8,11},{9,10},{10,... | collective-permute-start | bytes 86024 | tf_op jit(solution)/shard_map/ppermute | solution.py:471
  26.4 3.0 %collective-permute-start.14 = (f32[56,128]{1,0:T(8,128)S(1)}, f32[56,128]{1,0:T(8,128)S(1)}, u32[]{:S(2)}, u32[]{:S(2)}) collective-permute-start(f32[56,128]{1,0:T(8,128)S(1)} %get-tuple-element.93), channel_id=1, source_target_pairs={{0,1},{1,0},{2,3},{3,2},{4,5},{5,4},{6,7},{7,6},{8,9},{9,8},{10,11... | collective-permute-start | bytes 86024 | tf_op jit(solution)/shard_map/ppermute | solution.py:472
  30.0 6.5 %collective-permute-start.15 = (f32[56,128]{1,0:T(8,128)S(1)}, f32[56,128]{1,0:T(8,128)S(1)}, u32[]{:S(2)}, u32[]{:S(2)}) collective-permute-start(f32[56,128]{1,0:T(8,128)S(1)} %get-tuple-element.101), channel_id=1, source_target_pairs={{0,15},{1,11},{2,7},{3,6},{4,14},{5,10},{6,3},{7,2},{8,13},{9,12},... | collective-permute-start | bytes 86024 | tf_op jit(solution)/shard_map/ppermute | solution.py:468
  31.3 6.0 %collective-permute-start.16 = (f32[56,128]{1,0:T(8,128)S(1)}, f32[56,128]{1,0:T(8,128)S(1)}, u32[]{:S(2)}, u32[]{:S(2)}) collective-permute-start(f32[56,128]{1,0:T(8,128)S(1)} %get-tuple-element.102), channel_id=1, source_target_pairs={{0,12},{1,13},{2,14},{3,15},{4,8},{5,9},{6,10},{7,11},{8,4},{9,5},... | collective-permute-start | bytes 86024 | tf_op jit(solution)/shard_map/ppermute | solution.py:469
  32.4 4.9 %collective-permute-start.17 = (f32[56,128]{1,0:T(8,128)S(1)}, f32[56,128]{1,0:T(8,128)S(1)}, u32[]{:S(2)}, u32[]{:S(2)}) collective-permute-start(f32[56,128]{1,0:T(8,128)S(1)} %get-tuple-element.103), channel_id=1, source_target_pairs={{0,4},{1,5},{2,6},{3,7},{4,0},{5,1},{6,2},{7,3},{8,12},{9,13},{10,... | collective-permute-start | bytes 86024 | tf_op jit(solution)/shard_map/ppermute | solution.py:470
  33.2 4.1 %collective-permute-start.18 = (f32[56,128]{1,0:T(8,128)S(1)}, f32[56,128]{1,0:T(8,128)S(1)}, u32[]{:S(2)}, u32[]{:S(2)}) collective-permute-start(f32[56,128]{1,0:T(8,128)S(1)} %get-tuple-element.104), channel_id=1, source_target_pairs={{0,3},{1,2},{2,1},{3,0},{4,7},{5,6},{6,5},{7,4},{8,11},{9,10},{10,... | collective-permute-start | bytes 86024 | tf_op jit(solution)/shard_map/ppermute | solution.py:471
  34.8 2.5 %collective-permute-start.19 = (f32[56,128]{1,0:T(8,128)S(1)}, f32[56,128]{1,0:T(8,128)S(1)}, u32[]{:S(2)}, u32[]{:S(2)}) collective-permute-start(f32[56,128]{1,0:T(8,128)S(1)} %get-tuple-element.105), channel_id=1, source_target_pairs={{0,1},{1,0},{2,3},{3,2},{4,5},{5,4},{6,7},{7,6},{8,9},{9,8},{10,11... | collective-permute-start | bytes 86024 | tf_op jit(solution)/shard_map/ppermute | solution.py:472

commit v7 on v6

--- a/solution.py
+++ b/solution.py
@@ -136,11 +136,13 @@
     def shift(place):
         return jnp.where(place == 0, 1, jnp.where(place == side - 1, FACES - 1, 0))
 
+    middle = (col > 0) & (col < side - 1)
+    up, down = jnp.where(even_row, NORTH, SOUTH), jnp.where(even_row, SOUTH, NORTH)
     plans = (
         (core_ref, jnp.where(even_col, EAST, WEST), 0),
         (mirror_ref, jnp.where(even_col, WEST, EAST), shift(col)),
-        (near_ref, jnp.where(even_row, NORTH, SOUTH), 0),
-        (far_ref, jnp.where(even_row, SOUTH, NORTH), shift(row)),
+        (near_ref, jnp.where(middle, down, up), jnp.where(middle, shift(row), 0)),
+        (far_ref, jnp.where(middle, up, down), jnp.where(middle, 0, shift(row))),
     )
     rest = jnp.zeros((ROWS - FACES * PER_FACE, BLK), jnp.float32)
     for out_ref, which, by in plans:
@@ -166,8 +168,7 @@
 
 
 TABLES = (
-    ("reach", (2 * BLK, BLK), jnp.bfloat16),
-    ("same", (BLK, BLK), jnp.float32),
+    ("corner", (BLK, BLK), jnp.int32),
     ("order", (BLK, 2 * BLK), jnp.bfloat16),
     ("spread", (2 * BLK, BLK), jnp.bfloat16),
     ("band_x", (2 * BLK, BLK), jnp.bfloat16),
@@ -181,22 +182,18 @@
 )
 
 
-def tables_kernel(reach, same, order, spread, band_x, band_y):
-    lower, plane, cell = plane_row((BLK, BLK), 0)
-    _, plane_src, _ = plane_row((BLK, BLK), 1)
+def tables_kernel(corner, order, spread, band_x, band_y):
     for ref, value, axis in (
         (order, lane_order(), 1),
         (band_x, band_matrix(), 0),
         (band_y, band_matrix(), 1),
     ):
         ref[...] = jnp.concatenate([value, value], axis=axis)
+    spread[...] = jnp.concatenate([lane_order()] * 2, axis=0)
+    _, plane, _ = plane_row((BLK, BLK), 0)
     to = iota((BLK, BLK), 1)
-    low = weight_of(jnp.where(to < 3, 3 + to - cell, 0))
-    high = weight_of(jnp.where(to >= BLK - 3, 3 + cell - (to - (BLK - 3)), 0))
-    value = jnp.where(plane < FACES * LEV, jnp.where(lower, low, high), 0.0).astype(jnp.bfloat16)
-    reach[...] = jnp.concatenate([value, value], axis=0)
-    spread[...] = jnp.concatenate([lane_order()] * 2, axis=0)
-    same[...] = jnp.where(plane == plane_src, 1.0, 0.0)
+    low, high = 3 * plane + to, HALF + 3 * plane + to - (BLK - 3)
+    corner[...] = jnp.where(to < 3, low, jnp.where(to >= BLK - 3, high, 0))
 
 
 def seam_rows(place, low_turned):
@@ -251,9 +248,11 @@
 
 
 def ghosts_of(side, received, own_a_ref, own_b_ref, taps_ref, weights_ref):
-    turned, far, near, mirror, core = [ref[...] for ref in received]
+    far, turned, near, mirror, core = [ref[...] for ref in received]
     col, row = position(side)
     even_col, even_row = lax.rem(col, 2) == 0, lax.rem(row, 2) == 0
+    middle = (col > 0) & (col < side - 1)
+    near, far = jnp.where(middle, far, near), jnp.where(middle, near, far)
     alone = ((row == 0) & (col == side - 1)) | ((col == 0) & (row == side - 1))
     pairs = (
         (
@@ -312,32 +311,29 @@
     return adds[:, :BLK], adds[:, BLK:]
 
 
-def corner_part(ghosts, same):
-    turned = ghosts.T
+def corner_part(adds, corner):
+    turned = adds.T
     cell = plane_row((HALF, BLK), 0)[2]
     halves = []
     for first in (0, BLK - 3):
         lines = [turned[first + at : first + at + 1, :] for at in range(3)]
         halves.append(jnp.where(cell == 0, lines[0], jnp.where(cell == 1, lines[1], lines[2])))
-    return jnp.concatenate(split2(jnp.concatenate(halves, axis=0) * same), axis=1)
+    lines = jnp.concatenate(halves, axis=0)
+    taken = jnp.take_along_axis(lines, corner, axis=1, mode="promise_in_bounds")
+    lane = iota((1, BLK), 1)
+    return jnp.where((lane < 3) | (lane >= BLK - 3), taken, 0.0)
 
 
 def edge_kernel(side, *refs):
     across, along = ghosts_of(side, refs[:5], *refs[5:9])
-    reach_ref, same_ref, gain_ref, old_columns_ref, old_rows_ref = refs[9:14]
-    add_x_ref, add_y_ref = refs[14:16]
-    outs = refs[16:23]
-    columns_ref, rows_ref, strips_ref = refs[23:]
+    corner_ref, gain_ref, old_columns_ref, old_rows_ref = refs[9:13]
+    add_x_ref, add_y_ref = refs[13:15]
+    outs = refs[15:22]
+    columns_ref, rows_ref, strips_ref = refs[22:]
     add_x, add_y = ghost_additions((across, along))
-    same = same_ref[...]
-    corners = jnp.dot(
-        jnp.concatenate([corner_part(along, same), corner_part(across, same)], axis=0),
-        reach_ref[...],
-        preferred_element_type=jnp.float32,
-    )
-    gain = gain_ref[...]
-    columns_ref[...] = old_columns_ref[...] + gain * (add_x + corners[:BLK])
-    rows_ref[...] = old_rows_ref[...] + gain * (add_y + corners[BLK:])
+    gain, corner = gain_ref[...], corner_ref[...]
+    columns_ref[...] = old_columns_ref[...] + gain * (add_x + corner_part(add_y, corner))
+    rows_ref[...] = old_rows_ref[...] + gain * (add_y + corner_part(add_x, corner))
     add_x_ref[...] = add_x
     add_y_ref[...] = add_y
     pack(columns_ref, rows_ref, side, outs, strips_ref)
@@ -450,9 +446,9 @@
 
     core = [(at(r, c), at(r, swap(c, False))) for r, c in cells]
     mirror = [(at(r, c), at(r, swap(c, True))) for r, c in cells]
-    near = [(at(r, c), at(swap(r, False), c)) for r, c in cells]
-    far = [(at(r, c), at(swap(r, True), c)) for r, c in cells]
     edge = side - 1
+    near = [(at(r, c), at(swap(r, 0 < c < edge), c)) for r, c in cells]
+    far = [(at(r, c), at(swap(r, not 0 < c < edge), c)) for r, c in cells]
     turn = set()
     for x in range(edge):
         turn |= {(at(0, x), at(edge - x, edge)), (at(edge - x, edge), at(0, x))}
@@ -470,7 +466,7 @@
     near_in = lax.ppermute(near_out, "tile", near)
     mirror_in = lax.ppermute(mirror_out, "tile", mirror)
     core_in = lax.ppermute(core_out, "tile", core)
-    return turn_in, far_in, near_in, mirror_in, core_in
+    return far_in, turn_in, near_in, mirror_in, core_in
 
 
 def call(kernel, name, outs, ins, scratch=(), out_hbm=False, cost=0, aliases=None):
@@ -548,7 +544,7 @@
             lambda *refs: edge_kernel(side, *refs),
             "edges",
             [tile] * 2 + [strip] * 7,
-            [*ghosts, made["reach"], made["same"], made["gain"], *edges],
+            [*ghosts, made["corner"], made["gain"], *edges],
             work,
         )
         adds, sent = updates[:2], updates[2:]

time: 39.6 us -> 39.3 us (level)
  waiting for transfers between devices: 5.47 us -> 3.02 us
  starting transfers between devices: 22.3 us -> 24.5 us
    ppermute x4, starting transfers between devices: 1.22 us -> 6.74 us  [exchange(): core_in = lax.ppermute(core_out, 'tile', core)]
    ppermute x4, waiting for transfers between devices: 5.4 us -> 0.05 us  [exchange(): far_in = lax.ppermute(far_out, 'tile', far)]
    ppermute x4, starting transfers between devices: 5.14 us -> 0.01 us  [exchange(): mirror_in = lax.ppermute(mirror_out, 'tile', mirror)]
    ppermute x4, starting transfers between devices: 3.31 us -> 7.65 us  [exchange(): far_in = lax.ppermute(far_out, 'tile', far)]
    ppermute x4, starting transfers between devices: 10.2 us -> 6.68 us  [exchange(): turn_in = lax.ppermute(turn_out, 'tile', sorted(turn))]
    ppermute x4, waiting for transfers between devices: 0.04 us -> 2.67 us  [exchange(): turn_in = lax.ppermute(turn_out, 'tile', sorted(turn))]
    ppermute x4, starting transfers between devices: 2.44 us -> 3.44 us  [exchange(): near_in = lax.ppermute(near_out, 'tile', near)]
  transfers between devices with their start and end apart: 20 -> 20, of which waited for: 4 -> 5; matrix products, arithmetic and copies ran while one was open for 0% -> 0% of each run, Pallas kernels for 14% -> 14%
where the time goes in v7:
time: 39.3 us; the launch traced here: 39.2 us
  starting transfers between devices  24.5 us (62%)
  Pallas kernels  10 us (25%)
  waiting for transfers between devices  3.02 us (8%)
  local copies, waits for them, and re-layouts  1.49 us (4%)
    pallas_call x11, Pallas kernels, call(): pl.pallas_call(kernel, out_shape=outs, in_specs=[vmem] * len(ins), out_sp...  10 us
    ppermute x4, starting transfers between devices, exchange(): far_in = lax.ppermute(far_out, 'tile', far)  7.65 us
    ppermute x4, starting transfers between devices, exchange(): core_in = lax.ppermute(core_out, 'tile', core)  6.74 us
    ppermute x4, starting transfers between devices, exchange(): turn_in = lax.ppermute(turn_out, 'tile', sorted(turn))  6.68 us
    ppermute x4, starting transfers between devices, exchange(): near_in = lax.ppermute(near_out, 'tile', near)  3.44 us
    ppermute x4, waiting for transfers between devices, exchange(): turn_in = lax.ppermute(turn_out, 'tile', sorted(turn))  2.67 us
    unnamed x10, local copies, waits for them, and re-layouts  1.49 us
  transfers between devices with their start and end apart: 20, of which 5 were waited for; matrix products, arithmetic and copies ran while one was open for 0% of the time, Pallas kernels for 14%

profile of v7, /device:TPU:0, one launch (start us, length us, event | category | flops | bytes accessed | tf_op | source)
XLA Modules:
  0.0 39.2 jit_solution(13429043080051462158)
XLA Ops:
  0.1 0.6 %copy-done.2 = f32[3,128]{1,0:T(4,128)S(1)} copy-done((f32[3,128]{1,0:T(4,128)S(1)}, f32[3,128]{1,0:T(4,128)}, u32[]{:S(2)}) %copy-start.2) | copy-done | bytes 1560
  0.7 0.2 constants.1
  0.9 0.9 %copy-done = f32[1,6,6,128,128]{4,3,2,1,0:T(8,128)S(1)} copy-done((f32[1,6,6,128,128]{4,3,2,1,0:T(8,128)S(1)}, f32[1,6,6,128,128]{4,3,2,1,0:T(8,128)}, u32[]{:S(2)}) %copy-start) | copy-done | bytes 2359320
  1.8 0.6 %first_edges.1 = (f32[56,128]{1,0:T(8,128)S(1)}, f32[56,128]{1,0:T(8,128)S(1)}, f32[56,128]{1,0:T(8,128)S(1)}, f32[56,128]{1,0:T(8,128)S(1)}, f32[56,128]{1,0:T(...) custom-call(f32[6,6,128,128]{3,2,1,0:T(8,128)S(1)} %bitcast.4, f32[8,128]{1,0:T(8,128)S(1)} %get-tuple-element.57.refs_1_, ...), custom_call_target="tpu_custom_call" | custom-call | flops 1000000000 | bytes 2000000 | tf_op jit(solution)/shard_map/first_edges/pallas_call | solution.py:475
  2.4 5.1 %collective-permute-start = (f32[56,128]{1,0:T(8,128)S(1)}, f32[56,128]{1,0:T(8,128)S(1)}, u32[]{:S(2)}, u32[]{:S(2)}) collective-permute-start(f32[56,128]{1,0:T(8,128)S(1)} %get-tuple-element.59), channel_id=1, source_target_pairs={{0,12},{1,5},{2,6},{3,15},{4,8},{5,1},{6,2},{7,11},{8,4},{9,13},{1... | collective-permute-start | bytes 86024 | tf_op jit(solution)/shard_map/ppermute | solution.py:465
  7.5 0.5 %collective-permute-start.1 = (f32[56,128]{1,0:T(8,128)S(1)}, f32[56,128]{1,0:T(8,128)S(1)}, u32[]{:S(2)}, u32[]{:S(2)}) collective-permute-start(f32[56,128]{1,0:T(8,128)S(1)} %get-tuple-element.60), channel_id=1, source_target_pairs={{0,15},{1,11},{2,7},{3,6},{4,14},{5,10},{6,3},{7,2},{8,13},{9,12},... | collective-permute-start | bytes 86024 | tf_op jit(solution)/shard_map/ppermute | solution.py:464
  8.0 1.5 %collective-permute-start.2 = (f32[56,128]{1,0:T(8,128)S(1)}, f32[56,128]{1,0:T(8,128)S(1)}, u32[]{:S(2)}, u32[]{:S(2)}) collective-permute-start(f32[56,128]{1,0:T(8,128)S(1)} %get-tuple-element.61), channel_id=1, source_target_pairs={{0,4},{1,13},{2,14},{3,7},{4,0},{5,9},{6,10},{7,3},{8,12},{9,5},{1... | collective-permute-start | bytes 86024 | tf_op jit(solution)/shard_map/ppermute | solution.py:466
  9.5 1.5 %collective-permute-start.4 = (f32[56,128]{1,0:T(8,128)S(1)}, f32[56,128]{1,0:T(8,128)S(1)}, u32[]{:S(2)}, u32[]{:S(2)}) collective-permute-start(f32[56,128]{1,0:T(8,128)S(1)} %get-tuple-element.63), channel_id=1, source_target_pairs={{0,1},{1,0},{2,3},{3,2},{4,5},{5,4},{6,7},{7,6},{8,9},{9,8},{10,11... | collective-permute-start | bytes 86024 | tf_op jit(solution)/shard_map/ppermute | solution.py:468
  11.0 1.0 %inner.4 = (f32[6,6,128,128]{3,2,1,0:T(8,128)S(1)}, f32[128,128]{1,0:T(8,128)S(1)}, f32[128,128]{1,0:T(8,128)S(1)}) custom-call(f32[6,6,128,128]{3,2,1,0:T(8,128)S(1)} %bitcast.5, f32[8,128]{1,0:T(8,128)S(1)} %get-tuple-element.57.refs_1_, bf16[256,128]{1,0:T(8,128)(2,1)S(1)} %get-tuple-element.70.refs_2_, bf16[128,256]{1,0:T(8,128)(2,1)S(1)} %get-tuple-element.71.refs_3_, ...), custom_call_target="tpu_custom_call" | custom-call | flops 2000000000 | bytes 4000000 | tf_op jit(solution)/shard_map/inner/pallas_call | solution.py:475
  11.9 1.5 %collective-permute-done.1.refs_1_ = f32[56,128]{1,0:T(8,128)S(1)} collective-permute-done((f32[56,128]{1,0:T(8,128)S(1)}, f32[56,128]{1,0:T(8,128)S(1)}, u32[]{:S(2)}, u32[]{:S(2)}) %collective-permute-start.1) | collective-permute-done | bytes 28704 | tf_op jit(solution)/shard_map/ppermute | solution.py:464
  13.5 0.5 %edges.3 = (f32[128,128]{1,0:T(8,128)S(1)}, f32[128,128]{1,0:T(8,128)S(1)}, f32[56,128]{1,0:T(8,128)S(1)}, f32[56,128]{1,0:T(8,128)S(1)}, f32[56,128]{1,0:T(8,12...) custom-call(f32[56,128]{1,0:T(8,128)S(1)} %collective-permute-done.refs_0, ...), custom_call_target="tpu_custom_call" | custom-call | tf_op jit(solution)/shard_map/edges/pallas_call | solution.py:475
  14.0 0.8 %collective-permute-start.5 = (f32[56,128]{1,0:T(8,128)S(1)}, f32[56,128]{1,0:T(8,128)S(1)}, u32[]{:S(2)}, u32[]{:S(2)}) collective-permute-start(f32[56,128]{1,0:T(8,128)S(1)} %get-tuple-element.75), channel_id=1, source_target_pairs={{0,12},{1,5},{2,6},{3,15},{4,8},{5,1},{6,2},{7,11},{8,4},{9,13},{1... | collective-permute-start | bytes 86024 | tf_op jit(solution)/shard_map/ppermute | solution.py:465
  14.8 1.8 %collective-permute-start.6 = (f32[56,128]{1,0:T(8,128)S(1)}, f32[56,128]{1,0:T(8,128)S(1)}, u32[]{:S(2)}, u32[]{:S(2)}) collective-permute-start(f32[56,128]{1,0:T(8,128)S(1)} %get-tuple-element.76), channel_id=1, source_target_pairs={{0,15},{1,11},{2,7},{3,6},{4,14},{5,10},{6,3},{7,2},{8,13},{9,12},... | collective-permute-start | bytes 86024 | tf_op jit(solution)/shard_map/ppermute | solution.py:464
  16.6 0.6 %collective-permute-start.7 = (f32[56,128]{1,0:T(8,128)S(1)}, f32[56,128]{1,0:T(8,128)S(1)}, u32[]{:S(2)}, u32[]{:S(2)}) collective-permute-start(f32[56,128]{1,0:T(8,128)S(1)} %get-tuple-element.77), channel_id=1, source_target_pairs={{0,4},{1,13},{2,14},{3,7},{4,0},{5,9},{6,10},{7,3},{8,12},{9,5},{1... | collective-permute-start | bytes 86024 | tf_op jit(solution)/shard_map/ppermute | solution.py:466
  17.2 2.5 %collective-permute-start.9 = (f32[56,128]{1,0:T(8,128)S(1)}, f32[56,128]{1,0:T(8,128)S(1)}, u32[]{:S(2)}, u32[]{:S(2)}) collective-permute-start(f32[56,128]{1,0:T(8,128)S(1)} %get-tuple-element.79), channel_id=1, source_target_pairs={{0,1},{1,0},{2,3},{3,2},{4,5},{5,4},{6,7},{7,6},{8,9},{9,8},{10,11... | collective-permute-start | bytes 86024 | tf_op jit(solution)/shard_map/ppermute | solution.py:468
  19.7 1.6 %inner.5 = (f32[6,6,128,128]{3,2,1,0:T(8,128)S(1)}, f32[128,128]{1,0:T(8,128)S(1)}, f32[128,128]{1,0:T(8,128)S(1)}) custom-call(f32[6,6,128,128]{3,2,1,0:T(8,128)S(1)} %get-tuple-element.82.refs_0_, f32[8,128]{1,0:T(8,128)S(1)} %get-tuple-element.57.refs_1_, bf16[256,128]{1,0:T(8,128)(2,1)S(1)} %get-tuple-element.70.refs_2_, ...), custom_call_target="tpu_custom_call", output_to_operand_aliasing={{0}: (0, {})} | custom-call | flops 2000000000 | bytes 4000000 | tf_op jit(solution)/shard_map/inner/pallas_call | solution.py:475
  21.4 0.5 %edges.4 = (f32[128,128]{1,0:T(8,128)S(1)}, f32[128,128]{1,0:T(8,128)S(1)}, f32[56,128]{1,0:T(8,128)S(1)}, f32[56,128]{1,0:T(8,128)S(1)}, f32[56,128]{1,0:T(8,12...) custom-call(f32[56,128]{1,0:T(8,128)S(1)} %collective-permute-done.5.refs, ...), custom_call_target="tpu_custom_call" | custom-call | tf_op jit(solution)/shard_map/edges/pallas_call | solution.py:475
  21.9 1.3 %collective-permute-start.10 = (f32[56,128]{1,0:T(8,128)S(1)}, f32[56,128]{1,0:T(8,128)S(1)}, u32[]{:S(2)}, u32[]{:S(2)}) collective-permute-start(f32[56,128]{1,0:T(8,128)S(1)} %get-tuple-element.87), channel_id=1, source_target_pairs={{0,12},{1,5},{2,6},{3,15},{4,8},{5,1},{6,2},{7,11},{8,4},{9,13},{1... | collective-permute-start | bytes 86024 | tf_op jit(solution)/shard_map/ppermute | solution.py:465
  23.2 1.8 %collective-permute-start.11 = (f32[56,128]{1,0:T(8,128)S(1)}, f32[56,128]{1,0:T(8,128)S(1)}, u32[]{:S(2)}, u32[]{:S(2)}) collective-permute-start(f32[56,128]{1,0:T(8,128)S(1)} %get-tuple-element.88), channel_id=1, source_target_pairs={{0,15},{1,11},{2,7},{3,6},{4,14},{5,10},{6,3},{7,2},{8,13},{9,12},... | collective-permute-start | bytes 86024 | tf_op jit(solution)/shard_map/ppermute | solution.py:464
  24.9 1.0 %collective-permute-start.12 = (f32[56,128]{1,0:T(8,128)S(1)}, f32[56,128]{1,0:T(8,128)S(1)}, u32[]{:S(2)}, u32[]{:S(2)}) collective-permute-start(f32[56,128]{1,0:T(8,128)S(1)} %get-tuple-element.89), channel_id=1, source_target_pairs={{0,4},{1,13},{2,14},{3,7},{4,0},{5,9},{6,10},{7,3},{8,12},{9,5},{1... | collective-permute-start | bytes 86024 | tf_op jit(solution)/shard_map/ppermute | solution.py:466
  25.9 1.0 %collective-permute-start.14 = (f32[56,128]{1,0:T(8,128)S(1)}, f32[56,128]{1,0:T(8,128)S(1)}, u32[]{:S(2)}, u32[]{:S(2)}) collective-permute-start(f32[56,128]{1,0:T(8,128)S(1)} %get-tuple-element.91), channel_id=1, source_target_pairs={{0,1},{1,0},{2,3},{3,2},{4,5},{5,4},{6,7},{7,6},{8,9},{9,8},{10,11... | collective-permute-start | bytes 86024 | tf_op jit(solution)/shard_map/ppermute | solution.py:468
  26.9 1.6 %inner.6 = (f32[6,6,128,128]{3,2,1,0:T(8,128)S(1)}, f32[128,128]{1,0:T(8,128)S(1)}, f32[128,128]{1,0:T(8,128)S(1)}) custom-call(f32[6,6,128,128]{3,2,1,0:T(8,128)S(1)} %get-tuple-element.94.refs_0_, f32[8,128]{1,0:T(8,128)S(1)} %get-tuple-element.57.refs_1_, bf16[256,128]{1,0:T(8,128)(2,1)S(1)} %get-tuple-element.70.refs_2_, ...), custom_call_target="tpu_custom_call", output_to_operand_aliasing={{0}: (0, {})} | custom-call | flops 2000000000 | bytes 4000000 | tf_op jit(solution)/shard_map/inner/pallas_call | solution.py:475
  28.5 0.9 %collective-permute-done.11.refs_1_ = f32[56,128]{1,0:T(8,128)S(1)} collective-permute-done((f32[56,128]{1,0:T(8,128)S(1)}, f32[56,128]{1,0:T(8,128)S(1)}, u32[]{:S(2)}, u32[]{:S(2)}) %collective-permute-start.11) | collective-permute-done | bytes 28704 | tf_op jit(solution)/shard_map/ppermute | solution.py:464
  29.5 0.5 %edges.5 = (f32[128,128]{1,0:T(8,128)S(1)}, f32[128,128]{1,0:T(8,128)S(1)}, f32[56,128]{1,0:T(8,128)S(1)}, f32[56,128]{1,0:T(8,128)S(1)}, f32[56,128]{1,0:T(8,12...) custom-call(f32[56,128]{1,0:T(8,128)S(1)} %collective-permute-done.10.ref, ...), custom_call_target="tpu_custom_call" | custom-call | tf_op jit(solution)/shard_map/edges/pallas_call | solution.py:475
  30.0 0.4 %collective-permute-start.15 = (f32[56,128]{1,0:T(8,128)S(1)}, f32[56,128]{1,0:T(8,128)S(1)}, u32[]{:S(2)}, u32[]{:S(2)}) collective-permute-start(f32[56,128]{1,0:T(8,128)S(1)} %get-tuple-element.99), channel_id=1, source_target_pairs={{0,12},{1,5},{2,6},{3,15},{4,8},{5,1},{6,2},{7,11},{8,4},{9,13},{1... | collective-permute-start | bytes 86024 | tf_op jit(solution)/shard_map/ppermute | solution.py:465
  30.5 2.7 %collective-permute-start.16 = (f32[56,128]{1,0:T(8,128)S(1)}, f32[56,128]{1,0:T(8,128)S(1)}, u32[]{:S(2)}, u32[]{:S(2)}) collective-permute-start(f32[56,128]{1,0:T(8,128)S(1)} %get-tuple-element.100), channel_id=1, source_target_pairs={{0,15},{1,11},{2,7},{3,6},{4,14},{5,10},{6,3},{7,2},{8,13},{9,12},... | collective-permute-start | bytes 86024 | tf_op jit(solution)/shard_map/ppermute | solution.py:464
  33.1 0.4 collective-permute-start.17
  33.5 1.8 %collective-permute-start.19 = (f32[56,128]{1,0:T(8,128)S(1)}, f32[56,128]{1,0:T(8,128)S(1)}, u32[]{:S(2)}, u32[]{:S(2)}) collective-permute-start(f32[56,128]{1,0:T(8,128)S(1)} %get-tuple-element.103), channel_id=1, source_target_pairs={{0,1},{1,0},{2,3},{3,2},{4,5},{5,4},{6,7},{7,6},{8,9},{9,8},{10,11... | collective-permute-start | bytes 86024 | tf_op jit(solution)/shard_map/ppermute | solution.py:468
  35.2 1.3 %inner.7.refs_10_ = f32[6,6,128,128]{3,2,1,0:T(8,128)S(1)} custom-call(f32[6,6,128,128]{3,2,1,0:T(8,128)S(1)} %get-tuple-element.106.refs_0_, f32[8,128]{1,0:T(8,128)S(1)} %get-tuple-element.57.refs_1_, bf16[256,128]{1,0:T(8,128)(2,1)S(1)} %get-tuple-element.70.refs_2_, ...), custom_call_target="tpu_custom_call", output_to_operand_aliasing={{}: (0, {})} | custom-call | flops 2000000000 | bytes 4000000 | tf_op jit(solution)/shard_map/inner/pallas_call | solution.py:475
  36.6 0.2 collective-permute-done.16.refs_1_
  36.8 0.2 collective-permute-done.17.refs_2_
  37.0 2.2 %final.1 = f32[6,6,128,128]{3,2,1,0:T(8,128)} custom-call(f32[56,128]{1,0:T(8,128)S(1)} %collective-permute-done.15.refs_0_, f32[56,128]{1,0:T(8,128)S(1)} %collective-permute-done.16.refs_1_, f32[56,128]{1,0:T(8,128)S(1)} %collective-permute-done.17.refs_2_, f32[56,128]{1,0:T(8,128)S(1)} %collective-permute-done.18.refs_3_, ...), custom_call_target="tpu_custom_call" | custom-call | tf_op jit(solution)/shard_map/final/pallas_call | solution.py:475
  (29 shorter events, 0.3 us)
Async XLA Ops:
  0.0 0.7 %copy-start.2 = (f32[3,128]{1,0:T(4,128)S(1)}, f32[3,128]{1,0:T(4,128)}, u32[]{:S(2)}) copy-start(f32[3,128]{1,0:T(4,128)} %refs_3_.1) | copy-start | bytes 4612
  0.0 0.7 %copy-start.1 = (s32[3,128]{1,0:T(4,128)S(1)}, s32[3,128]{1,0:T(4,128)}, u32[]{:S(2)}) copy-start(s32[3,128]{1,0:T(4,128)} %refs_2_.1) | copy-start | bytes 4612
  0.0 0.7 %copy-start.4 = (f32[3]{0:T(128)S(1)}, f32[3]{0:T(128)}, u32[]{:S(2)}) copy-start(f32[3]{0:T(128)} %param.7) | copy-start | bytes 40
  0.0 0.7 %copy-start.3 = (f32[3]{0:T(128)S(1)}, f32[3]{0:T(128)}, u32[]{:S(2)}) copy-start(f32[3]{0:T(128)} %param.6) | copy-start | bytes 40
  0.1 1.7 %copy-start = (f32[1,6,6,128,128]{4,3,2,1,0:T(8,128)S(1)}, f32[1,6,6,128,128]{4,3,2,1,0:T(8,128)}, u32[]{:S(2)}) copy-start(f32[1,6,6,128,128]{4,3,2,1,0:T(8,128)} %param.5) | copy-start | bytes 7077892
  2.4 9.6 %collective-permute-start = (f32[56,128]{1,0:T(8,128)S(1)}, f32[56,128]{1,0:T(8,128)S(1)}, u32[]{:S(2)}, u32[]{:S(2)}) collective-permute-start(f32[56,128]{1,0:T(8,128)S(1)} %get-tuple-element.59), channel_id=1, source_target_pairs={{0,12},{1,5},{2,6},{3,15},{4,8},{5,1},{6,2},{7,11},{8,4},{9,13},{1... | collective-permute-start | bytes 86024 | tf_op jit(solution)/shard_map/ppermute | solution.py:465
  7.5 6.0 %collective-permute-start.1 = (f32[56,128]{1,0:T(8,128)S(1)}, f32[56,128]{1,0:T(8,128)S(1)}, u32[]{:S(2)}, u32[]{:S(2)}) collective-permute-start(f32[56,128]{1,0:T(8,128)S(1)} %get-tuple-element.60), channel_id=1, source_target_pairs={{0,15},{1,11},{2,7},{3,6},{4,14},{5,10},{6,3},{7,2},{8,13},{9,12},... | collective-permute-start | bytes 86024 | tf_op jit(solution)/shard_map/ppermute | solution.py:464
  8.0 5.5 %collective-permute-start.2 = (f32[56,128]{1,0:T(8,128)S(1)}, f32[56,128]{1,0:T(8,128)S(1)}, u32[]{:S(2)}, u32[]{:S(2)}) collective-permute-start(f32[56,128]{1,0:T(8,128)S(1)} %get-tuple-element.61), channel_id=1, source_target_pairs={{0,4},{1,13},{2,14},{3,7},{4,0},{5,9},{6,10},{7,3},{8,12},{9,5},{1... | collective-permute-start | bytes 86024 | tf_op jit(solution)/shard_map/ppermute | solution.py:466
  9.5 4.0 %collective-permute-start.3 = (f32[56,128]{1,0:T(8,128)S(1)}, f32[56,128]{1,0:T(8,128)S(1)}, u32[]{:S(2)}, u32[]{:S(2)}) collective-permute-start(f32[56,128]{1,0:T(8,128)S(1)} %get-tuple-element.62), channel_id=1, source_target_pairs={{0,3},{1,2},{2,1},{3,0},{4,7},{5,6},{6,5},{7,4},{8,11},{9,10},{10,... | collective-permute-start | bytes 86024 | tf_op jit(solution)/shard_map/ppermute | solution.py:467
  9.5 4.0 %collective-permute-start.4 = (f32[56,128]{1,0:T(8,128)S(1)}, f32[56,128]{1,0:T(8,128)S(1)}, u32[]{:S(2)}, u32[]{:S(2)}) collective-permute-start(f32[56,128]{1,0:T(8,128)S(1)} %get-tuple-element.63), channel_id=1, source_target_pairs={{0,1},{1,0},{2,3},{3,2},{4,5},{5,4},{6,7},{7,6},{8,9},{9,8},{10,11... | collective-permute-start | bytes 86024 | tf_op jit(solution)/shard_map/ppermute | solution.py:468
  14.0 7.3 %collective-permute-start.5 = (f32[56,128]{1,0:T(8,128)S(1)}, f32[56,128]{1,0:T(8,128)S(1)}, u32[]{:S(2)}, u32[]{:S(2)}) collective-permute-start(f32[56,128]{1,0:T(8,128)S(1)} %get-tuple-element.75), channel_id=1, source_target_pairs={{0,12},{1,5},{2,6},{3,15},{4,8},{5,1},{6,2},{7,11},{8,4},{9,13},{1... | collective-permute-start | bytes 86024 | tf_op jit(solution)/shard_map/ppermute | solution.py:465
  14.8 6.5 %collective-permute-start.6 = (f32[56,128]{1,0:T(8,128)S(1)}, f32[56,128]{1,0:T(8,128)S(1)}, u32[]{:S(2)}, u32[]{:S(2)}) collective-permute-start(f32[56,128]{1,0:T(8,128)S(1)} %get-tuple-element.76), channel_id=1, source_target_pairs={{0,15},{1,11},{2,7},{3,6},{4,14},{5,10},{6,3},{7,2},{8,13},{9,12},... | collective-permute-start | bytes 86024 | tf_op jit(solution)/shard_map/ppermute | solution.py:464
  16.6 4.7 %collective-permute-start.7 = (f32[56,128]{1,0:T(8,128)S(1)}, f32[56,128]{1,0:T(8,128)S(1)}, u32[]{:S(2)}, u32[]{:S(2)}) collective-permute-start(f32[56,128]{1,0:T(8,128)S(1)} %get-tuple-element.77), channel_id=1, source_target_pairs={{0,4},{1,13},{2,14},{3,7},{4,0},{5,9},{6,10},{7,3},{8,12},{9,5},{1... | collective-permute-start | bytes 86024 | tf_op jit(solution)/shard_map/ppermute | solution.py:466
  17.2 4.2 %collective-permute-start.8 = (f32[56,128]{1,0:T(8,128)S(1)}, f32[56,128]{1,0:T(8,128)S(1)}, u32[]{:S(2)}, u32[]{:S(2)}) collective-permute-start(f32[56,128]{1,0:T(8,128)S(1)} %get-tuple-element.78), channel_id=1, source_target_pairs={{0,3},{1,2},{2,1},{3,0},{4,7},{5,6},{6,5},{7,4},{8,11},{9,10},{10,... | collective-permute-start | bytes 86024 | tf_op jit(solution)/shard_map/ppermute | solution.py:467
  17.2 4.2 %collective-permute-start.9 = (f32[56,128]{1,0:T(8,128)S(1)}, f32[56,128]{1,0:T(8,128)S(1)}, u32[]{:S(2)}, u32[]{:S(2)}) collective-permute-start(f32[56,128]{1,0:T(8,128)S(1)} %get-tuple-element.79), channel_id=1, source_target_pairs={{0,1},{1,0},{2,3},{3,2},{4,5},{5,4},{6,7},{7,6},{8,9},{9,8},{10,11... | collective-permute-start | bytes 86024 | tf_op jit(solution)/shard_map/ppermute | solution.py:468
  21.9 6.6 %collective-permute-start.10 = (f32[56,128]{1,0:T(8,128)S(1)}, f32[56,128]{1,0:T(8,128)S(1)}, u32[]{:S(2)}, u32[]{:S(2)}) collective-permute-start(f32[56,128]{1,0:T(8,128)S(1)} %get-tuple-element.87), channel_id=1, source_target_pairs={{0,12},{1,5},{2,6},{3,15},{4,8},{5,1},{6,2},{7,11},{8,4},{9,13},{1... | collective-permute-start | bytes 86024 | tf_op jit(solution)/shard_map/ppermute | solution.py:465
  23.2 6.2 %collective-permute-start.11 = (f32[56,128]{1,0:T(8,128)S(1)}, f32[56,128]{1,0:T(8,128)S(1)}, u32[]{:S(2)}, u32[]{:S(2)}) collective-permute-start(f32[56,128]{1,0:T(8,128)S(1)} %get-tuple-element.88), channel_id=1, source_target_pairs={{0,15},{1,11},{2,7},{3,6},{4,14},{5,10},{6,3},{7,2},{8,13},{9,12},... | collective-permute-start | bytes 86024 | tf_op jit(solution)/shard_map/ppermute | solution.py:464
  24.9 4.5 %collective-permute-start.12 = (f32[56,128]{1,0:T(8,128)S(1)}, f32[56,128]{1,0:T(8,128)S(1)}, u32[]{:S(2)}, u32[]{:S(2)}) collective-permute-start(f32[56,128]{1,0:T(8,128)S(1)} %get-tuple-element.89), channel_id=1, source_target_pairs={{0,4},{1,13},{2,14},{3,7},{4,0},{5,9},{6,10},{7,3},{8,12},{9,5},{1... | collective-permute-start | bytes 86024 | tf_op jit(solution)/shard_map/ppermute | solution.py:466
  25.9 3.6 %collective-permute-start.13 = (f32[56,128]{1,0:T(8,128)S(1)}, f32[56,128]{1,0:T(8,128)S(1)}, u32[]{:S(2)}, u32[]{:S(2)}) collective-permute-start(f32[56,128]{1,0:T(8,128)S(1)} %get-tuple-element.90), channel_id=1, source_target_pairs={{0,3},{1,2},{2,1},{3,0},{4,7},{5,6},{6,5},{7,4},{8,11},{9,10},{10,... | collective-permute-start | bytes 86024 | tf_op jit(solution)/shard_map/ppermute | solution.py:467
  25.9 3.6 %collective-permute-start.14 = (f32[56,128]{1,0:T(8,128)S(1)}, f32[56,128]{1,0:T(8,128)S(1)}, u32[]{:S(2)}, u32[]{:S(2)}) collective-permute-start(f32[56,128]{1,0:T(8,128)S(1)} %get-tuple-element.91), channel_id=1, source_target_pairs={{0,1},{1,0},{2,3},{3,2},{4,5},{5,4},{6,7},{7,6},{8,9},{9,8},{10,11... | collective-permute-start | bytes 86024 | tf_op jit(solution)/shard_map/ppermute | solution.py:468
  30.0 6.5 %collective-permute-start.15 = (f32[56,128]{1,0:T(8,128)S(1)}, f32[56,128]{1,0:T(8,128)S(1)}, u32[]{:S(2)}, u32[]{:S(2)}) collective-permute-start(f32[56,128]{1,0:T(8,128)S(1)} %get-tuple-element.99), channel_id=1, source_target_pairs={{0,12},{1,5},{2,6},{3,15},{4,8},{5,1},{6,2},{7,11},{8,4},{9,13},{1... | collective-permute-start | bytes 86024 | tf_op jit(solution)/shard_map/ppermute | solution.py:465
  30.5 6.4 %collective-permute-start.16 = (f32[56,128]{1,0:T(8,128)S(1)}, f32[56,128]{1,0:T(8,128)S(1)}, u32[]{:S(2)}, u32[]{:S(2)}) collective-permute-start(f32[56,128]{1,0:T(8,128)S(1)} %get-tuple-element.100), channel_id=1, source_target_pairs={{0,15},{1,11},{2,7},{3,6},{4,14},{5,10},{6,3},{7,2},{8,13},{9,12},... | collective-permute-start | bytes 86024 | tf_op jit(solution)/shard_map/ppermute | solution.py:464
  33.1 3.9 %collective-permute-start.17 = (f32[56,128]{1,0:T(8,128)S(1)}, f32[56,128]{1,0:T(8,128)S(1)}, u32[]{:S(2)}, u32[]{:S(2)}) collective-permute-start(f32[56,128]{1,0:T(8,128)S(1)} %get-tuple-element.101), channel_id=1, source_target_pairs={{0,4},{1,13},{2,14},{3,7},{4,0},{5,9},{6,10},{7,3},{8,12},{9,5},{1... | collective-permute-start | bytes 86024 | tf_op jit(solution)/shard_map/ppermute | solution.py:466
  33.5 3.5 %collective-permute-start.18 = (f32[56,128]{1,0:T(8,128)S(1)}, f32[56,128]{1,0:T(8,128)S(1)}, u32[]{:S(2)}, u32[]{:S(2)}) collective-permute-start(f32[56,128]{1,0:T(8,128)S(1)} %get-tuple-element.102), channel_id=1, source_target_pairs={{0,3},{1,2},{2,1},{3,0},{4,7},{5,6},{6,5},{7,4},{8,11},{9,10},{10,... | collective-permute-start | bytes 86024 | tf_op jit(solution)/shard_map/ppermute | solution.py:467
  33.5 3.5 %collective-permute-start.19 = (f32[56,128]{1,0:T(8,128)S(1)}, f32[56,128]{1,0:T(8,128)S(1)}, u32[]{:S(2)}, u32[]{:S(2)}) collective-permute-start(f32[56,128]{1,0:T(8,128)S(1)} %get-tuple-element.103), channel_id=1, source_target_pairs={{0,1},{1,0},{2,3},{3,2},{4,5},{5,4},{6,7},{7,6},{8,9},{9,8},{10,11... | collective-permute-start | bytes 86024 | tf_op jit(solution)/shard_map/ppermute | solution.py:468

commit v8 on v7

--- a/solution.py
+++ b/solution.py
@@ -122,15 +122,15 @@
     rows_ref[HALF + used :, :] = rest
 
 
-def pack(columns_ref, rows_ref, side, outs, strips_ref):
+def pack(columns, rows, side, outs, strips_ref):
     turn_ref, far_ref, near_ref, mirror_ref, core_ref, own_a_ref, own_b_ref = outs
     col, row = position(side)
     for face in range(FACES):
         at = PER_FACE * face
-        strips_ref[WEST, face, :PER_FACE, :] = columns_ref[at : at + PER_FACE, :]
-        strips_ref[EAST, face, :PER_FACE, :] = columns_ref[HALF + at : HALF + at + PER_FACE, :]
-        strips_ref[SOUTH, face, :PER_FACE, :] = rows_ref[at : at + PER_FACE, :]
-        strips_ref[NORTH, face, :PER_FACE, :] = rows_ref[HALF + at : HALF + at + PER_FACE, :]
+        strips_ref[WEST, face, :PER_FACE, :] = columns[at : at + PER_FACE, :]
+        strips_ref[EAST, face, :PER_FACE, :] = columns[HALF + at : HALF + at + PER_FACE, :]
+        strips_ref[SOUTH, face, :PER_FACE, :] = rows[at : at + PER_FACE, :]
+        strips_ref[NORTH, face, :PER_FACE, :] = rows[HALF + at : HALF + at + PER_FACE, :]
     even_col, even_row = lax.rem(col, 2) == 0, lax.rem(row, 2) == 0
 
     def shift(place):
@@ -139,12 +139,12 @@
     middle = (col > 0) & (col < side - 1)
     up, down = jnp.where(even_row, NORTH, SOUTH), jnp.where(even_row, SOUTH, NORTH)
     plans = (
-        (core_ref, jnp.where(even_col, EAST, WEST), 0),
         (mirror_ref, jnp.where(even_col, WEST, EAST), shift(col)),
         (near_ref, jnp.where(middle, down, up), jnp.where(middle, shift(row), 0)),
         (far_ref, jnp.where(middle, up, down), jnp.where(middle, 0, shift(row))),
     )
     rest = jnp.zeros((ROWS - FACES * PER_FACE, BLK), jnp.float32)
+    core_ref[...] = jnp.where(even_col, columns[HALF : HALF + ROWS, :], columns[:ROWS, :])
     for out_ref, which, by in plans:
         for face in range(FACES):
             at = PER_FACE * face
@@ -235,7 +235,7 @@
 
 def first_kernel(side, state_ref, coef_ref, order_ref, *rest):
     outs = rest[:7]
-    columns_ref, rows_ref, strips_ref = rest[7:]
+    rows_ref, strips_ref = rest[7:]
     clear_rest(rows_ref)
     columns = jnp.zeros((BLK // 8, 8, BLK), jnp.float32)
     for plane in range(FACES * LEV):
@@ -243,8 +243,8 @@
         a, b = coef_ref[level : level + 1, :], coef_ref[LEV + level : LEV + level + 1, :]
         q = a * state_ref[face, level] + b * state_ref[face, LEV + level]
         columns = take_edges(tiles_of(q), plane, columns, rows_ref)
-    columns_ref[...] = rows_from_columns(columns, order_ref[...])
-    pack(columns_ref, rows_ref, side, outs, strips_ref)
+    packed = rows_from_columns(columns, order_ref[...])
+    pack(packed, rows_ref[...], side, outs, strips_ref)
 
 
 def ghosts_of(side, received, own_a_ref, own_b_ref, taps_ref, weights_ref):
@@ -329,14 +329,14 @@
     corner_ref, gain_ref, old_columns_ref, old_rows_ref = refs[9:13]
     add_x_ref, add_y_ref = refs[13:15]
     outs = refs[15:22]
-    columns_ref, rows_ref, strips_ref = refs[22:]
+    strips_ref = refs[22]
     add_x, add_y = ghost_additions((across, along))
     gain, corner = gain_ref[...], corner_ref[...]
-    columns_ref[...] = old_columns_ref[...] + gain * (add_x + corner_part(add_y, corner))
-    rows_ref[...] = old_rows_ref[...] + gain * (add_y + corner_part(add_x, corner))
+    columns = old_columns_ref[...] + gain * (add_x + corner_part(add_y, corner))
+    rows = old_rows_ref[...] + gain * (add_y + corner_part(add_x, corner))
     add_x_ref[...] = add_x
     add_y_ref[...] = add_y
-    pack(columns_ref, rows_ref, side, outs, strips_ref)
+    pack(columns, rows, side, outs, strips_ref)
 
 
 def spread_lanes(add_x, spread_ref):
@@ -495,11 +495,7 @@
     tile = array(BLK, BLK)
     strip = array(ROWS, BLK)
     whole = array(*field.shape)
-    work = [
-        pltpu.VMEM((BLK, BLK), jnp.float32),
-        pltpu.VMEM((BLK, BLK), jnp.float32),
-        pltpu.VMEM((4, FACES, 16, BLK), jnp.float32),
-    ]
+    strips = pltpu.VMEM((4, FACES, 16, BLK), jnp.float32)
     values = call(
         tables_kernel,
         "tables",
@@ -521,7 +517,7 @@
         "first_edges",
         [strip] * 7,
         [field, made["coef"], made["order"]],
-        work,
+        [pltpu.VMEM((BLK, BLK), jnp.float32), strips],
         cost=1_000_000_000,
     )
     adds = []
@@ -545,7 +541,7 @@
             "edges",
             [tile] * 2 + [strip] * 7,
             [*ghosts, made["corner"], made["gain"], *edges],
-            work,
+            [strips],
         )
         adds, sent = updates[:2], updates[2:]
     (field,) = call(

time: 39.3 us -> 39.3 us (level)
  no operation moved by 1% of the time
where the time goes in v8:
time: 39.3 us; the launch traced here: 39.1 us
  starting transfers between devices  24.5 us (62%)
  Pallas kernels  9.94 us (25%)
  waiting for transfers between devices  3.02 us (8%)
  local copies, waits for them, and re-layouts  1.49 us (4%)
    pallas_call x11, Pallas kernels, call(): pl.pallas_call(kernel, out_shape=outs, in_specs=[vmem] * len(ins), out_sp...  9.94 us
    ppermute x4, starting transfers between devices, exchange(): far_in = lax.ppermute(far_out, 'tile', far)  7.66 us
    ppermute x4, starting transfers between devices, exchange(): core_in = lax.ppermute(core_out, 'tile', core)  6.73 us
    ppermute x4, starting transfers between devices, exchange(): turn_in = lax.ppermute(turn_out, 'tile', sorted(turn))  6.68 us
    ppermute x4, starting transfers between devices, exchange(): near_in = lax.ppermute(near_out, 'tile', near)  3.43 us
    ppermute x4, waiting for transfers between devices, exchange(): turn_in = lax.ppermute(turn_out, 'tile', sorted(turn))  2.67 us
    unnamed x10, local copies, waits for them, and re-layouts  1.49 us
  transfers between devices with their start and end apart: 20, of which 5 were waited for; matrix products, arithmetic and copies ran while one was open for 0% of the time, Pallas kernels for 14%

profile of v8, /device:TPU:0, one launch (start us, length us, event | category | flops | bytes accessed | tf_op | source)
XLA Modules:
  0.0 39.1 jit_solution(7627258839053296032)
XLA Ops:
  0.1 0.6 %copy-done.2 = f32[3,128]{1,0:T(4,128)S(1)} copy-done((f32[3,128]{1,0:T(4,128)S(1)}, f32[3,128]{1,0:T(4,128)}, u32[]{:S(2)}) %copy-start.2) | copy-done | bytes 1560
  0.7 0.2 constants.1
  0.9 0.9 %copy-done = f32[1,6,6,128,128]{4,3,2,1,0:T(8,128)S(1)} copy-done((f32[1,6,6,128,128]{4,3,2,1,0:T(8,128)S(1)}, f32[1,6,6,128,128]{4,3,2,1,0:T(8,128)}, u32[]{:S(2)}) %copy-start) | copy-done | bytes 2359320
  1.8 0.6 %first_edges.1 = (f32[56,128]{1,0:T(8,128)S(1)}, f32[56,128]{1,0:T(8,128)S(1)}, f32[56,128]{1,0:T(8,128)S(1)}, f32[56,128]{1,0:T(8,128)S(1)}, f32[56,128]{1,0:T(...) custom-call(f32[6,6,128,128]{3,2,1,0:T(8,128)S(1)} %bitcast.4, f32[8,128]{1,0:T(8,128)S(1)} %get-tuple-element.57.refs_1_, ...), custom_call_target="tpu_custom_call" | custom-call | flops 1000000000 | bytes 2000000 | tf_op jit(solution)/shard_map/first_edges/pallas_call | solution.py:475
  2.3 5.1 %collective-permute-start = (f32[56,128]{1,0:T(8,128)S(1)}, f32[56,128]{1,0:T(8,128)S(1)}, u32[]{:S(2)}, u32[]{:S(2)}) collective-permute-start(f32[56,128]{1,0:T(8,128)S(1)} %get-tuple-element.59), channel_id=1, source_target_pairs={{0,12},{1,5},{2,6},{3,15},{4,8},{5,1},{6,2},{7,11},{8,4},{9,13},{1... | collective-permute-start | bytes 86024 | tf_op jit(solution)/shard_map/ppermute | solution.py:465
  7.5 0.5 %collective-permute-start.1 = (f32[56,128]{1,0:T(8,128)S(1)}, f32[56,128]{1,0:T(8,128)S(1)}, u32[]{:S(2)}, u32[]{:S(2)}) collective-permute-start(f32[56,128]{1,0:T(8,128)S(1)} %get-tuple-element.60), channel_id=1, source_target_pairs={{0,15},{1,11},{2,7},{3,6},{4,14},{5,10},{6,3},{7,2},{8,13},{9,12},... | collective-permute-start | bytes 86024 | tf_op jit(solution)/shard_map/ppermute | solution.py:464
  7.9 1.5 %collective-permute-start.2 = (f32[56,128]{1,0:T(8,128)S(1)}, f32[56,128]{1,0:T(8,128)S(1)}, u32[]{:S(2)}, u32[]{:S(2)}) collective-permute-start(f32[56,128]{1,0:T(8,128)S(1)} %get-tuple-element.61), channel_id=1, source_target_pairs={{0,4},{1,13},{2,14},{3,7},{4,0},{5,9},{6,10},{7,3},{8,12},{9,5},{1... | collective-permute-start | bytes 86024 | tf_op jit(solution)/shard_map/ppermute | solution.py:466
  9.4 1.5 %collective-permute-start.4 = (f32[56,128]{1,0:T(8,128)S(1)}, f32[56,128]{1,0:T(8,128)S(1)}, u32[]{:S(2)}, u32[]{:S(2)}) collective-permute-start(f32[56,128]{1,0:T(8,128)S(1)} %get-tuple-element.63), channel_id=1, source_target_pairs={{0,1},{1,0},{2,3},{3,2},{4,5},{5,4},{6,7},{7,6},{8,9},{9,8},{10,11... | collective-permute-start | bytes 86024 | tf_op jit(solution)/shard_map/ppermute | solution.py:468
  11.0 1.0 %inner.4 = (f32[6,6,128,128]{3,2,1,0:T(8,128)S(1)}, f32[128,128]{1,0:T(8,128)S(1)}, f32[128,128]{1,0:T(8,128)S(1)}) custom-call(f32[6,6,128,128]{3,2,1,0:T(8,128)S(1)} %bitcast.5, f32[8,128]{1,0:T(8,128)S(1)} %get-tuple-element.57.refs_1_, bf16[256,128]{1,0:T(8,128)(2,1)S(1)} %get-tuple-element.70.refs_2_, bf16[128,256]{1,0:T(8,128)(2,1)S(1)} %get-tuple-element.71.refs_3_, ...), custom_call_target="tpu_custom_call" | custom-call | flops 2000000000 | bytes 4000000 | tf_op jit(solution)/shard_map/inner/pallas_call | solution.py:475
  11.9 1.5 %collective-permute-done.1.refs_1_ = f32[56,128]{1,0:T(8,128)S(1)} collective-permute-done((f32[56,128]{1,0:T(8,128)S(1)}, f32[56,128]{1,0:T(8,128)S(1)}, u32[]{:S(2)}, u32[]{:S(2)}) %collective-permute-start.1) | collective-permute-done | bytes 28704 | tf_op jit(solution)/shard_map/ppermute | solution.py:464
  13.5 0.5 %edges.3 = (f32[128,128]{1,0:T(8,128)S(1)}, f32[128,128]{1,0:T(8,128)S(1)}, f32[56,128]{1,0:T(8,128)S(1)}, f32[56,128]{1,0:T(8,128)S(1)}, f32[56,128]{1,0:T(8,12...) custom-call(f32[56,128]{1,0:T(8,128)S(1)} %collective-permute-done.refs_0, ...), custom_call_target="tpu_custom_call" | custom-call | tf_op jit(solution)/shard_map/edges/pallas_call | solution.py:475
  14.0 0.8 %collective-permute-start.5 = (f32[56,128]{1,0:T(8,128)S(1)}, f32[56,128]{1,0:T(8,128)S(1)}, u32[]{:S(2)}, u32[]{:S(2)}) collective-permute-start(f32[56,128]{1,0:T(8,128)S(1)} %get-tuple-element.75), channel_id=1, source_target_pairs={{0,12},{1,5},{2,6},{3,15},{4,8},{5,1},{6,2},{7,11},{8,4},{9,13},{1... | collective-permute-start | bytes 86024 | tf_op jit(solution)/shard_map/ppermute | solution.py:465
  14.8 1.8 %collective-permute-start.6 = (f32[56,128]{1,0:T(8,128)S(1)}, f32[56,128]{1,0:T(8,128)S(1)}, u32[]{:S(2)}, u32[]{:S(2)}) collective-permute-start(f32[56,128]{1,0:T(8,128)S(1)} %get-tuple-element.76), channel_id=1, source_target_pairs={{0,15},{1,11},{2,7},{3,6},{4,14},{5,10},{6,3},{7,2},{8,13},{9,12},... | collective-permute-start | bytes 86024 | tf_op jit(solution)/shard_map/ppermute | solution.py:464
  16.6 0.6 %collective-permute-start.7 = (f32[56,128]{1,0:T(8,128)S(1)}, f32[56,128]{1,0:T(8,128)S(1)}, u32[]{:S(2)}, u32[]{:S(2)}) collective-permute-start(f32[56,128]{1,0:T(8,128)S(1)} %get-tuple-element.77), channel_id=1, source_target_pairs={{0,4},{1,13},{2,14},{3,7},{4,0},{5,9},{6,10},{7,3},{8,12},{9,5},{1... | collective-permute-start | bytes 86024 | tf_op jit(solution)/shard_map/ppermute | solution.py:466
  17.2 2.5 %collective-permute-start.9 = (f32[56,128]{1,0:T(8,128)S(1)}, f32[56,128]{1,0:T(8,128)S(1)}, u32[]{:S(2)}, u32[]{:S(2)}) collective-permute-start(f32[56,128]{1,0:T(8,128)S(1)} %get-tuple-element.79), channel_id=1, source_target_pairs={{0,1},{1,0},{2,3},{3,2},{4,5},{5,4},{6,7},{7,6},{8,9},{9,8},{10,11... | collective-permute-start | bytes 86024 | tf_op jit(solution)/shard_map/ppermute | solution.py:468
  19.7 1.6 %inner.5 = (f32[6,6,128,128]{3,2,1,0:T(8,128)S(1)}, f32[128,128]{1,0:T(8,128)S(1)}, f32[128,128]{1,0:T(8,128)S(1)}) custom-call(f32[6,6,128,128]{3,2,1,0:T(8,128)S(1)} %get-tuple-element.82.refs_0_, f32[8,128]{1,0:T(8,128)S(1)} %get-tuple-element.57.refs_1_, bf16[256,128]{1,0:T(8,128)(2,1)S(1)} %get-tuple-element.70.refs_2_, ...), custom_call_target="tpu_custom_call", output_to_operand_aliasing={{0}: (0, {})} | custom-call | flops 2000000000 | bytes 4000000 | tf_op jit(solution)/shard_map/inner/pallas_call | solution.py:475
  21.3 0.5 %edges.4 = (f32[128,128]{1,0:T(8,128)S(1)}, f32[128,128]{1,0:T(8,128)S(1)}, f32[56,128]{1,0:T(8,128)S(1)}, f32[56,128]{1,0:T(8,128)S(1)}, f32[56,128]{1,0:T(8,12...) custom-call(f32[56,128]{1,0:T(8,128)S(1)} %collective-permute-done.5.refs, ...), custom_call_target="tpu_custom_call" | custom-call | tf_op jit(solution)/shard_map/edges/pallas_call | solution.py:475
  21.8 1.3 %collective-permute-start.10 = (f32[56,128]{1,0:T(8,128)S(1)}, f32[56,128]{1,0:T(8,128)S(1)}, u32[]{:S(2)}, u32[]{:S(2)}) collective-permute-start(f32[56,128]{1,0:T(8,128)S(1)} %get-tuple-element.87), channel_id=1, source_target_pairs={{0,12},{1,5},{2,6},{3,15},{4,8},{5,1},{6,2},{7,11},{8,4},{9,13},{1... | collective-permute-start | bytes 86024 | tf_op jit(solution)/shard_map/ppermute | solution.py:465
  23.1 1.8 %collective-permute-start.11 = (f32[56,128]{1,0:T(8,128)S(1)}, f32[56,128]{1,0:T(8,128)S(1)}, u32[]{:S(2)}, u32[]{:S(2)}) collective-permute-start(f32[56,128]{1,0:T(8,128)S(1)} %get-tuple-element.88), channel_id=1, source_target_pairs={{0,15},{1,11},{2,7},{3,6},{4,14},{5,10},{6,3},{7,2},{8,13},{9,12},... | collective-permute-start | bytes 86024 | tf_op jit(solution)/shard_map/ppermute | solution.py:464
  24.9 1.0 %collective-permute-start.12 = (f32[56,128]{1,0:T(8,128)S(1)}, f32[56,128]{1,0:T(8,128)S(1)}, u32[]{:S(2)}, u32[]{:S(2)}) collective-permute-start(f32[56,128]{1,0:T(8,128)S(1)} %get-tuple-element.89), channel_id=1, source_target_pairs={{0,4},{1,13},{2,14},{3,7},{4,0},{5,9},{6,10},{7,3},{8,12},{9,5},{1... | collective-permute-start | bytes 86024 | tf_op jit(solution)/shard_map/ppermute | solution.py:466
  25.9 1.0 %collective-permute-start.14 = (f32[56,128]{1,0:T(8,128)S(1)}, f32[56,128]{1,0:T(8,128)S(1)}, u32[]{:S(2)}, u32[]{:S(2)}) collective-permute-start(f32[56,128]{1,0:T(8,128)S(1)} %get-tuple-element.91), channel_id=1, source_target_pairs={{0,1},{1,0},{2,3},{3,2},{4,5},{5,4},{6,7},{7,6},{8,9},{9,8},{10,11... | collective-permute-start | bytes 86024 | tf_op jit(solution)/shard_map/ppermute | solution.py:468
  26.8 1.6 %inner.6 = (f32[6,6,128,128]{3,2,1,0:T(8,128)S(1)}, f32[128,128]{1,0:T(8,128)S(1)}, f32[128,128]{1,0:T(8,128)S(1)}) custom-call(f32[6,6,128,128]{3,2,1,0:T(8,128)S(1)} %get-tuple-element.94.refs_0_, f32[8,128]{1,0:T(8,128)S(1)} %get-tuple-element.57.refs_1_, bf16[256,128]{1,0:T(8,128)(2,1)S(1)} %get-tuple-element.70.refs_2_, ...), custom_call_target="tpu_custom_call", output_to_operand_aliasing={{0}: (0, {})} | custom-call | flops 2000000000 | bytes 4000000 | tf_op jit(solution)/shard_map/inner/pallas_call | solution.py:475
  28.4 0.9 %collective-permute-done.11.refs_1_ = f32[56,128]{1,0:T(8,128)S(1)} collective-permute-done((f32[56,128]{1,0:T(8,128)S(1)}, f32[56,128]{1,0:T(8,128)S(1)}, u32[]{:S(2)}, u32[]{:S(2)}) %collective-permute-start.11) | collective-permute-done | bytes 28704 | tf_op jit(solution)/shard_map/ppermute | solution.py:464
  29.5 0.5 %edges.5 = (f32[128,128]{1,0:T(8,128)S(1)}, f32[128,128]{1,0:T(8,128)S(1)}, f32[56,128]{1,0:T(8,128)S(1)}, f32[56,128]{1,0:T(8,128)S(1)}, f32[56,128]{1,0:T(8,12...) custom-call(f32[56,128]{1,0:T(8,128)S(1)} %collective-permute-done.10.ref, ...), custom_call_target="tpu_custom_call" | custom-call | tf_op jit(solution)/shard_map/edges/pallas_call | solution.py:475
  30.0 0.4 %collective-permute-start.15 = (f32[56,128]{1,0:T(8,128)S(1)}, f32[56,128]{1,0:T(8,128)S(1)}, u32[]{:S(2)}, u32[]{:S(2)}) collective-permute-start(f32[56,128]{1,0:T(8,128)S(1)} %get-tuple-element.99), channel_id=1, source_target_pairs={{0,12},{1,5},{2,6},{3,15},{4,8},{5,1},{6,2},{7,11},{8,4},{9,13},{1... | collective-permute-start | bytes 86024 | tf_op jit(solution)/shard_map/ppermute | solution.py:465
  30.4 2.6 %collective-permute-start.16 = (f32[56,128]{1,0:T(8,128)S(1)}, f32[56,128]{1,0:T(8,128)S(1)}, u32[]{:S(2)}, u32[]{:S(2)}) collective-permute-start(f32[56,128]{1,0:T(8,128)S(1)} %get-tuple-element.100), channel_id=1, source_target_pairs={{0,15},{1,11},{2,7},{3,6},{4,14},{5,10},{6,3},{7,2},{8,13},{9,12},... | collective-permute-start | bytes 86024 | tf_op jit(solution)/shard_map/ppermute | solution.py:464
  33.0 0.4 collective-permute-start.17
  33.4 1.8 %collective-permute-start.19 = (f32[56,128]{1,0:T(8,128)S(1)}, f32[56,128]{1,0:T(8,128)S(1)}, u32[]{:S(2)}, u32[]{:S(2)}) collective-permute-start(f32[56,128]{1,0:T(8,128)S(1)} %get-tuple-element.103), channel_id=1, source_target_pairs={{0,1},{1,0},{2,3},{3,2},{4,5},{5,4},{6,7},{7,6},{8,9},{9,8},{10,11... | collective-permute-start | bytes 86024 | tf_op jit(solution)/shard_map/ppermute | solution.py:468
  35.2 1.3 %inner.7.refs_10_ = f32[6,6,128,128]{3,2,1,0:T(8,128)S(1)} custom-call(f32[6,6,128,128]{3,2,1,0:T(8,128)S(1)} %get-tuple-element.106.refs_0_, f32[8,128]{1,0:T(8,128)S(1)} %get-tuple-element.57.refs_1_, bf16[256,128]{1,0:T(8,128)(2,1)S(1)} %get-tuple-element.70.refs_2_, ...), custom_call_target="tpu_custom_call", output_to_operand_aliasing={{}: (0, {})} | custom-call | flops 2000000000 | bytes 4000000 | tf_op jit(solution)/shard_map/inner/pallas_call | solution.py:475
  36.5 0.2 collective-permute-done.16.refs_1_
  36.7 0.2 collective-permute-done.17.refs_2_
  36.9 2.2 %final.1 = f32[6,6,128,128]{3,2,1,0:T(8,128)} custom-call(f32[56,128]{1,0:T(8,128)S(1)} %collective-permute-done.15.refs_0_, f32[56,128]{1,0:T(8,128)S(1)} %collective-permute-done.16.refs_1_, f32[56,128]{1,0:T(8,128)S(1)} %collective-permute-done.17.refs_2_, f32[56,128]{1,0:T(8,128)S(1)} %collective-permute-done.18.refs_3_, ...), custom_call_target="tpu_custom_call" | custom-call | tf_op jit(solution)/shard_map/final/pallas_call | solution.py:475
  (29 shorter events, 0.3 us)
Async XLA Ops:
  0.0 0.7 %copy-start.2 = (f32[3,128]{1,0:T(4,128)S(1)}, f32[3,128]{1,0:T(4,128)}, u32[]{:S(2)}) copy-start(f32[3,128]{1,0:T(4,128)} %refs_3_.1) | copy-start | bytes 4612
  0.0 0.7 %copy-start.1 = (s32[3,128]{1,0:T(4,128)S(1)}, s32[3,128]{1,0:T(4,128)}, u32[]{:S(2)}) copy-start(s32[3,128]{1,0:T(4,128)} %refs_2_.1) | copy-start | bytes 4612
  0.0 0.7 %copy-start.4 = (f32[3]{0:T(128)S(1)}, f32[3]{0:T(128)}, u32[]{:S(2)}) copy-start(f32[3]{0:T(128)} %param.7) | copy-start | bytes 40
  0.0 0.7 %copy-start.3 = (f32[3]{0:T(128)S(1)}, f32[3]{0:T(128)}, u32[]{:S(2)}) copy-start(f32[3]{0:T(128)} %param.6) | copy-start | bytes 40
  0.1 1.7 %copy-start = (f32[1,6,6,128,128]{4,3,2,1,0:T(8,128)S(1)}, f32[1,6,6,128,128]{4,3,2,1,0:T(8,128)}, u32[]{:S(2)}) copy-start(f32[1,6,6,128,128]{4,3,2,1,0:T(8,128)} %param.5) | copy-start | bytes 7077892
  2.3 9.6 %collective-permute-start = (f32[56,128]{1,0:T(8,128)S(1)}, f32[56,128]{1,0:T(8,128)S(1)}, u32[]{:S(2)}, u32[]{:S(2)}) collective-permute-start(f32[56,128]{1,0:T(8,128)S(1)} %get-tuple-element.59), channel_id=1, source_target_pairs={{0,12},{1,5},{2,6},{3,15},{4,8},{5,1},{6,2},{7,11},{8,4},{9,13},{1... | collective-permute-start | bytes 86024 | tf_op jit(solution)/shard_map/ppermute | solution.py:465
  7.5 6.0 %collective-permute-start.1 = (f32[56,128]{1,0:T(8,128)S(1)}, f32[56,128]{1,0:T(8,128)S(1)}, u32[]{:S(2)}, u32[]{:S(2)}) collective-permute-start(f32[56,128]{1,0:T(8,128)S(1)} %get-tuple-element.60), channel_id=1, source_target_pairs={{0,15},{1,11},{2,7},{3,6},{4,14},{5,10},{6,3},{7,2},{8,13},{9,12},... | collective-permute-start | bytes 86024 | tf_op jit(solution)/shard_map/ppermute | solution.py:464
  7.9 5.5 %collective-permute-start.2 = (f32[56,128]{1,0:T(8,128)S(1)}, f32[56,128]{1,0:T(8,128)S(1)}, u32[]{:S(2)}, u32[]{:S(2)}) collective-permute-start(f32[56,128]{1,0:T(8,128)S(1)} %get-tuple-element.61), channel_id=1, source_target_pairs={{0,4},{1,13},{2,14},{3,7},{4,0},{5,9},{6,10},{7,3},{8,12},{9,5},{1... | collective-permute-start | bytes 86024 | tf_op jit(solution)/shard_map/ppermute | solution.py:466
  9.4 4.0 %collective-permute-start.3 = (f32[56,128]{1,0:T(8,128)S(1)}, f32[56,128]{1,0:T(8,128)S(1)}, u32[]{:S(2)}, u32[]{:S(2)}) collective-permute-start(f32[56,128]{1,0:T(8,128)S(1)} %get-tuple-element.62), channel_id=1, source_target_pairs={{0,3},{1,2},{2,1},{3,0},{4,7},{5,6},{6,5},{7,4},{8,11},{9,10},{10,... | collective-permute-start | bytes 86024 | tf_op jit(solution)/shard_map/ppermute | solution.py:467
  9.4 4.0 %collective-permute-start.4 = (f32[56,128]{1,0:T(8,128)S(1)}, f32[56,128]{1,0:T(8,128)S(1)}, u32[]{:S(2)}, u32[]{:S(2)}) collective-permute-start(f32[56,128]{1,0:T(8,128)S(1)} %get-tuple-element.63), channel_id=1, source_target_pairs={{0,1},{1,0},{2,3},{3,2},{4,5},{5,4},{6,7},{7,6},{8,9},{9,8},{10,11... | collective-permute-start | bytes 86024 | tf_op jit(solution)/shard_map/ppermute | solution.py:468
  14.0 7.3 %collective-permute-start.5 = (f32[56,128]{1,0:T(8,128)S(1)}, f32[56,128]{1,0:T(8,128)S(1)}, u32[]{:S(2)}, u32[]{:S(2)}) collective-permute-start(f32[56,128]{1,0:T(8,128)S(1)} %get-tuple-element.75), channel_id=1, source_target_pairs={{0,12},{1,5},{2,6},{3,15},{4,8},{5,1},{6,2},{7,11},{8,4},{9,13},{1... | collective-permute-start | bytes 86024 | tf_op jit(solution)/shard_map/ppermute | solution.py:465
  14.8 6.5 %collective-permute-start.6 = (f32[56,128]{1,0:T(8,128)S(1)}, f32[56,128]{1,0:T(8,128)S(1)}, u32[]{:S(2)}, u32[]{:S(2)}) collective-permute-start(f32[56,128]{1,0:T(8,128)S(1)} %get-tuple-element.76), channel_id=1, source_target_pairs={{0,15},{1,11},{2,7},{3,6},{4,14},{5,10},{6,3},{7,2},{8,13},{9,12},... | collective-permute-start | bytes 86024 | tf_op jit(solution)/shard_map/ppermute | solution.py:464
  16.6 4.7 %collective-permute-start.7 = (f32[56,128]{1,0:T(8,128)S(1)}, f32[56,128]{1,0:T(8,128)S(1)}, u32[]{:S(2)}, u32[]{:S(2)}) collective-permute-start(f32[56,128]{1,0:T(8,128)S(1)} %get-tuple-element.77), channel_id=1, source_target_pairs={{0,4},{1,13},{2,14},{3,7},{4,0},{5,9},{6,10},{7,3},{8,12},{9,5},{1... | collective-permute-start | bytes 86024 | tf_op jit(solution)/shard_map/ppermute | solution.py:466
  17.2 4.2 %collective-permute-start.8 = (f32[56,128]{1,0:T(8,128)S(1)}, f32[56,128]{1,0:T(8,128)S(1)}, u32[]{:S(2)}, u32[]{:S(2)}) collective-permute-start(f32[56,128]{1,0:T(8,128)S(1)} %get-tuple-element.78), channel_id=1, source_target_pairs={{0,3},{1,2},{2,1},{3,0},{4,7},{5,6},{6,5},{7,4},{8,11},{9,10},{10,... | collective-permute-start | bytes 86024 | tf_op jit(solution)/shard_map/ppermute | solution.py:467
  17.2 4.2 %collective-permute-start.9 = (f32[56,128]{1,0:T(8,128)S(1)}, f32[56,128]{1,0:T(8,128)S(1)}, u32[]{:S(2)}, u32[]{:S(2)}) collective-permute-start(f32[56,128]{1,0:T(8,128)S(1)} %get-tuple-element.79), channel_id=1, source_target_pairs={{0,1},{1,0},{2,3},{3,2},{4,5},{5,4},{6,7},{7,6},{8,9},{9,8},{10,11... | collective-permute-start | bytes 86024 | tf_op jit(solution)/shard_map/ppermute | solution.py:468
  21.8 6.6 %collective-permute-start.10 = (f32[56,128]{1,0:T(8,128)S(1)}, f32[56,128]{1,0:T(8,128)S(1)}, u32[]{:S(2)}, u32[]{:S(2)}) collective-permute-start(f32[56,128]{1,0:T(8,128)S(1)} %get-tuple-element.87), channel_id=1, source_target_pairs={{0,12},{1,5},{2,6},{3,15},{4,8},{5,1},{6,2},{7,11},{8,4},{9,13},{1... | collective-permute-start | bytes 86024 | tf_op jit(solution)/shard_map/ppermute | solution.py:465
  23.1 6.2 %collective-permute-start.11 = (f32[56,128]{1,0:T(8,128)S(1)}, f32[56,128]{1,0:T(8,128)S(1)}, u32[]{:S(2)}, u32[]{:S(2)}) collective-permute-start(f32[56,128]{1,0:T(8,128)S(1)} %get-tuple-element.88), channel_id=1, source_target_pairs={{0,15},{1,11},{2,7},{3,6},{4,14},{5,10},{6,3},{7,2},{8,13},{9,12},... | collective-permute-start | bytes 86024 | tf_op jit(solution)/shard_map/ppermute | solution.py:464
  24.9 4.5 %collective-permute-start.12 = (f32[56,128]{1,0:T(8,128)S(1)}, f32[56,128]{1,0:T(8,128)S(1)}, u32[]{:S(2)}, u32[]{:S(2)}) collective-permute-start(f32[56,128]{1,0:T(8,128)S(1)} %get-tuple-element.89), channel_id=1, source_target_pairs={{0,4},{1,13},{2,14},{3,7},{4,0},{5,9},{6,10},{7,3},{8,12},{9,5},{1... | collective-permute-start | bytes 86024 | tf_op jit(solution)/shard_map/ppermute | solution.py:466
  25.9 3.6 %collective-permute-start.13 = (f32[56,128]{1,0:T(8,128)S(1)}, f32[56,128]{1,0:T(8,128)S(1)}, u32[]{:S(2)}, u32[]{:S(2)}) collective-permute-start(f32[56,128]{1,0:T(8,128)S(1)} %get-tuple-element.90), channel_id=1, source_target_pairs={{0,3},{1,2},{2,1},{3,0},{4,7},{5,6},{6,5},{7,4},{8,11},{9,10},{10,... | collective-permute-start | bytes 86024 | tf_op jit(solution)/shard_map/ppermute | solution.py:467
  25.9 3.6 %collective-permute-start.14 = (f32[56,128]{1,0:T(8,128)S(1)}, f32[56,128]{1,0:T(8,128)S(1)}, u32[]{:S(2)}, u32[]{:S(2)}) collective-permute-start(f32[56,128]{1,0:T(8,128)S(1)} %get-tuple-element.91), channel_id=1, source_target_pairs={{0,1},{1,0},{2,3},{3,2},{4,5},{5,4},{6,7},{7,6},{8,9},{9,8},{10,11... | collective-permute-start | bytes 86024 | tf_op jit(solution)/shard_map/ppermute | solution.py:468
  30.0 6.5 %collective-permute-start.15 = (f32[56,128]{1,0:T(8,128)S(1)}, f32[56,128]{1,0:T(8,128)S(1)}, u32[]{:S(2)}, u32[]{:S(2)}) collective-permute-start(f32[56,128]{1,0:T(8,128)S(1)} %get-tuple-element.99), channel_id=1, source_target_pairs={{0,12},{1,5},{2,6},{3,15},{4,8},{5,1},{6,2},{7,11},{8,4},{9,13},{1... | collective-permute-start | bytes 86024 | tf_op jit(solution)/shard_map/ppermute | solution.py:465
  30.4 6.3 %collective-permute-start.16 = (f32[56,128]{1,0:T(8,128)S(1)}, f32[56,128]{1,0:T(8,128)S(1)}, u32[]{:S(2)}, u32[]{:S(2)}) collective-permute-start(f32[56,128]{1,0:T(8,128)S(1)} %get-tuple-element.100), channel_id=1, source_target_pairs={{0,15},{1,11},{2,7},{3,6},{4,14},{5,10},{6,3},{7,2},{8,13},{9,12},... | collective-permute-start | bytes 86024 | tf_op jit(solution)/shard_map/ppermute | solution.py:464
  33.0 3.9 %collective-permute-start.17 = (f32[56,128]{1,0:T(8,128)S(1)}, f32[56,128]{1,0:T(8,128)S(1)}, u32[]{:S(2)}, u32[]{:S(2)}) collective-permute-start(f32[56,128]{1,0:T(8,128)S(1)} %get-tuple-element.101), channel_id=1, source_target_pairs={{0,4},{1,13},{2,14},{3,7},{4,0},{5,9},{6,10},{7,3},{8,12},{9,5},{1... | collective-permute-start | bytes 86024 | tf_op jit(solution)/shard_map/ppermute | solution.py:466
  33.4 3.5 %collective-permute-start.18 = (f32[56,128]{1,0:T(8,128)S(1)}, f32[56,128]{1,0:T(8,128)S(1)}, u32[]{:S(2)}, u32[]{:S(2)}) collective-permute-start(f32[56,128]{1,0:T(8,128)S(1)} %get-tuple-element.102), channel_id=1, source_target_pairs={{0,3},{1,2},{2,1},{3,0},{4,7},{5,6},{6,5},{7,4},{8,11},{9,10},{10,... | collective-permute-start | bytes 86024 | tf_op jit(solution)/shard_map/ppermute | solution.py:467
  33.4 3.5 %collective-permute-start.19 = (f32[56,128]{1,0:T(8,128)S(1)}, f32[56,128]{1,0:T(8,128)S(1)}, u32[]{:S(2)}, u32[]{:S(2)}) collective-permute-start(f32[56,128]{1,0:T(8,128)S(1)} %get-tuple-element.103), channel_id=1, source_target_pairs={{0,1},{1,0},{2,3},{3,2},{4,5},{5,4},{6,7},{7,6},{8,9},{9,8},{10,11... | collective-permute-start | bytes 86024 | tf_op jit(solution)/shard_map/ppermute | solution.py:468

commit v9 on v8

--- a/solution.py
+++ b/solution.py
@@ -162,9 +162,16 @@
         own_b_ref[at : at + PER_FACE, :] = strips_ref[b[0], b[1] % FACES, :PER_FACE, :]
     own_a_ref[FACES * PER_FACE :, :] = rest
     own_b_ref[FACES * PER_FACE :, :] = rest
-    odd, _ = row_codes((ROWS, BLK))
-    use_a = jnp.where(odd, (row == 0).astype(jnp.int32), (row == side - 1).astype(jnp.int32))
-    turn_ref[...] = jnp.where(use_a == 1, own_a_ref[...], own_b_ref[...])
+    for face in range(FACES):
+        at = PER_FACE * face
+        if face % 2:
+            use_a, a, b = row == 0, (SOUTH, face + 2), (EAST, face - 2)
+        else:
+            use_a, a, b = row == side - 1, (NORTH, face - 2), (WEST, face + 2)
+        which = jnp.where(use_a, a[0], b[0])
+        source = jnp.where(use_a, a[1] % FACES, b[1] % FACES)
+        turn_ref[at : at + PER_FACE, :] = strips_ref[which, source, :PER_FACE, :]
+    turn_ref[FACES * PER_FACE :, :] = rest
 
 
 TABLES = (

time: 39.3 us -> 39.3 us (level)
  no operation moved by 1% of the time
where the time goes in v9:
time: 39.3 us; the launch traced here: 39.1 us
  starting transfers between devices  24.5 us (62%)
  Pallas kernels  9.96 us (25%)
  waiting for transfers between devices  3.01 us (8%)
  local copies, waits for them, and re-layouts  1.49 us (4%)
    pallas_call x11, Pallas kernels, call(): pl.pallas_call(kernel, out_shape=outs, in_specs=[vmem] * len(ins), out_sp...  9.96 us
    ppermute x4, starting transfers between devices, exchange(): far_in = lax.ppermute(far_out, 'tile', far)  7.65 us
    ppermute x4, starting transfers between devices, exchange(): core_in = lax.ppermute(core_out, 'tile', core)  6.74 us
    ppermute x4, starting transfers between devices, exchange(): turn_in = lax.ppermute(turn_out, 'tile', sorted(turn))  6.69 us
    ppermute x4, starting transfers between devices, exchange(): near_in = lax.ppermute(near_out, 'tile', near)  3.43 us
    ppermute x4, waiting for transfers between devices, exchange(): turn_in = lax.ppermute(turn_out, 'tile', sorted(turn))  2.68 us
    unnamed x10, local copies, waits for them, and re-layouts  1.49 us
  transfers between devices with their start and end apart: 20, of which 5 were waited for; matrix products, arithmetic and copies ran while one was open for 0% of the time, Pallas kernels for 14%

profile of v9, /device:TPU:0, one launch (start us, length us, event | category | flops | bytes accessed | tf_op | source)
XLA Modules:
  0.0 39.1 jit_solution(3319121924464346806)
XLA Ops:
  0.1 0.6 %copy-done.2 = f32[3,128]{1,0:T(4,128)S(1)} copy-done((f32[3,128]{1,0:T(4,128)S(1)}, f32[3,128]{1,0:T(4,128)}, u32[]{:S(2)}) %copy-start.2) | copy-done | bytes 1560
  0.7 0.2 constants.1
  0.9 0.9 %copy-done = f32[1,6,6,128,128]{4,3,2,1,0:T(8,128)S(1)} copy-done((f32[1,6,6,128,128]{4,3,2,1,0:T(8,128)S(1)}, f32[1,6,6,128,128]{4,3,2,1,0:T(8,128)}, u32[]{:S(2)}) %copy-start) | copy-done | bytes 2359320
  1.8 0.6 %first_edges.1 = (f32[56,128]{1,0:T(8,128)S(1)}, f32[56,128]{1,0:T(8,128)S(1)}, f32[56,128]{1,0:T(8,128)S(1)}, f32[56,128]{1,0:T(8,128)S(1)}, f32[56,128]{1,0:T(...) custom-call(f32[6,6,128,128]{3,2,1,0:T(8,128)S(1)} %bitcast.4, f32[8,128]{1,0:T(8,128)S(1)} %get-tuple-element.57.refs_1_, ...), custom_call_target="tpu_custom_call" | custom-call | flops 1000000000 | bytes 2000000 | tf_op jit(solution)/shard_map/first_edges/pallas_call | solution.py:482
  2.3 5.1 %collective-permute-start = (f32[56,128]{1,0:T(8,128)S(1)}, f32[56,128]{1,0:T(8,128)S(1)}, u32[]{:S(2)}, u32[]{:S(2)}) collective-permute-start(f32[56,128]{1,0:T(8,128)S(1)} %get-tuple-element.59), channel_id=1, source_target_pairs={{0,12},{1,5},{2,6},{3,15},{4,8},{5,1},{6,2},{7,11},{8,4},{9,13},{1... | collective-permute-start | bytes 86024 | tf_op jit(solution)/shard_map/ppermute | solution.py:472
  7.5 0.5 %collective-permute-start.1 = (f32[56,128]{1,0:T(8,128)S(1)}, f32[56,128]{1,0:T(8,128)S(1)}, u32[]{:S(2)}, u32[]{:S(2)}) collective-permute-start(f32[56,128]{1,0:T(8,128)S(1)} %get-tuple-element.60), channel_id=1, source_target_pairs={{0,15},{1,11},{2,7},{3,6},{4,14},{5,10},{6,3},{7,2},{8,13},{9,12},... | collective-permute-start | bytes 86024 | tf_op jit(solution)/shard_map/ppermute | solution.py:471
  7.9 1.5 %collective-permute-start.2 = (f32[56,128]{1,0:T(8,128)S(1)}, f32[56,128]{1,0:T(8,128)S(1)}, u32[]{:S(2)}, u32[]{:S(2)}) collective-permute-start(f32[56,128]{1,0:T(8,128)S(1)} %get-tuple-element.61), channel_id=1, source_target_pairs={{0,4},{1,13},{2,14},{3,7},{4,0},{5,9},{6,10},{7,3},{8,12},{9,5},{1... | collective-permute-start | bytes 86024 | tf_op jit(solution)/shard_map/ppermute | solution.py:473
  9.4 1.5 %collective-permute-start.4 = (f32[56,128]{1,0:T(8,128)S(1)}, f32[56,128]{1,0:T(8,128)S(1)}, u32[]{:S(2)}, u32[]{:S(2)}) collective-permute-start(f32[56,128]{1,0:T(8,128)S(1)} %get-tuple-element.63), channel_id=1, source_target_pairs={{0,1},{1,0},{2,3},{3,2},{4,5},{5,4},{6,7},{7,6},{8,9},{9,8},{10,11... | collective-permute-start | bytes 86024 | tf_op jit(solution)/shard_map/ppermute | solution.py:475
  11.0 1.0 %inner.4 = (f32[6,6,128,128]{3,2,1,0:T(8,128)S(1)}, f32[128,128]{1,0:T(8,128)S(1)}, f32[128,128]{1,0:T(8,128)S(1)}) custom-call(f32[6,6,128,128]{3,2,1,0:T(8,128)S(1)} %bitcast.5, f32[8,128]{1,0:T(8,128)S(1)} %get-tuple-element.57.refs_1_, bf16[256,128]{1,0:T(8,128)(2,1)S(1)} %get-tuple-element.70.refs_2_, bf16[128,256]{1,0:T(8,128)(2,1)S(1)} %get-tuple-element.71.refs_3_, ...), custom_call_target="tpu_custom_call" | custom-call | flops 2000000000 | bytes 4000000 | tf_op jit(solution)/shard_map/inner/pallas_call | solution.py:482
  11.9 1.5 %collective-permute-done.1.refs_1_ = f32[56,128]{1,0:T(8,128)S(1)} collective-permute-done((f32[56,128]{1,0:T(8,128)S(1)}, f32[56,128]{1,0:T(8,128)S(1)}, u32[]{:S(2)}, u32[]{:S(2)}) %collective-permute-start.1) | collective-permute-done | bytes 28704 | tf_op jit(solution)/shard_map/ppermute | solution.py:471
  13.5 0.5 %edges.3 = (f32[128,128]{1,0:T(8,128)S(1)}, f32[128,128]{1,0:T(8,128)S(1)}, f32[56,128]{1,0:T(8,128)S(1)}, f32[56,128]{1,0:T(8,128)S(1)}, f32[56,128]{1,0:T(8,12...) custom-call(f32[56,128]{1,0:T(8,128)S(1)} %collective-permute-done.refs_0, ...), custom_call_target="tpu_custom_call" | custom-call | tf_op jit(solution)/shard_map/edges/pallas_call | solution.py:482
  14.0 0.8 %collective-permute-start.5 = (f32[56,128]{1,0:T(8,128)S(1)}, f32[56,128]{1,0:T(8,128)S(1)}, u32[]{:S(2)}, u32[]{:S(2)}) collective-permute-start(f32[56,128]{1,0:T(8,128)S(1)} %get-tuple-element.75), channel_id=1, source_target_pairs={{0,12},{1,5},{2,6},{3,15},{4,8},{5,1},{6,2},{7,11},{8,4},{9,13},{1... | collective-permute-start | bytes 86024 | tf_op jit(solution)/shard_map/ppermute | solution.py:472
  14.8 1.8 %collective-permute-start.6 = (f32[56,128]{1,0:T(8,128)S(1)}, f32[56,128]{1,0:T(8,128)S(1)}, u32[]{:S(2)}, u32[]{:S(2)}) collective-permute-start(f32[56,128]{1,0:T(8,128)S(1)} %get-tuple-element.76), channel_id=1, source_target_pairs={{0,15},{1,11},{2,7},{3,6},{4,14},{5,10},{6,3},{7,2},{8,13},{9,12},... | collective-permute-start | bytes 86024 | tf_op jit(solution)/shard_map/ppermute | solution.py:471
  16.6 0.6 %collective-permute-start.7 = (f32[56,128]{1,0:T(8,128)S(1)}, f32[56,128]{1,0:T(8,128)S(1)}, u32[]{:S(2)}, u32[]{:S(2)}) collective-permute-start(f32[56,128]{1,0:T(8,128)S(1)} %get-tuple-element.77), channel_id=1, source_target_pairs={{0,4},{1,13},{2,14},{3,7},{4,0},{5,9},{6,10},{7,3},{8,12},{9,5},{1... | collective-permute-start | bytes 86024 | tf_op jit(solution)/shard_map/ppermute | solution.py:473
  17.2 2.5 %collective-permute-start.9 = (f32[56,128]{1,0:T(8,128)S(1)}, f32[56,128]{1,0:T(8,128)S(1)}, u32[]{:S(2)}, u32[]{:S(2)}) collective-permute-start(f32[56,128]{1,0:T(8,128)S(1)} %get-tuple-element.79), channel_id=1, source_target_pairs={{0,1},{1,0},{2,3},{3,2},{4,5},{5,4},{6,7},{7,6},{8,9},{9,8},{10,11... | collective-permute-start | bytes 86024 | tf_op jit(solution)/shard_map/ppermute | solution.py:475
  19.7 1.6 %inner.5 = (f32[6,6,128,128]{3,2,1,0:T(8,128)S(1)}, f32[128,128]{1,0:T(8,128)S(1)}, f32[128,128]{1,0:T(8,128)S(1)}) custom-call(f32[6,6,128,128]{3,2,1,0:T(8,128)S(1)} %get-tuple-element.82.refs_0_, f32[8,128]{1,0:T(8,128)S(1)} %get-tuple-element.57.refs_1_, bf16[256,128]{1,0:T(8,128)(2,1)S(1)} %get-tuple-element.70.refs_2_, ...), custom_call_target="tpu_custom_call", output_to_operand_aliasing={{0}: (0, {})} | custom-call | flops 2000000000 | bytes 4000000 | tf_op jit(solution)/shard_map/inner/pallas_call | solution.py:482
  21.3 0.5 %edges.4 = (f32[128,128]{1,0:T(8,128)S(1)}, f32[128,128]{1,0:T(8,128)S(1)}, f32[56,128]{1,0:T(8,128)S(1)}, f32[56,128]{1,0:T(8,128)S(1)}, f32[56,128]{1,0:T(8,12...) custom-call(f32[56,128]{1,0:T(8,128)S(1)} %collective-permute-done.5.refs, ...), custom_call_target="tpu_custom_call" | custom-call | tf_op jit(solution)/shard_map/edges/pallas_call | solution.py:482
  21.8 1.3 %collective-permute-start.10 = (f32[56,128]{1,0:T(8,128)S(1)}, f32[56,128]{1,0:T(8,128)S(1)}, u32[]{:S(2)}, u32[]{:S(2)}) collective-permute-start(f32[56,128]{1,0:T(8,128)S(1)} %get-tuple-element.87), channel_id=1, source_target_pairs={{0,12},{1,5},{2,6},{3,15},{4,8},{5,1},{6,2},{7,11},{8,4},{9,13},{1... | collective-permute-start | bytes 86024 | tf_op jit(solution)/shard_map/ppermute | solution.py:472
  23.1 1.8 %collective-permute-start.11 = (f32[56,128]{1,0:T(8,128)S(1)}, f32[56,128]{1,0:T(8,128)S(1)}, u32[]{:S(2)}, u32[]{:S(2)}) collective-permute-start(f32[56,128]{1,0:T(8,128)S(1)} %get-tuple-element.88), channel_id=1, source_target_pairs={{0,15},{1,11},{2,7},{3,6},{4,14},{5,10},{6,3},{7,2},{8,13},{9,12},... | collective-permute-start | bytes 86024 | tf_op jit(solution)/shard_map/ppermute | solution.py:471
  24.9 1.0 %collective-permute-start.12 = (f32[56,128]{1,0:T(8,128)S(1)}, f32[56,128]{1,0:T(8,128)S(1)}, u32[]{:S(2)}, u32[]{:S(2)}) collective-permute-start(f32[56,128]{1,0:T(8,128)S(1)} %get-tuple-element.89), channel_id=1, source_target_pairs={{0,4},{1,13},{2,14},{3,7},{4,0},{5,9},{6,10},{7,3},{8,12},{9,5},{1... | collective-permute-start | bytes 86024 | tf_op jit(solution)/shard_map/ppermute | solution.py:473
  25.9 1.0 %collective-permute-start.14 = (f32[56,128]{1,0:T(8,128)S(1)}, f32[56,128]{1,0:T(8,128)S(1)}, u32[]{:S(2)}, u32[]{:S(2)}) collective-permute-start(f32[56,128]{1,0:T(8,128)S(1)} %get-tuple-element.91), channel_id=1, source_target_pairs={{0,1},{1,0},{2,3},{3,2},{4,5},{5,4},{6,7},{7,6},{8,9},{9,8},{10,11... | collective-permute-start | bytes 86024 | tf_op jit(solution)/shard_map/ppermute | solution.py:475
  26.8 1.6 %inner.6 = (f32[6,6,128,128]{3,2,1,0:T(8,128)S(1)}, f32[128,128]{1,0:T(8,128)S(1)}, f32[128,128]{1,0:T(8,128)S(1)}) custom-call(f32[6,6,128,128]{3,2,1,0:T(8,128)S(1)} %get-tuple-element.94.refs_0_, f32[8,128]{1,0:T(8,128)S(1)} %get-tuple-element.57.refs_1_, bf16[256,128]{1,0:T(8,128)(2,1)S(1)} %get-tuple-element.70.refs_2_, ...), custom_call_target="tpu_custom_call", output_to_operand_aliasing={{0}: (0, {})} | custom-call | flops 2000000000 | bytes 4000000 | tf_op jit(solution)/shard_map/inner/pallas_call | solution.py:482
  28.5 0.9 %collective-permute-done.11.refs_1_ = f32[56,128]{1,0:T(8,128)S(1)} collective-permute-done((f32[56,128]{1,0:T(8,128)S(1)}, f32[56,128]{1,0:T(8,128)S(1)}, u32[]{:S(2)}, u32[]{:S(2)}) %collective-permute-start.11) | collective-permute-done | bytes 28704 | tf_op jit(solution)/shard_map/ppermute | solution.py:471
  29.5 0.5 %edges.5 = (f32[128,128]{1,0:T(8,128)S(1)}, f32[128,128]{1,0:T(8,128)S(1)}, f32[56,128]{1,0:T(8,128)S(1)}, f32[56,128]{1,0:T(8,128)S(1)}, f32[56,128]{1,0:T(8,12...) custom-call(f32[56,128]{1,0:T(8,128)S(1)} %collective-permute-done.10.ref, ...), custom_call_target="tpu_custom_call" | custom-call | tf_op jit(solution)/shard_map/edges/pallas_call | solution.py:482
  30.0 0.4 %collective-permute-start.15 = (f32[56,128]{1,0:T(8,128)S(1)}, f32[56,128]{1,0:T(8,128)S(1)}, u32[]{:S(2)}, u32[]{:S(2)}) collective-permute-start(f32[56,128]{1,0:T(8,128)S(1)} %get-tuple-element.99), channel_id=1, source_target_pairs={{0,12},{1,5},{2,6},{3,15},{4,8},{5,1},{6,2},{7,11},{8,4},{9,13},{1... | collective-permute-start | bytes 86024 | tf_op jit(solution)/shard_map/ppermute | solution.py:472
  30.4 2.7 %collective-permute-start.16 = (f32[56,128]{1,0:T(8,128)S(1)}, f32[56,128]{1,0:T(8,128)S(1)}, u32[]{:S(2)}, u32[]{:S(2)}) collective-permute-start(f32[56,128]{1,0:T(8,128)S(1)} %get-tuple-element.100), channel_id=1, source_target_pairs={{0,15},{1,11},{2,7},{3,6},{4,14},{5,10},{6,3},{7,2},{8,13},{9,12},... | collective-permute-start | bytes 86024 | tf_op jit(solution)/shard_map/ppermute | solution.py:471
  33.1 0.4 collective-permute-start.17
  33.4 1.8 %collective-permute-start.19 = (f32[56,128]{1,0:T(8,128)S(1)}, f32[56,128]{1,0:T(8,128)S(1)}, u32[]{:S(2)}, u32[]{:S(2)}) collective-permute-start(f32[56,128]{1,0:T(8,128)S(1)} %get-tuple-element.103), channel_id=1, source_target_pairs={{0,1},{1,0},{2,3},{3,2},{4,5},{5,4},{6,7},{7,6},{8,9},{9,8},{10,11... | collective-permute-start | bytes 86024 | tf_op jit(solution)/shard_map/ppermute | solution.py:475
  35.2 1.3 %inner.7.refs_10_ = f32[6,6,128,128]{3,2,1,0:T(8,128)S(1)} custom-call(f32[6,6,128,128]{3,2,1,0:T(8,128)S(1)} %get-tuple-element.106.refs_0_, f32[8,128]{1,0:T(8,128)S(1)} %get-tuple-element.57.refs_1_, bf16[256,128]{1,0:T(8,128)(2,1)S(1)} %get-tuple-element.70.refs_2_, ...), custom_call_target="tpu_custom_call", output_to_operand_aliasing={{}: (0, {})} | custom-call | flops 2000000000 | bytes 4000000 | tf_op jit(solution)/shard_map/inner/pallas_call | solution.py:482
  36.5 0.2 collective-permute-done.16.refs_1_
  36.8 0.2 collective-permute-done.17.refs_2_
  36.9 2.2 %final.1 = f32[6,6,128,128]{3,2,1,0:T(8,128)} custom-call(f32[56,128]{1,0:T(8,128)S(1)} %collective-permute-done.15.refs_0_, f32[56,128]{1,0:T(8,128)S(1)} %collective-permute-done.16.refs_1_, f32[56,128]{1,0:T(8,128)S(1)} %collective-permute-done.17.refs_2_, f32[56,128]{1,0:T(8,128)S(1)} %collective-permute-done.18.refs_3_, ...), custom_call_target="tpu_custom_call" | custom-call | tf_op jit(solution)/shard_map/final/pallas_call | solution.py:482
  (29 shorter events, 0.3 us)
Async XLA Ops:
  0.0 0.7 %copy-start.2 = (f32[3,128]{1,0:T(4,128)S(1)}, f32[3,128]{1,0:T(4,128)}, u32[]{:S(2)}) copy-start(f32[3,128]{1,0:T(4,128)} %refs_3_.1) | copy-start | bytes 4612
  0.0 0.7 %copy-start.1 = (s32[3,128]{1,0:T(4,128)S(1)}, s32[3,128]{1,0:T(4,128)}, u32[]{:S(2)}) copy-start(s32[3,128]{1,0:T(4,128)} %refs_2_.1) | copy-start | bytes 4612
  0.0 0.7 %copy-start.4 = (f32[3]{0:T(128)S(1)}, f32[3]{0:T(128)}, u32[]{:S(2)}) copy-start(f32[3]{0:T(128)} %param.7) | copy-start | bytes 40
  0.0 0.7 %copy-start.3 = (f32[3]{0:T(128)S(1)}, f32[3]{0:T(128)}, u32[]{:S(2)}) copy-start(f32[3]{0:T(128)} %param.6) | copy-start | bytes 40
  0.1 1.7 %copy-start = (f32[1,6,6,128,128]{4,3,2,1,0:T(8,128)S(1)}, f32[1,6,6,128,128]{4,3,2,1,0:T(8,128)}, u32[]{:S(2)}) copy-start(f32[1,6,6,128,128]{4,3,2,1,0:T(8,128)} %param.5) | copy-start | bytes 7077892
  2.3 9.6 %collective-permute-start = (f32[56,128]{1,0:T(8,128)S(1)}, f32[56,128]{1,0:T(8,128)S(1)}, u32[]{:S(2)}, u32[]{:S(2)}) collective-permute-start(f32[56,128]{1,0:T(8,128)S(1)} %get-tuple-element.59), channel_id=1, source_target_pairs={{0,12},{1,5},{2,6},{3,15},{4,8},{5,1},{6,2},{7,11},{8,4},{9,13},{1... | collective-permute-start | bytes 86024 | tf_op jit(solution)/shard_map/ppermute | solution.py:472
  7.5 6.0 %collective-permute-start.1 = (f32[56,128]{1,0:T(8,128)S(1)}, f32[56,128]{1,0:T(8,128)S(1)}, u32[]{:S(2)}, u32[]{:S(2)}) collective-permute-start(f32[56,128]{1,0:T(8,128)S(1)} %get-tuple-element.60), channel_id=1, source_target_pairs={{0,15},{1,11},{2,7},{3,6},{4,14},{5,10},{6,3},{7,2},{8,13},{9,12},... | collective-permute-start | bytes 86024 | tf_op jit(solution)/shard_map/ppermute | solution.py:471
  7.9 5.5 %collective-permute-start.2 = (f32[56,128]{1,0:T(8,128)S(1)}, f32[56,128]{1,0:T(8,128)S(1)}, u32[]{:S(2)}, u32[]{:S(2)}) collective-permute-start(f32[56,128]{1,0:T(8,128)S(1)} %get-tuple-element.61), channel_id=1, source_target_pairs={{0,4},{1,13},{2,14},{3,7},{4,0},{5,9},{6,10},{7,3},{8,12},{9,5},{1... | collective-permute-start | bytes 86024 | tf_op jit(solution)/shard_map/ppermute | solution.py:473
  9.4 4.0 %collective-permute-start.3 = (f32[56,128]{1,0:T(8,128)S(1)}, f32[56,128]{1,0:T(8,128)S(1)}, u32[]{:S(2)}, u32[]{:S(2)}) collective-permute-start(f32[56,128]{1,0:T(8,128)S(1)} %get-tuple-element.62), channel_id=1, source_target_pairs={{0,3},{1,2},{2,1},{3,0},{4,7},{5,6},{6,5},{7,4},{8,11},{9,10},{10,... | collective-permute-start | bytes 86024 | tf_op jit(solution)/shard_map/ppermute | solution.py:474
  9.4 4.0 %collective-permute-start.4 = (f32[56,128]{1,0:T(8,128)S(1)}, f32[56,128]{1,0:T(8,128)S(1)}, u32[]{:S(2)}, u32[]{:S(2)}) collective-permute-start(f32[56,128]{1,0:T(8,128)S(1)} %get-tuple-element.63), channel_id=1, source_target_pairs={{0,1},{1,0},{2,3},{3,2},{4,5},{5,4},{6,7},{7,6},{8,9},{9,8},{10,11... | collective-permute-start | bytes 86024 | tf_op jit(solution)/shard_map/ppermute | solution.py:475
  14.0 7.3 %collective-permute-start.5 = (f32[56,128]{1,0:T(8,128)S(1)}, f32[56,128]{1,0:T(8,128)S(1)}, u32[]{:S(2)}, u32[]{:S(2)}) collective-permute-start(f32[56,128]{1,0:T(8,128)S(1)} %get-tuple-element.75), channel_id=1, source_target_pairs={{0,12},{1,5},{2,6},{3,15},{4,8},{5,1},{6,2},{7,11},{8,4},{9,13},{1... | collective-permute-start | bytes 86024 | tf_op jit(solution)/shard_map/ppermute | solution.py:472
  14.8 6.5 %collective-permute-start.6 = (f32[56,128]{1,0:T(8,128)S(1)}, f32[56,128]{1,0:T(8,128)S(1)}, u32[]{:S(2)}, u32[]{:S(2)}) collective-permute-start(f32[56,128]{1,0:T(8,128)S(1)} %get-tuple-element.76), channel_id=1, source_target_pairs={{0,15},{1,11},{2,7},{3,6},{4,14},{5,10},{6,3},{7,2},{8,13},{9,12},... | collective-permute-start | bytes 86024 | tf_op jit(solution)/shard_map/ppermute | solution.py:471
  16.6 4.7 %collective-permute-start.7 = (f32[56,128]{1,0:T(8,128)S(1)}, f32[56,128]{1,0:T(8,128)S(1)}, u32[]{:S(2)}, u32[]{:S(2)}) collective-permute-start(f32[56,128]{1,0:T(8,128)S(1)} %get-tuple-element.77), channel_id=1, source_target_pairs={{0,4},{1,13},{2,14},{3,7},{4,0},{5,9},{6,10},{7,3},{8,12},{9,5},{1... | collective-permute-start | bytes 86024 | tf_op jit(solution)/shard_map/ppermute | solution.py:473
  17.2 4.2 %collective-permute-start.8 = (f32[56,128]{1,0:T(8,128)S(1)}, f32[56,128]{1,0:T(8,128)S(1)}, u32[]{:S(2)}, u32[]{:S(2)}) collective-permute-start(f32[56,128]{1,0:T(8,128)S(1)} %get-tuple-element.78), channel_id=1, source_target_pairs={{0,3},{1,2},{2,1},{3,0},{4,7},{5,6},{6,5},{7,4},{8,11},{9,10},{10,... | collective-permute-start | bytes 86024 | tf_op jit(solution)/shard_map/ppermute | solution.py:474
  17.2 4.2 %collective-permute-start.9 = (f32[56,128]{1,0:T(8,128)S(1)}, f32[56,128]{1,0:T(8,128)S(1)}, u32[]{:S(2)}, u32[]{:S(2)}) collective-permute-start(f32[56,128]{1,0:T(8,128)S(1)} %get-tuple-element.79), channel_id=1, source_target_pairs={{0,1},{1,0},{2,3},{3,2},{4,5},{5,4},{6,7},{7,6},{8,9},{9,8},{10,11... | collective-permute-start | bytes 86024 | tf_op jit(solution)/shard_map/ppermute | solution.py:475
  21.8 6.6 %collective-permute-start.10 = (f32[56,128]{1,0:T(8,128)S(1)}, f32[56,128]{1,0:T(8,128)S(1)}, u32[]{:S(2)}, u32[]{:S(2)}) collective-permute-start(f32[56,128]{1,0:T(8,128)S(1)} %get-tuple-element.87), channel_id=1, source_target_pairs={{0,12},{1,5},{2,6},{3,15},{4,8},{5,1},{6,2},{7,11},{8,4},{9,13},{1... | collective-permute-start | bytes 86024 | tf_op jit(solution)/shard_map/ppermute | solution.py:472
  23.1 6.2 %collective-permute-start.11 = (f32[56,128]{1,0:T(8,128)S(1)}, f32[56,128]{1,0:T(8,128)S(1)}, u32[]{:S(2)}, u32[]{:S(2)}) collective-permute-start(f32[56,128]{1,0:T(8,128)S(1)} %get-tuple-element.88), channel_id=1, source_target_pairs={{0,15},{1,11},{2,7},{3,6},{4,14},{5,10},{6,3},{7,2},{8,13},{9,12},... | collective-permute-start | bytes 86024 | tf_op jit(solution)/shard_map/ppermute | solution.py:471
  24.9 4.5 %collective-permute-start.12 = (f32[56,128]{1,0:T(8,128)S(1)}, f32[56,128]{1,0:T(8,128)S(1)}, u32[]{:S(2)}, u32[]{:S(2)}) collective-permute-start(f32[56,128]{1,0:T(8,128)S(1)} %get-tuple-element.89), channel_id=1, source_target_pairs={{0,4},{1,13},{2,14},{3,7},{4,0},{5,9},{6,10},{7,3},{8,12},{9,5},{1... | collective-permute-start | bytes 86024 | tf_op jit(solution)/shard_map/ppermute | solution.py:473
  25.9 3.6 %collective-permute-start.13 = (f32[56,128]{1,0:T(8,128)S(1)}, f32[56,128]{1,0:T(8,128)S(1)}, u32[]{:S(2)}, u32[]{:S(2)}) collective-permute-start(f32[56,128]{1,0:T(8,128)S(1)} %get-tuple-element.90), channel_id=1, source_target_pairs={{0,3},{1,2},{2,1},{3,0},{4,7},{5,6},{6,5},{7,4},{8,11},{9,10},{10,... | collective-permute-start | bytes 86024 | tf_op jit(solution)/shard_map/ppermute | solution.py:474
  25.9 3.6 %collective-permute-start.14 = (f32[56,128]{1,0:T(8,128)S(1)}, f32[56,128]{1,0:T(8,128)S(1)}, u32[]{:S(2)}, u32[]{:S(2)}) collective-permute-start(f32[56,128]{1,0:T(8,128)S(1)} %get-tuple-element.91), channel_id=1, source_target_pairs={{0,1},{1,0},{2,3},{3,2},{4,5},{5,4},{6,7},{7,6},{8,9},{9,8},{10,11... | collective-permute-start | bytes 86024 | tf_op jit(solution)/shard_map/ppermute | solution.py:475
  30.0 6.5 %collective-permute-start.15 = (f32[56,128]{1,0:T(8,128)S(1)}, f32[56,128]{1,0:T(8,128)S(1)}, u32[]{:S(2)}, u32[]{:S(2)}) collective-permute-start(f32[56,128]{1,0:T(8,128)S(1)} %get-tuple-element.99), channel_id=1, source_target_pairs={{0,12},{1,5},{2,6},{3,15},{4,8},{5,1},{6,2},{7,11},{8,4},{9,13},{1... | collective-permute-start | bytes 86024 | tf_op jit(solution)/shard_map/ppermute | solution.py:472
  30.4 6.4 %collective-permute-start.16 = (f32[56,128]{1,0:T(8,128)S(1)}, f32[56,128]{1,0:T(8,128)S(1)}, u32[]{:S(2)}, u32[]{:S(2)}) collective-permute-start(f32[56,128]{1,0:T(8,128)S(1)} %get-tuple-element.100), channel_id=1, source_target_pairs={{0,15},{1,11},{2,7},{3,6},{4,14},{5,10},{6,3},{7,2},{8,13},{9,12},... | collective-permute-start | bytes 86024 | tf_op jit(solution)/shard_map/ppermute | solution.py:471
  33.1 3.9 %collective-permute-start.17 = (f32[56,128]{1,0:T(8,128)S(1)}, f32[56,128]{1,0:T(8,128)S(1)}, u32[]{:S(2)}, u32[]{:S(2)}) collective-permute-start(f32[56,128]{1,0:T(8,128)S(1)} %get-tuple-element.101), channel_id=1, source_target_pairs={{0,4},{1,13},{2,14},{3,7},{4,0},{5,9},{6,10},{7,3},{8,12},{9,5},{1... | collective-permute-start | bytes 86024 | tf_op jit(solution)/shard_map/ppermute | solution.py:473
  33.4 3.5 %collective-permute-start.18 = (f32[56,128]{1,0:T(8,128)S(1)}, f32[56,128]{1,0:T(8,128)S(1)}, u32[]{:S(2)}, u32[]{:S(2)}) collective-permute-start(f32[56,128]{1,0:T(8,128)S(1)} %get-tuple-element.102), channel_id=1, source_target_pairs={{0,3},{1,2},{2,1},{3,0},{4,7},{5,6},{6,5},{7,4},{8,11},{9,10},{10,... | collective-permute-start | bytes 86024 | tf_op jit(solution)/shard_map/ppermute | solution.py:474
  33.4 3.5 %collective-permute-start.19 = (f32[56,128]{1,0:T(8,128)S(1)}, f32[56,128]{1,0:T(8,128)S(1)}, u32[]{:S(2)}, u32[]{:S(2)}) collective-permute-start(f32[56,128]{1,0:T(8,128)S(1)} %get-tuple-element.103), channel_id=1, source_target_pairs={{0,1},{1,0},{2,3},{3,2},{4,5},{5,4},{6,7},{7,6},{8,9},{9,8},{10,11... | collective-permute-start | bytes 86024 | tf_op jit(solution)/shard_map/ppermute | solution.py:475
